TPU v7x, 32 devices: a whole 2x2x4 slice. The times are simulated.
32 devices in a mesh: rep: 4 (over y, core), wide: 8 (over z, x).
Axes of the slice: x: 2, y: 2, z: 4, core: 2. Of those that a mesh axis runs over, the one named last changes fastest.
Arguments:
- tokens: bfloat16 [32768, 768], P(('rep', 'wide')), may hold values from -6 to 6
- segment_ids: int32 [64, 512], P(('rep', 'wide')), may hold values from 0 to 3, never falling along the last dimension, each value on 1 to 256 neighbouring positions
- cotangent: bfloat16 [32768, 768], P(('rep', 'wide')), may hold values from -6 to 6
- w_query: bfloat16 [768, 768], P('rep'), may hold values from -0.21875 to 0.21875
- w_key: bfloat16 [768, 768], P('rep'), may hold values from -0.21875 to 0.21875
- w_value: bfloat16 [768, 768], P('rep'), may hold values from -0.21875 to 0.21875
- w_output: bfloat16 [768, 768], P('rep'), may hold values from -0.625 to 0.625
- w_inner: bfloat16 [768, 3072], P('rep'), may hold values from -0.21875 to 0.21875
- w_outer: bfloat16 [3072, 768], P('rep'), may hold values from -0.109375 to 0.109375
- b_query: float32 [768], replicated, may hold values from -3 to 3
- b_value: float32 [768], replicated, may hold values from -3 to 3
- b_output: float32 [768], replicated, may hold values from -3 to 3
- b_inner: float32 [3072], replicated, may hold values from -3 to 3
- b_outer: float32 [768], replicated, may hold values from -3 to 3
- norm1_gain: float32 [768], replicated, may hold values from 0.5 to 1.5
- norm1_shift: float32 [768], replicated, may hold values from -3 to 3
- norm2_gain: float32 [768], replicated, may hold values from 0.5 to 1.5
- norm2_shift: float32 [768], replicated, may hold values from -3 to 3
- factors: float32 [24576], replicated, may hold values from -3 to 3, as said below
- first_moment: float32 [24576], P('wide'), may hold values from -0.005740992 to 0.005740992
- second_moment: float32 [24576], P('wide'), may hold values from 2.0345052e-08 to 2.0345052e-07
Outputs:
- layer_out: bfloat16 [32768, 768], P(('rep', 'wide'))
- input_grad: bfloat16 [32768, 768], P(('rep', 'wide'))
- factor_grads: float32 [24576], P('wide')
- new_factors: float32 [24576], replicated
- new_first: float32 [24576], P('wide')
- new_second: float32 [24576], P('wide')
Inputs may be any that keep to these rules, and one draw needn't show every extreme that they name: `factors`: entries of the A half are at most a few times 768^-0.5 in size, those of the B half at most a few times 8^-0.5.
All inputs are finite; a program needn't handle non-finite values.
Results may differ from a plain program's by a relative error of at most 0.028.
The roundings to bfloat16 on the way count: a program that leaves them out, or rounds other values in their place, can miss the bound.
Values may be sent and summed in bfloat16 or wider, within the bound.
No kernel may reach another device: no remote copies, remote signals or barrier semaphores. Data moves between devices by JAX's collectives and lax.ppermute only.
A program may use at most 192 MiB of HBM per device.

v0:
```python
import jax
import jax.numpy as jnp
from jax import lax
from jax.sharding import PartitionSpec as P

HEADS = 12
ADAPTER_RANK = 8
STEP = 10


rate_low = 0.015
rate_high = 0.24
decay_rate = 0.01


def matrix_transposed(left, right):
    return lax.dot_general(
        left, right, (((1,), (1,)), ((), ())), preferred_element_type=jnp.float32
    )


def rows_transposed(left, right):
    return lax.dot_general(
        left, right, (((0,), (0,)), ((), ())), preferred_element_type=jnp.float32
    )


def layer_norm(hidden, gain, shift):
    mean = jnp.mean(hidden, -1, keepdims=True)
    centre = hidden - mean
    rstd = lax.rsqrt(jnp.mean(centre * centre, -1, keepdims=True) + 1e-05)
    normal = centre * rstd
    return (normal * gain + shift, normal, rstd)


def norm_back(grad, normal, rstd, gain):
    scaled = grad * gain
    return rstd * (
        scaled
        - jnp.mean(scaled, -1, keepdims=True)
        - normal * jnp.mean(scaled * normal, -1, keepdims=True)
    )


def masked_scores(query, key, seg):
    width = query.shape[1] // HEADS
    qh = query.reshape(-1, HEADS, width)
    kh = key.reshape(-1, HEADS, width)
    scores = jnp.einsum("qhd,khd->hqk", qh, kh, preferred_element_type=jnp.float32) * width ** (
        -0.5
    )
    same = seg[:, None] == seg[None, :]
    return jnp.where(same[None], scores, -1e30)


def attend(item):
    query, key, value, seg = item
    width = query.shape[1] // HEADS
    scores = masked_scores(query, key, seg)
    top = jnp.max(scores, -1, keepdims=True)
    expo = jnp.exp(scores - top)
    total = jnp.sum(expo, -1, keepdims=True)
    probs = expo / total
    vh = value.reshape(-1, HEADS, width)
    ctx = jnp.einsum(
        "hqk,khd->qhd", probs.astype(jnp.bfloat16), vh, preferred_element_type=jnp.float32
    )
    return (ctx.reshape(query.shape[0], -1), (top + jnp.log(total))[..., 0])


def attend_back(item):
    query, key, value, seg, lse, dctx = item
    width = query.shape[1] // HEADS
    scale = width ** (-0.5)
    probs = jnp.exp(masked_scores(query, key, seg) - lse[..., None])
    qh = query.reshape(-1, HEADS, width)
    kh = key.reshape(-1, HEADS, width)
    vh = value.reshape(-1, HEADS, width)
    dch = dctx.reshape(-1, HEADS, width)
    value_gradient = jnp.einsum(
        "hqk,qhd->khd", probs.astype(jnp.bfloat16), dch, preferred_element_type=jnp.float32
    )
    dprob = jnp.einsum("qhd,khd->hqk", dch, vh, preferred_element_type=jnp.float32)
    inner = jnp.sum(dprob * probs, -1, keepdims=True)
    dscore = (probs * (dprob - inner)).astype(jnp.bfloat16)
    query_gradient = (
        jnp.einsum("hqk,khd->qhd", dscore, kh, preferred_element_type=jnp.float32) * scale
    )
    dk = jnp.einsum("hqk,qhd->khd", dscore, qh, preferred_element_type=jnp.float32) * scale
    rows = query.shape[0]
    return (
        query_gradient.reshape(rows, -1),
        dk.reshape(rows, -1),
        value_gradient.reshape(rows, -1),
    )


def fetch(w_query, w_key, w_value, w_output, w_inner, w_outer):
    return (
        lax.all_gather(w_query, "rep", axis=0, tiled=True),
        lax.all_gather(w_key, "rep", axis=0, tiled=True),
        lax.all_gather(w_value, "rep", axis=0, tiled=True),
        lax.all_gather(w_output, "rep", axis=0, tiled=True),
        lax.all_gather(w_inner, "rep", axis=0, tiled=True),
        lax.all_gather(w_outer, "rep", axis=0, tiled=True),
    )


def run_forward(tokens, seg, weights, vectors, factors):
    wq, wk, wv, wo, w1, w2 = weights
    bq, bv, bo, bi, bo2, g1, s1, g2, s2 = vectors
    rd = factors.shape[0] // 4
    down_factors_pair = factors[: 2 * rd].reshape(2 * ADAPTER_RANK, -1).astype(jnp.bfloat16)
    query_factor = factors[2 * rd : 3 * rd].reshape(ADAPTER_RANK, -1).astype(jnp.bfloat16)
    value_factor = factors[3 * rd :].reshape(ADAPTER_RANK, -1).astype(jnp.bfloat16)
    adapter_factors = matrix_transposed(tokens, down_factors_pair).astype(jnp.bfloat16)
    query = (
        jnp.dot(tokens, wq, preferred_element_type=jnp.float32)
        + bq
        + 2.0
        * jnp.dot(
            adapter_factors[:, :ADAPTER_RANK], query_factor, preferred_element_type=jnp.float32
        )
    ).astype(jnp.bfloat16)
    key = jnp.dot(tokens, wk, preferred_element_type=jnp.float32).astype(jnp.bfloat16)
    value = (
        jnp.dot(tokens, wv, preferred_element_type=jnp.float32)
        + bv
        + 2.0
        * jnp.dot(
            adapter_factors[:, ADAPTER_RANK:], value_factor, preferred_element_type=jnp.float32
        )
    ).astype(jnp.bfloat16)
    count = seg.shape[0]
    width = tokens.shape[1]
    ctx, lse = lax.map(
        attend,
        (
            query.reshape(count, -1, width),
            key.reshape(count, -1, width),
            value.reshape(count, -1, width),
            seg,
        ),
    )
    ctx_low = ctx.reshape(-1, width).astype(jnp.bfloat16)
    attn = jnp.dot(ctx_low, wo, preferred_element_type=jnp.float32) + bo
    first, norm_one, rstd_one = layer_norm(tokens.astype(jnp.float32) + attn, g1, s1)
    first_low = first.astype(jnp.bfloat16)
    inner = jnp.dot(first_low, w1, preferred_element_type=jnp.float32) + bi
    act = jax.nn.gelu(inner, approximate=False).astype(jnp.bfloat16)
    ffn = jnp.dot(act, w2, preferred_element_type=jnp.float32) + bo2
    result, norm_two, rstd_two = layer_norm(first + ffn, g2, s2)
    return (
        query,
        key,
        value,
        lse,
        adapter_factors,
        norm_one,
        rstd_one,
        inner,
        norm_two,
        rstd_two,
        result,
        down_factors_pair,
        query_factor,
        value_factor,
    )


def local(
    tokens,
    segment_ids,
    cotangent,
    w_query,
    w_key,
    w_value,
    w_output,
    w_inner,
    w_outer,
    b_query,
    b_value,
    b_output,
    b_inner,
    b_outer,
    norm1_gain,
    norm1_shift,
    norm2_gain,
    norm2_shift,
    factors,
    first_moment,
    second_moment,
):
    vectors = (
        b_query,
        b_value,
        b_output,
        b_inner,
        b_outer,
        norm1_gain,
        norm1_shift,
        norm2_gain,
        norm2_shift,
    )
    weights = fetch(w_query, w_key, w_value, w_output, w_inner, w_outer)
    result = run_forward(tokens, segment_ids, weights, vectors, factors)[10]
    state = run_forward(tokens, segment_ids, weights, vectors, factors)
    wq, wk, wv, wo, w1, w2 = weights
    (
        query,
        key,
        value,
        lse,
        adapter_factors,
        norm_one,
        rstd_one,
        inner,
        norm_two,
        rstd_two,
        unused_out,
        down_factors_pair,
        query_factor,
        value_factor,
    ) = state
    layer_out = result.astype(jnp.bfloat16)
    dh2 = norm_back(cotangent.astype(jnp.float32), norm_two, rstd_two, norm2_gain)
    dact = matrix_transposed(dh2.astype(jnp.bfloat16), w2)
    pull = jax.vjp(lambda val: jax.nn.gelu(val, approximate=False), inner)[1]
    dinner = pull(dact)[0].astype(jnp.bfloat16)
    dfirst = dh2 + matrix_transposed(dinner, w1)
    dh1 = norm_back(dfirst, norm_one, rstd_one, norm1_gain)
    dctx = matrix_transposed(dh1.astype(jnp.bfloat16), wo).astype(jnp.bfloat16)
    count = segment_ids.shape[0]
    width = tokens.shape[1]
    query_gradient, dk, value_gradient = lax.map(
        attend_back,
        (
            query.reshape(count, -1, width),
            key.reshape(count, -1, width),
            value.reshape(count, -1, width),
            segment_ids,
            lse,
            dctx.reshape(count, -1, width),
        ),
    )
    query_gradient = query_gradient.reshape(-1, width).astype(jnp.bfloat16)
    dk = dk.reshape(-1, width).astype(jnp.bfloat16)
    value_gradient = value_gradient.reshape(-1, width).astype(jnp.bfloat16)
    dlora = jnp.concatenate(
        [
            2.0 * matrix_transposed(query_gradient, query_factor),
            2.0 * matrix_transposed(value_gradient, value_factor),
        ],
        axis=1,
    ).astype(jnp.bfloat16)
    dx = (
        dh1
        + matrix_transposed(query_gradient, wq)
        + matrix_transposed(dk, wk)
        + matrix_transposed(value_gradient, wv)
        + jnp.dot(dlora, down_factors_pair, preferred_element_type=jnp.float32)
    )
    input_grad = dx.astype(jnp.bfloat16)
    grad_a = rows_transposed(dlora, tokens)
    query_up_gradient = 2.0 * rows_transposed(adapter_factors[:, :ADAPTER_RANK], query_gradient)
    value_up_gradient = 2.0 * rows_transposed(adapter_factors[:, ADAPTER_RANK:], value_gradient)
    local_grad = jnp.concatenate(
        [grad_a.reshape(-1), query_up_gradient.reshape(-1), value_up_gradient.reshape(-1)]
    )
    summed = lax.psum(local_grad.astype(jnp.bfloat16), "rep")
    piece = lax.psum_scatter(summed, "wide", scatter_dimension=0, tiled=True).astype(jnp.float32)
    length = piece.shape[0]
    start = lax.axis_index("wide") * length
    own = lax.dynamic_slice_in_dim(factors, start, length)
    position = start + jnp.arange(length, dtype=jnp.int32)
    rate = jnp.where(position < factors.shape[0] // 2, rate_low, rate_high)
    squares = lax.psum(jnp.sum(piece * piece), "wide")
    clip = jnp.minimum(1.0, 1.0 / (jnp.sqrt(squares) + 1e-06))
    clipped = piece * clip
    new_first = 0.9 * first_moment + 0.1 * clipped
    new_second = 0.999 * second_moment + 0.001 * clipped * clipped
    steps_done = jnp.float32(STEP)
    fix_first = 1.0 - jnp.power(jnp.float32(0.9), steps_done)
    fix_second = 1.0 - jnp.power(jnp.float32(0.999), steps_done)
    update = new_first / fix_first / (jnp.sqrt(new_second / fix_second) + 1e-08) + decay_rate * own
    new_piece = own - rate * update
    new_factors = lax.all_gather(new_piece, "wide", axis=0, tiled=True)
    return (layer_out, input_grad, piece, new_factors, new_first, new_second)


def solution(mesh):
    placed = (
        P(("rep", "wide"), None),
        P(("rep", "wide"), None),
        P(("rep", "wide"), None),
        P("rep", None),
        P("rep", None),
        P("rep", None),
        P("rep", None),
        P("rep", None),
        P("rep", None),
        P(),
        P(),
        P(),
        P(),
        P(),
        P(),
        P(),
        P(),
        P(),
        P(),
        P("wide"),
        P("wide"),
    )
    return jax.shard_map(
        local,
        mesh=mesh,
        in_specs=placed,
        out_specs=(
            P(("rep", "wide"), None),
            P(("rep", "wide"), None),
            P("wide"),
            P(),
            P("wide"),
            P("wide"),
        ),
        check_vma=False,
    )
```

profile of v0, /device:TPU:0, one launch (start us, length us, event | category | flops | bytes accessed | tf_op | source)
XLA Modules:
  0.0 558.9 jit_solution(7465730519789743999)
XLA Ops:
  16.4 13.3 %all-gather.7.cloned.1.call-done = bf16[768,768]{1,0:T(8,128)(2,1)} async-done(((bf16[192,768]{1,0:T(8,128)(2,1)}), bf16[768,768]{1,0:T(8,128)(2,1)}) %all-gather.7.cloned.1.call-update) | async-done | bytes 1179664 | tf_op jit(solution)/shard_map/all_gather | solution.py:102
  29.8 2.7 fusion.123
  36.0 12.9 %all-gather.9.cloned.1.call-done = bf16[768,768]{1,0:T(8,128)(2,1)} async-done(((bf16[192,768]{1,0:T(8,128)(2,1)}), bf16[768,768]{1,0:T(8,128)(2,1)}) %all-gather.9.cloned.1.call-update) | async-done | bytes 1179664 | tf_op jit(solution)/shard_map/all_gather | solution.py:100
  48.8 2.7 fusion.124
  55.0 12.9 %all-gather.11.cloned.1.call-done = bf16[768,768]{1,0:T(8,128)(2,1)} async-done(((bf16[192,768]{1,0:T(8,128)(2,1)}), bf16[768,768]{1,0:T(8,128)(2,1)}) %all-gather.11.cloned.1.call-update) | async-done | bytes 1179664 | tf_op jit(solution)/shard_map/all_gather | solution.py:101
  67.9 4.3 convolution_convert_fusion.1
  72.2 2.6 copy.86
  76.0 49.0 %while.36 = (s32[]{:T(128)}, bf16[2,512,768]{2,1,0:T(8,128)(2,1)}, bf16[2,512,768]{1,2,0:T(8,128)(2,1)S(1)}, s32[2,512]{1,0:T(2,128)S(1)}, bf16[2,512,768]{1,2,0...) while((s32[]{:T(128)}, bf16[2,512,768]{2,1,0:T(8,128)(2,1)}, bf16[2,512,768]{1,2,0:T(8,128)(2,1)S(1)}, ...), condition=%wide.region_3.4_spmd, body=%wide.region_0.3_spmd.sunk | while | flops 824443392 | bytes 36756056 | solution.py:136
  76.0 2.5 constant_dynamic-slice_fusion.26
  78.7 10.5 %fusion.222 = (f32[12,512]{1,0:T(8,128)S(1)}, f32[12,512,512]{1,2,0:T(8,128)}) fusion(pred[512,512]{0,1:T(8,128)(4,1)S(1)} %broadcast_compare_fusion.6, bf16[512,12,64]{0,2,1:T(8,128)(2,1)} %bitcast.192, bf16[512,12,64]{0,2,1:T(8,128)(2,1)} %bitcast.191), kind=kOutput, calls=%fused_computation.204.clone.1 | convolution fusion | flops 415236608 | bytes 14442496 | tf_op jit(solution)/shard_map/while/body/eval_jaxpr/sub | solution.py:61
  89.3 6.7 %fusion.223 = bf16[12,64,512]{2,1,0:T(8,128)(2,1)} fusion(bf16[512,12,64]{0,2,1:T(8,128)(2,1)S(1)} %bitcast.190, f32[12,512,512]{1,2,0:T(8,128)} %get-tuple-element.444, f32[12,512]{1,0:T(8,128)S(1)} %get-tuple-element.445), kind=kOutput, calls=%fused_computation.8.clone.1 | convolution fusion | flops 408944640 | bytes 14180352 | tf_op jit(solution)/shard_map/while/body/eval_jaxpr/hqk,khd->qhd/dot_general | solution.py:65
  96.0 2.4 copy.145
  98.4 2.1 constant_dynamic-update-slice_fusion.9
  100.4 2.5 constant_dynamic-slice_fusion.26
  103.1 10.5 %fusion.222 = (f32[12,512]{1,0:T(8,128)S(1)}, f32[12,512,512]{1,2,0:T(8,128)}) fusion(pred[512,512]{0,1:T(8,128)(4,1)S(1)} %broadcast_compare_fusion.6, bf16[512,12,64]{0,2,1:T(8,128)(2,1)} %bitcast.192, bf16[512,12,64]{0,2,1:T(8,128)(2,1)} %bitcast.191), kind=kOutput, calls=%fused_computation.204.clone.1 | convolution fusion | flops 415236608 | bytes 14442496 | tf_op jit(solution)/shard_map/while/body/eval_jaxpr/sub | solution.py:61
  113.7 6.8 %fusion.223 = bf16[12,64,512]{2,1,0:T(8,128)(2,1)} fusion(bf16[512,12,64]{0,2,1:T(8,128)(2,1)S(1)} %bitcast.190, f32[12,512,512]{1,2,0:T(8,128)} %get-tuple-element.444, f32[12,512]{1,0:T(8,128)S(1)} %get-tuple-element.445), kind=kOutput, calls=%fused_computation.8.clone.1 | convolution fusion | flops 408944640 | bytes 14180352 | tf_op jit(solution)/shard_map/while/body/eval_jaxpr/hqk,khd->qhd/dot_general | solution.py:65
  120.4 2.3 copy.145
  122.7 2.1 constant_dynamic-update-slice_fusion.9
  125.0 3.9 fusion.118
  132.2 30.1 %while.37 = (s32[]{:T(128)}, bf16[2,512,768]{2,1,0:T(8,128)(2,1)}, f32[2,12,512]{2,1,0:T(8,128)S(1)}, bf16[2,512,768]{1,2,0:T(8,128)(2,1)S(1)}, s32[2,512]{1,0:T...) while((s32[]{:T(128)}, bf16[2,512,768]{2,1,0:T(8,128)(2,1)}, ...), condition=%wide.region_11.12_spmd, body=%wide.region_8.11_spmd.sunk | while | flops 843311104 | bytes 50035300 | solution.py:136
  133.8 2.1 fusion.227
  135.9 2.6 fusion.228
  138.6 4.4 fusion.229
  143.0 2.3 copy.146
  145.2 2.1 constant_dynamic-update-slice_fusion.10
  148.8 2.1 fusion.227
  150.9 2.6 fusion.228
  153.6 4.4 fusion.229
  158.0 2.3 copy.146
  160.2 2.1 constant_dynamic-update-slice_fusion.10
  162.3 5.1 fusion.116
  170.5 49.2 %fusion.47.clone.4 = bf16[1024,3072]{1,0:T(8,128)(2,1)} fusion(f32[3072]{0:T(1024)S(1)} %copy-done.52, bf16[768,3072]{1,0:T(8,128)(2,1)} %all-gather.15.cloned.1.call-done, f32[1024,768]{0,1:T(8,128)S(1)} %copy-done.16, f32[768]{0:T(1024)S(1)} %copy-done.55, f32[768]{0:T(1024)S(1)} %copy-done.56, ...), kind=kOutput, calls=%fused_computation.57.clone.clone.clone.clone.clone.clone.1 | convolution fusion | flops 5043388416 | bytes 14182400 | tf_op jit(solution)/shard_map/dot_general | solution.py:149
  219.7 9.1 %fusion.119 = (f32[1024]{0:T(1024)S(1)}, f32[1024,768]{0,1:T(8,128)S(1)}) fusion(f32[768]{0:T(1024)S(1)} %copy-done.54, bf16[3072,768]{1,0:T(8,128)(2,1)} %all-gather.17.cloned.1.call-done, f32[768]{0:T(1024)S(1)} %copy-done.55, f32[768]{0:T(1024)S(1)} %copy-done.56, f32[1024]{0:T(1024)S(1)} %add_rsqrt_fusion.3, f32[1024,768]{0,1:T(8,128)S(1)} %copy-done.16, ...), kind=kOutput, calls=%fused_computation.209 | convolution fusion | flops 4837342208 | bytes 17323008 | tf_op jit(solution)/shard_map/dot_general | solution.py:151
  229.3 2.6 copy-done.11
  231.9 36.4 %fusion.24 = (f32[1024,3072]{1,0:T(8,128)}, f32[1024,3072]{1,0:T(8,128)}) fusion(f32[3072]{0:T(1024)S(1)} %copy-done.52, bf16[768,3072]{1,0:T(8,128)(2,1)S(1)} %copy-done.49, f32[1024,768]{0,1:T(8,128)S(1)} %copy-done.11, f32[1024]{0:T(1024)S(1)} %add_rsqrt_fusion.1, f32[1024]{0:T(1024)S(1)} %broadcast_multiply_fusion.5, f32[768]{0:T(1024)S(1)} %copy-done.55, ...), kind=kOutput, calls=%fused_computation.58 | convolution fusion | flops 5033951232 | bytes 33056768 | tf_op jit(solution)/shard_map/dot_general | solution.py:149
  268.3 16.2 %fusion.117 = (f32[1024]{0:T(1024)S(1)}, f32[1024,768]{0,1:T(8,128)S(1)}) fusion(f32[768]{0:T(1024)S(1)} %copy-done.54, bf16[3072,768]{1,0:T(8,128)(2,1)} %all-gather.17.cloned.1.call-done, f32[1024,3072]{1,0:T(8,128)} %get-tuple-element.295, f32[1024,3072]{1,0:T(8,128)} %get-tuple-element.296, f32[3072]{0:T(1024)S(1)} %copy-done.52, ...), kind=kOutput, calls=%fused_computation.207 | convolution fusion | flops 4849925120 | bytes 36209664 | tf_op jit(solution)/shard_map/dot_general | solution.py:151
  286.3 3.6 fusion.43
  290.0 28.1 %fusion.112 = (f32[1024]{0:T(1024)S(1)}, f32[1024]{0:T(1024)S(1)}, f32[1024,768]{0,1:T(8,128)}) fusion(f32[1024]{0:T(1024)S(1)} %add_rsqrt_fusion.1, f32[1024,768]{0,1:T(8,128)} %copy-done.10, f32[1024]{0:T(1024)S(1)} %broadcast_multiply_fusion.5, f32[768]{0:T(1024)S(1)} %copy-done.56, bf16[768,3072]{1,0:T(8,128)(2,1)} %all-gather.15.cloned.1.call-done, ...), kind=kOutput, calls=%fused_computation.203 | convolution fusion | flops 9729734656 | bytes 45664256 | tf_op jit(solution)/shard_map/dot_general | solution.py:17
  318.1 6.4 %convolution_convert_fusion = bf16[1024,768]{1,0:T(8,128)(2,1)} fusion(bf16[768,768]{1,0:T(8,128)(2,1)} %all-gather.13.cloned.1.call-done, f32[1024,768]{0,1:T(8,128)} %get-tuple-element.303, f32[1024,768]{0,1:T(8,128)} %copy-done.10, f32[1024]{0:T(1024)S(1)} %broadcast_multiply_fusion, f32[1024]{0:T(1024)S(1)} %broadcast_multiply_fusion.1, ...), kind=kOutput, calls=%fused_computation.118 | convolution fusion | flops 1214251008 | bytes 9060352 | tf_op jit(solution)/shard_map/dot_general | solution.py:17
  328.3 110.6 %while.38 = (s32[]{:T(128)}, bf16[2,512,768]{2,1,0:T(8,128)(2,1)}, bf16[2,512,768]{2,1,0:T(8,128)(2,1)}, bf16[2,512,768]{2,1,0:T(8,128)(2,1)}, bf16[2,512,768]{1...) while((s32[]{:T(128)}, bf16[2,512,768]{2,1,0:T(8,128)(2,1)}, ...), condition=%wide.region_22.23_spmd, body=%wide.region_20.22_spmd.sunk | while | flops 2062280704 | bytes 189971728 | solution.py:235
  331.0 6.3 %fusion.240 = f32[12,512,512]{1,2,0:T(8,128)} fusion(bf16[512,12,64]{0,2,1:T(8,128)(2,1)S(1)} %bitcast.177, bf16[512,12,64]{0,2,1:T(8,128)(2,1)S(1)} %bitcast.175), kind=kOutput, calls=%fused_computation.210.clone.1 | convolution fusion | flops 402653184 | bytes 14155776 | tf_op jit(solution)/shard_map/while/body/eval_jaxpr/qhd,khd->hqk/dot_general | solution.py:49
  338.5 2.3 copy.147
  340.9 11.4 %multiply_reduce_fusion.9 = (f32[12,512]{1,0:T(8,128)S(1)}, f32[12,512,512]{1,2,0:T(8,128)}) fusion(f32[12,512,512]{1,2,0:T(8,128)} %fusion.240, f32[12,512]{1,0:T(8,128)S(1)} %dynamic-slice_bitcast_fusion.2, pred[512,512]{0,1:T(8,128)(4,1)S(1)} %broadcast_compare_fusion.8, bf16[512,12,64]{0,2,1:T(8,128)(2,1)} %bitcast.180, ...), kind=kOutput, calls=%fused_computation.34.clone.1 | convolution fusion | flops 418375680 | bytes 27049984 | tf_op jit(solution)/shard_map/while/body/eval_jaxpr/qhd,khd->hqk/dot_general | solution.py:83
  353.7 7.0 %multiply_convert_fusion.6 = bf16[12,512,512]{1,2,0:T(8,128)(2,1)S(1)} fusion(f32[12,512,512]{1,2,0:T(8,128)} %get-tuple-element.467, f32[12,512,512]{1,2,0:T(8,128)S(1)} %bitcast.174, f32[12,512]{1,0:T(8,128)S(1)} %get-tuple-element.468, f32[12,512]{1,0:T(8,128)S(1)} %dynamic-slice_bitcast_fusion.2, pred[512,512]{0,1:T(8,128)(4,1)S(1)} %broadcast_compare_fusion.8), kind=kLoop, calls=%fused_computation.33.clone.1 | loop fusion | flops 18874368 | bytes 31768576 | tf_op jit(solution)/shard_map/while/body/eval_jaxpr/convert_element_type | solution.py:85
  360.7 2.9 convolution_multiply_fusion.9
  365.0 8.8 %fusion.241 = bf16[12,64,512]{2,1,0:T(8,128)(2,1)} fusion(bf16[512,12,64]{0,2,1:T(8,128)(2,1)} %bitcast.181, f32[12,512,512]{1,2,0:T(8,128)} %fusion.240, f32[12,512]{1,0:T(8,128)S(1)} %dynamic-slice_bitcast_fusion.2, pred[512,512]{0,1:T(8,128)(4,1)S(1)} %broadcast_compare_fusion.8), kind=kOutput, calls=%fused_computation.37.clone.1 | convolution fusion | flops 415236096 | bytes 14442496 | tf_op jit(solution)/shard_map/while/body/eval_jaxpr/hqk,qhd->khd/dot_general | solution.py:80
  373.8 2.3 copy.149
  376.1 2.4 constant_dynamic-update-slice_fusion.12
  378.5 3.9 convolution_multiply_fusion.8
  386.0 6.3 %fusion.240 = f32[12,512,512]{1,2,0:T(8,128)} fusion(bf16[512,12,64]{0,2,1:T(8,128)(2,1)S(1)} %bitcast.177, bf16[512,12,64]{0,2,1:T(8,128)(2,1)S(1)} %bitcast.175), kind=kOutput, calls=%fused_computation.210.clone.1 | convolution fusion | flops 402653184 | bytes 14155776 | tf_op jit(solution)/shard_map/while/body/eval_jaxpr/qhd,khd->hqk/dot_general | solution.py:49
  393.6 2.3 copy.147
  395.9 11.4 %multiply_reduce_fusion.9 = (f32[12,512]{1,0:T(8,128)S(1)}, f32[12,512,512]{1,2,0:T(8,128)}) fusion(f32[12,512,512]{1,2,0:T(8,128)} %fusion.240, f32[12,512]{1,0:T(8,128)S(1)} %dynamic-slice_bitcast_fusion.2, pred[512,512]{0,1:T(8,128)(4,1)S(1)} %broadcast_compare_fusion.8, bf16[512,12,64]{0,2,1:T(8,128)(2,1)} %bitcast.180, ...), kind=kOutput, calls=%fused_computation.34.clone.1 | convolution fusion | flops 418375680 | bytes 27049984 | tf_op jit(solution)/shard_map/while/body/eval_jaxpr/qhd,khd->hqk/dot_general | solution.py:83
  408.8 7.0 %multiply_convert_fusion.6 = bf16[12,512,512]{1,2,0:T(8,128)(2,1)S(1)} fusion(f32[12,512,512]{1,2,0:T(8,128)} %get-tuple-element.467, f32[12,512,512]{1,2,0:T(8,128)S(1)} %bitcast.174, f32[12,512]{1,0:T(8,128)S(1)} %get-tuple-element.468, f32[12,512]{1,0:T(8,128)S(1)} %dynamic-slice_bitcast_fusion.2, pred[512,512]{0,1:T(8,128)(4,1)S(1)} %broadcast_compare_fusion.8), kind=kLoop, calls=%fused_computation.33.clone.1 | loop fusion | flops 18874368 | bytes 31768576 | tf_op jit(solution)/shard_map/while/body/eval_jaxpr/convert_element_type | solution.py:85
  415.8 2.9 convolution_multiply_fusion.9
  420.1 8.8 %fusion.241 = bf16[12,64,512]{2,1,0:T(8,128)(2,1)} fusion(bf16[512,12,64]{0,2,1:T(8,128)(2,1)} %bitcast.181, f32[12,512,512]{1,2,0:T(8,128)} %fusion.240, f32[12,512]{1,0:T(8,128)S(1)} %dynamic-slice_bitcast_fusion.2, pred[512,512]{0,1:T(8,128)(4,1)S(1)} %broadcast_compare_fusion.8), kind=kOutput, calls=%fused_computation.37.clone.1 | convolution fusion | flops 415236096 | bytes 14442496 | tf_op jit(solution)/shard_map/while/body/eval_jaxpr/hqk,qhd->khd/dot_general | solution.py:80
  428.9 2.3 copy.149
  431.2 2.4 constant_dynamic-update-slice_fusion.12
  433.6 3.9 convolution_multiply_fusion.8
  439.0 2.1 fusion.63
  444.3 37.5 %all-reduce = bf16[24576]{0:T(1024)(128)(2,1)S(1)} all-reduce(bf16[24576]{0:T(1024)(128)(2,1)S(1)} %pad_maximum_fusion), channel_id=2, replica_groups=mesh['rep'=4,'wide'=8] {'wide'}, use_global_device_ids=true, to_apply=%region_24.25.clone | all-reduce | flops 24576 | bytes 98304
  481.8 6.1 %psum.16 = bf16[3072]{0:T(1024)(128)(2,1)S(1)} all-reduce(bf16[3072]{0:T(1024)(128)(2,1)S(1)} %dynamic-slice.1), channel_id=1, replica_groups=mesh['rep'=4,'wide'=8] {'rep'}, use_global_device_ids=true, to_apply=%region_23.24 | all-reduce | flops 3072 | bytes 12288 | tf_op jit(solution)/shard_map/psum | solution.py:270
  488.6 17.7 %psum.15 = f32[]{:T(128)} all-reduce(f32[]{:T(128)} %get-tuple-element.276), channel_id=1, replica_groups=mesh['rep'=4,'wide'=8] {'wide'}, use_global_device_ids=true, to_apply=%region_26.27 | all-reduce | flops 1 | bytes 8 | tf_op jit(solution)/shard_map/psum | solution.py:277
  508.4 30.5 %all_gather.27 = f32[24576]{0:T(1024)S(1)} all-gather(f32[3072]{0:T(1024)S(1)} %get-tuple-element.273), channel_id=1, replica_groups=mesh['rep'=4,'wide'=8] {'wide'}, dimensions={0}, use_global_device_ids=true | all-gather | bytes 110592 | tf_op jit(solution)/shard_map/all_gather | solution.py:287
  538.9 2.8 fusion.125
  (236 shorter events, 62.9 us)
Async XLA Ops:
  7.2 4.0 copy-start.29
  7.2 4.1 copy-start.4
  7.2 22.6 %all-gather.7.cloned.1.call-start = ((), (), s32[]{:S(2)}) async-start(), calls=%async_computation | async-start | bytes 1474560 | tf_op jit(solution)/shard_map/all_gather | solution.py:102
  7.9 40.9 %all-gather.9.cloned.1.call-start = ((), (), s32[]{:S(2)}) async-start(), calls=%async_computation.1 | async-start | bytes 1474560 | tf_op jit(solution)/shard_map/all_gather | solution.py:100
  8.7 59.2 %all-gather.11.cloned.1.call-start = ((), (), s32[]{:S(2)}) async-start(), calls=%async_computation.2 | async-start | bytes 1474560 | tf_op jit(solution)/shard_map/all_gather | solution.py:101
  9.4 115.6 %all-gather.13.cloned.1.call-start = ((), (), s32[]{:S(2)}) async-start(), calls=%async_computation.3 | async-start | bytes 1474560 | tf_op jit(solution)/shard_map/all_gather | solution.py:103
  10.0 159.6 %all-gather.15.cloned.1.call-start = ((), (), s32[]{:S(2)}) async-start(), calls=%async_computation.4 | async-start | bytes 5898240 | tf_op jit(solution)/shard_map/all_gather | solution.py:104
  10.6 3.0 copy-start.18
  10.6 209.1 %all-gather.17.cloned.1.call-start = ((), (), s32[]{:S(2)}) async-start(), calls=%async_computation.5 | async-start | bytes 5898240 | tf_op jit(solution)/shard_map/all_gather | solution.py:105
  11.3 3.9 copy-start.27
  12.9 2.3 copy-start.57
  13.5 38.0 %copy-start.22 = (bf16[1024,16]{0,1:T(8,128)(2,1)}, bf16[1024,16]{0,1:T(8,128)(2,1)S(1)}, u32[]{:S(2)}) copy-start(bf16[1024,16]{0,1:T(8,128)(2,1)S(1)} %convolution_convert_fusion.2) | copy-start | bytes 98308
  13.5 19.0 %copy-start.30 = (bf16[8,768]{1,0:T(8,128)(2,1)}, bf16[8,768]{1,0:T(8,128)(2,1)S(1)}, u32[]{:S(2)}) copy-start(bf16[8,768]{1,0:T(8,128)(2,1)S(1)} %convert_element_type.118) | copy-start | bytes 36868
  13.6 38.0 %copy-start.32 = (bf16[8,768]{1,0:T(8,128)(2,1)}, bf16[8,768]{1,0:T(8,128)(2,1)S(1)}, u32[]{:S(2)}) copy-start(bf16[8,768]{1,0:T(8,128)(2,1)S(1)} %convert_element_type.120) | copy-start | bytes 36868
  16.4 16.0 %copy-start.45 = (f32[768]{0:T(1024)S(1)}, f32[768]{0:T(1024)}, u32[]{:S(2)}) copy-start(f32[768]{0:T(1024)} %param.37) | copy-start | bytes 9220
  36.0 15.6 %copy-start.46 = (f32[768]{0:T(1024)S(1)}, f32[768]{0:T(1024)}, u32[]{:S(2)}) copy-start(f32[768]{0:T(1024)} %param.36) | copy-start | bytes 9220
  72.2 3.8 copy-start.24
  76.0 49.0 %copy-start.53 = (f32[768]{0:T(1024)S(1)}, f32[768]{0:T(1024)}, u32[]{:S(2)}) copy-start(f32[768]{0:T(1024)} %param.38) | copy-start | bytes 9220
  162.3 5.1 copy-start.1
  162.3 5.1 copy-start.3
  162.3 5.1 copy-start.20
  162.3 5.1 copy-start.25
  167.5 2.1 copy-start.52
  167.5 2.1 copy-start.55
  167.5 2.1 copy-start.56
  167.5 3.0 copy-start.16
  167.5 150.6 %copy-start.35 = (f32[1024]{0:T(1024)}, f32[1024]{0:T(1024)S(1)}, u32[]{:S(2)}) copy-start(f32[1024]{0:T(1024)S(1)} %broadcast_multiply_fusion.5) | copy-start | bytes 12292
  169.5 148.6 %copy-start.37 = (f32[1024]{0:T(1024)}, f32[1024]{0:T(1024)S(1)}, u32[]{:S(2)}) copy-start(f32[1024]{0:T(1024)S(1)} %add_rsqrt_fusion.1) | copy-start | bytes 12292
  169.5 50.2 %copy-start.54 = (f32[768]{0:T(1024)S(1)}, f32[768]{0:T(1024)}, u32[]{:S(2)}) copy-start(f32[768]{0:T(1024)} %param.40) | copy-start | bytes 9220
  219.7 9.5 %copy-start.49 = (bf16[768,3072]{1,0:T(8,128)(2,1)S(1)}, bf16[768,3072]{1,0:T(8,128)(2,1)}, u32[]{:S(2)}) copy-start(bf16[768,3072]{1,0:T(8,128)(2,1)} %all-gather.15.cloned.1.call-done) | copy-start | bytes 14155780
  228.8 39.4 %copy-start.8 = (f32[1024,768]{0,1:T(8,128)}, f32[1024,768]{0,1:T(8,128)S(1)}, u32[]{:S(2)}) copy-start(f32[1024,768]{0,1:T(8,128)S(1)} %get-tuple-element.302) | copy-start | bytes 9437188
  228.8 3.0 copy-start.11
  284.4 1.9 copy-start.9
  318.1 6.4 %copy-start.39 = (f32[1024]{0:T(1024)}, f32[1024]{0:T(1024)S(1)}, u32[]{:S(2)}) copy-start(f32[1024]{0:T(1024)S(1)} %broadcast_multiply_fusion) | copy-start | bytes 12292
  318.1 6.4 %copy-start.41 = (f32[1024]{0:T(1024)}, f32[1024]{0:T(1024)S(1)}, u32[]{:S(2)}) copy-start(f32[1024]{0:T(1024)S(1)} %broadcast_multiply_fusion.1) | copy-start | bytes 12292
  324.5 3.8 copy-start.2
  324.5 3.8 copy-start.21
  324.5 3.8 copy-start.26
  328.3 110.7 %copy-start.33 = (bf16[8,768]{1,0:T(8,128)(2,1)S(1)}, bf16[8,768]{1,0:T(8,128)(2,1)}, u32[]{:S(2)}) copy-start(bf16[8,768]{1,0:T(8,128)(2,1)} %copy-done.32) | copy-start | bytes 36868
  328.3 112.8 %copy-start.23 = (bf16[1024,16]{0,1:T(8,128)(2,1)S(1)}, bf16[1024,16]{0,1:T(8,128)(2,1)}, u32[]{:S(2)}) copy-start(bf16[1024,16]{0,1:T(8,128)(2,1)} %copy-done.22) | copy-start | bytes 98308
  330.9 6.6 %copy-start.13 = (bf16[2,512,768]{2,1,0:T(8,128)(2,1)S(1)}, bf16[2,512,768]{2,1,0:T(8,128)(2,1)}, u32[]{:S(2)}) copy-start(bf16[2,512,768]{2,1,0:T(8,128)(2,1)} %get-tuple-element.546) | copy-start | bytes 4718596 | tf_op jit(solution)/shard_map/while
  340.9 11.5 %slice-start = ((s8[12582912]{0:T(1024)(128)(4,1)}), s8[4194304]{0:T(1024)(128)(4,1)S(1)}, s32[]{:S(2)}) async-start(s8[12582912]{0:T(1024)(128)(4,1)} %bitcast.173), calls=%async_computation.6 | async-start | bytes 8388608 | tf_op jit(solution)/shard_map/while
  340.9 11.5 %slice-start.1 = ((s8[12582912]{0:T(1024)(128)(4,1)}), s8[4194304]{0:T(1024)(128)(4,1)S(1)}, s32[]{:S(2)}) async-start(s8[12582912]{0:T(1024)(128)(4,1)} %bitcast.173), calls=%async_computation.7 | async-start | bytes 8388608 | tf_op jit(solution)/shard_map/while
  340.9 12.8 %slice-start.2 = ((s8[12582912]{0:T(1024)(128)(4,1)}), s8[4194304]{0:T(1024)(128)(4,1)S(1)}, s32[]{:S(2)}) async-start(s8[12582912]{0:T(1024)(128)(4,1)} %bitcast.173), calls=%async_computation.8 | async-start | bytes 8388608 | tf_op jit(solution)/shard_map/while
  360.7 2.9 copy-start
  386.0 6.6 %copy-start.13 = (bf16[2,512,768]{2,1,0:T(8,128)(2,1)S(1)}, bf16[2,512,768]{2,1,0:T(8,128)(2,1)}, u32[]{:S(2)}) copy-start(bf16[2,512,768]{2,1,0:T(8,128)(2,1)} %get-tuple-element.546) | copy-start | bytes 4718596 | tf_op jit(solution)/shard_map/while
  395.9 11.5 %slice-start = ((s8[12582912]{0:T(1024)(128)(4,1)}), s8[4194304]{0:T(1024)(128)(4,1)S(1)}, s32[]{:S(2)}) async-start(s8[12582912]{0:T(1024)(128)(4,1)} %bitcast.173), calls=%async_computation.6 | async-start | bytes 8388608 | tf_op jit(solution)/shard_map/while
  395.9 11.5 %slice-start.1 = ((s8[12582912]{0:T(1024)(128)(4,1)}), s8[4194304]{0:T(1024)(128)(4,1)S(1)}, s32[]{:S(2)}) async-start(s8[12582912]{0:T(1024)(128)(4,1)} %bitcast.173), calls=%async_computation.7 | async-start | bytes 8388608 | tf_op jit(solution)/shard_map/while
  395.9 12.8 %slice-start.2 = ((s8[12582912]{0:T(1024)(128)(4,1)}), s8[4194304]{0:T(1024)(128)(4,1)S(1)}, s32[]{:S(2)}) async-start(s8[12582912]{0:T(1024)(128)(4,1)} %bitcast.173), calls=%async_computation.8 | async-start | bytes 8388608 | tf_op jit(solution)/shard_map/while
  415.7 2.9 copy-start
  439.0 4.0 copy-start.7
  439.0 4.0 copy-start.31
  439.0 4.8 copy-start.5
  441.1 66.0 %copy-start.43 = (f32[3072]{0:T(1024)S(1)}, f32[3072]{0:T(1024)}, u32[]{:S(2)}) copy-start(f32[3072]{0:T(1024)} %param.47) | copy-start | bytes 36868
  441.1 65.9 %copy-start.44 = (f32[3072]{0:T(1024)S(1)}, f32[3072]{0:T(1024)}, u32[]{:S(2)}) copy-start(f32[3072]{0:T(1024)} %param.46) | copy-start | bytes 36868
  441.1 97.8 %copy-start.6 = (bf16[2,512,768]{2,1,0:T(8,128)(2,1)S(1)}, bf16[2,512,768]{2,1,0:T(8,128)(2,1)}, u32[]{:S(2)}) copy-start(bf16[2,512,768]{2,1,0:T(8,128)(2,1)} %get-tuple-element.133) | copy-start | bytes 4718596
  488.6 53.2 %copy-start.34 = (f32[3072]{0:T(1024)}, f32[3072]{0:T(1024)S(1)}, u32[]{:S(2)}) copy-start(f32[3072]{0:T(1024)S(1)} %get-tuple-element.557) | copy-start | bytes 36868
  538.9 2.8 copy-start.50
  543.5 2.8 copy-start.17
  543.5 2.8 copy-start.28
  543.5 2.8 copy-start.36
  543.5 2.8 copy-start.38
  543.5 2.8 copy-start.40
  543.5 2.8 copy-start.42
  (8 other events, 13.7 us)
Sparse Core Ops, SparseCore 0:
  9.6 20.1 all-gather.6
  31.3 17.4 all-gather.8
  50.4 17.4 all-gather.10
  69.3 17.4 all-gather.12
  88.2 37.4 all-gather.14
  127.1 37.4 all-gather.16
where the time goes:
time: 570 us; the launch traced here: 559 us
  matrix products  294 us (52%)
  blocking collectives  91.9 us (16%)
  local copies, waits for them, and re-layouts  84.3 us (15%)
  waiting for transfers between devices  42.7 us (7%)
  other arithmetic  27.6 us (5%)
  between operations  16.8 us (3%)
    dot_general x2, matrix products, run_forward(): inner = jnp.dot(first_low, w1, preferred_element_type=jnp.float32) + bi  85.6 us
    dot_general x8, matrix products, matrix_transposed(): lax.dot_general(left, right, (((1,), (1,)), ((), ())), preferred_element_...  43.1 us
    unnamed x1, blocking collectives  37.5 us
    dynamic_update_slice x18, local copies, waits for them, and re-layouts, run_forward(): lax.map(attend, (query.reshape(count, -1, width), key.reshape(count, -1,...  32.1 us
    all_gather x1, blocking collectives, local(): new_factors = lax.all_gather(new_piece, 'wide', axis=0, tiled=True)  30.5 us
    dot_general x2, matrix products, run_forward(): ffn = jnp.dot(act, w2, preferred_element_type=jnp.float32) + bo2  25.3 us
    dot_general x2, matrix products, attend_back(): jnp.einsum('qhd,khd->hqk', dch, vh, preferred_element_type=jnp.float32)  22.9 us
    dot_general x4, matrix products, attend(): jnp.einsum('hqk,khd->qhd', probs.astype(jnp.bfloat16), vh, preferred_elem...  22.2 us
  transfers between devices with their start and end apart: 6, of which 3 were waited for; matrix products, arithmetic and copies ran while one was open for 29% of the time, Pallas kernels for 0%

commit v1 on v0

v1 whole, which is shorter than its diff:
```python
import functools

import jax
import jax.numpy as jnp
from jax import lax
from jax.experimental import pallas as pl
from jax.experimental.pallas import tpu as pltpu
from jax.sharding import PartitionSpec as P

HEADS = 12
ADAPTER_RANK = 8
STEP = 10
LANES = 128
MASKED = 1e30

rate_low = 0.015
rate_high = 0.24
decay_rate = 0.01

BF16 = jnp.bfloat16
F32 = jnp.float32
NN = (((1,), (0,)), ((), ()))
NT = (((1,), (1,)), ((), ()))
TN = (((0,), (0,)), ((), ()))
ANY = pl.BlockSpec(memory_space=pl.ANY)
VMEM_LIMIT = 56 * 2**20


def dot(left, right, dims):
    return lax.dot_general(left, right, dims, preferred_element_type=F32)


def beside(*parts):
    return jnp.concatenate(parts, axis=1)


def mean(value):
    return jnp.mean(value, -1, keepdims=True)


def layer_norm(hidden):
    centre = hidden - mean(hidden)
    rstd = lax.rsqrt(mean(centre * centre) + 1e-05)
    return (centre * rstd, rstd)


def norm_back(grad, normal, rstd, gain):
    scaled = grad * gain
    return rstd * (scaled - mean(scaled) - normal * mean(scaled * normal))


def gelu_pair(value):
    below = 0.5 + 0.5 * lax.erf(value * 2.0 ** (-0.5))
    density = jnp.exp(-0.5 * value * value) * 0.3989422804014327
    return (value * below, below + value * density)


def three_parts(value):
    high = value.astype(BF16).astype(F32)
    rest = value - high
    middle = rest.astype(BF16).astype(F32)
    return (high, middle, rest - middle)


def pieces(rank, refs, target, semaphores):
    rows = refs[0].shape[0]
    return [
        pltpu.make_async_copy(
            ref,
            target.at[pl.ds(pl.multiple_of(jnp.bitwise_xor(rank, flip) * rows, 16), rows)],
            semaphores.at[flip],
        )
        for flip, ref in enumerate(refs)
    ]


def attend_kernel(group, rank_ref, seg_ref, x_ref, fac_ref, bq_ref, bv_ref, *rest):
    shards, rest = rest[:group], rest[group:]
    q_ref, k_ref, v_ref, ctx_ref, aug_ref, down_ref, weights, low, semaphores = rest
    at = pl.program_id(1)
    width = q_ref.shape[1]
    total = x_ref.shape[1]
    rows = x_ref.shape[0]

    @pl.when((pl.program_id(0) == 0) & (at == 0))
    def _():
        copies = pieces(rank_ref[0], shards, weights, semaphores)
        for copy in copies:
            copy.start()
        for copy in copies:
            copy.wait()

    rank2 = 2 * ADAPTER_RANK

    @pl.when(at == 0)
    def _():
        down = fac_ref[0:rank2, :].astype(BF16)
        low[...] = dot(x_ref[...], down, NT).astype(BF16)
        down_ref[...] = low[...]

    start = pl.multiple_of(at * width, LANES)
    columns = pl.ds(start, width)
    up = fac_ref[rank2 : 2 * rank2, columns]
    row = lax.broadcasted_iota(jnp.int32, up.shape, 0)
    up_q = jnp.where(row < ADAPTER_RANK, up, 0.0).astype(BF16)
    up_v = jnp.where(row < ADAPTER_RANK, 0.0, up).astype(BF16)
    x = x_ref[...]
    q_ref[...] = (
        dot(x, weights[:, columns], NN) + bq_ref[:, columns] + 2.0 * dot(low[...], up_q, NN)
    ).astype(BF16)
    k_ref[...] = dot(
        x, weights[:, pl.ds(pl.multiple_of(total + start, LANES), width)], NN
    ).astype(BF16)
    v_ref[...] = (
        dot(x, weights[:, pl.ds(pl.multiple_of(2 * total + start, LANES), width)], NN)
        + bv_ref[:, columns]
        + 2.0 * dot(low[...], up_v, NN)
    ).astype(BF16)

    lane = lax.broadcasted_iota(jnp.int32, (rows, LANES), 1)
    seg = seg_ref[0].astype(F32).T.astype(jnp.int32)
    own = jnp.where(lane == seg, 1.0, 0.0)
    aug_k = jnp.where((lane < 4) & (lane != seg), -MASKED, 0.0).astype(BF16)
    aug_q = own.astype(BF16)
    ones = jnp.ones((rows, LANES), BF16)
    half = LANES // 2
    scale = BF16(half ** (-0.5))
    for pair in range(width // LANES):
        here = slice(LANES * pair, LANES * (pair + 1))
        keys = beside(k_ref[:, here], aug_k)
        values = beside(v_ref[:, here], ones)
        query = q_ref[:, here] * scale
        out = None
        for side in range(2):
            mask = (lane // half) == side
            scores = dot(beside(jnp.where(mask, query, BF16(0)), aug_q), keys, NT)
            top = jnp.max(scores, axis=1, keepdims=True)
            expo = jnp.exp(scores - top).astype(BF16)
            both = dot(expo, values, NN)
            sums = both[:, LANES:]
            ctx = both[:, :LANES] / sums
            out = ctx if side == 0 else jnp.where(mask, ctx, out)
            high, middle, little = three_parts(-(top + jnp.log(sums)))
            aug = jnp.where(
                lane == 4, high, jnp.where(lane == 5, middle, jnp.where(lane == 6, little, own))
            )
            aug_ref[:, (2 * pair + side) * LANES : (2 * pair + side + 1) * LANES] = aug.astype(BF16)
        ctx_ref[:, here] = out.astype(BF16)


def attend(rank, seg, x, factors, bq, bv, shards, pairs):
    packs, size = seg.shape
    rows, width = x.shape
    cut = pairs * LANES
    block = pl.BlockSpec((size, cut), lambda p, g: (p, g))
    whole = lambda shape: pl.BlockSpec(shape, lambda p, g: (0, 0), pipeline_mode=pl.Buffered(1))
    like = jax.ShapeDtypeStruct
    return pl.pallas_call(
        functools.partial(attend_kernel, len(shards)),
        grid=(packs, width // cut),
        in_specs=[
            pl.BlockSpec(memory_space=pltpu.SMEM),
            pl.BlockSpec((1, 1, size), lambda p, g: (p, 0, 0)),
            pl.BlockSpec((size, width), lambda p, g: (p, 0)),
            whole(factors.shape),
            whole(bq.shape),
            whole(bv.shape),
        ]
        + [ANY] * len(shards),
        out_specs=[
            block,
            block,
            block,
            block,
            pl.BlockSpec((size, 2 * cut), lambda p, g: (p, g)),
            pl.BlockSpec((size, 2 * ADAPTER_RANK), lambda p, g: (p, 0)),
        ],
        out_shape=[like((rows, width), BF16)] * 4
        + [like((rows, 2 * width), BF16), like((rows, 2 * ADAPTER_RANK), BF16)],
        scratch_shapes=[
            pltpu.VMEM((width, 3 * width), BF16),
            pltpu.VMEM((size, 2 * ADAPTER_RANK), BF16),
            pltpu.SemaphoreType.DMA((len(shards),)),
        ],
        compiler_params=pltpu.CompilerParams(vmem_limit_bytes=VMEM_LIMIT),
        cost_estimate=pl.CostEstimate(
            flops=rows * width * (6 * width + 16 * size),
            bytes_accessed=16 * rows * width,
            transcendentals=rows * size * HEADS,
        ),
        name="project_and_attend",
    )(rank, seg.reshape(packs, 1, size), x, factors, bq, bv, *shards)


def dense_kernel(group, cut, rank_ref, x_ref, ctx_ref, cot_ref, *rest):
    vectors, rest = rest[:7], rest[7:]
    bo_ref, bi_ref, bo2_ref, g1_ref, s1_ref, g2_ref, s2_ref = vectors
    first, second, rest = rest[:group], rest[group : 2 * group], rest[2 * group :]
    out_ref, dh_ref, dctx_ref, ahead, outer, slope, semaphores = rest
    width = x_ref.shape[1]
    hidden = outer.shape[0]

    @pl.when(pl.program_id(0) == 0)
    def _():
        copies = pieces(rank_ref[0], first, ahead, semaphores.at[0])
        copies += pieces(rank_ref[0], second, outer, semaphores.at[1])
        for copy in copies:
            copy.start()
        for copy in copies:
            copy.wait()

    wo = lambda: ahead[:, :width]
    w1 = lambda j: ahead[:, width + j : width + j + cut]
    h1 = x_ref[...].astype(F32) + dot(ctx_ref[...], wo(), NN) + bo_ref[...]
    norm1, rstd1 = layer_norm(h1)
    y1 = norm1 * g1_ref[...] + s1_ref[...]
    y1_low = y1.astype(BF16)
    h2 = y1 + bo2_ref[...]
    for j in range(0, hidden, cut):
        inner = dot(y1_low, w1(j), NN) + bi_ref[:, j : j + cut]
        act, gradient = gelu_pair(inner)
        slope[:, j : j + cut] = gradient
        h2 = h2 + dot(act.astype(BF16), outer[j : j + cut, :], NN)
    norm2, rstd2 = layer_norm(h2)
    out_ref[...] = (norm2 * g2_ref[...] + s2_ref[...]).astype(BF16)
    dh2 = norm_back(cot_ref[...].astype(F32), norm2, rstd2, g2_ref[...])
    df = dh2.astype(BF16)
    dy1 = dh2
    for j in range(0, hidden, cut):
        du = (dot(df, outer[j : j + cut, :], NT) * slope[:, j : j + cut]).astype(BF16)
        dy1 = dy1 + dot(du, w1(j), NT)
    dh1 = norm_back(dy1, norm1, rstd1, g1_ref[...]).astype(BF16)
    dh_ref[...] = dh1
    dctx_ref[...] = dot(dh1, wo(), NT).astype(BF16)


def dense(rank, x, ctx, cot, vectors, first, second, size, cut):
    rows, width = x.shape
    hidden = vectors[1].shape[1]
    block = pl.BlockSpec((size, width), lambda i: (i, 0))
    whole = lambda shape: pl.BlockSpec(shape, lambda i: (0, 0), pipeline_mode=pl.Buffered(1))
    return pl.pallas_call(
        functools.partial(dense_kernel, len(first), cut),
        grid=(rows // size,),
        in_specs=[pl.BlockSpec(memory_space=pltpu.SMEM), block, block, block]
        + [whole(vector.shape) for vector in vectors]
        + [ANY] * (2 * len(first)),
        out_specs=[block] * 3,
        out_shape=[jax.ShapeDtypeStruct((rows, width), BF16)] * 3,
        scratch_shapes=[
            pltpu.VMEM((width, width + hidden), BF16),
            pltpu.VMEM((hidden, width), BF16),
            pltpu.VMEM((size, hidden), F32),
            pltpu.SemaphoreType.DMA((2, len(first))),
        ],
        compiler_params=pltpu.CompilerParams(vmem_limit_bytes=VMEM_LIMIT),
        cost_estimate=pl.CostEstimate(
            flops=rows * width * (4 * width + 8 * hidden),
            bytes_accessed=12 * rows * width + 4 * width * hidden,
            transcendentals=2 * rows * hidden,
        ),
        name="dense_both_ways",
    )(rank, x, ctx, cot, *vectors, *first, *second)


def attend_back_kernel(seg_ref, x_ref, fac_ref, down_ref, *rest):
    q_ref, k_ref, v_ref, dctx_ref, ctx_ref, aug_ref, *rest = rest
    dq_ref, dk_ref, dv_ref, dlow_ref, grad_ref, low, total = rest
    pack, at = pl.program_id(0), pl.program_id(1)
    rows, width = q_ref.shape
    rank2 = 2 * ADAPTER_RANK
    columns = pl.ds(pl.multiple_of(at * width, LANES), width)
    lane = lax.broadcasted_iota(jnp.int32, (rows, LANES), 1)
    seg = seg_ref[0].astype(F32).T.astype(jnp.int32)
    aug_k = jnp.where(
        (lane < 4) & (lane != seg), -MASKED, jnp.where((lane >= 4) & (lane < 7), 1.0, 0.0)
    ).astype(BF16)
    aug_v = jnp.where(lane < 3, 1.0, 0.0).astype(BF16)
    zero = BF16(0)
    half = LANES // 2
    scale = BF16(half ** (-0.5))
    for pair in range(width // LANES):
        here = slice(LANES * pair, LANES * (pair + 1))
        key = k_ref[:, here]
        query = q_ref[:, here] * scale
        grad = dctx_ref[:, here]
        keys = beside(key, aug_k)
        values = beside(v_ref[:, here], aug_v)
        key = key * scale
        product = grad.astype(F32) * ctx_ref[:, here].astype(F32)
        dq = dk = dv = 0.0
        for side in range(2):
            mask = (lane // half) == side
            one_query = jnp.where(mask, query, zero)
            one_grad = jnp.where(mask, grad, zero)
            one_key = jnp.where(mask, key, zero)
            inner = -jnp.sum(jnp.where(mask, product, 0.0), axis=1, keepdims=True)
            high, middle, little = three_parts(inner)
            aug_d = jnp.where(
                lane == 0, high, jnp.where(lane == 1, middle, jnp.where(lane == 2, little, 0.0))
            ).astype(BF16)
            aug_q = aug_ref[:, (2 * pair + side) * LANES : (2 * pair + side + 1) * LANES]
            probs = jnp.exp(dot(keys, beside(one_query, aug_q), NT))
            dprobs = dot(values, beside(one_grad, aug_d), NT)
            dscores = (probs * dprobs).astype(BF16)
            dv = dv + dot(probs.astype(BF16), one_grad, NN)
            dk = dk + dot(dscores, one_query, NN)
            dq = dq + dot(dscores, one_key, TN)
        dq_ref[:, here] = dq.astype(BF16)
        dk_ref[:, here] = dk.astype(BF16)
        dv_ref[:, here] = dv.astype(BF16)

    up = fac_ref[rank2 : 2 * rank2, columns]
    row = lax.broadcasted_iota(jnp.int32, up.shape, 0)
    up_q = jnp.where(row < ADAPTER_RANK, up, 0.0).astype(BF16)
    up_v = jnp.where(row < ADAPTER_RANK, 0.0, up).astype(BF16)
    dlow = dot(dq_ref[...], up_q, NT) + dot(dv_ref[...], up_v, NT)
    low[...] = dlow + jnp.where(at == 0, 0.0, low[...])
    down = down_ref[...]
    from_q = dot(down, dq_ref[...], TN)
    from_v = dot(down, dv_ref[...], TN)
    share = 2.0 * jnp.where(row < ADAPTER_RANK, from_q, from_v)
    later = pack > 0
    total[rank2 : 2 * rank2, columns] = share + jnp.where(
        later, total[rank2 : 2 * rank2, columns], 0.0
    )

    @pl.when(at == pl.num_programs(1) - 1)
    def _():
        dlow_low = (2.0 * low[...]).astype(BF16)
        dlow_ref[...] = dlow_low
        total[0:rank2, :] = dot(dlow_low, x_ref[...], TN) + jnp.where(
            later, total[0:rank2, :], 0.0
        )
        grad_ref[...] = total[...].astype(BF16)


def attend_back(seg, x, factors, down, q, k, v, dctx, ctx, aug, pairs):
    packs, size = seg.shape
    rows, width = x.shape
    cut = pairs * LANES
    rank2 = 2 * ADAPTER_RANK
    block = pl.BlockSpec((size, cut), lambda p, g: (p, g))
    whole = lambda shape: pl.BlockSpec(shape, lambda p, g: (0, 0), pipeline_mode=pl.Buffered(1))
    like = jax.ShapeDtypeStruct
    return pl.pallas_call(
        attend_back_kernel,
        grid=(packs, width // cut),
        in_specs=[
            pl.BlockSpec((1, 1, size), lambda p, g: (p, 0, 0)),
            pl.BlockSpec((size, width), lambda p, g: (p, 0)),
            whole(factors.shape),
            pl.BlockSpec((size, rank2), lambda p, g: (p, 0)),
            block,
            block,
            block,
            block,
            block,
            pl.BlockSpec((size, 2 * cut), lambda p, g: (p, g)),
        ],
        out_specs=[
            block,
            block,
            block,
            pl.BlockSpec((size, rank2), lambda p, g: (p, 0)),
            whole(factors.shape),
        ],
        out_shape=[like((rows, width), BF16)] * 3
        + [like((rows, rank2), BF16), like(factors.shape, BF16)],
        scratch_shapes=[pltpu.VMEM((size, rank2), F32), pltpu.VMEM(factors.shape, F32)],
        compiler_params=pltpu.CompilerParams(vmem_limit_bytes=VMEM_LIMIT),
        cost_estimate=pl.CostEstimate(
            flops=rows * width * 30 * size,
            bytes_accessed=24 * rows * width,
            transcendentals=rows * size * HEADS,
        ),
        name="attend_back",
    )(seg.reshape(packs, 1, size), x, factors, down, q, k, v, dctx, ctx, aug)


def input_kernel(group, rank_ref, dh_ref, dq_ref, dk_ref, dv_ref, dlow_ref, fac_ref, *rest):
    shards, (out_ref, weights, semaphores) = rest[:group], rest[group:]
    width = dh_ref.shape[1]

    @pl.when(pl.program_id(0) == 0)
    def _():
        copies = pieces(rank_ref[0], shards, weights, semaphores)
        for copy in copies:
            copy.start()
        for copy in copies:
            copy.wait()

    down = fac_ref[0 : 2 * ADAPTER_RANK, :].astype(BF16)
    out_ref[...] = (
        dh_ref[...].astype(F32)
        + dot(dq_ref[...], weights[:, :width], NT)
        + dot(dk_ref[...], weights[:, width : 2 * width], NT)
        + dot(dv_ref[...], weights[:, 2 * width :], NT)
        + dot(dlow_ref[...], down, NN)
    ).astype(BF16)


def input_back(rank, dh, dq, dk, dv, dlow, factors, shards, size):
    rows, width = dh.shape
    block = pl.BlockSpec((size, width), lambda i: (i, 0))
    return pl.pallas_call(
        functools.partial(input_kernel, len(shards)),
        grid=(rows // size,),
        in_specs=[
            pl.BlockSpec(memory_space=pltpu.SMEM),
            block,
            block,
            block,
            block,
            pl.BlockSpec((size, dlow.shape[1]), lambda i: (i, 0)),
            pl.BlockSpec(factors.shape, lambda i: (0, 0)),
        ]
        + [ANY] * len(shards),
        out_specs=block,
        out_shape=jax.ShapeDtypeStruct((rows, width), BF16),
        scratch_shapes=[
            pltpu.VMEM((width, 3 * width), BF16),
            pltpu.SemaphoreType.DMA((len(shards),)),
        ],
        compiler_params=pltpu.CompilerParams(vmem_limit_bytes=VMEM_LIMIT),
        cost_estimate=pl.CostEstimate(
            flops=6 * rows * width * width,
            bytes_accessed=10 * rows * width + 6 * width * width,
            transcendentals=0,
        ),
        name="input_gradient",
    )(rank, dh, dq, dk, dv, dlow, factors, *shards)


def update_kernel(near_ref, far_ref, fac_ref, first_ref, second_ref, *outs):
    grad_ref, new_ref, new_first_ref, new_second_ref = outs
    grad = near_ref[...].astype(F32) + far_ref[...].astype(F32)
    grad_ref[...] = grad
    clip = jnp.minimum(1.0, 1.0 / (jnp.sqrt(jnp.sum(grad * grad)) + 1e-06))
    clipped = grad * clip
    new_first = 0.9 * first_ref[...] + 0.1 * clipped
    new_second = 0.999 * second_ref[...] + 0.001 * clipped * clipped
    new_first_ref[...] = new_first
    new_second_ref[...] = new_second
    factors = fac_ref[...]
    row = lax.broadcasted_iota(jnp.int32, factors.shape, 0)
    rate = jnp.where(row < 2 * ADAPTER_RANK, rate_low, rate_high)
    fix_first = 1.0 - 0.9**STEP
    fix_second = 1.0 - 0.999**STEP
    step = new_first / fix_first / (jnp.sqrt(new_second / fix_second) + 1e-08)
    new_ref[...] = factors - rate * (step + decay_rate * factors)


def update(near, far, factors, first, second):
    return pl.pallas_call(
        update_kernel,
        out_shape=[jax.ShapeDtypeStruct(factors.shape, F32)] * 4,
        name="adapter_update",
    )(near, far, factors, first, second)


def swap(value, axis, size, flip):
    return lax.ppermute(value, axis, [(i, i ^ flip) for i in range(size)])


def bits(size):
    return [1 << at for at in range(size.bit_length() - 1)]


def group_shards(shard, size):
    held = [shard]
    for flip in bits(size)[1:]:
        held += [swap(value, "rep", size, flip) for value in held]
    return [value for near in held for value in (near, swap(near, "rep", size, 1))]


def gather_moments(first, second, size):
    length = first.shape[0]
    place = lax.axis_index("wide")
    held = jnp.stack([first, second])
    for flip in bits(size):
        other = swap(held, "wide", size, flip)
        low = (place // flip) % 2 == 0
        held = jnp.where(
            low, jnp.concatenate([held, other], 1), jnp.concatenate([other, held], 1)
        )
    return (held[0], held[1])


def local(sizes, *args):
    (
        tokens,
        segment_ids,
        cotangent,
        w_query,
        w_key,
        w_value,
        w_output,
        w_inner,
        w_outer,
        b_query,
        b_value,
        b_output,
        b_inner,
        b_outer,
        norm1_gain,
        norm1_shift,
        norm2_gain,
        norm2_shift,
        factors,
        first_moment,
        second_moment,
    ) = args
    reps, wide = sizes
    width = tokens.shape[1]
    size = segment_ids.shape[1]
    flat = lambda vector: vector.reshape(1, -1)
    rank = lax.axis_index("rep").reshape(1)
    table = factors.reshape(4 * ADAPTER_RANK, width)
    qkv = group_shards(jnp.concatenate([w_query, w_key, w_value], 1), reps)
    ahead = group_shards(jnp.concatenate([w_output, w_inner], 1), reps)
    outer = group_shards(w_outer, reps)
    first, second = gather_moments(first_moment, second_moment, wide)
    q, k, v, ctx, aug, down = attend(
        rank, segment_ids, tokens, table, flat(b_query), flat(b_value), qkv, 3
    )
    vectors = [
        flat(vector)
        for vector in (
            b_output,
            b_inner,
            b_outer,
            norm1_gain,
            norm1_shift,
            norm2_gain,
            norm2_shift,
        )
    ]
    layer_out, dh, dctx = dense(rank, tokens, ctx, cotangent, vectors, ahead, outer, size, 1024)
    dq, dk, dv, dlow, grad = attend_back(
        segment_ids, tokens, table, down, q, k, v, dctx, ctx, aug, 3
    )
    input_grad = input_back(rank, dh, dq, dk, dv, dlow, table, qkv, size)
    rounds = [("rep", reps, flip) for flip in bits(reps)]
    rounds += [("wide", wide, flip) for flip in bits(wide)]
    for axis, count, flip in rounds[:-1]:
        grad = grad + swap(grad, axis, count, flip)
    axis, count, flip = rounds[-1]
    new = update(
        grad,
        swap(grad, axis, count, flip),
        table,
        first.reshape(table.shape),
        second.reshape(table.shape),
    )
    length = first_moment.shape[0]
    start = lax.axis_index("wide") * length
    whole_grad, new_factors, new_first, new_second = [value.reshape(-1) for value in new]
    mine = lambda value: lax.dynamic_slice_in_dim(value, start, length)
    return (
        layer_out,
        input_grad,
        mine(whole_grad),
        new_factors,
        mine(new_first),
        mine(new_second),
    )


def solution(mesh):
    rows = P(("rep", "wide"), None)
    shard = P("rep", None)
    piece = P("wide")
    placed = (rows,) * 3 + (shard,) * 6 + (P(),) * 10 + (piece,) * 2
    return jax.shard_map(
        functools.partial(local, (mesh.shape["rep"], mesh.shape["wide"])),
        mesh=mesh,
        in_specs=placed,
        out_specs=(rows, rows, piece, P(), piece, piece),
        check_vma=False,
    )
```

time: 570 us -> 207 us (0.36); the launches traced: 559 us -> 207 us
  matrix products: 294 us -> 0 us
  Pallas kernels: 0 us -> 94.9 us
  blocking collectives: 91.9 us -> 0 us
  local copies, waits for them, and re-layouts: 84.3 us -> 18.9 us
  waiting for transfers between devices: 42.7 us -> 72.6 us
  other arithmetic: 27.6 us -> 1.12 us
  starting transfers between devices: 0.23 us -> 17.9 us
  between operations: 16.8 us -> 1.04 us
    dot_general x39 -> x0, matrix products: 273 us -> none  [the longest x2 85.6 us: run_forward(): inner = jnp.dot(first_low, w1, preferred_element_type=jnp.float32) + bi]
    pallas_call x0 -> x5, Pallas kernels: none -> 94.9 us  [the longest x1 35 us: dense(): pl.pallas_call(functools.partial(dense_kernel, len(first), cut), grid=(ro...]
    ppermute x0 -> x17, waiting for transfers between devices: none -> 72.6 us  [swap(): return lax.ppermute(value, axis, [(i, i ^ flip) for i in range(size)])]
    all_gather x6 -> x0, waiting for transfers between devices: 39.1 us -> none  [the longest x1 13.3 us: fetch(): lax.all_gather(w_value, 'rep', axis=0, tiled=True)]
    unnamed x1 -> x0, blocking collectives: 37.5 us -> none
    dynamic_update_slice x18 -> x0, local copies, waits for them, and re-layouts: 32.1 us -> none  [run_forward(): lax.map(attend, (query.reshape(count, -1, width), key.reshape(count, -1,...]
    all_gather x1 -> x0, blocking collectives: 30.5 us -> none  [local(): new_factors = lax.all_gather(new_piece, 'wide', axis=0, tiled=True)]
    psum x2 -> x0, blocking collectives: 23.9 us -> none  [the longest x1 17.7 us: local(): squares = lax.psum(jnp.sum(piece * piece), 'wide')]
  transfers between devices with their start and end apart: 6 -> 17, of which waited for: 3 -> 5; matrix products, arithmetic and copies ran while one was open for 29% -> 4% of each run, Pallas kernels for 0% -> 45%
where the time goes in v1:
time: 207 us
  Pallas kernels  94.9 us (46%)
  waiting for transfers between devices  72.6 us (35%)
  local copies, waits for them, and re-layouts  18.9 us (9%)
  starting transfers between devices  17.9 us (9%)
    ppermute x17, waiting for transfers between devices, swap(): return lax.ppermute(value, axis, [(i, i ^ flip) for i in range(size)])  72.6 us
    pallas_call x1, Pallas kernels, dense(): pl.pallas_call(functools.partial(dense_kernel, len(first), cut), grid=(ro...  35 us
    pallas_call x1, Pallas kernels, attend_back(): pl.pallas_call(attend_back_kernel, grid=(packs, width // cut), in_specs=[...  24.8 us
    pallas_call x1, Pallas kernels, attend(): pl.pallas_call(functools.partial(attend_kernel, len(shards)), grid=(packs...  23.1 us
    ppermute x17, starting transfers between devices, swap(): return lax.ppermute(value, axis, [(i, i ^ flip) for i in range(size)])  17.9 us
    pallas_call x1, Pallas kernels, input_back(): pl.pallas_call(functools.partial(input_kernel, len(shards)), grid=(rows /...  10.1 us
    reshape x8, local copies, waits for them, and re-layouts, local(): flat = lambda vector: vector.reshape(1, -1)  4.7 us
    reshape x4, local copies, waits for them, and re-layouts, local(): value.reshape(-1)  4.24 us
  transfers between devices with their start and end apart: 17, of which 5 were waited for; matrix products, arithmetic and copies ran while one was open for 4% of the time, Pallas kernels for 45%

profile of v1, /device:TPU:0, one launch (start us, length us, event | category | flops | bytes accessed | tf_op | source)
XLA Modules:
  0.0 206.5 jit_solution(9720993877734554526)
XLA Ops:
  0.6 1.0 constant_dynamic-update-slice_fusion.4
  1.7 0.0 copy-start.1
  1.7 0.0 copy-start.2
  1.7 1.4 constant_dynamic-update-slice_fusion.3.rest_7_
  3.1 0.0 copy-start.8
  3.1 0.0 copy-start.9
  3.1 0.0 copy-start.4
  3.2 0.0 copy-start.18
  3.2 0.0 copy-start.10
  3.2 0.0 copy-start.11
  3.2 0.0 copy-start.12
  3.2 0.0 copy-start.15
  3.2 0.0 copy-start.16
  3.3 3.0 %collective-permute-start.4 = (bf16[192,3840]{1,0:T(8,128)(2,1)S(1)}, bf16[192,3840]{1,0:T(8,128)(2,1)}, u32[]{:S(2)}, u32[]{:S(2)}) collective-permute-start(bf16[192,3840]{1,0:T(8,128)(2,1)S(1)} %constant_dynamic-update-slice_fusion.3.rest_7_), channel_id=1, source_target_pairs={{0,16},{8,24},{16,0},{24,8},{1,17},{9,25},{17,1},{25,9},{2,18},{10... | collective-permute-start | bytes 4423688 | tf_op jit(solution)/shard_map/ppermute | solution.py:463
  6.4 0.1 collective-permute-start.1
  6.5 2.0 collective-permute-start.7
  8.5 49.9 %collective-permute-done.1.rest_2_ = bf16[192,2304]{1,0:T(8,128)(2,1)S(1)} collective-permute-done((bf16[192,2304]{1,0:T(8,128)(2,1)S(1)}, bf16[192,2304]{1,0:T(8,128)(2,1)S(1)}, u32[]{:S(2)}, u32[]{:S(2)}) %collective-permute-start.1) | collective-permute-done | bytes 884768 | tf_op jit(solution)/shard_map/ppermute | solution.py:463
  58.4 2.1 %collective-permute-start.14 = (f32[2,3072]{1,0:T(2,128)S(1)}, f32[2,3072]{1,0:T(2,128)S(1)}, u32[]{:S(2)}, u32[]{:S(2)}) collective-permute-start(f32[2,3072]{1,0:T(2,128)S(1)} %pad_maximum_fusion), channel_id=1, source_target_pairs={{0,1},{1,0},{2,3},{3,2},{4,5},{5,4},{6,7},{7,6},{8,9},{9,8},{10,11... | collective-permute-start | bytes 73736 | tf_op jit(solution)/shard_map/ppermute | solution.py:463
  60.5 0.7 reshape.63.fac_ref
  61.2 0.6 reshape.62.seg_ref
  61.8 0.6 reshape.64.bq_ref
  62.4 0.6 reshape.65.bv_ref
  63.0 0.6 reshape.66.rest_0_
  63.6 0.6 reshape.68.rest_2_
  64.1 0.6 reshape.69.rest_3_
  64.7 0.6 reshape.70.rest_4_
  65.3 0.6 reshape.71.rest_5_
  65.9 0.6 reshape.72.rest_6_
  66.5 0.2 collective-permute-start.3
  66.7 0.3 collective-permute-start.6
  67.0 15.9 %collective-permute-done.7.rest_13_ = bf16[768,768]{1,0:T(8,128)(2,1)} collective-permute-done((bf16[768,768]{1,0:T(8,128)(2,1)}, bf16[768,768]{1,0:T(8,128)(2,1)}, u32[]{:S(2)}, u32[]{:S(2)}) %collective-permute-start.7) | collective-permute-done | bytes 1179680 | tf_op jit(solution)/shard_map/ppermute | solution.py:463
  82.9 0.5 collective-permute-start.5
  83.5 1.9 collective-permute-start.15
  85.4 23.1 %project_and_attend.1 = (bf16[1024,768]{1,0:T(8,128)(2,1)}, bf16[1024,768]{1,0:T(8,128)(2,1)}, bf16[1024,768]{1,0:T(8,128)(2,1)}, bf16[1024,768]{1,0:T(8,128)(2,...) custom-call(s32[1]{0:T(128)} %bitcast.rank_ref, s32[2,1,512]{2,1,0:T(1,128)} %reshape.62.seg_ref, ...), custom_call_target="tpu_custom_call" | custom-call | flops 10066329600 | bytes 12582912 | tf_op jit(solution)/shard_map/project_and_attend/pallas_call | solution.py:158
  108.5 1.0 copy-done.21
  109.5 0.5 copy-done.19
  109.9 0.5 copy-done.20
  110.4 35.0 %dense_both_ways.1 = (bf16[1024,768]{1,0:T(8,128)(2,1)}, bf16[1024,768]{1,0:T(8,128)(2,1)}, bf16[1024,768]{1,0:T(8,128)(2,1)}) custom-call(s32[1]{0:T(128)} %bitcast.rank_ref, bf16[1024,768]{1,0:T(8,128)(2,1)} %x_ref.5, bf16[1024,768]{1,0:T(8,128)(2,1)} %get-tuple-element.24.ctx_ref.rest_4_, bf16[1024,768]{1,0:T(8,128)(2,1)} %cot_ref.1, ...), custom_call_target="tpu_custom_call" | custom-call | flops 21743271936 | bytes 18874368 | tf_op jit(solution)/shard_map/dense_both_ways/pallas_call | solution.py:242
  145.4 24.8 %attend_back.1 = (bf16[1024,768]{1,0:T(8,128)(2,1)}, bf16[1024,768]{1,0:T(8,128)(2,1)}, bf16[1024,768]{1,0:T(8,128)(2,1)}, bf16[1024,16]{1,0:T(8,128)(2,1)}, bf16[32,768]{1,0:T(8,128)(2,1)}) custom-call(s32[2,1,512]{2,1,0:T(1,128)} %reshape.62.seg_ref, bf16[1024,768]{1,0:T(8,128)(2,1)} %x_ref.5, f32[32,768]{1,0:T(8,128)} %reshape.63.fac_ref, ...), custom_call_target="tpu_custom_call" | custom-call | flops 12079595520 | bytes 18874368 | tf_op jit(solution)/shard_map/attend_back/pallas_call | solution.py:346
  170.1 0.1 collective-permute-start.9
  170.2 0.1 maximum_select_fusion.1
  170.3 2.6 %collective-permute-start.16 = (f32[2,12288]{1,0:T(2,128)S(1)}, f32[2,12288]{1,0:T(2,128)S(1)}, u32[]{:S(2)}, u32[]{:S(2)}) collective-permute-start(f32[2,12288]{1,0:T(2,128)S(1)} %maximum_select_fusion.1), channel_id=1, source_target_pairs={{0,4},{1,5},{2,6},{3,7},{4,0},{5,1},{6,2},{7,3},{8,12},{9,13},{10,... | collective-permute-start | bytes 294920 | tf_op jit(solution)/shard_map/ppermute | solution.py:463
  172.9 0.8 add.30
  173.7 1.6 collective-permute-start.10
  175.3 2.6 %collective-permute-done.10 = bf16[32,768]{1,0:T(8,128)(2,1)S(1)} collective-permute-done((bf16[32,768]{1,0:T(8,128)(2,1)S(1)}, bf16[32,768]{1,0:T(8,128)(2,1)S(1)}, u32[]{:S(2)}, u32[]{:S(2)}) %collective-permute-start.10) | collective-permute-done | bytes 49184 | tf_op jit(solution)/shard_map/ppermute | solution.py:463
  177.9 1.6 collective-permute-start.11
  179.5 0.2 maximum_select_fusion
  179.6 2.4 %collective-permute-done.11 = bf16[32,768]{1,0:T(8,128)(2,1)S(1)} collective-permute-done((bf16[32,768]{1,0:T(8,128)(2,1)S(1)}, bf16[32,768]{1,0:T(8,128)(2,1)S(1)}, u32[]{:S(2)}, u32[]{:S(2)}) %collective-permute-start.11) | collective-permute-done | bytes 49184 | tf_op jit(solution)/shard_map/ppermute | solution.py:463
  182.1 0.5 collective-permute-start.12
  182.6 0.5 slice_reduce_fusion
  183.1 0.7 reshape_squeeze.6.first_ref
  183.8 0.7 reshape_squeeze.7.second_ref
  184.4 1.8 collective-permute-done.12
  186.3 1.4 collective-permute-start.13
  187.7 10.1 %input_gradient.1 = bf16[1024,768]{1,0:T(8,128)(2,1)} custom-call(s32[1]{0:T(128)} %bitcast.rank_ref, bf16[1024,768]{1,0:T(8,128)(2,1)} %get-tuple-element.26.dh_ref, bf16[1024,768]{1,0:T(8,128)(2,1)} %get-tuple-element.33.dq_ref, bf16[1024,768]{1,0:T(8,128)(2,1)} %get-tuple-element.34.dk_ref, bf16[1024,768]{1,0:T(8,128)(2,1)} %get-tuple-element.35.dv_ref, ...), custom_call_target="tpu_custom_call" | custom-call | flops 3623878656 | bytes 11403264 | tf_op jit(solution)/shard_map/input_gradient/pallas_call | solution.py:406
  197.8 0.6 copy-done.7
  198.4 2.1 adapter_update.1
  200.5 0.9 reshape.75
  201.4 0.9 reshape.76
  202.3 0.6 dynamic_slice.10
  202.9 0.6 dynamic_slice.11
  203.5 0.9 reshape.73
  204.4 0.6 dynamic_slice.9
  205.0 1.5 reshape.74
  (54 shorter events, 0.3 us)
Async XLA Ops:
  0.6 5.7 %copy-start = (bf16[192,768]{1,0:T(8,128)(2,1)S(1)}, bf16[192,768]{1,0:T(8,128)(2,1)}, u32[]{:S(2)}) copy-start(bf16[192,768]{1,0:T(8,128)(2,1)} %param.24) | copy-start | bytes 884740
  1.7 4.7 %copy-start.1 = (bf16[192,768]{1,0:T(8,128)(2,1)S(1)}, bf16[192,768]{1,0:T(8,128)(2,1)}, u32[]{:S(2)}) copy-start(bf16[192,768]{1,0:T(8,128)(2,1)} %param.25) | copy-start | bytes 884740
  1.7 4.7 %copy-start.2 = (bf16[192,768]{1,0:T(8,128)(2,1)S(1)}, bf16[192,768]{1,0:T(8,128)(2,1)}, u32[]{:S(2)}) copy-start(bf16[192,768]{1,0:T(8,128)(2,1)} %param.26) | copy-start | bytes 884740
  3.1 105.3 %copy-start.6 = (bf16[192,3840]{1,0:T(8,128)(2,1)}, bf16[192,3840]{1,0:T(8,128)(2,1)S(1)}, u32[]{:S(2)}) copy-start(bf16[192,3840]{1,0:T(8,128)(2,1)S(1)} %constant_dynamic-update-slice_fusion.3.rest_7_) | copy-start | bytes 4423684
  3.1 55.3 %copy-start.8 = (f32[3072]{0:T(1024)S(1)}, f32[3072]{0:T(1024)}, u32[]{:S(2)}) copy-start(f32[3072]{0:T(1024)} %param.41) | copy-start | bytes 36868
  3.1 55.3 %copy-start.9 = (f32[3072]{0:T(1024)S(1)}, f32[3072]{0:T(1024)}, u32[]{:S(2)}) copy-start(f32[3072]{0:T(1024)} %param.40) | copy-start | bytes 36868
  3.1 57.4 %copy-start.4 = (f32[24576]{0:T(1024)S(1)}, f32[24576]{0:T(1024)}, u32[]{:S(2)}) copy-start(f32[24576]{0:T(1024)} %param.39) | copy-start | bytes 294916
  3.2 58.0 %copy-start.18 = (s32[2,512]{1,0:T(2,128)S(1)}, s32[2,512]{1,0:T(2,128)}, u32[]{:S(2)}) copy-start(s32[2,512]{1,0:T(2,128)} %param.22) | copy-start | bytes 12292
  3.2 58.6 %copy-start.10 = (f32[768]{0:T(1024)S(1)}, f32[768]{0:T(1024)}, u32[]{:S(2)}) copy-start(f32[768]{0:T(1024)} %param.30) | copy-start | bytes 9220
  3.2 59.2 %copy-start.11 = (f32[768]{0:T(1024)S(1)}, f32[768]{0:T(1024)}, u32[]{:S(2)}) copy-start(f32[768]{0:T(1024)} %param.31) | copy-start | bytes 9220
  3.2 59.8 %copy-start.12 = (f32[768]{0:T(1024)S(1)}, f32[768]{0:T(1024)}, u32[]{:S(2)}) copy-start(f32[768]{0:T(1024)} %param.32) | copy-start | bytes 9220
  3.2 60.4 %copy-start.13 = (f32[768]{0:T(1024)S(1)}, f32[768]{0:T(1024)}, u32[]{:S(2)}) copy-start(f32[768]{0:T(1024)} %param.34) | copy-start | bytes 9220
  3.2 60.9 %copy-start.14 = (f32[768]{0:T(1024)S(1)}, f32[768]{0:T(1024)}, u32[]{:S(2)}) copy-start(f32[768]{0:T(1024)} %param.35) | copy-start | bytes 9220
  3.2 61.5 %copy-start.15 = (f32[768]{0:T(1024)S(1)}, f32[768]{0:T(1024)}, u32[]{:S(2)}) copy-start(f32[768]{0:T(1024)} %param.36) | copy-start | bytes 9220
  3.2 62.1 %copy-start.16 = (f32[768]{0:T(1024)S(1)}, f32[768]{0:T(1024)}, u32[]{:S(2)}) copy-start(f32[768]{0:T(1024)} %param.37) | copy-start | bytes 9220
  3.2 62.7 %copy-start.17 = (f32[768]{0:T(1024)S(1)}, f32[768]{0:T(1024)}, u32[]{:S(2)}) copy-start(f32[768]{0:T(1024)} %param.38) | copy-start | bytes 9220
  3.3 79.7 %collective-permute-start.4 = (bf16[192,3840]{1,0:T(8,128)(2,1)S(1)}, bf16[192,3840]{1,0:T(8,128)(2,1)}, u32[]{:S(2)}, u32[]{:S(2)}) collective-permute-start(bf16[192,3840]{1,0:T(8,128)(2,1)S(1)} %constant_dynamic-update-slice_fusion.3.rest_7_), channel_id=1, source_target_pairs={{0,16},{8,24},{16,0},{24,8},{1,17},{9,25},{17,1},{25,9},{2,18},{10... | collective-permute-start | bytes 4423688 | tf_op jit(solution)/shard_map/ppermute | solution.py:463
  6.4 79.0 %copy-start.5 = (bf16[192,2304]{1,0:T(8,128)(2,1)}, bf16[192,2304]{1,0:T(8,128)(2,1)S(1)}, u32[]{:S(2)}) copy-start(bf16[192,2304]{1,0:T(8,128)(2,1)S(1)} %constant_dynamic-update-slice_fusion.rest_0_) | copy-start | bytes 2654212
  6.4 52.0 %collective-permute-start.1 = (bf16[192,2304]{1,0:T(8,128)(2,1)S(1)}, bf16[192,2304]{1,0:T(8,128)(2,1)S(1)}, u32[]{:S(2)}, u32[]{:S(2)}) collective-permute-start(bf16[192,2304]{1,0:T(8,128)(2,1)S(1)} %constant_dynamic-update-slice_fusion.rest_0_), channel_id=1, source_target_pairs={{0,16},{8,24},{16,0},{24,8},{1,17},{9,25},{17,1},{25,9},{2,18},{10... | collective-permute-start | bytes 2654216 | tf_op jit(solution)/shard_map/ppermute | solution.py:463
  6.5 76.4 %collective-permute-start.7 = (bf16[768,768]{1,0:T(8,128)(2,1)}, bf16[768,768]{1,0:T(8,128)(2,1)}, u32[]{:S(2)}, u32[]{:S(2)}) collective-permute-start(bf16[768,768]{1,0:T(8,128)(2,1)} %rest_11_.1), channel_id=1, source_target_pairs={{0,16},{8,24},{16,0},{24,8},{1,17},{9,25},{17,1},{25,9},{2,18},{10... | collective-permute-start | bytes 3538952 | tf_op jit(solution)/shard_map/ppermute | solution.py:463
  8.5 58.2 %collective-permute-start = (bf16[192,2304]{1,0:T(8,128)(2,1)S(1)}, bf16[192,2304]{1,0:T(8,128)(2,1)}, u32[]{:S(2)}, u32[]{:S(2)}) collective-permute-start(bf16[192,2304]{1,0:T(8,128)(2,1)S(1)} %constant_dynamic-update-slice_fusion.rest_0_), channel_id=1, source_target_pairs={{0,8},{8,0},{16,24},{24,16},{1,9},{9,1},{17,25},{25,17},{2,10},{10... | collective-permute-start | bytes 2654216 | tf_op jit(solution)/shard_map/ppermute | solution.py:463
  58.4 27.0 %copy-start.22 = (bf16[192,2304]{1,0:T(8,128)(2,1)}, bf16[192,2304]{1,0:T(8,128)(2,1)S(1)}, u32[]{:S(2)}) copy-start(bf16[192,2304]{1,0:T(8,128)(2,1)S(1)} %collective-permute-done.1.rest_2_) | copy-start | bytes 2654212
  58.4 25.1 %collective-permute-start.2 = (bf16[192,2304]{1,0:T(8,128)(2,1)S(1)}, bf16[192,2304]{1,0:T(8,128)(2,1)}, u32[]{:S(2)}, u32[]{:S(2)}) collective-permute-start(bf16[192,2304]{1,0:T(8,128)(2,1)S(1)} %collective-permute-done.1.rest_2_), channel_id=1, source_target_pairs={{0,8},{8,0},{16,24},{24,16},{1,9},{9,1},{17,25},{25,17},{2,10},{10... | collective-permute-start | bytes 2654216 | tf_op jit(solution)/shard_map/ppermute | solution.py:463
  58.4 8.1 %collective-permute-start.14 = (f32[2,3072]{1,0:T(2,128)S(1)}, f32[2,3072]{1,0:T(2,128)S(1)}, u32[]{:S(2)}, u32[]{:S(2)}) collective-permute-start(f32[2,3072]{1,0:T(2,128)S(1)} %pad_maximum_fusion), channel_id=1, source_target_pairs={{0,1},{1,0},{2,3},{3,2},{4,5},{5,4},{6,7},{7,6},{8,9},{9,8},{10,11... | collective-permute-start | bytes 73736 | tf_op jit(solution)/shard_map/ppermute | solution.py:463
  66.5 42.0 %collective-permute-start.3 = (bf16[192,3840]{1,0:T(8,128)(2,1)S(1)}, bf16[192,3840]{1,0:T(8,128)(2,1)S(1)}, u32[]{:S(2)}, u32[]{:S(2)}) collective-permute-start(bf16[192,3840]{1,0:T(8,128)(2,1)S(1)} %constant_dynamic-update-slice_fusion.3.rest_7_), channel_id=1, source_target_pairs={{0,8},{8,0},{16,24},{24,16},{1,9},{9,1},{17,25},{25,17},{2,10},{10... | collective-permute-start | bytes 4423688 | tf_op jit(solution)/shard_map/ppermute | solution.py:463
  66.7 41.7 %collective-permute-start.6 = (bf16[768,768]{1,0:T(8,128)(2,1)}, bf16[768,768]{1,0:T(8,128)(2,1)S(1)}, u32[]{:S(2)}, u32[]{:S(2)}) collective-permute-start(bf16[768,768]{1,0:T(8,128)(2,1)} %rest_11_.1), channel_id=1, source_target_pairs={{0,8},{8,0},{16,24},{24,16},{1,9},{9,1},{17,25},{25,17},{2,10},{10... | collective-permute-start | bytes 3538952 | tf_op jit(solution)/shard_map/ppermute | solution.py:463
  82.9 25.6 %collective-permute-start.8 = (bf16[768,768]{1,0:T(8,128)(2,1)}, bf16[768,768]{1,0:T(8,128)(2,1)}, u32[]{:S(2)}, u32[]{:S(2)}) collective-permute-start(bf16[768,768]{1,0:T(8,128)(2,1)} %collective-permute-done.7.rest_13_), channel_id=1, source_target_pairs={{0,8},{8,0},{16,24},{24,16},{1,9},{9,1},{17,25},{25,17},{2,10},{10... | collective-permute-start | bytes 3538952 | tf_op jit(solution)/shard_map/ppermute | solution.py:463
  82.9 25.6 %collective-permute-start.5 = (bf16[192,3840]{1,0:T(8,128)(2,1)}, bf16[192,3840]{1,0:T(8,128)(2,1)S(1)}, u32[]{:S(2)}, u32[]{:S(2)}) collective-permute-start(bf16[192,3840]{1,0:T(8,128)(2,1)} %collective-permute-done.4.rest_9_), channel_id=1, source_target_pairs={{0,8},{8,0},{16,24},{24,16},{1,9},{9,1},{17,25},{25,17},{2,10},{10... | collective-permute-start | bytes 4423688 | tf_op jit(solution)/shard_map/ppermute | solution.py:463
  83.5 86.7 %collective-permute-start.15 = (f32[2,6144]{1,0:T(2,128)S(1)}, f32[2,6144]{1,0:T(2,128)S(1)}, u32[]{:S(2)}, u32[]{:S(2)}) collective-permute-start(f32[2,6144]{1,0:T(2,128)S(1)} %maximum_select_fusion.2), channel_id=1, source_target_pairs={{0,2},{1,3},{2,0},{3,1},{4,6},{5,7},{6,4},{7,5},{8,10},{9,11},{10,... | collective-permute-start | bytes 147464 | tf_op jit(solution)/shard_map/ppermute | solution.py:463
  108.5 1.0 copy-start.21
  108.5 1.5 copy-start.19
  108.5 1.9 copy-start.20
  170.1 2.8 %collective-permute-start.9 = (bf16[32,768]{1,0:T(8,128)(2,1)}, bf16[32,768]{1,0:T(8,128)(2,1)S(1)}, u32[]{:S(2)}, u32[]{:S(2)}) collective-permute-start(bf16[32,768]{1,0:T(8,128)(2,1)} %get-tuple-element.37), channel_id=1, source_target_pairs={{0,8},{8,0},{16,24},{24,16},{1,9},{9,1},{17,25},{25,17},{2,10},{10... | collective-permute-start | bytes 147464 | tf_op jit(solution)/shard_map/ppermute | solution.py:463
  170.3 9.2 %collective-permute-start.16 = (f32[2,12288]{1,0:T(2,128)S(1)}, f32[2,12288]{1,0:T(2,128)S(1)}, u32[]{:S(2)}, u32[]{:S(2)}) collective-permute-start(f32[2,12288]{1,0:T(2,128)S(1)} %maximum_select_fusion.1), channel_id=1, source_target_pairs={{0,4},{1,5},{2,6},{3,7},{4,0},{5,1},{6,2},{7,3},{8,12},{9,13},{10,... | collective-permute-start | bytes 294920 | tf_op jit(solution)/shard_map/ppermute | solution.py:463
  173.7 4.2 %collective-permute-start.10 = (bf16[32,768]{1,0:T(8,128)(2,1)S(1)}, bf16[32,768]{1,0:T(8,128)(2,1)S(1)}, u32[]{:S(2)}, u32[]{:S(2)}) collective-permute-start(bf16[32,768]{1,0:T(8,128)(2,1)S(1)} %add.30), channel_id=1, source_target_pairs={{0,16},{8,24},{16,0},{24,8},{1,17},{9,25},{17,1},{25,9},{2,18},{10... | collective-permute-start | bytes 147464 | tf_op jit(solution)/shard_map/ppermute | solution.py:463
  177.9 4.2 %collective-permute-start.11 = (bf16[32,768]{1,0:T(8,128)(2,1)S(1)}, bf16[32,768]{1,0:T(8,128)(2,1)S(1)}, u32[]{:S(2)}, u32[]{:S(2)}) collective-permute-start(bf16[32,768]{1,0:T(8,128)(2,1)S(1)} %add.31), channel_id=1, source_target_pairs={{0,1},{1,0},{2,3},{3,2},{4,5},{5,4},{6,7},{7,6},{8,9},{9,8},{10,11... | collective-permute-start | bytes 147464 | tf_op jit(solution)/shard_map/ppermute | solution.py:463
  182.1 4.2 %collective-permute-start.12 = (bf16[32,768]{1,0:T(8,128)(2,1)S(1)}, bf16[32,768]{1,0:T(8,128)(2,1)S(1)}, u32[]{:S(2)}, u32[]{:S(2)}) collective-permute-start(bf16[32,768]{1,0:T(8,128)(2,1)S(1)} %add.32), channel_id=1, source_target_pairs={{0,2},{1,3},{2,0},{3,1},{4,6},{5,7},{6,4},{7,5},{8,10},{9,11},{10,... | collective-permute-start | bytes 147464 | tf_op jit(solution)/shard_map/ppermute | solution.py:463
  186.3 11.5 %copy-start.3 = (bf16[32,768]{1,0:T(8,128)(2,1)}, bf16[32,768]{1,0:T(8,128)(2,1)S(1)}, u32[]{:S(2)}) copy-start(bf16[32,768]{1,0:T(8,128)(2,1)S(1)} %add.33.near_ref) | copy-start | bytes 147460
  186.3 11.5 %collective-permute-start.13 = (bf16[32,768]{1,0:T(8,128)(2,1)S(1)}, bf16[32,768]{1,0:T(8,128)(2,1)S(1)}, u32[]{:S(2)}, u32[]{:S(2)}) collective-permute-start(bf16[32,768]{1,0:T(8,128)(2,1)S(1)} %add.33.near_ref), channel_id=1, source_target_pairs={{0,4},{1,5},{2,6},{3,7},{4,0},{5,1},{6,2},{7,3},{8,12},{9,13},{10,... | collective-permute-start | bytes 147464 | tf_op jit(solution)/shard_map/ppermute | solution.py:463
  197.8 0.6 copy-start.7

commit v2 on v1

v2 whole, which is shorter than its diff:
```python
import functools

import jax
import jax.numpy as jnp
from jax import lax
from jax.experimental import pallas as pl
from jax.experimental.pallas import tpu as pltpu
from jax.sharding import PartitionSpec as P

HEADS = 12
ADAPTER_RANK = 8
STEP = 10
LANES = 128
MASKED = 1e30

rate_low = 0.015
rate_high = 0.24
decay_rate = 0.01

BF16 = jnp.bfloat16
F32 = jnp.float32
NN = (((1,), (0,)), ((), ()))
NT = (((1,), (1,)), ((), ()))
TN = (((0,), (0,)), ((), ()))
ANY = pl.BlockSpec(memory_space=pl.ANY)
HBM = pl.BlockSpec(memory_space=pltpu.HBM)
VMEM_LIMIT = 56 * 2**20
INPUT_VMEM = 24 * 2**20
BACK_VMEM = 44 * 2**20
GATE = 5 * 10**9


def dot(left, right, dims):
    return lax.dot_general(left, right, dims, preferred_element_type=F32)


def beside(*parts):
    return jnp.concatenate(parts, axis=1)


def mean(value):
    return jnp.mean(value, -1, keepdims=True)


def layer_norm(hidden):
    centre = hidden - mean(hidden)
    rstd = lax.rsqrt(mean(centre * centre) + 1e-05)
    return (centre * rstd, rstd)


def norm_back(grad, normal, rstd, gain):
    scaled = grad * gain
    return rstd * (scaled - mean(scaled) - normal * mean(scaled * normal))


def gelu_pair(value):
    below = 0.5 + 0.5 * lax.erf(value * 2.0 ** (-0.5))
    density = jnp.exp(-0.5 * value * value) * 0.3989422804014327
    return (value * below, below + value * density)


def adapter_rows(lines_ref, first, count, width):
    step = width // LANES
    return beside(
        *[lines_ref[pl.ds(first * step + at, count, stride=step), :] for at in range(step)]
    )


def three_parts(value):
    high = value.astype(BF16).astype(F32)
    rest = value - high
    middle = rest.astype(BF16).astype(F32)
    return (high, middle, rest - middle)


def rows_at(rank, flip, side, rows):
    return pl.multiple_of((jnp.bitwise_xor(rank, flip) * 2 + side) * rows, 16)


def side_of(place):
    return jnp.bitwise_and(jnp.bitwise_xor(place, place >> 1), 1)


class Parts:
    def __init__(self, own, blocks, near, others):
        self.own, self.blocks, self.near = own, blocks, near
        self.flips = [flip for flip, _ in others]
        self.operands = list(own) + [near] + [piece for _, piece in others]
        self.copies = len(blocks) * (3 + len(others))

    def into(self, refs, rank, place, views, semaphores):
        count = len(self.own)
        own, near, others = refs[:count], refs[count], refs[count + 1 :]
        rows, width = near.shape[2:]
        mine = side_of(place)
        found = []
        for at, ((source, start), view) in enumerate(zip(self.blocks, views)):
            whole = own[source].at[:, pl.ds(start, width)]
            found.append((whole, view(rows_at(rank, 0, 0, rows), 2 * rows)))
            for side in range(2):
                found.append((near.at[side, at], view(rows_at(rank, 1, side, rows), rows)))
            for (flip, other), ref in zip(self.flips, others):
                if other is None:
                    target = view(rows_at(rank, flip, 0, rows), 2 * rows)
                else:
                    target = view(rows_at(rank, flip, jnp.bitwise_xor(mine, other), rows), rows)
                found.append((ref.at[at], target))
        return [
            pltpu.make_async_copy(source, target, semaphores.at[at])
            for at, (source, target) in enumerate(found)
        ]


def stacked(weights):
    def view(at):
        return lambda row, rows: weights.at[at, pl.ds(row, rows)]

    return [view(at) for at in range(weights.shape[0])]


def in_columns(weights, width):
    def view(start):
        return lambda row, rows: weights.at[pl.ds(row, rows), start : start + width]

    return [view(start) for start in range(0, weights.shape[1], width)]


def run_copies(copies):
    for copy in copies:
        copy.start()
    for copy in copies:
        copy.wait()


def pack_kernel(sets, count, place_ref, *rest):
    sources, rest = rest[:count], rest[count:]
    outs, rest = rest[: 2 * len(sets)], rest[2 * len(sets) :]
    holds, (arrive, leave) = rest[:-2], rest[-2:]
    side = side_of(place_ref[0])
    incoming, outgoing = [], []
    copy = pltpu.make_async_copy
    for blocks, near_ref, mine_ref, hold in zip(sets, outs[::2], outs[1::2], holds):
        rows, width = mine_ref.shape[1:]
        for block, (source, first) in enumerate(blocks):
            for half in range(2):
                part = sources[source].at[pl.ds(half * rows, rows), pl.ds(first, width)]
                incoming.append(copy(part, hold.at[half, block], arrive.at[len(incoming)]))
        outgoing.append((len(incoming), copy(hold.at[side], mine_ref, leave.at[len(outgoing)])))
        outgoing.append((len(incoming), copy(hold, near_ref, leave.at[len(outgoing)])))
    for one in incoming:
        one.start()
    done = 0
    for needed, one in outgoing:
        for other in incoming[done:needed]:
            other.wait()
        done = needed
        one.start()
    for _, one in outgoing:
        one.wait()


def pack(place, shards, sets):
    shapes = []
    holds = []
    copies = 0
    for blocks, width in sets:
        rows = shards[blocks[0][0]].shape[0] // 2
        holds.append((2, len(blocks), rows, width))
        shapes += [holds[-1], holds[-1][1:]]
        copies += 2 * len(blocks)
    found = pl.pallas_call(
        functools.partial(pack_kernel, [blocks for blocks, _ in sets], len(shards)),
        in_specs=[pl.BlockSpec(memory_space=pltpu.SMEM)] + [HBM] * len(shards),
        out_specs=[HBM] * len(shapes),
        out_shape=[jax.ShapeDtypeStruct(shape, BF16) for shape in shapes],
        scratch_shapes=[pltpu.VMEM(shape, BF16) for shape in holds]
        + [pltpu.SemaphoreType.DMA((copies,)), pltpu.SemaphoreType.DMA((len(shapes),))],
        compiler_params=pltpu.CompilerParams(vmem_limit_bytes=VMEM_LIMIT),
        name="pack_shards",
    )(place, *shards)
    return list(zip(found[::2], found[1::2]))


def attend_kernel(parts, rank_ref, place_ref, seg_ref, x_ref, fac_ref, bq_ref, bv_ref, *rest):
    shards, rest = rest[: len(parts.operands)], rest[len(parts.operands) :]
    q_ref, k_ref, v_ref, ctx_ref, aug_ref, down_ref, weights, bias, table, semaphores = rest
    at = pl.program_id(1)
    width = q_ref.shape[1]
    rows = x_ref.shape[0]

    @pl.when((pl.program_id(0) == 0) & (at == 0))
    def _():
        run_copies(parts.into(shards, rank_ref[0], place_ref[0], stacked(weights), semaphores))
        bias[0:1, :] = bq_ref[...].reshape(1, -1)
        bias[1:2, :] = bv_ref[...].reshape(1, -1)
        table[...] = adapter_rows(fac_ref, 0, *table.shape)

    rank2 = 2 * ADAPTER_RANK
    columns = pl.ds(pl.multiple_of(at * width, LANES), width)
    x = x_ref[...]
    low = dot(x, table[0:rank2, :].astype(BF16), NT).astype(BF16)
    down_ref[...] = low
    up = table[rank2 : 2 * rank2, columns]
    row = lax.broadcasted_iota(jnp.int32, up.shape, 0)
    up_q = jnp.where(row < ADAPTER_RANK, up, 0.0).astype(BF16)
    up_v = jnp.where(row < ADAPTER_RANK, 0.0, up).astype(BF16)
    q_ref[...] = (dot(x, weights[0, :, columns], NN) + bias[0:1, columns] + 2.0 * dot(low, up_q, NN)).astype(BF16)
    k_ref[...] = dot(x, weights[1, :, columns], NN).astype(BF16)
    v_ref[...] = (dot(x, weights[2, :, columns], NN) + bias[1:2, columns] + 2.0 * dot(low, up_v, NN)).astype(BF16)

    lane = lax.broadcasted_iota(jnp.int32, (rows, LANES), 1)
    seg = seg_ref[pl.ds(pl.program_id(0), 1), :].astype(F32).T.astype(jnp.int32)
    own = jnp.where(lane == seg, 1.0, 0.0)
    aug_k = jnp.where((lane < 4) & (lane != seg), -MASKED, 0.0).astype(BF16)
    aug_q = own.astype(BF16)
    ones = jnp.ones((rows, LANES), BF16)
    half = LANES // 2
    scale = BF16(half ** (-0.5))
    for pair in range(width // LANES):
        here = slice(LANES * pair, LANES * (pair + 1))
        keys = beside(k_ref[:, here], aug_k)
        values = beside(v_ref[:, here], ones)
        query = q_ref[:, here] * scale
        out = None
        for side in range(2):
            mask = (lane // half) == side
            scores = dot(beside(jnp.where(mask, query, BF16(0)), aug_q), keys, NT)
            top = jnp.max(scores, axis=1, keepdims=True)
            expo = jnp.exp(scores - top).astype(BF16)
            both = dot(expo, values, NN)
            sums = both[:, LANES:]
            ctx = both[:, :LANES] / sums
            out = ctx if side == 0 else jnp.where(mask, ctx, out)
            high, middle, little = three_parts(-(top + jnp.log(sums)))
            aug = jnp.where(
                lane == 4, high, jnp.where(lane == 5, middle, jnp.where(lane == 6, little, own))
            )
            aug_ref[:, (2 * pair + side) * LANES : (2 * pair + side + 1) * LANES] = aug.astype(BF16)
        ctx_ref[:, here] = out.astype(BF16)


def attend(rank, place, seg, x, factors, bq, bv, parts, pairs):
    packs, size = seg.shape
    rows, width = x.shape
    cut = pairs * LANES
    block = pl.BlockSpec((size, cut), lambda p, g: (p, g))
    vmem = pl.BlockSpec(memory_space=pltpu.VMEM)
    smem = pl.BlockSpec(memory_space=pltpu.SMEM)
    like = jax.ShapeDtypeStruct
    return pl.pallas_call(
        functools.partial(attend_kernel, parts),
        grid=(packs, width // cut),
        in_specs=[
            smem,
            smem,
            pl.BlockSpec(memory_space=pltpu.VMEM),
            pl.BlockSpec((size, width), lambda p, g: (p, 0)),
            vmem,
            vmem,
            vmem,
        ]
        + [ANY] * len(parts.operands),
        out_specs=[
            block,
            block,
            block,
            block,
            pl.BlockSpec((size, 2 * cut), lambda p, g: (p, g)),
            pl.BlockSpec((size, 2 * ADAPTER_RANK), lambda p, g: (p, 0)),
            pl.BlockSpec((3, width, width), lambda p, g: (0, 0, 0)),
        ],
        out_shape=[like((rows, width), BF16)] * 4
        + [
            like((rows, 2 * width), BF16),
            like((rows, 2 * ADAPTER_RANK), BF16),
            like((3, width, width), BF16),
        ],
        scratch_shapes=[
            pltpu.VMEM((8, width), F32),
            pltpu.VMEM((4 * ADAPTER_RANK, width), F32),
            pltpu.SemaphoreType.DMA((parts.copies,)),
        ],
        compiler_params=pltpu.CompilerParams(vmem_limit_bytes=VMEM_LIMIT),
        cost_estimate=pl.CostEstimate(flops=1, bytes_accessed=1, transcendentals=0),
        name="project_and_attend",
    )(rank, place, seg, x, factors, bq, bv, *parts.operands)


def dense_kernel(first, second, cut, rank_ref, place_ref, x_ref, ctx_ref, cot_ref, *rest):
    vectors, rest = rest[:7], rest[7:]
    bo_ref, bi_ref, bo2_ref, g1_ref, s1_ref, g2_ref, s2_ref = vectors
    one, two = len(first.operands), len(second.operands)
    near, far, rest = rest[:one], rest[one : one + two], rest[one + two :]
    out_ref, dh_ref, dctx_ref, ahead, outer, slope, semaphores = rest
    width = x_ref.shape[1]
    hidden = outer.shape[0]

    at = pl.program_id(0)
    rank, place = rank_ref[0], place_ref[0]
    start = first.into(near, rank, place, in_columns(ahead, width), semaphores.at[0])
    later = second.into(far, rank, place, in_columns(outer, width), semaphores.at[1])
    count = len(start) // len(first.blocks)
    start, later = start[:count], start[count:] + later

    @pl.when(at == 0)
    def _():
        for copy in start + later:
            copy.start()
        for copy in start:
            copy.wait()

    row = lambda ref: ref[...].reshape(1, -1)
    wo = lambda: ahead[:, :width]
    w1 = lambda j: ahead[:, width + j : width + j + cut]
    inner_bias = row(bi_ref)
    h1 = x_ref[...].astype(F32) + dot(ctx_ref[...], wo(), NN) + row(bo_ref)
    norm1, rstd1 = layer_norm(h1)
    y1 = norm1 * row(g1_ref) + row(s1_ref)
    y1_low = y1.astype(BF16)

    @pl.when(at == 0)
    def _():
        for copy in later:
            copy.wait()

    h2 = y1 + row(bo2_ref)
    for j in range(0, hidden, cut):
        inner = dot(y1_low, w1(j), NN) + inner_bias[:, j : j + cut]
        act, gradient = gelu_pair(inner)
        slope[:, j : j + cut] = gradient
        h2 = h2 + dot(act.astype(BF16), outer[j : j + cut, :], NN)
    norm2, rstd2 = layer_norm(h2)
    out_ref[...] = (norm2 * row(g2_ref) + row(s2_ref)).astype(BF16)
    dh2 = norm_back(cot_ref[...].astype(F32), norm2, rstd2, row(g2_ref))
    df = dh2.astype(BF16)
    dy1 = dh2
    for j in range(0, hidden, cut):
        du = (dot(df, outer[j : j + cut, :], NT) * slope[:, j : j + cut]).astype(BF16)
        dy1 = dy1 + dot(du, w1(j), NT)
    dh1 = norm_back(dy1, norm1, rstd1, row(g1_ref)).astype(BF16)
    dh_ref[...] = dh1
    dctx_ref[...] = dot(dh1, wo(), NT).astype(BF16)


def dense(rank, place, x, ctx, cot, vectors, first, second, size, cut):
    rows, width = x.shape
    hidden = vectors[1].shape[0]
    block = pl.BlockSpec((size, width), lambda i: (i, 0))
    smem = pl.BlockSpec(memory_space=pltpu.SMEM)
    return pl.pallas_call(
        functools.partial(dense_kernel, first, second, cut),
        grid=(rows // size,),
        in_specs=[smem, smem, block, block, block]
        + [pl.BlockSpec(memory_space=pltpu.VMEM)] * len(vectors)
        + [ANY] * (len(first.operands) + len(second.operands)),
        out_specs=[block] * 3,
        out_shape=[jax.ShapeDtypeStruct((rows, width), BF16)] * 3,
        scratch_shapes=[
            pltpu.VMEM((width, width + hidden), BF16),
            pltpu.VMEM((hidden, width), BF16),
            pltpu.VMEM((size, hidden), F32),
            pltpu.SemaphoreType.DMA((2, max(first.copies, second.copies))),
        ],
        compiler_params=pltpu.CompilerParams(vmem_limit_bytes=VMEM_LIMIT),
        cost_estimate=pl.CostEstimate(
            flops=rows * width * (4 * width + 8 * hidden),
            bytes_accessed=12 * rows * width + 4 * width * hidden,
            transcendentals=2 * rows * hidden,
        ),
        name="dense_both_ways",
    )(rank, place, x, ctx, cot, *vectors, *first.operands, *second.operands)


def attend_back_kernel(seg_ref, x_ref, fac_ref, down_ref, *rest):
    q_ref, k_ref, v_ref, dctx_ref, ctx_ref, aug_ref, *rest = rest
    dq_ref, dk_ref, dv_ref, dlow_ref, grad_ref, low, total, table = rest
    pack, at = pl.program_id(0), pl.program_id(1)
    rows, width = q_ref.shape
    rank2 = 2 * ADAPTER_RANK
    columns = pl.ds(pl.multiple_of(at * width, LANES), width)

    @pl.when((pack == 0) & (at == 0))
    def _():
        table[...] = adapter_rows(fac_ref, 0, *table.shape)

    lane = lax.broadcasted_iota(jnp.int32, (rows, LANES), 1)
    seg = seg_ref[pl.ds(pl.program_id(0), 1), :].astype(F32).T.astype(jnp.int32)
    aug_k = jnp.where(
        (lane < 4) & (lane != seg), -MASKED, jnp.where((lane >= 4) & (lane < 7), 1.0, 0.0)
    ).astype(BF16)
    aug_v = jnp.where(lane < 3, 1.0, 0.0).astype(BF16)
    zero = BF16(0)
    half = LANES // 2
    scale = BF16(half ** (-0.5))
    for pair in range(width // LANES):
        here = slice(LANES * pair, LANES * (pair + 1))
        key = k_ref[:, here]
        query = q_ref[:, here] * scale
        grad = dctx_ref[:, here]
        keys = beside(key, aug_k)
        values = beside(v_ref[:, here], aug_v)
        key = key * scale
        product = grad.astype(F32) * ctx_ref[:, here].astype(F32)
        dq = dk = dv = 0.0
        for side in range(2):
            mask = (lane // half) == side
            one_query = jnp.where(mask, query, zero)
            one_grad = jnp.where(mask, grad, zero)
            one_key = jnp.where(mask, key, zero)
            inner = -jnp.sum(jnp.where(mask, product, 0.0), axis=1, keepdims=True)
            high, middle, little = three_parts(inner)
            aug_d = jnp.where(
                lane == 0, high, jnp.where(lane == 1, middle, jnp.where(lane == 2, little, 0.0))
            ).astype(BF16)
            aug_q = aug_ref[:, (2 * pair + side) * LANES : (2 * pair + side + 1) * LANES]
            probs = jnp.exp(dot(keys, beside(one_query, aug_q), NT))
            dprobs = dot(values, beside(one_grad, aug_d), NT)
            dscores = (probs * dprobs).astype(BF16)
            dv = dv + dot(probs.astype(BF16), one_grad, NN)
            dk = dk + dot(dscores, one_query, NN)
            dq = dq + dot(dscores, one_key, TN)
        dq_ref[:, here] = dq.astype(BF16)
        dk_ref[:, here] = dk.astype(BF16)
        dv_ref[:, here] = dv.astype(BF16)

    up = table[rank2 : 2 * rank2, columns]
    row = lax.broadcasted_iota(jnp.int32, up.shape, 0)
    up_q = jnp.where(row < ADAPTER_RANK, up, 0.0).astype(BF16)
    up_v = jnp.where(row < ADAPTER_RANK, 0.0, up).astype(BF16)
    dlow = dot(dq_ref[...], up_q, NT) + dot(dv_ref[...], up_v, NT)
    low[...] = dlow + jnp.where(at == 0, 0.0, low[...])
    down = down_ref[...]
    from_q = dot(down, dq_ref[...], TN)
    from_v = dot(down, dv_ref[...], TN)
    share = 2.0 * jnp.where(row < ADAPTER_RANK, from_q, from_v)
    later = pack > 0
    total[rank2 : 2 * rank2, columns] = share + jnp.where(
        later, total[rank2 : 2 * rank2, columns], 0.0
    )

    @pl.when(at == pl.num_programs(1) - 1)
    def _():
        dlow_low = (2.0 * low[...]).astype(BF16)
        dlow_ref[...] = dlow_low
        total[0:rank2, :] = dot(dlow_low, x_ref[...], TN) + jnp.where(
            later, total[0:rank2, :], 0.0
        )
        grad_ref[...] = total[...].astype(BF16)


def attend_back(seg, x, factors, down, q, k, v, dctx, ctx, aug, pairs):
    packs, size = seg.shape
    rows, width = x.shape
    cut = pairs * LANES
    rank2 = 2 * ADAPTER_RANK
    block = pl.BlockSpec((size, cut), lambda p, g: (p, g))
    whole = lambda shape: pl.BlockSpec(shape, lambda p, g: (0, 0), pipeline_mode=pl.Buffered(1))
    like = jax.ShapeDtypeStruct
    return pl.pallas_call(
        attend_back_kernel,
        grid=(packs, width // cut),
        in_specs=[
            pl.BlockSpec(memory_space=pltpu.VMEM),
            pl.BlockSpec((size, width), lambda p, g: (p, 0)),
            pl.BlockSpec(memory_space=pltpu.VMEM),
            pl.BlockSpec((size, rank2), lambda p, g: (p, 0)),
            block,
            block,
            block,
            block,
            block,
            pl.BlockSpec((size, 2 * cut), lambda p, g: (p, g)),
        ],
        out_specs=[
            block,
            block,
            block,
            pl.BlockSpec((size, rank2), lambda p, g: (p, 0)),
            whole((2 * rank2, width)),
        ],
        out_shape=[like((rows, width), BF16)] * 3
        + [like((rows, rank2), BF16), like((2 * rank2, width), BF16)],
        scratch_shapes=[pltpu.VMEM((size, rank2), F32)]
        + [pltpu.VMEM((2 * rank2, width), F32)] * 2,
        compiler_params=pltpu.CompilerParams(vmem_limit_bytes=BACK_VMEM),
        cost_estimate=pl.CostEstimate(
            flops=rows * width * 30 * size,
            bytes_accessed=24 * rows * width,
            transcendentals=rows * size * HEADS,
        ),
        name="attend_back",
    )(seg, x, factors, down, q, k, v, dctx, ctx, aug)


def input_kernel(first, dh_ref, dq_ref, dk_ref, dv_ref, dlow_ref, fac_ref, weights, *rest):
    out_ref = rest[-1]
    size, width = out_ref.shape
    block = slice(first, first + size)
    down = adapter_rows(fac_ref, 0, 2 * ADAPTER_RANK, width).astype(BF16)
    total = dh_ref[block, :].astype(F32) + dot(dlow_ref[block, :], down, NN)
    for at, grad in enumerate((dq_ref, dk_ref, dv_ref)):
        total = total + dot(grad[block, :], weights[at], NT)
    out_ref[...] = total.astype(BF16)


def input_back(dh, dq, dk, dv, dlow, factors, weights, size, at, carry):
    rows, width = dh.shape
    vmem = pl.BlockSpec(memory_space=pltpu.VMEM)
    return pl.pallas_call(
        functools.partial(input_kernel, at * size),
        grid=(1,),
        in_specs=[vmem] * 7 + [ANY] * len(carry),
        out_specs=pl.BlockSpec((size, width), lambda i: (at, 0)),
        out_shape=jax.ShapeDtypeStruct((rows, width), BF16),
        input_output_aliases={7 + i: i for i in range(len(carry))},
        compiler_params=pltpu.CompilerParams(vmem_limit_bytes=INPUT_VMEM),
        cost_estimate=pl.CostEstimate(
            flops=6 * size * width * width,
            bytes_accessed=10 * size * width,
            transcendentals=0,
        ),
        name="input_gradient",
    )(dh, dq, dk, dv, dlow, factors, weights, *carry)


def update_kernel(place_ref, near_ref, far_ref, fac_ref, held_ref, other_ref, *rest):
    grad_ref, new_ref, new_first_ref, new_second_ref, lines, table, first, second = rest
    place = place_ref[0]
    owners, length, lanes = fac_ref.shape
    grad = near_ref[...].astype(F32) + far_ref[...].astype(F32)
    rows, width = grad.shape
    step = width // lanes
    for at in range(step):
        lines[pl.ds(at, rows, stride=step), :] = grad[:, at * lanes : (at + 1) * lanes]
    for owner in range(owners):
        table[owner] = lines[owner * length : (owner + 1) * length, :]
    half = owners // 2
    for at in range(owners):
        ref = held_ref if at < half else other_ref
        owner = jnp.bitwise_xor(place, at)
        first[owner] = ref[at % half, 0]
        second[owner] = ref[at % half, 1]
    clip = jnp.minimum(1.0, 1.0 / (jnp.sqrt(jnp.sum(grad * grad)) + 1e-06))
    clipped = table[...] * clip
    new_first = 0.9 * first[...] + 0.1 * clipped
    new_second = 0.999 * second[...] + 0.001 * clipped * clipped
    first[...] = new_first
    second[...] = new_second
    grad_ref[...] = table[place]
    new_first_ref[...] = first[place]
    new_second_ref[...] = second[place]
    factors = fac_ref[...]
    owner = lax.broadcasted_iota(jnp.int32, factors.shape, 0)
    rate = jnp.where(owner < half, rate_low, rate_high)
    fix_first = 1.0 - 0.9**STEP
    fix_second = 1.0 - 0.999**STEP
    move = new_first / fix_first / (jnp.sqrt(new_second / fix_second) + 1e-08)
    new_ref[...] = factors - rate * (move + decay_rate * factors)


def update(place, near, far, factors, held, other):
    like = lambda shape: jax.ShapeDtypeStruct(shape, F32)
    owners, length, lanes = factors.shape
    vmem = pl.BlockSpec(memory_space=pltpu.VMEM)
    piece = like((length, lanes))
    return pl.pallas_call(
        update_kernel,
        in_specs=[pl.BlockSpec(memory_space=pltpu.SMEM)] + [vmem] * 5,
        out_shape=[piece, like(factors.shape), piece, piece],
        scratch_shapes=[pltpu.VMEM((owners * length, lanes), F32)]
        + [pltpu.VMEM(factors.shape, F32)] * 3,
        name="adapter_update",
    )(place, near, far, factors, held, other)


def bits(size):
    return [1 << at for at in range(size.bit_length() - 1)]


def swap(value, axis, size, flip):
    return lax.ppermute(value, axis, [(i, i ^ flip) for i in range(size)])


def cross(value, reps, wide):
    pairs = []
    for rank in range(reps):
        for place in range(wide):
            other = place ^ (1 if rank % 2 == 0 else 2)
            pairs.append((rank * wide + place, rank * wide + other))
    return lax.ppermute(value, ("rep", "wide"), pairs)


def fetch(mine, reps):
    held = [(0, mine)]
    for flip in bits(reps)[1:]:
        held += [(have ^ flip, swap(value, "rep", reps, flip)) for have, value in held]
    return held[1:]


def both_cores(halves, reps):
    return [
        ((flip ^ core, other), swap(value, "rep", reps, 1) if core else value)
        for (flip, other), value in halves
        for core in range(2)
    ]


def finish(own, blocks, near, halves, crossed, reps):
    pieces = [((flip, 0), value) for flip, value in halves]
    pieces += [((flip, 1), value) for flip, value in crossed]
    return Parts(own, blocks, swap(near, "rep", reps, 1), both_cores(pieces, reps))


def across(halves, reps, wide):
    return [(flip, cross(value, reps, wide)) for flip, value in halves]


def together(*values):
    return lax.optimization_barrier(values)


def gate_kernel(value_ref, other_ref, out_ref):
    pass


def gate(value, other, flops=10**11):
    return pl.pallas_call(
        gate_kernel,
        in_specs=[ANY, ANY],
        out_specs=ANY,
        out_shape=jax.ShapeDtypeStruct(value.shape, value.dtype),
        input_output_aliases={0: 0},
        cost_estimate=pl.CostEstimate(flops=flops, bytes_accessed=1, transcendentals=0),
        name="gate",
    )(value, other)


def local(sizes, *args):
    (
        tokens,
        segment_ids,
        cotangent,
        w_query,
        w_key,
        w_value,
        w_output,
        w_inner,
        w_outer,
        b_query,
        b_value,
        *vectors,
        factors,
        first_moment,
        second_moment,
    ) = args
    reps, wide = sizes
    width = tokens.shape[1]
    packs, size = segment_ids.shape
    rank = lax.axis_index("rep").reshape(1)
    place = lax.axis_index("wide").reshape(1)
    table = factors.reshape(-1, LANES)

    hidden = w_inner.shape[1]
    own = [w_query, w_key, w_value]
    set_heads = [(at, 0) for at in range(3)]
    own_ahead = [w_output, w_inner]
    set_ahead = [(0, 0)] + [(1, start) for start in range(0, hidden, width)]
    near, mine = pack(place, own, [(set_heads, width)])[0]
    place, mine = together(place, mine)
    near_ahead, mine_ahead = pack(place, own_ahead, [(set_ahead, width)])[0]

    halves = fetch(mine, reps)
    length = first_moment.shape[0] // LANES
    held = jnp.stack([first_moment, second_moment]).reshape(1, 2, length, LANES)
    held, mine_ahead = together(held, mine_ahead)
    flips = bits(wide)
    held = jnp.concatenate([held, swap(held, "wide", wide, flips[0])])
    flip, sent = halves[-1]
    sent, mine_ahead, near, near_ahead, near_outer = together(
        sent, mine_ahead, near, near_ahead, w_outer
    )
    halves_ahead = fetch(mine_ahead, reps)
    sent = gate(sent, held)
    sent, whole_outer = together(sent, w_outer)
    whole_outer = fetch(whole_outer, reps)
    halves = halves[:-1] + [(flip, sent)]
    crossed = across(halves, reps, wide)
    heads = finish(own, set_heads, near, halves, crossed, reps)

    q, k, v, ctx, aug, down, weights = attend(
        rank, place, segment_ids, tokens, table, b_query, b_value, heads, 3
    )
    down, held, *values = together(down, held, *[value for _, value in halves_ahead])
    values = [gate(value, down, GATE) for value in values]
    halves_ahead = [(flip, value) for (flip, _), value in zip(halves_ahead, values)]
    for flip in flips[1:-1]:
        held = jnp.concatenate([held, swap(held, "wide", wide, flip)])
    other = swap(held, "wide", wide, flips[-1])
    crossed_ahead = across(halves_ahead, reps, wide)
    ahead = finish(own_ahead, set_ahead, near_ahead, halves_ahead, crossed_ahead, reps)
    whole = [(flip, value) for flip, value in whole_outer]
    near_outer = swap(near_outer, "rep", reps, 1)
    outer = Parts(
        [w_outer],
        [(0, 0)],
        near_outer.reshape(2, 1, -1, width),
        both_cores([((flip, None), value[None]) for flip, value in whole], reps),
    )
    layer_out, dh, dctx = dense(
        rank, place, tokens, ctx, cotangent, vectors, ahead, outer, size, 1024
    )
    dq, dk, dv, dlow, grad = attend_back(
        segment_ids, tokens, table, down, q, k, v, dctx, ctx, aug, 3
    )
    rounds = [("rep", reps, flip) for flip in bits(reps)]
    rounds += [("wide", wide, flip) for flip in bits(wide)]
    pieces = 4
    part = tokens.shape[0] // pieces
    input_grad = []
    for at, (axis, count, flip) in enumerate(rounds):
        far = swap(grad, axis, count, flip)
        start = at - (len(rounds) - pieces)
        if start >= 0:
            dh, grad = together(dh, grad)
            args = (dh, dq, dk, dv, dlow, table, weights, part, start)
            input_grad = [input_back(*args, input_grad)]
        if at < len(rounds) - 1:
            grad = grad + far
            if start >= 0:
                grad, *input_grad = together(grad, *input_grad)
    flat = factors.reshape(wide, length, LANES)
    new = update(place, grad, far, flat, held, other)
    piece, new_factors, new_first, new_second = [value.reshape(-1) for value in new]
    return (layer_out, input_grad[0], piece, new_factors, new_first, new_second)


def solution(mesh):
    rows = P(("rep", "wide"), None)
    shard = P("rep", None)
    piece = P("wide")
    placed = (rows,) * 3 + (shard,) * 6 + (P(),) * 10 + (piece,) * 2
    return jax.shard_map(
        functools.partial(local, (mesh.shape["rep"], mesh.shape["wide"])),
        mesh=mesh,
        in_specs=placed,
        out_specs=(rows, rows, piece, P(), piece, piece),
        check_vma=False,
    )
```

time: 207 us -> 151 us (0.73)
  waiting for transfers between devices: 72.6 us -> 26.6 us
  local copies, waits for them, and re-layouts: 18.9 us -> 3.85 us
  starting transfers between devices: 17.9 us -> 21.7 us
  Pallas kernels: 94.9 us -> 98 us
    ppermute x17 -> x19, waiting for transfers between devices: 72.6 us -> 19.7 us  [swap(): return lax.ppermute(value, axis, [(i, i ^ flip) for i in range(size)])]
    reshape x14 -> x0, local copies, waits for them, and re-layouts: 10.2 us -> none  [the longest x8 4.7 us: local(): flat = lambda vector: vector.reshape(1, -1)]
    ppermute x0 -> x2, waiting for transfers between devices: none -> 6.88 us  [cross(): return lax.ppermute(value, ('rep', 'wide'), pairs)]
    pallas_call x4 -> x11, Pallas kernels: 70.1 us -> 74.4 us  [the longest x1 35.6 us: dense(): pl.pallas_call(functools.partial(dense_kernel, first, second, cut), grid=...]
    ppermute x0 -> x2, starting transfers between devices: none -> 3.27 us  [cross(): return lax.ppermute(value, ('rep', 'wide'), pairs)]
    ppermute x17 -> x19, starting transfers between devices: 17.9 us -> 18.5 us  [swap(): return lax.ppermute(value, axis, [(i, i ^ flip) for i in range(size)])]
  transfers between devices with their start and end apart: 17 -> 21, of which waited for: 5 -> 11; matrix products, arithmetic and copies ran while one was open for 4% -> 0% of each run, Pallas kernels for 45% -> 62%
where the time goes in v2:
time: 151 us
  Pallas kernels  98 us (65%)
  waiting for transfers between devices  26.6 us (18%)
  starting transfers between devices  21.7 us (14%)
  local copies, waits for them, and re-layouts  3.85 us (3%)
    pallas_call x1, Pallas kernels, dense(): pl.pallas_call(functools.partial(dense_kernel, first, second, cut), grid=...  35.6 us
    pallas_call x1, Pallas kernels, attend(): pl.pallas_call(functools.partial(attend_kernel, parts), grid=(packs, widt...  23.9 us
    pallas_call x1, Pallas kernels, attend_back(): pl.pallas_call(attend_back_kernel, grid=(packs, width // cut), in_specs=[...  23.6 us
    ppermute x19, waiting for transfers between devices, swap(): return lax.ppermute(value, axis, [(i, i ^ flip) for i in range(size)])  19.7 us
    ppermute x19, starting transfers between devices, swap(): return lax.ppermute(value, axis, [(i, i ^ flip) for i in range(size)])  18.5 us
    pallas_call x4, Pallas kernels, input_back(): pl.pallas_call(functools.partial(input_kernel, at * size), grid=(1,), in_...  7.61 us
    ppermute x2, waiting for transfers between devices, cross(): return lax.ppermute(value, ('rep', 'wide'), pairs)  6.88 us
    pallas_call x2, Pallas kernels, pack(): pl.pallas_call(functools.partial(pack_kernel, [blocks for blocks, _ in se...  5.26 us
  transfers between devices with their start and end apart: 21, of which 11 were waited for; matrix products, arithmetic and copies ran while one was open for 0% of the time, Pallas kernels for 62%

profile of v2, /device:TPU:0, one launch (start us, length us, event | category | flops | bytes accessed | tf_op | source)
XLA Modules:
  0.0 151.2 jit_solution(2882468355909220870)
XLA Ops:
  0.7 2.4 %pack_shards.2 = (bf16[2,3,96,768]{3,2,1,0:T(8,128)(2,1)}, bf16[3,96,768]{2,1,0:T(8,128)(2,1)}) custom-call(s32[1]{0:T(128)} %bitcast.1.place_ref, bf16[192,768]{1,0:T(8,128)(2,1)} %rest_0_.6, bf16[192,768]{1,0:T(8,128)(2,1)} %rest_1_.6, bf16[192,768]{1,0:T(8,128)(2,1)} %rest_2_.4), custom_call_target="tpu_custom_call" | custom-call | tf_op jit(solution)/shard_map/pack_shards/pallas_call | solution.py:171
  3.0 3.0 %collective-permute-start = (bf16[3,96,768]{2,1,0:T(8,128)(2,1)}, bf16[3,96,768]{2,1,0:T(8,128)(2,1)S(1)}, u32[]{:S(2)}, u32[]{:S(2)}) collective-permute-start(bf16[3,96,768]{2,1,0:T(8,128)(2,1)} %get-tuple-element.59), channel_id=1, source_target_pairs={{0,16},{8,24},{16,0},{24,8},{1,17},{9,25},{17,1},{25,9},{2,18},{10... | collective-permute-start | bytes 1327112 | tf_op jit(solution)/shard_map/ppermute | solution.py:581
  6.1 2.9 %pack_shards.3 = (bf16[2,5,96,768]{3,2,1,0:T(8,128)(2,1)}, bf16[5,96,768]{2,1,0:T(8,128)(2,1)}) custom-call(s32[1]{0:T(128)} %bitcast.1.place_ref, bf16[192,768]{1,0:T(8,128)(2,1)} %rest_7_.1, bf16[192,3072]{1,0:T(8,128)(2,1)} %rest_8_.1), custom_call_target="tpu_custom_call" | custom-call | tf_op jit(solution)/shard_map/pack_shards/pallas_call | solution.py:171
  9.0 1.6 %collective-permute-start.2 = (f32[1,2,24,128]{3,2,1,0:T(8,128)S(1)}, f32[1,2,24,128]{3,2,1,0:T(8,128)S(1)}, u32[]{:S(2)}, u32[]{:S(2)}) collective-permute-start(f32[1,2,24,128]{3,2,1,0:T(8,128)S(1)} %pad_maximum_fusion), channel_id=1, source_target_pairs={{0,1},{1,0},{2,3},{3,2},{4,5},{5,4},{6,7},{7,6},{8,9},{9,8},{10,11... | collective-permute-start | bytes 73736 | tf_op jit(solution)/shard_map/ppermute | solution.py:581
  10.6 2.3 %collective-permute-done.2 = f32[1,2,24,128]{3,2,1,0:T(8,128)S(1)} collective-permute-done((f32[1,2,24,128]{3,2,1,0:T(8,128)S(1)}, f32[1,2,24,128]{3,2,1,0:T(8,128)S(1)}, u32[]{:S(2)}, u32[]{:S(2)}) %collective-permute-start.2) | collective-permute-done | bytes 24608 | tf_op jit(solution)/shard_map/ppermute | solution.py:581
  12.9 3.6 %collective-permute-done.value_ref = bf16[3,96,768]{2,1,0:T(8,128)(2,1)S(1)} collective-permute-done((bf16[3,96,768]{2,1,0:T(8,128)(2,1)}, bf16[3,96,768]{2,1,0:T(8,128)(2,1)S(1)}, u32[]{:S(2)}, u32[]{:S(2)}) %collective-permute-start) | collective-permute-done | bytes 442400 | tf_op jit(solution)/shard_map/ppermute | solution.py:581
  16.5 0.0 collective-permute-start.1
  16.5 0.8 copy-done.12
  17.2 1.7 %collective-permute-start.4 = (bf16[3,96,768]{2,1,0:T(8,128)(2,1)}, bf16[3,96,768]{2,1,0:T(8,128)(2,1)S(1)}, u32[]{:S(2)}, u32[]{:S(2)}) collective-permute-start(bf16[3,96,768]{2,1,0:T(8,128)(2,1)} %gate.2.rest_4_), channel_id=1, source_target_pairs={{0,1},{1,0},{2,3},{3,2},{4,5},{5,4},{6,7},{7,6},{8,10},{9,11},{10,... | collective-permute-start | bytes 1327112 | tf_op jit(solution)/shard_map/ppermute | solution.py:590
  19.0 1.5 %collective-permute-start.7 = (bf16[5,96,768]{2,1,0:T(8,128)(2,1)}, bf16[5,96,768]{2,1,0:T(8,128)(2,1)}, u32[]{:S(2)}, u32[]{:S(2)}) collective-permute-start(bf16[5,96,768]{2,1,0:T(8,128)(2,1)} %get-tuple-element.71), channel_id=1, source_target_pairs={{0,16},{8,24},{16,0},{24,8},{1,17},{9,25},{17,1},{25,9},{2,18},{10... | collective-permute-start | bytes 2211848 | tf_op jit(solution)/shard_map/ppermute | solution.py:581
  20.5 0.0 collective-permute-start.3
  20.5 5.3 %collective-permute-done.4.rest_6_ = bf16[3,96,768]{2,1,0:T(8,128)(2,1)S(1)} collective-permute-done((bf16[3,96,768]{2,1,0:T(8,128)(2,1)}, bf16[3,96,768]{2,1,0:T(8,128)(2,1)S(1)}, u32[]{:S(2)}, u32[]{:S(2)}) %collective-permute-start.4) | collective-permute-done | bytes 442400 | tf_op jit(solution)/shard_map/ppermute | solution.py:590
  25.8 0.0 collective-permute-start.5
  25.8 0.0 copy-done.21
  25.8 1.8 %collective-permute-start.12 = (bf16[768,768]{1,0:T(8,128)(2,1)S(1)}, bf16[768,768]{1,0:T(8,128)(2,1)}, u32[]{:S(2)}, u32[]{:S(2)}) collective-permute-start(bf16[768,768]{1,0:T(8,128)(2,1)S(1)} %copy-done.21), channel_id=1, source_target_pairs={{0,16},{8,24},{16,0},{24,8},{1,17},{9,25},{17,1},{25,9},{2,18},{10... | collective-permute-start | bytes 3538952 | tf_op jit(solution)/shard_map/ppermute | solution.py:581
  27.6 0.0 collective-permute-done.3.rest_5_
  27.6 0.2 collective-permute-start.6
  27.7 0.0 collective-permute-done.1.rest_3_
  27.8 0.0 collective-permute-done.5.rest_7_
  27.8 0.0 copy-start.11
  27.8 0.6 copy-done.10
  28.3 0.4 copy-done.8
  28.7 0.2 copy-done.11
  28.9 23.9 %project_and_attend.1 = (bf16[1024,768]{1,0:T(8,128)(2,1)}, bf16[1024,768]{1,0:T(8,128)(2,1)}, bf16[1024,768]{1,0:T(8,128)(2,1)}, bf16[1024,768]{1,0:T(8,128)(2,...) custom-call(s32[1]{0:T(128)} %bitcast.rank_ref, s32[1]{0:T(128)} %bitcast.1.place_ref, ...), custom_call_target="tpu_custom_call" | custom-call | flops 1 | bytes 1 | tf_op jit(solution)/shard_map/project_and_attend/pallas_call | solution.py:250
  52.8 0.0 collective-permute-done.7.value_ref
  52.8 0.0 copy-start.16
  52.9 1.6 %collective-permute-start.9 = (bf16[5,96,768]{2,1,0:T(8,128)(2,1)}, bf16[5,96,768]{2,1,0:T(8,128)(2,1)S(1)}, u32[]{:S(2)}, u32[]{:S(2)}) collective-permute-start(bf16[5,96,768]{2,1,0:T(8,128)(2,1)} %gate.3.rest_10_), channel_id=1, source_target_pairs={{0,1},{1,0},{2,3},{3,2},{4,5},{5,4},{6,7},{7,6},{8,10},{9,11},{10,... | collective-permute-start | bytes 2211848 | tf_op jit(solution)/shard_map/ppermute | solution.py:590
  54.4 0.2 collective-permute-start.11
  54.6 7.9 %collective-permute-done.12 = bf16[768,768]{1,0:T(8,128)(2,1)} collective-permute-done((bf16[768,768]{1,0:T(8,128)(2,1)S(1)}, bf16[768,768]{1,0:T(8,128)(2,1)}, u32[]{:S(2)}, u32[]{:S(2)}) %collective-permute-start.12) | collective-permute-done | bytes 1179680 | tf_op jit(solution)/shard_map/ppermute | solution.py:581
  62.5 0.0 collective-permute-start.13
  62.5 0.5 collective-permute-start.8
  63.0 1.6 %collective-permute-done.9.rest_12_ = bf16[5,96,768]{2,1,0:T(8,128)(2,1)S(1)} collective-permute-done((bf16[5,96,768]{2,1,0:T(8,128)(2,1)}, bf16[5,96,768]{2,1,0:T(8,128)(2,1)S(1)}, u32[]{:S(2)}, u32[]{:S(2)}) %collective-permute-start.9) | collective-permute-done | bytes 737312 | tf_op jit(solution)/shard_map/ppermute | solution.py:590
  64.6 0.0 collective-permute-start.10
  64.6 0.0 collective-permute-done.11
  64.6 1.6 %collective-permute-start.19 = (f32[2,2,24,128]{3,2,1,0:T(8,128)S(1)}, f32[2,2,24,128]{3,2,1,0:T(8,128)S(1)}, u32[]{:S(2)}, u32[]{:S(2)}) collective-permute-start(f32[2,2,24,128]{3,2,1,0:T(8,128)S(1)} %copy-done.16), channel_id=1, source_target_pairs={{0,2},{1,3},{2,0},{3,1},{4,6},{5,7},{6,4},{7,5},{8,10},{9,11},{10,... | collective-permute-start | bytes 147464 | tf_op jit(solution)/shard_map/ppermute | solution.py:581
  66.3 0.0 collective-permute-done.6.rest_9_
  66.3 0.3 collective-permute-done.8.rest_11_
  66.6 0.8 collective-permute-done.10.rest_13_
  67.4 0.0 collective-permute-done.13.rest_17_
  67.5 0.0 copy-done.25
  67.5 0.9 copy-done.26
  68.3 0.4 copy-done.23
  68.7 0.0 copy-start.5
  68.8 35.6 %dense_both_ways.1 = (bf16[1024,768]{1,0:T(8,128)(2,1)}, bf16[1024,768]{1,0:T(8,128)(2,1)}, bf16[1024,768]{1,0:T(8,128)(2,1)}) custom-call(s32[1]{0:T(128)} %bitcast.rank_ref, s32[1]{0:T(128)} %bitcast.1.place_ref, bf16[1024,768]{1,0:T(8,128)(2,1)} %x_ref.5, bf16[1024,768]{1,0:T(8,128)(2,1)} %get-tuple-element.68.ctx_ref.rest_4_, bf16[1024,768]{1,0:T(8,128)(2,1)} %cot_ref.1, ...), custom_call_target="tpu_custom_call" | custom-call | flops 21743271936 | bytes 18874368 | tf_op jit(solution)/shard_map/dense_both_ways/pallas_call | solution.py:350
  104.4 23.6 %attend_back.1 = (bf16[1024,768]{1,0:T(8,128)(2,1)S(1)}, bf16[1024,768]{1,0:T(8,128)(2,1)S(1)}, bf16[1024,768]{1,0:T(8,128)(2,1)S(1)}, bf16[1024,16]{1,0:T(8,128)(2,1)S(1)}, bf16[32,768]{1,0:T(8,128)(2,1)S(1)}) custom-call(s32[2,512]{1,0:T(2,128)S(1)} %copy-done.4, bf16[1024,768]{1,0:T(8,128)(2,1)S(1)} %copy-done.3, f32[192,128]{1,0:T(8,128)S(1)} %bitcast.14, ...), custom_call_target="tpu_custom_call" | custom-call | flops 12079595520 | bytes 18874368 | tf_op jit(solution)/shard_map/attend_back/pallas_call | solution.py:459
  128.0 0.2 collective-permute-start.14
  128.2 0.0 collective-permute-done.19
  128.2 2.7 %collective-permute-start.20 = (f32[4,2,24,128]{3,2,1,0:T(8,128)S(1)}, f32[4,2,24,128]{3,2,1,0:T(8,128)S(1)}, u32[]{:S(2)}, u32[]{:S(2)}) collective-permute-start(f32[4,2,24,128]{3,2,1,0:T(8,128)S(1)} %constant_dynamic-update-slice_fusion.2.held_ref), channel_id=1, source_target_pairs={{0,4},{1,5},{2,6},{3,7},{4,0},{5,1},{6,2},{7,3},{8,12},{9,13},{10,... | collective-permute-start | bytes 294920 | tf_op jit(solution)/shard_map/ppermute | solution.py:581
  130.9 0.0 collective-permute-done.14
  131.0 1.6 %collective-permute-start.15 = (bf16[32,768]{1,0:T(8,128)(2,1)S(1)}, bf16[32,768]{1,0:T(8,128)(2,1)S(1)}, u32[]{:S(2)}, u32[]{:S(2)}) collective-permute-start(bf16[32,768]{1,0:T(8,128)(2,1)S(1)} %add.12), channel_id=1, source_target_pairs={{0,16},{8,24},{16,0},{24,8},{1,17},{9,25},{17,1},{25,9},{2,18},{10... | collective-permute-start | bytes 147464 | tf_op jit(solution)/shard_map/ppermute | solution.py:581
  132.5 1.9 %input_gradient.4.rest_0_ = bf16[1024,768]{1,0:T(8,128)(2,1)} custom-call(bf16[1024,768]{1,0:T(8,128)(2,1)S(1)} %copy-done.1, bf16[1024,768]{1,0:T(8,128)(2,1)S(1)} %get-tuple-element.86.dq_ref, bf16[1024,768]{1,0:T(8,128)(2,1)S(1)} %get-tuple-element.87.dk_ref, bf16[1024,768]{1,0:T(8,128)(2,1)S(1)} %get-tuple-element.88.dv_ref, ...), custom_call_target="tpu_custom_call" | custom-call | flops 905969664 | bytes 1966080 | tf_op jit(solution)/shard_map/input_gradient/pallas_call | solution.py:509
  134.4 0.7 collective-permute-done.15
  135.1 1.5 %collective-permute-start.16 = (bf16[32,768]{1,0:T(8,128)(2,1)S(1)}, bf16[32,768]{1,0:T(8,128)(2,1)S(1)}, u32[]{:S(2)}, u32[]{:S(2)}) collective-permute-start(bf16[32,768]{1,0:T(8,128)(2,1)S(1)} %add.13), channel_id=1, source_target_pairs={{0,1},{1,0},{2,3},{3,2},{4,5},{5,4},{6,7},{7,6},{8,9},{9,8},{10,11... | collective-permute-start | bytes 147464 | tf_op jit(solution)/shard_map/ppermute | solution.py:581
  136.7 1.9 %input_gradient.5.rest_0_ = bf16[1024,768]{1,0:T(8,128)(2,1)} custom-call(bf16[1024,768]{1,0:T(8,128)(2,1)S(1)} %copy-done.1, bf16[1024,768]{1,0:T(8,128)(2,1)S(1)} %get-tuple-element.86.dq_ref, bf16[1024,768]{1,0:T(8,128)(2,1)S(1)} %get-tuple-element.87.dk_ref, bf16[1024,768]{1,0:T(8,128)(2,1)S(1)} %get-tuple-element.88.dv_ref, ...), custom_call_target="tpu_custom_call", output_to_operand_aliasing={{}: (7, {})} | custom-call | flops 905969664 | bytes 1966080 | tf_op jit(solution)/shard_map/input_gradient/pallas_call | solution.py:509
  138.6 0.7 collective-permute-done.16
  139.3 1.0 collective-permute-start.17
  140.3 1.9 %input_gradient.6.rest_0_ = bf16[1024,768]{1,0:T(8,128)(2,1)} custom-call(bf16[1024,768]{1,0:T(8,128)(2,1)S(1)} %copy-done.1, bf16[1024,768]{1,0:T(8,128)(2,1)S(1)} %get-tuple-element.86.dq_ref, bf16[1024,768]{1,0:T(8,128)(2,1)S(1)} %get-tuple-element.87.dk_ref, bf16[1024,768]{1,0:T(8,128)(2,1)S(1)} %get-tuple-element.88.dv_ref, ...), custom_call_target="tpu_custom_call", output_to_operand_aliasing={{}: (7, {})} | custom-call | flops 905969664 | bytes 1966080 | tf_op jit(solution)/shard_map/input_gradient/pallas_call | solution.py:509
  142.2 1.2 collective-permute-done.17
  143.5 1.1 collective-permute-start.18
  144.5 1.9 %input_gradient.7 = bf16[1024,768]{1,0:T(8,128)(2,1)} custom-call(bf16[1024,768]{1,0:T(8,128)(2,1)S(1)} %copy-done.1, bf16[1024,768]{1,0:T(8,128)(2,1)S(1)} %get-tuple-element.86.dq_ref, bf16[1024,768]{1,0:T(8,128)(2,1)S(1)} %get-tuple-element.87.dk_ref, bf16[1024,768]{1,0:T(8,128)(2,1)S(1)} %get-tuple-element.88.dv_ref, ...), custom_call_target="tpu_custom_call", output_to_operand_aliasing={{}: (7, {})} | custom-call | flops 905969664 | bytes 1966080 | tf_op jit(solution)/shard_map/input_gradient/pallas_call | solution.py:509
  146.4 0.0 collective-permute-done.20.other_ref
  146.5 2.1 %collective-permute-done.18.far_ref = bf16[32,768]{1,0:T(8,128)(2,1)S(1)} collective-permute-done((bf16[32,768]{1,0:T(8,128)(2,1)S(1)}, bf16[32,768]{1,0:T(8,128)(2,1)S(1)}, u32[]{:S(2)}, u32[]{:S(2)}) %collective-permute-start.18) | collective-permute-done | bytes 49184 | tf_op jit(solution)/shard_map/ppermute | solution.py:581
  148.5 0.6 copy-done.18
  149.1 2.0 %adapter_update.1 = (f32[24,128]{1,0:T(8,128)}, f32[8,24,128]{2,1,0:T(8,128)}, f32[24,128]{1,0:T(8,128)}, f32[24,128]{1,0:T(8,128)}) custom-call(s32[1]{0:T(128)} %bitcast.1.place_ref, bf16[32,768]{1,0:T(8,128)(2,1)} %copy-done.14, bf16[32,768]{1,0:T(8,128)(2,1)} %copy-done.18, f32[8,24,128]{2,1,0:T(8,128)} %bitcast.13, f32[4,2,24,128]{3,2,1,0:T(8,128)} %copy-done.13, ...), custom_call_target="tpu_custom_call" | custom-call | tf_op jit(solution)/shard_map/adapter_update/pallas_call | solution.py:566
  (53 shorter events, 0.2 us)
Async XLA Ops:
  0.6 8.3 %copy-start.19 = (f32[3072]{0:T(1024)S(1)}, f32[3072]{0:T(1024)}, u32[]{:S(2)}) copy-start(f32[3072]{0:T(1024)} %param.41) | copy-start | bytes 36868
  0.6 8.3 %copy-start.20 = (f32[3072]{0:T(1024)S(1)}, f32[3072]{0:T(1024)}, u32[]{:S(2)}) copy-start(f32[3072]{0:T(1024)} %param.40) | copy-start | bytes 36868
  3.0 13.4 %collective-permute-start = (bf16[3,96,768]{2,1,0:T(8,128)(2,1)}, bf16[3,96,768]{2,1,0:T(8,128)(2,1)S(1)}, u32[]{:S(2)}, u32[]{:S(2)}) collective-permute-start(bf16[3,96,768]{2,1,0:T(8,128)(2,1)} %get-tuple-element.59), channel_id=1, source_target_pairs={{0,16},{8,24},{16,0},{24,8},{1,17},{9,25},{17,1},{25,9},{2,18},{10... | collective-permute-start | bytes 1327112 | tf_op jit(solution)/shard_map/ppermute | solution.py:581
  9.0 3.9 %collective-permute-start.2 = (f32[1,2,24,128]{3,2,1,0:T(8,128)S(1)}, f32[1,2,24,128]{3,2,1,0:T(8,128)S(1)}, u32[]{:S(2)}, u32[]{:S(2)}) collective-permute-start(f32[1,2,24,128]{3,2,1,0:T(8,128)S(1)} %pad_maximum_fusion), channel_id=1, source_target_pairs={{0,1},{1,0},{2,3},{3,2},{4,5},{5,4},{6,7},{7,6},{8,9},{9,8},{10,11... | collective-permute-start | bytes 73736 | tf_op jit(solution)/shard_map/ppermute | solution.py:581
  12.9 3.6 %copy-start.15 = (f32[2,2,24,128]{3,2,1,0:T(8,128)}, f32[2,2,24,128]{3,2,1,0:T(8,128)S(1)}, u32[]{:S(2)}) copy-start(f32[2,2,24,128]{3,2,1,0:T(8,128)S(1)} %constant_dynamic-update-slice_fusion.other_ref) | copy-start | bytes 147460
  16.5 0.8 copy-start.12
  16.5 9.3 %copy-start.21 = (bf16[768,768]{1,0:T(8,128)(2,1)S(1)}, bf16[768,768]{1,0:T(8,128)(2,1)}, u32[]{:S(2)}) copy-start(bf16[768,768]{1,0:T(8,128)(2,1)} %rest_14_.1) | copy-start | bytes 3538948
  16.5 11.3 %collective-permute-start.1 = (bf16[2,3,96,768]{3,2,1,0:T(8,128)(2,1)}, bf16[2,3,96,768]{3,2,1,0:T(8,128)(2,1)S(1)}, u32[]{:S(2)}, u32[]{:S(2)}) collective-permute-start(bf16[2,3,96,768]{3,2,1,0:T(8,128)(2,1)} %get-tuple-element.64), channel_id=1, source_target_pairs={{0,8},{8,0},{16,24},{24,16},{1,9},{9,1},{17,25},{25,17},{2,10},{10... | collective-permute-start | bytes 2654216 | tf_op jit(solution)/shard_map/ppermute | solution.py:581
  17.2 8.5 %collective-permute-start.4 = (bf16[3,96,768]{2,1,0:T(8,128)(2,1)}, bf16[3,96,768]{2,1,0:T(8,128)(2,1)S(1)}, u32[]{:S(2)}, u32[]{:S(2)}) collective-permute-start(bf16[3,96,768]{2,1,0:T(8,128)(2,1)} %gate.2.rest_4_), channel_id=1, source_target_pairs={{0,1},{1,0},{2,3},{3,2},{4,5},{5,4},{6,7},{7,6},{8,10},{9,11},{10,... | collective-permute-start | bytes 1327112 | tf_op jit(solution)/shard_map/ppermute | solution.py:590
  19.0 33.9 %collective-permute-start.7 = (bf16[5,96,768]{2,1,0:T(8,128)(2,1)}, bf16[5,96,768]{2,1,0:T(8,128)(2,1)}, u32[]{:S(2)}, u32[]{:S(2)}) collective-permute-start(bf16[5,96,768]{2,1,0:T(8,128)(2,1)} %get-tuple-element.71), channel_id=1, source_target_pairs={{0,16},{8,24},{16,0},{24,8},{1,17},{9,25},{17,1},{25,9},{2,18},{10... | collective-permute-start | bytes 2211848 | tf_op jit(solution)/shard_map/ppermute | solution.py:581
  20.5 7.1 %collective-permute-start.3 = (bf16[3,96,768]{2,1,0:T(8,128)(2,1)}, bf16[3,96,768]{2,1,0:T(8,128)(2,1)S(1)}, u32[]{:S(2)}, u32[]{:S(2)}) collective-permute-start(bf16[3,96,768]{2,1,0:T(8,128)(2,1)} %gate.2.rest_4_), channel_id=1, source_target_pairs={{0,8},{8,0},{16,24},{24,16},{1,9},{9,1},{17,25},{25,17},{2,10},{10... | collective-permute-start | bytes 1327112 | tf_op jit(solution)/shard_map/ppermute | solution.py:581
  25.8 2.0 %copy-start.9 = (bf16[3,96,768]{2,1,0:T(8,128)(2,1)}, bf16[3,96,768]{2,1,0:T(8,128)(2,1)S(1)}, u32[]{:S(2)}) copy-start(bf16[3,96,768]{2,1,0:T(8,128)(2,1)S(1)} %collective-permute-done.4.rest_6_) | copy-start | bytes 1327108
  25.8 2.0 %collective-permute-start.5 = (bf16[3,96,768]{2,1,0:T(8,128)(2,1)S(1)}, bf16[3,96,768]{2,1,0:T(8,128)(2,1)S(1)}, u32[]{:S(2)}, u32[]{:S(2)}) collective-permute-start(bf16[3,96,768]{2,1,0:T(8,128)(2,1)S(1)} %collective-permute-done.4.rest_6_), channel_id=1, source_target_pairs={{0,8},{8,0},{16,24},{24,16},{1,9},{9,1},{17,25},{25,17},{2,10},{10... | collective-permute-start | bytes 1327112 | tf_op jit(solution)/shard_map/ppermute | solution.py:581
  25.8 36.7 %collective-permute-start.12 = (bf16[768,768]{1,0:T(8,128)(2,1)S(1)}, bf16[768,768]{1,0:T(8,128)(2,1)}, u32[]{:S(2)}, u32[]{:S(2)}) collective-permute-start(bf16[768,768]{1,0:T(8,128)(2,1)S(1)} %copy-done.21), channel_id=1, source_target_pairs={{0,16},{8,24},{16,0},{24,8},{1,17},{9,25},{17,1},{25,9},{2,18},{10... | collective-permute-start | bytes 3538952 | tf_op jit(solution)/shard_map/ppermute | solution.py:581
  27.6 0.8 copy-start.10
  27.6 38.7 %collective-permute-start.6 = (bf16[2,5,96,768]{3,2,1,0:T(8,128)(2,1)}, bf16[2,5,96,768]{3,2,1,0:T(8,128)(2,1)}, u32[]{:S(2)}, u32[]{:S(2)}) collective-permute-start(bf16[2,5,96,768]{3,2,1,0:T(8,128)(2,1)} %get-tuple-element.69), channel_id=1, source_target_pairs={{0,8},{8,0},{16,24},{24,16},{1,9},{9,1},{17,25},{25,17},{2,10},{10... | collective-permute-start | bytes 4423688 | tf_op jit(solution)/shard_map/ppermute | solution.py:581
  27.8 1.0 copy-start.8
  27.8 1.1 copy-start.11
  52.8 11.8 %copy-start.16 = (f32[2,2,24,128]{3,2,1,0:T(8,128)S(1)}, f32[2,2,24,128]{3,2,1,0:T(8,128)}, u32[]{:S(2)}) copy-start(f32[2,2,24,128]{3,2,1,0:T(8,128)} %copy-done.15) | copy-start | bytes 147460
  52.9 11.7 %collective-permute-start.9 = (bf16[5,96,768]{2,1,0:T(8,128)(2,1)}, bf16[5,96,768]{2,1,0:T(8,128)(2,1)S(1)}, u32[]{:S(2)}, u32[]{:S(2)}) collective-permute-start(bf16[5,96,768]{2,1,0:T(8,128)(2,1)} %gate.3.rest_10_), channel_id=1, source_target_pairs={{0,1},{1,0},{2,3},{3,2},{4,5},{5,4},{6,7},{7,6},{8,10},{9,11},{10,... | collective-permute-start | bytes 2211848 | tf_op jit(solution)/shard_map/ppermute | solution.py:590
  54.4 10.2 %collective-permute-start.11 = (bf16[768,768]{1,0:T(8,128)(2,1)S(1)}, bf16[768,768]{1,0:T(8,128)(2,1)S(1)}, u32[]{:S(2)}, u32[]{:S(2)}) collective-permute-start(bf16[768,768]{1,0:T(8,128)(2,1)S(1)} %copy-done.21), channel_id=1, source_target_pairs={{0,8},{8,0},{16,24},{24,16},{1,9},{9,1},{17,25},{25,17},{2,10},{10... | collective-permute-start | bytes 3538952 | tf_op jit(solution)/shard_map/ppermute | solution.py:581
  62.5 5.0 %collective-permute-start.13 = (bf16[1,768,768]{2,1,0:T(8,128)(2,1)}, bf16[1,768,768]{2,1,0:T(8,128)(2,1)S(1)}, u32[]{:S(2)}, u32[]{:S(2)}) collective-permute-start(bf16[1,768,768]{2,1,0:T(8,128)(2,1)} %bitcast.6.rest_16_), channel_id=1, source_target_pairs={{0,8},{8,0},{16,24},{24,16},{1,9},{9,1},{17,25},{25,17},{2,10},{10... | collective-permute-start | bytes 3538952 | tf_op jit(solution)/shard_map/ppermute | solution.py:581
  62.5 4.1 %collective-permute-start.8 = (bf16[5,96,768]{2,1,0:T(8,128)(2,1)}, bf16[5,96,768]{2,1,0:T(8,128)(2,1)S(1)}, u32[]{:S(2)}, u32[]{:S(2)}) collective-permute-start(bf16[5,96,768]{2,1,0:T(8,128)(2,1)} %gate.3.rest_10_), channel_id=1, source_target_pairs={{0,8},{8,0},{16,24},{24,16},{1,9},{9,1},{17,25},{25,17},{2,10},{10... | collective-permute-start | bytes 2211848 | tf_op jit(solution)/shard_map/ppermute | solution.py:581
  64.6 4.1 %copy-start.24 = (bf16[5,96,768]{2,1,0:T(8,128)(2,1)}, bf16[5,96,768]{2,1,0:T(8,128)(2,1)S(1)}, u32[]{:S(2)}) copy-start(bf16[5,96,768]{2,1,0:T(8,128)(2,1)S(1)} %collective-permute-done.9.rest_12_) | copy-start | bytes 2211844
  64.6 2.8 %collective-permute-start.10 = (bf16[5,96,768]{2,1,0:T(8,128)(2,1)S(1)}, bf16[5,96,768]{2,1,0:T(8,128)(2,1)S(1)}, u32[]{:S(2)}, u32[]{:S(2)}) collective-permute-start(bf16[5,96,768]{2,1,0:T(8,128)(2,1)S(1)} %collective-permute-done.9.rest_12_), channel_id=1, source_target_pairs={{0,8},{8,0},{16,24},{24,16},{1,9},{9,1},{17,25},{25,17},{2,10},{10... | collective-permute-start | bytes 2211848 | tf_op jit(solution)/shard_map/ppermute | solution.py:581
  64.6 2.8 %copy-start.22 = (bf16[768,768]{1,0:T(8,128)(2,1)}, bf16[768,768]{1,0:T(8,128)(2,1)S(1)}, u32[]{:S(2)}) copy-start(bf16[768,768]{1,0:T(8,128)(2,1)S(1)} %collective-permute-done.11) | copy-start | bytes 3538948
  64.6 63.6 %collective-permute-start.19 = (f32[2,2,24,128]{3,2,1,0:T(8,128)S(1)}, f32[2,2,24,128]{3,2,1,0:T(8,128)S(1)}, u32[]{:S(2)}, u32[]{:S(2)}) collective-permute-start(f32[2,2,24,128]{3,2,1,0:T(8,128)S(1)} %copy-done.16), channel_id=1, source_target_pairs={{0,2},{1,3},{2,0},{3,1},{4,6},{5,7},{6,4},{7,5},{8,10},{9,11},{10,... | collective-permute-start | bytes 147464 | tf_op jit(solution)/shard_map/ppermute | solution.py:581
  66.6 0.9 copy-start.25
  67.4 0.9 copy-start.26
  67.4 1.3 copy-start.23
  68.7 35.6 %copy-start.2 = (f32[24576]{0:T(1024)S(1)}, f32[24576]{0:T(1024)}, u32[]{:S(2)}) copy-start(f32[24576]{0:T(1024)} %param.39) | copy-start | bytes 294916
  68.7 35.6 %copy-start.3 = (bf16[1024,768]{1,0:T(8,128)(2,1)S(1)}, bf16[1024,768]{1,0:T(8,128)(2,1)}, u32[]{:S(2)}) copy-start(bf16[1024,768]{1,0:T(8,128)(2,1)} %x_ref.5) | copy-start | bytes 4718596
  68.7 35.7 %copy-start.4 = (s32[2,512]{1,0:T(2,128)S(1)}, s32[2,512]{1,0:T(2,128)}, u32[]{:S(2)}) copy-start(s32[2,512]{1,0:T(2,128)} %seg_ref.3) | copy-start | bytes 12292
  68.7 35.7 %copy-start.5 = (bf16[1024,768]{1,0:T(8,128)(2,1)S(1)}, bf16[1024,768]{1,0:T(8,128)(2,1)}, u32[]{:S(2)}) copy-start(bf16[1024,768]{1,0:T(8,128)(2,1)} %get-tuple-element.78.rest_0_) | copy-start | bytes 4718596
  68.7 35.7 %copy-start.6 = (bf16[1024,768]{1,0:T(8,128)(2,1)S(1)}, bf16[1024,768]{1,0:T(8,128)(2,1)}, u32[]{:S(2)}) copy-start(bf16[1024,768]{1,0:T(8,128)(2,1)} %get-tuple-element.79.rest_1_) | copy-start | bytes 4718596
  68.7 35.7 %copy-start.7 = (bf16[1024,16]{1,0:T(8,128)(2,1)S(1)}, bf16[1024,16]{1,0:T(8,128)(2,1)}, u32[]{:S(2)}) copy-start(bf16[1024,16]{1,0:T(8,128)(2,1)} %get-tuple-element.73.other_ref.down_ref) | copy-start | bytes 98308
  104.4 28.1 %copy-start = (bf16[3,768,768]{2,1,0:T(8,128)(2,1)S(1)}, bf16[3,768,768]{2,1,0:T(8,128)(2,1)}, u32[]{:S(2)}) copy-start(bf16[3,768,768]{2,1,0:T(8,128)(2,1)} %get-tuple-element.90.weights) | copy-start | bytes 10616836
  104.4 28.1 %copy-start.1 = (bf16[1024,768]{1,0:T(8,128)(2,1)S(1)}, bf16[1024,768]{1,0:T(8,128)(2,1)}, u32[]{:S(2)}) copy-start(bf16[1024,768]{1,0:T(8,128)(2,1)} %get-tuple-element.100.dh_ref) | copy-start | bytes 4718596
  128.0 2.9 %collective-permute-start.14 = (bf16[32,768]{1,0:T(8,128)(2,1)S(1)}, bf16[32,768]{1,0:T(8,128)(2,1)S(1)}, u32[]{:S(2)}, u32[]{:S(2)}) collective-permute-start(bf16[32,768]{1,0:T(8,128)(2,1)S(1)} %get-tuple-element.83), channel_id=1, source_target_pairs={{0,8},{8,0},{16,24},{24,16},{1,9},{9,1},{17,25},{25,17},{2,10},{10... | collective-permute-start | bytes 147464 | tf_op jit(solution)/shard_map/ppermute | solution.py:581
  128.2 6.2 %copy-start.13 = (f32[4,2,24,128]{3,2,1,0:T(8,128)}, f32[4,2,24,128]{3,2,1,0:T(8,128)S(1)}, u32[]{:S(2)}) copy-start(f32[4,2,24,128]{3,2,1,0:T(8,128)S(1)} %constant_dynamic-update-slice_fusion.2.held_ref) | copy-start | bytes 294916
  128.2 18.2 %collective-permute-start.20 = (f32[4,2,24,128]{3,2,1,0:T(8,128)S(1)}, f32[4,2,24,128]{3,2,1,0:T(8,128)S(1)}, u32[]{:S(2)}, u32[]{:S(2)}) collective-permute-start(f32[4,2,24,128]{3,2,1,0:T(8,128)S(1)} %constant_dynamic-update-slice_fusion.2.held_ref), channel_id=1, source_target_pairs={{0,4},{1,5},{2,6},{3,7},{4,0},{5,1},{6,2},{7,3},{8,12},{9,13},{10,... | collective-permute-start | bytes 294920 | tf_op jit(solution)/shard_map/ppermute | solution.py:581
  131.0 4.2 %collective-permute-start.15 = (bf16[32,768]{1,0:T(8,128)(2,1)S(1)}, bf16[32,768]{1,0:T(8,128)(2,1)S(1)}, u32[]{:S(2)}, u32[]{:S(2)}) collective-permute-start(bf16[32,768]{1,0:T(8,128)(2,1)S(1)} %add.12), channel_id=1, source_target_pairs={{0,16},{8,24},{16,0},{24,8},{1,17},{9,25},{17,1},{25,9},{2,18},{10... | collective-permute-start | bytes 147464 | tf_op jit(solution)/shard_map/ppermute | solution.py:581
  135.1 4.2 %collective-permute-start.16 = (bf16[32,768]{1,0:T(8,128)(2,1)S(1)}, bf16[32,768]{1,0:T(8,128)(2,1)S(1)}, u32[]{:S(2)}, u32[]{:S(2)}) collective-permute-start(bf16[32,768]{1,0:T(8,128)(2,1)S(1)} %add.13), channel_id=1, source_target_pairs={{0,1},{1,0},{2,3},{3,2},{4,5},{5,4},{6,7},{7,6},{8,9},{9,8},{10,11... | collective-permute-start | bytes 147464 | tf_op jit(solution)/shard_map/ppermute | solution.py:581
  139.3 4.2 %collective-permute-start.17 = (bf16[32,768]{1,0:T(8,128)(2,1)S(1)}, bf16[32,768]{1,0:T(8,128)(2,1)S(1)}, u32[]{:S(2)}, u32[]{:S(2)}) collective-permute-start(bf16[32,768]{1,0:T(8,128)(2,1)S(1)} %add.14), channel_id=1, source_target_pairs={{0,2},{1,3},{2,0},{3,1},{4,6},{5,7},{6,4},{7,5},{8,10},{9,11},{10,... | collective-permute-start | bytes 147464 | tf_op jit(solution)/shard_map/ppermute | solution.py:581
  143.5 3.0 %copy-start.14 = (bf16[32,768]{1,0:T(8,128)(2,1)}, bf16[32,768]{1,0:T(8,128)(2,1)S(1)}, u32[]{:S(2)}) copy-start(bf16[32,768]{1,0:T(8,128)(2,1)S(1)} %add.15.near_ref) | copy-start | bytes 147460
  143.5 5.1 %collective-permute-start.18 = (bf16[32,768]{1,0:T(8,128)(2,1)S(1)}, bf16[32,768]{1,0:T(8,128)(2,1)S(1)}, u32[]{:S(2)}, u32[]{:S(2)}) collective-permute-start(bf16[32,768]{1,0:T(8,128)(2,1)S(1)} %add.15.near_ref), channel_id=1, source_target_pairs={{0,4},{1,5},{2,6},{3,7},{4,0},{5,1},{6,2},{7,3},{8,12},{9,13},{10,... | collective-permute-start | bytes 147464 | tf_op jit(solution)/shard_map/ppermute | solution.py:581
  146.5 2.1 %copy-start.17 = (f32[4,2,24,128]{3,2,1,0:T(8,128)}, f32[4,2,24,128]{3,2,1,0:T(8,128)S(1)}, u32[]{:S(2)}) copy-start(f32[4,2,24,128]{3,2,1,0:T(8,128)S(1)} %collective-permute-done.20.other_ref) | copy-start | bytes 294916
  148.5 0.6 copy-start.18

commit v3 on v2

--- a/solution.py
+++ b/solution.py
@@ -27,6 +27,8 @@
 VMEM_LIMIT = 56 * 2**20
 INPUT_VMEM = 24 * 2**20
 BACK_VMEM = 44 * 2**20
+DENSE_VMEM = 56 * 2**20
+ATTEND_VMEM = 56 * 2**20
 GATE = 5 * 10**9
 
 
@@ -82,33 +84,27 @@
 
 
 class Parts:
-    def __init__(self, own, blocks, near, others):
-        self.own, self.blocks, self.near = own, blocks, near
-        self.flips = [flip for flip, _ in others]
-        self.operands = list(own) + [near] + [piece for _, piece in others]
-        self.copies = len(blocks) * (3 + len(others))
+    def __init__(self):
+        self.operands, self.places = [], []
+
+    def add(self, array, *places):
+        self.places += [(len(self.operands),) + place for place in places]
+        self.operands.append(array)
+
+    @property
+    def copies(self):
+        return len(self.places)
 
     def into(self, refs, rank, place, views, semaphores):
-        count = len(self.own)
-        own, near, others = refs[:count], refs[count], refs[count + 1 :]
-        rows, width = near.shape[2:]
         mine = side_of(place)
-        found = []
-        for at, ((source, start), view) in enumerate(zip(self.blocks, views)):
-            whole = own[source].at[:, pl.ds(start, width)]
-            found.append((whole, view(rows_at(rank, 0, 0, rows), 2 * rows)))
-            for side in range(2):
-                found.append((near.at[side, at], view(rows_at(rank, 1, side, rows), rows)))
-            for (flip, other), ref in zip(self.flips, others):
-                if other is None:
-                    target = view(rows_at(rank, flip, 0, rows), 2 * rows)
-                else:
-                    target = view(rows_at(rank, flip, jnp.bitwise_xor(mine, other), rows), rows)
-                found.append((ref.at[at], target))
-        return [
-            pltpu.make_async_copy(source, target, semaphores.at[at])
-            for at, (source, target) in enumerate(found)
-        ]
+        found = [[] for _ in views]
+        for at, (operand, index, block, flip, side, rows, halves) in enumerate(self.places):
+            source = refs[operand].at[index] if index else refs[operand]
+            if isinstance(side, tuple):
+                side = jnp.bitwise_xor(mine, side[0])
+            target = views[block](rows_at(rank, flip, side, rows), rows * halves)
+            found[block].append(pltpu.make_async_copy(source, target, semaphores.at[at]))
+        return found
 
 
 def stacked(weights):
@@ -181,16 +177,26 @@
     return list(zip(found[::2], found[1::2]))
 
 
-def attend_kernel(parts, rank_ref, place_ref, seg_ref, x_ref, fac_ref, bq_ref, bv_ref, *rest):
-    shards, rest = rest[: len(parts.operands)], rest[len(parts.operands) :]
-    q_ref, k_ref, v_ref, ctx_ref, aug_ref, down_ref, weights, bias, table, semaphores = rest
+def attend_kernel(parts, first, rank_ref, place_ref, seg_ref, x_ref, fac_ref, bq_ref, bv_ref, *rest):
     at = pl.program_id(1)
+    begin = (pl.program_id(0) == 0) & (at == 0)
+    if parts is None:
+        weights, rest = rest[0], rest[7:]
+        q_ref, k_ref, v_ref, ctx_ref, aug_ref, down_ref, bias, table = rest
+    else:
+        shards, rest = rest[: len(parts.operands)], rest[len(parts.operands) :]
+        q_ref, k_ref, v_ref, ctx_ref, aug_ref, down_ref, weights, bias, table, semaphores = rest
+
+        @pl.when(begin)
+        def _():
+            blocks = parts.into(shards, rank_ref[0], place_ref[0], stacked(weights), semaphores)
+            run_copies(sum(blocks, []))
+
     width = q_ref.shape[1]
     rows = x_ref.shape[0]
 
-    @pl.when((pl.program_id(0) == 0) & (at == 0))
+    @pl.when(begin)
     def _():
-        run_copies(parts.into(shards, rank_ref[0], place_ref[0], stacked(weights), semaphores))
         bias[0:1, :] = bq_ref[...].reshape(1, -1)
         bias[1:2, :] = bv_ref[...].reshape(1, -1)
         table[...] = adapter_rows(fac_ref, 0, *table.shape)
@@ -209,7 +215,7 @@
     v_ref[...] = (dot(x, weights[2, :, columns], NN) + bias[1:2, columns] + 2.0 * dot(low, up_v, NN)).astype(BF16)
 
     lane = lax.broadcasted_iota(jnp.int32, (rows, LANES), 1)
-    seg = seg_ref[pl.ds(pl.program_id(0), 1), :].astype(F32).T.astype(jnp.int32)
+    seg = seg_ref[pl.ds(first + pl.program_id(0), 1), :].astype(F32).T.astype(jnp.int32)
     own = jnp.where(lane == seg, 1.0, 0.0)
     aug_k = jnp.where((lane < 4) & (lane != seg), -MASKED, 0.0).astype(BF16)
     aug_q = own.astype(BF16)
@@ -239,51 +245,55 @@
         ctx_ref[:, here] = out.astype(BF16)
 
 
-def attend(rank, place, seg, x, factors, bq, bv, parts, pairs):
+def attend(rank, place, seg, x, factors, bq, bv, pairs, first, count, parts, weights=None, carry=()):
     packs, size = seg.shape
     rows, width = x.shape
     cut = pairs * LANES
-    block = pl.BlockSpec((size, cut), lambda p, g: (p, g))
+    block = pl.BlockSpec((size, cut), lambda p, g: (first + p, g))
     vmem = pl.BlockSpec(memory_space=pltpu.VMEM)
     smem = pl.BlockSpec(memory_space=pltpu.SMEM)
     like = jax.ShapeDtypeStruct
+    out_specs = [
+        block,
+        block,
+        block,
+        block,
+        pl.BlockSpec((size, 2 * cut), lambda p, g: (first + p, g)),
+        pl.BlockSpec((size, 2 * ADAPTER_RANK), lambda p, g: (first + p, 0)),
+    ]
+    out_shape = [like((rows, width), BF16)] * 4
+    out_shape += [like((rows, 2 * width), BF16), like((rows, 2 * ADAPTER_RANK), BF16)]
+    scratch = [pltpu.VMEM((8, width), F32), pltpu.VMEM((4 * ADAPTER_RANK, width), F32)]
+    if parts is None:
+        operands, specs = [weights, *carry], [vmem] + [ANY] * len(carry)
+    else:
+        operands, specs = parts.operands, [ANY] * len(parts.operands)
+        out_specs.append(pl.BlockSpec((3, width, width), lambda p, g: (0, 0, 0)))
+        out_shape.append(like((3, width, width), BF16))
+        scratch.append(pltpu.SemaphoreType.DMA((parts.copies,)))
     return pl.pallas_call(
-        functools.partial(attend_kernel, parts),
-        grid=(packs, width // cut),
+        functools.partial(attend_kernel, parts, first),
+        grid=(count, width // cut),
         in_specs=[
             smem,
             smem,
-            pl.BlockSpec(memory_space=pltpu.VMEM),
-            pl.BlockSpec((size, width), lambda p, g: (p, 0)),
+            vmem,
+            pl.BlockSpec((size, width), lambda p, g: (first + p, 0)),
             vmem,
             vmem,
             vmem,
         ]
-        + [ANY] * len(parts.operands),
-        out_specs=[
-            block,
-            block,
-            block,
-            block,
-            pl.BlockSpec((size, 2 * cut), lambda p, g: (p, g)),
-            pl.BlockSpec((size, 2 * ADAPTER_RANK), lambda p, g: (p, 0)),
-            pl.BlockSpec((3, width, width), lambda p, g: (0, 0, 0)),
-        ],
-        out_shape=[like((rows, width), BF16)] * 4
-        + [
-            like((rows, 2 * width), BF16),
-            like((rows, 2 * ADAPTER_RANK), BF16),
-            like((3, width, width), BF16),
-        ],
-        scratch_shapes=[
-            pltpu.VMEM((8, width), F32),
-            pltpu.VMEM((4 * ADAPTER_RANK, width), F32),
-            pltpu.SemaphoreType.DMA((parts.copies,)),
-        ],
-        compiler_params=pltpu.CompilerParams(vmem_limit_bytes=VMEM_LIMIT),
-        cost_estimate=pl.CostEstimate(flops=1, bytes_accessed=1, transcendentals=0),
+        + specs,
+        out_specs=out_specs,
+        out_shape=out_shape,
+        input_output_aliases={8 + at: at for at in range(len(carry))},
+        scratch_shapes=scratch,
+        compiler_params=pltpu.CompilerParams(vmem_limit_bytes=ATTEND_VMEM),
+        cost_estimate=pl.CostEstimate(
+            flops=1 if carry == () else 10**10, bytes_accessed=1, transcendentals=0
+        ),
         name="project_and_attend",
-    )(rank, place, seg, x, factors, bq, bv, *parts.operands)
+    )(rank, place, seg, x, factors, bq, bv, *operands)
 
 
 def dense_kernel(first, second, cut, rank_ref, place_ref, x_ref, ctx_ref, cot_ref, *rest):
@@ -297,10 +307,8 @@
 
     at = pl.program_id(0)
     rank, place = rank_ref[0], place_ref[0]
-    start = first.into(near, rank, place, in_columns(ahead, width), semaphores.at[0])
-    later = second.into(far, rank, place, in_columns(outer, width), semaphores.at[1])
-    count = len(start) // len(first.blocks)
-    start, later = start[:count], start[count:] + later
+    start, *later = first.into(near, rank, place, in_columns(ahead, width), semaphores.at[0])
+    later = sum(later + second.into(far, rank, place, in_columns(outer, width), semaphores.at[1]), [])
 
     @pl.when(at == 0)
     def _():
@@ -361,7 +369,7 @@
             pltpu.VMEM((size, hidden), F32),
             pltpu.SemaphoreType.DMA((2, max(first.copies, second.copies))),
         ],
-        compiler_params=pltpu.CompilerParams(vmem_limit_bytes=VMEM_LIMIT),
+        compiler_params=pltpu.CompilerParams(vmem_limit_bytes=DENSE_VMEM),
         cost_estimate=pl.CostEstimate(
             flops=rows * width * (4 * width + 8 * hidden),
             bytes_accessed=12 * rows * width + 4 * width * hidden,
@@ -597,18 +605,16 @@
     return held[1:]
 
 
-def both_cores(halves, reps):
-    return [
-        ((flip ^ core, other), swap(value, "rep", reps, 1) if core else value)
-        for (flip, other), value in halves
-        for core in range(2)
-    ]
-
-
-def finish(own, blocks, near, halves, crossed, reps):
-    pieces = [((flip, 0), value) for flip, value in halves]
-    pieces += [((flip, 1), value) for flip, value in crossed]
-    return Parts(own, blocks, swap(near, "rep", reps, 1), both_cores(pieces, reps))
+def finish(parts, block_of, halves, crossed, reps, early=None):
+    for side, values in enumerate((halves, crossed)):
+        for flip, value in values:
+            for core in range(2):
+                piece = swap(value, "rep", reps, 1) if core else value
+                if core and side == 0 and early is not None:
+                    piece = gate(piece, early, GATE)
+                rows = value.shape[-2]
+                places = [(index, block, flip ^ core, (side,), rows, 1) for index, block in block_of]
+                parts.add(piece, *places)
 
 
 def across(halves, reps, wide):
@@ -661,54 +667,78 @@
     table = factors.reshape(-1, LANES)
 
     hidden = w_inner.shape[1]
-    own = [w_query, w_key, w_value]
-    set_heads = [(at, 0) for at in range(3)]
+    side = side_of(place[0])
+    heads = Parts()
+    sent = []
+    for block, shard in enumerate((w_query, w_key, w_value)):
+        rows = shard.shape[0] // 2
+        heads.add(shard, ((), block, 0, 0, rows, 2))
+        sent.append(fetch(lax.dynamic_slice_in_dim(shard, side * rows, rows), reps))
+
     own_ahead = [w_output, w_inner]
     set_ahead = [(0, 0)] + [(1, start) for start in range(0, hidden, width)]
-    near, mine = pack(place, own, [(set_heads, width)])[0]
-    place, mine = together(place, mine)
     near_ahead, mine_ahead = pack(place, own_ahead, [(set_ahead, width)])[0]
-
-    halves = fetch(mine, reps)
+    flip, value = sent[0][-1]
+    value, near_outer, *shards = together(value, w_outer, w_query, w_key, w_value)
+    sent[0][-1] = (flip, value)
+    for block, shard in enumerate(shards):
+        heads.add(swap(shard, "rep", reps, 1), ((), block, 1, 0, shard.shape[0] // 2, 2))
+    flip, value = sent[-1][-1]
     length = first_moment.shape[0] // LANES
     held = jnp.stack([first_moment, second_moment]).reshape(1, 2, length, LANES)
-    held, mine_ahead = together(held, mine_ahead)
+    value, mine_ahead, near_ahead, held = together(value, mine_ahead, near_ahead, held)
+    sent[-1][-1] = (flip, value)
     flips = bits(wide)
-    held = jnp.concatenate([held, swap(held, "wide", wide, flips[0])])
-    flip, sent = halves[-1]
-    sent, mine_ahead, near, near_ahead, near_outer = together(
-        sent, mine_ahead, near, near_ahead, w_outer
+    pending = swap(held, "wide", wide, flips[0])
+    crossed = [across(halves, reps, wide) for halves in sent]
+    (flip, value), whole_outer = crossed[-1][-1], w_outer
+    value, whole_outer = together(value, whole_outer)
+    crossed[-1][-1] = (flip, value)
+    for block, (halves, others) in enumerate(zip(sent, crossed)):
+        finish(heads, [((), block)], halves, others, reps)
+    whole_outer = fetch(whole_outer, reps)
+    halves_ahead = fetch(mine_ahead, reps)
+
+    early = packs // 2
+    arguments = (rank, place, segment_ids, tokens, table, b_query, b_value, 3)
+    *attended, weights = attend(*arguments, 0, early, heads)
+    weights, *values = together(weights, *[value for _, value in halves_ahead])
+    values = [gate(value, weights, GATE) for value in values]
+    halves_ahead = [(flip, value) for (flip, _), value in zip(halves_ahead, values)]
+    crossed_ahead = across(halves_ahead, reps, wide)
+    q, k, v, ctx, aug, down = attend(
+        *arguments, early, packs - early, None, weights, attended
     )
-    halves_ahead = fetch(mine_ahead, reps)
-    sent = gate(sent, held)
-    sent, whole_outer = together(sent, w_outer)
-    whole_outer = fetch(whole_outer, reps)
-    halves = halves[:-1] + [(flip, sent)]
-    crossed = across(halves, reps, wide)
-    heads = finish(own, set_heads, near, halves, crossed, reps)
-
-    q, k, v, ctx, aug, down, weights = attend(
-        rank, place, segment_ids, tokens, table, b_query, b_value, heads, 3
-    )
-    down, held, *values = together(down, held, *[value for _, value in halves_ahead])
-    values = [gate(value, down, GATE) for value in values]
-    halves_ahead = [(flip, value) for (flip, _), value in zip(halves_ahead, values)]
+    flips_outer, whole_outer = zip(*whole_outer)
+    flips_ahead, crossed_ahead = zip(*crossed_ahead)
+    down, pending, held, *values = together(down, pending, held, *crossed_ahead, *whole_outer)
+    crossed_ahead = list(zip(flips_ahead, values))
+    whole_outer = list(zip(flips_outer, values[len(flips_ahead) :]))
     for flip in flips[1:-1]:
-        held = jnp.concatenate([held, swap(held, "wide", wide, flip)])
-    other = swap(held, "wide", wide, flips[-1])
-    crossed_ahead = across(halves_ahead, reps, wide)
-    ahead = finish(own_ahead, set_ahead, near_ahead, halves_ahead, crossed_ahead, reps)
-    whole = [(flip, value) for flip, value in whole_outer]
-    near_outer = swap(near_outer, "rep", reps, 1)
-    outer = Parts(
-        [w_outer],
-        [(0, 0)],
-        near_outer.reshape(2, 1, -1, width),
-        both_cores([((flip, None), value[None]) for flip, value in whole], reps),
-    )
+        held = jnp.concatenate([held, pending])
+        pending = swap(held, "wide", wide, flip)
+    rows = w_output.shape[0] // 2
+    ahead = Parts()
+    ahead.add(w_output, ((), 0, 0, 0, rows, 2))
+    columns = [(slice(None), slice(start, start + width)) for start in range(0, hidden, width)]
+    ahead.add(w_inner, *[(at, 1 + block, 0, 0, rows, 2) for block, at in enumerate(columns)])
+    blocks = range(len(set_ahead))
+    near_ahead = swap(near_ahead, "rep", reps, 1)
+    ahead.add(near_ahead, *[((s, at), at, 1, s, rows, 1) for at in blocks for s in range(2)])
+    finish(ahead, [((at,), at) for at in blocks], halves_ahead, crossed_ahead, reps, down)
+    rows = w_outer.shape[0] // 2
+    outer = Parts()
+    outer.add(w_outer, ((), 0, 0, 0, rows, 2))
+    outer.add(swap(near_outer, "rep", reps, 1), ((), 0, 1, 0, rows, 2))
+    for flip, value in whole_outer:
+        outer.add(value, ((), 0, flip, 0, rows, 2))
+        outer.add(swap(value, "rep", reps, 1), ((), 0, flip ^ 1, 0, rows, 2))
     layer_out, dh, dctx = dense(
         rank, place, tokens, ctx, cotangent, vectors, ahead, outer, size, 1024
     )
+    dctx, pending, held = together(dctx, pending, held)
+    held = jnp.concatenate([held, pending])
+    other = swap(held, "wide", wide, flips[-1])
     dq, dk, dv, dlow, grad = attend_back(
         segment_ids, tokens, table, down, q, k, v, dctx, ctx, aug, 3
     )

time: 151 us -> 147 us (0.974)
  waiting for transfers between devices: 26.6 us -> 17.8 us
  starting transfers between devices: 21.7 us -> 24.3 us
    ppermute x19 -> x27, waiting for transfers between devices: 19.7 us -> 13.7 us  [swap(): return lax.ppermute(value, axis, [(i, i ^ flip) for i in range(size)])]
    dynamic_slice x0 -> x3, local copies, waits for them, and re-layouts: none -> 2.83 us  [local(): sent.append(fetch(lax.dynamic_slice_in_dim(shard, side * rows, rows), reps))]
    ppermute x2 -> x4, waiting for transfers between devices: 6.88 us -> 4.1 us  [cross(): return lax.ppermute(value, ('rep', 'wide'), pairs)]
    pallas_call x1 -> x2, Pallas kernels: 23.9 us -> 26.5 us  [attend(): pl.pallas_call(functools.partial(attend_kernel, parts, first), grid=(coun...]
    pallas_call x2 -> x1, Pallas kernels: 5.26 us -> 2.88 us  [pack(): pl.pallas_call(functools.partial(pack_kernel, [blocks for blocks, _ in se...]
    unnamed x56 -> x68, local copies, waits for them, and re-layouts: 3.84 us -> 1.6 us
    ppermute x19 -> x27, starting transfers between devices: 18.5 us -> 20.2 us  [swap(): return lax.ppermute(value, axis, [(i, i ^ flip) for i in range(size)])]
    ppermute x2 -> x4, starting transfers between devices: 3.27 us -> 4.18 us  [cross(): return lax.ppermute(value, ('rep', 'wide'), pairs)]
  transfers between devices with their start and end apart: 21 -> 31, of which waited for: 11 -> 13; matrix products, arithmetic and copies ran while one was open for 0% -> 2% of each run, Pallas kernels for 62% -> 49%
where the time goes in v3:
time: 147 us
  Pallas kernels  98.2 us (67%)
  starting transfers between devices  24.3 us (17%)
  waiting for transfers between devices  17.8 us (12%)
  local copies, waits for them, and re-layouts  4.44 us (3%)
    pallas_call x1, Pallas kernels, dense(): pl.pallas_call(functools.partial(dense_kernel, first, second, cut), grid=...  35.6 us
    pallas_call x2, Pallas kernels, attend(): pl.pallas_call(functools.partial(attend_kernel, parts, first), grid=(coun...  26.5 us
    pallas_call x1, Pallas kernels, attend_back(): pl.pallas_call(attend_back_kernel, grid=(packs, width // cut), in_specs=[...  23.6 us
    ppermute x27, starting transfers between devices, swap(): return lax.ppermute(value, axis, [(i, i ^ flip) for i in range(size)])  20.2 us
    ppermute x27, waiting for transfers between devices, swap(): return lax.ppermute(value, axis, [(i, i ^ flip) for i in range(size)])  13.7 us
    pallas_call x4, Pallas kernels, input_back(): pl.pallas_call(functools.partial(input_kernel, at * size), grid=(1,), in_...  7.6 us
    ppermute x4, starting transfers between devices, cross(): return lax.ppermute(value, ('rep', 'wide'), pairs)  4.18 us
    ppermute x4, waiting for transfers between devices, cross(): return lax.ppermute(value, ('rep', 'wide'), pairs)  4.1 us
  transfers between devices with their start and end apart: 31, of which 13 were waited for; matrix products, arithmetic and copies ran while one was open for 2% of the time, Pallas kernels for 49%

profile of v3, /device:TPU:0, one launch (start us, length us, event | category | flops | bytes accessed | tf_op | source)
XLA Modules:
  0.0 146.6 jit_solution(10004393910766625768)
XLA Ops:
  0.6 0.0 copy-start.8
  0.6 0.0 copy-start.10
  0.7 0.0 copy-start.9
  0.7 1.0 constant_dynamic-slice_fusion.2
  1.7 3.0 %collective-permute-start = (bf16[96,768]{1,0:T(8,128)(2,1)S(1)}, bf16[96,768]{1,0:T(8,128)(2,1)S(1)}, u32[]{:S(2)}, u32[]{:S(2)}) collective-permute-start(bf16[96,768]{1,0:T(8,128)(2,1)S(1)} %constant_dynamic-slice_fusion.2), channel_id=1, source_target_pairs={{0,16},{8,24},{16,0},{24,8},{1,17},{9,25},{17,1},{25,9},{2,18},{10... | collective-permute-start | bytes 442376 | tf_op jit(solution)/shard_map/ppermute | solution.py:589
  4.7 0.9 constant_dynamic-slice_fusion
  5.6 0.1 collective-permute-start.11
  5.7 0.9 constant_dynamic-slice_fusion.1
  6.6 2.1 %collective-permute-start.7 = (bf16[96,768]{1,0:T(8,128)(2,1)S(1)}, bf16[96,768]{1,0:T(8,128)(2,1)S(1)}, u32[]{:S(2)}, u32[]{:S(2)}) collective-permute-start(bf16[96,768]{1,0:T(8,128)(2,1)S(1)} %constant_dynamic-slice_fusion.1), channel_id=1, source_target_pairs={{0,16},{8,24},{16,0},{24,8},{1,17},{9,25},{17,1},{25,9},{2,18},{10... | collective-permute-start | bytes 442376 | tf_op jit(solution)/shard_map/ppermute | solution.py:589
  8.7 0.7 pad_maximum_fusion
  9.4 2.9 %pack_shards.1 = (bf16[2,5,96,768]{3,2,1,0:T(8,128)(2,1)}, bf16[5,96,768]{2,1,0:T(8,128)(2,1)}) custom-call(s32[1]{0:T(128)} %bitcast.1.place_ref, bf16[192,768]{1,0:T(8,128)(2,1)} %rest_7_.1, bf16[192,3072]{1,0:T(8,128)(2,1)} %rest_8_.1), custom_call_target="tpu_custom_call" | custom-call | tf_op jit(solution)/shard_map/pack_shards/pallas_call | solution.py:167
  12.3 0.1 collective-permute-done.11.rest_14_
  12.5 2.1 %collective-permute-start.15 = (bf16[5,96,768]{2,1,0:T(8,128)(2,1)}, bf16[5,96,768]{2,1,0:T(8,128)(2,1)}, u32[]{:S(2)}, u32[]{:S(2)}) collective-permute-start(bf16[5,96,768]{2,1,0:T(8,128)(2,1)} %get-tuple-element.77), channel_id=1, source_target_pairs={{0,16},{8,24},{16,0},{24,8},{1,17},{9,25},{17,1},{25,9},{2,18},{10... | collective-permute-start | bytes 2211848 | tf_op jit(solution)/shard_map/ppermute | solution.py:589
  14.6 0.0 collective-permute-done.rest_6_
  14.6 0.0 collective-permute-start.4
  14.6 1.6 %collective-permute-start.5 = (bf16[96,768]{1,0:T(8,128)(2,1)S(1)}, bf16[96,768]{1,0:T(8,128)(2,1)S(1)}, u32[]{:S(2)}, u32[]{:S(2)}) collective-permute-start(bf16[96,768]{1,0:T(8,128)(2,1)S(1)} %collective-permute-done.rest_6_), channel_id=1, source_target_pairs={{0,1},{1,0},{2,3},{3,2},{4,5},{5,4},{6,7},{7,6},{8,10},{9,11},{10,... | collective-permute-start | bytes 442376 | tf_op jit(solution)/shard_map/ppermute | solution.py:598
  16.2 0.2 collective-permute-start.8
  16.4 1.5 %collective-permute-start.9 = (bf16[96,768]{1,0:T(8,128)(2,1)S(1)}, bf16[96,768]{1,0:T(8,128)(2,1)S(1)}, u32[]{:S(2)}, u32[]{:S(2)}) collective-permute-start(bf16[96,768]{1,0:T(8,128)(2,1)S(1)} %collective-permute-done.7.rest_10_), channel_id=1, source_target_pairs={{0,1},{1,0},{2,3},{3,2},{4,5},{5,4},{6,7},{7,6},{8,10},{9,11},{10,... | collective-permute-start | bytes 442376 | tf_op jit(solution)/shard_map/ppermute | solution.py:598
  17.9 0.5 collective-permute-start.13
  18.5 1.4 collective-permute-done.5.rest_8_
  19.8 0.0 collective-permute-done.8.rest_11_
  19.9 0.5 collective-permute-start.2
  20.4 1.2 collective-permute-done.9.rest_12_
  21.6 1.6 %collective-permute-done.13.rest_16_ = bf16[96,768]{1,0:T(8,128)(2,1)S(1)} collective-permute-done((bf16[96,768]{1,0:T(8,128)(2,1)S(1)}, bf16[96,768]{1,0:T(8,128)(2,1)S(1)}, u32[]{:S(2)}, u32[]{:S(2)}) %collective-permute-start.13) | collective-permute-done | bytes 147488 | tf_op jit(solution)/shard_map/ppermute | solution.py:598
  23.1 0.0 collective-permute-start.12
  23.2 1.4 collective-permute-done.12.rest_15_
  24.5 0.1 collective-permute-start.6
  24.7 0.4 collective-permute-start.10
  25.0 0.1 collective-permute-start.14
  25.2 0.4 collective-permute-start.16
  25.6 0.3 collective-permute-done.6.rest_9_
  25.9 1.5 %collective-permute-start.18 = (f32[1,2,24,128]{3,2,1,0:T(8,128)S(1)}, f32[1,2,24,128]{3,2,1,0:T(8,128)S(1)}, u32[]{:S(2)}, u32[]{:S(2)}) collective-permute-start(f32[1,2,24,128]{3,2,1,0:T(8,128)S(1)} %pad_maximum_fusion), channel_id=1, source_target_pairs={{0,1},{1,0},{2,3},{3,2},{4,5},{5,4},{6,7},{7,6},{8,9},{9,8},{10,11... | collective-permute-start | bytes 73736 | tf_op jit(solution)/shard_map/ppermute | solution.py:589
  27.4 1.3 collective-permute-start.20
  28.9 0.5 copy-done.27
  29.4 13.8 %project_and_attend.2 = (bf16[1024,768]{1,0:T(8,128)(2,1)}, bf16[1024,768]{1,0:T(8,128)(2,1)}, bf16[1024,768]{1,0:T(8,128)(2,1)}, bf16[1024,768]{1,0:T(8,128)(2,...) custom-call(s32[1]{0:T(128)} %bitcast.rank_ref, s32[1]{0:T(128)} %bitcast.1.place_ref, ...), custom_call_target="tpu_custom_call" | custom-call | flops 1 | bytes 1 | tf_op jit(solution)/shard_map/project_and_attend/pallas_call | solution.py:274
  43.2 0.1 collective-permute-start.17
  43.3 0.6 collective-permute-start.19
  43.9 12.7 %project_and_attend.3 = (bf16[1024,768]{1,0:T(8,128)(2,1)}, bf16[1024,768]{1,0:T(8,128)(2,1)}, bf16[1024,768]{1,0:T(8,128)(2,1)}, bf16[1024,768]{1,0:T(8,128)(2,...) custom-call(s32[1]{0:T(128)} %bitcast.rank_ref, ...), custom_call_target="tpu_custom_call", output_to_operand_aliasing={{0}: (8, {}), {1}: (9, {}), {2}: (10, {}), {3}: (11, {}), {... | custom-call | flops 10000000000 | bytes 1 | tf_op jit(solution)/shard_map/project_and_attend/pallas_call | solution.py:274
  56.6 1.3 collective-permute-start.22
  57.8 0.1 collective-permute-start.23
  57.9 0.5 collective-permute-start.21
  58.4 0.5 collective-permute-start.24
  59.0 0.3 copy-done.32
  59.3 1.7 %collective-permute-done.22.rest_15_ = bf16[768,768]{1,0:T(8,128)(2,1)} collective-permute-done((bf16[768,768]{1,0:T(8,128)(2,1)S(1)}, bf16[768,768]{1,0:T(8,128)(2,1)}, u32[]{:S(2)}, u32[]{:S(2)}) %collective-permute-start.22) | collective-permute-done | bytes 1179680 | tf_op jit(solution)/shard_map/ppermute | solution.py:589
  61.0 2.1 %collective-permute-done.21.rest_13_ = bf16[5,96,768]{2,1,0:T(8,128)(2,1)} collective-permute-done((bf16[5,96,768]{2,1,0:T(8,128)(2,1)S(1)}, bf16[5,96,768]{2,1,0:T(8,128)(2,1)}, u32[]{:S(2)}, u32[]{:S(2)}) %collective-permute-start.21) | collective-permute-done | bytes 737312 | tf_op jit(solution)/shard_map/ppermute | solution.py:589
  63.1 0.3 collective-permute-done.23.rest_17_
  63.4 35.6 %dense_both_ways.1 = (bf16[1024,768]{1,0:T(8,128)(2,1)}, bf16[1024,768]{1,0:T(8,128)(2,1)}, bf16[1024,768]{1,0:T(8,128)(2,1)}) custom-call(s32[1]{0:T(128)} %bitcast.rank_ref, s32[1]{0:T(128)} %bitcast.1.place_ref, bf16[1024,768]{1,0:T(8,128)(2,1)} %x_ref.7, bf16[1024,768]{1,0:T(8,128)(2,1)} %get-tuple-element.85.ctx_ref.rest_4_, bf16[1024,768]{1,0:T(8,128)(2,1)} %cot_ref.1, ...), custom_call_target="tpu_custom_call" | custom-call | flops 21743271936 | bytes 18874368 | tf_op jit(solution)/shard_map/dense_both_ways/pallas_call | solution.py:358
  99.1 23.6 %attend_back.1 = (bf16[1024,768]{1,0:T(8,128)(2,1)S(1)}, bf16[1024,768]{1,0:T(8,128)(2,1)S(1)}, bf16[1024,768]{1,0:T(8,128)(2,1)S(1)}, bf16[1024,16]{1,0:T(8,128)(2,1)S(1)}, bf16[32,768]{1,0:T(8,128)(2,1)S(1)}) custom-call(s32[2,512]{1,0:T(2,128)S(1)} %copy-done.4, bf16[1024,768]{1,0:T(8,128)(2,1)S(1)} %copy-done.3, f32[192,128]{1,0:T(8,128)S(1)} %bitcast.13, ...), custom_call_target="tpu_custom_call" | custom-call | flops 12079595520 | bytes 18874368 | tf_op jit(solution)/shard_map/attend_back/pallas_call | solution.py:467
  122.7 0.5 collective-permute-start.25
  123.2 2.6 %collective-permute-start.30 = (f32[4,2,24,128]{3,2,1,0:T(8,128)S(1)}, f32[4,2,24,128]{3,2,1,0:T(8,128)S(1)}, u32[]{:S(2)}, u32[]{:S(2)}) collective-permute-start(f32[4,2,24,128]{3,2,1,0:T(8,128)S(1)} %constant_dynamic-update-slice_fusion.2.held_ref), channel_id=1, source_target_pairs={{0,4},{1,5},{2,6},{3,7},{4,0},{5,1},{6,2},{7,3},{8,12},{9,13},{10,... | collective-permute-start | bytes 294920 | tf_op jit(solution)/shard_map/ppermute | solution.py:589
  125.9 0.6 collective-permute-start.26
  126.5 1.9 %input_gradient.4.rest_0_ = bf16[1024,768]{1,0:T(8,128)(2,1)} custom-call(bf16[1024,768]{1,0:T(8,128)(2,1)S(1)} %copy-done.1, bf16[1024,768]{1,0:T(8,128)(2,1)S(1)} %get-tuple-element.108.dq_ref, bf16[1024,768]{1,0:T(8,128)(2,1)S(1)} %get-tuple-element.109.dk_ref, bf16[1024,768]{1,0:T(8,128)(2,1)S(1)} %get-tuple-element.110.dv_ref, ...), custom_call_target="tpu_custom_call" | custom-call | flops 905969664 | bytes 1966080 | tf_op jit(solution)/shard_map/input_gradient/pallas_call | solution.py:517
  128.4 1.7 %collective-permute-done.26 = bf16[32,768]{1,0:T(8,128)(2,1)S(1)} collective-permute-done((bf16[32,768]{1,0:T(8,128)(2,1)S(1)}, bf16[32,768]{1,0:T(8,128)(2,1)S(1)}, u32[]{:S(2)}, u32[]{:S(2)}) %collective-permute-start.26) | collective-permute-done | bytes 49184 | tf_op jit(solution)/shard_map/ppermute | solution.py:589
  130.0 0.6 collective-permute-start.27
  130.7 1.9 %input_gradient.5.rest_0_ = bf16[1024,768]{1,0:T(8,128)(2,1)} custom-call(bf16[1024,768]{1,0:T(8,128)(2,1)S(1)} %copy-done.1, bf16[1024,768]{1,0:T(8,128)(2,1)S(1)} %get-tuple-element.108.dq_ref, bf16[1024,768]{1,0:T(8,128)(2,1)S(1)} %get-tuple-element.109.dk_ref, bf16[1024,768]{1,0:T(8,128)(2,1)S(1)} %get-tuple-element.110.dv_ref, ...), custom_call_target="tpu_custom_call", output_to_operand_aliasing={{}: (7, {})} | custom-call | flops 905969664 | bytes 1966080 | tf_op jit(solution)/shard_map/input_gradient/pallas_call | solution.py:517
  132.5 1.6 %collective-permute-done.27 = bf16[32,768]{1,0:T(8,128)(2,1)S(1)} collective-permute-done((bf16[32,768]{1,0:T(8,128)(2,1)S(1)}, bf16[32,768]{1,0:T(8,128)(2,1)S(1)}, u32[]{:S(2)}, u32[]{:S(2)}) %collective-permute-start.27) | collective-permute-done | bytes 49184 | tf_op jit(solution)/shard_map/ppermute | solution.py:589
  134.2 0.6 collective-permute-start.28
  134.8 1.9 %input_gradient.6.rest_0_ = bf16[1024,768]{1,0:T(8,128)(2,1)} custom-call(bf16[1024,768]{1,0:T(8,128)(2,1)S(1)} %copy-done.1, bf16[1024,768]{1,0:T(8,128)(2,1)S(1)} %get-tuple-element.108.dq_ref, bf16[1024,768]{1,0:T(8,128)(2,1)S(1)} %get-tuple-element.109.dk_ref, bf16[1024,768]{1,0:T(8,128)(2,1)S(1)} %get-tuple-element.110.dv_ref, ...), custom_call_target="tpu_custom_call", output_to_operand_aliasing={{}: (7, {})} | custom-call | flops 905969664 | bytes 1966080 | tf_op jit(solution)/shard_map/input_gradient/pallas_call | solution.py:517
  136.7 1.7 %collective-permute-done.28 = bf16[32,768]{1,0:T(8,128)(2,1)S(1)} collective-permute-done((bf16[32,768]{1,0:T(8,128)(2,1)S(1)}, bf16[32,768]{1,0:T(8,128)(2,1)S(1)}, u32[]{:S(2)}, u32[]{:S(2)}) %collective-permute-start.28) | collective-permute-done | bytes 49184 | tf_op jit(solution)/shard_map/ppermute | solution.py:589
  138.4 0.8 collective-permute-start.29
  139.3 1.9 %input_gradient.7 = bf16[1024,768]{1,0:T(8,128)(2,1)} custom-call(bf16[1024,768]{1,0:T(8,128)(2,1)S(1)} %copy-done.1, bf16[1024,768]{1,0:T(8,128)(2,1)S(1)} %get-tuple-element.108.dq_ref, bf16[1024,768]{1,0:T(8,128)(2,1)S(1)} %get-tuple-element.109.dk_ref, bf16[1024,768]{1,0:T(8,128)(2,1)S(1)} %get-tuple-element.110.dv_ref, ...), custom_call_target="tpu_custom_call", output_to_operand_aliasing={{}: (7, {})} | custom-call | flops 905969664 | bytes 1966080 | tf_op jit(solution)/shard_map/input_gradient/pallas_call | solution.py:517
  141.2 2.8 %collective-permute-done.29.far_ref = bf16[32,768]{1,0:T(8,128)(2,1)S(1)} collective-permute-done((bf16[32,768]{1,0:T(8,128)(2,1)S(1)}, bf16[32,768]{1,0:T(8,128)(2,1)S(1)}, u32[]{:S(2)}, u32[]{:S(2)}) %collective-permute-start.29) | collective-permute-done | bytes 49184 | tf_op jit(solution)/shard_map/ppermute | solution.py:589
  144.0 0.6 copy-done.29
  144.6 2.0 %adapter_update.1 = (f32[24,128]{1,0:T(8,128)}, f32[8,24,128]{2,1,0:T(8,128)}, f32[24,128]{1,0:T(8,128)}, f32[24,128]{1,0:T(8,128)}) custom-call(s32[1]{0:T(128)} %bitcast.1.place_ref, bf16[32,768]{1,0:T(8,128)(2,1)} %copy-done.15, bf16[32,768]{1,0:T(8,128)(2,1)} %copy-done.29, f32[8,24,128]{2,1,0:T(8,128)} %bitcast.12, f32[4,2,24,128]{3,2,1,0:T(8,128)} %copy-done.14, ...), custom_call_target="tpu_custom_call" | custom-call | tf_op jit(solution)/shard_map/adapter_update/pallas_call | solution.py:574
  (88 shorter events, 0.2 us)
Async XLA Ops:
  0.6 19.2 %copy-start.8 = (bf16[192,768]{1,0:T(8,128)(2,1)S(1)}, bf16[192,768]{1,0:T(8,128)(2,1)}, u32[]{:S(2)}) copy-start(bf16[192,768]{1,0:T(8,128)(2,1)} %rest_0_.4) | copy-start | bytes 884740
  0.6 20.9 %copy-start.10 = (bf16[192,768]{1,0:T(8,128)(2,1)S(1)}, bf16[192,768]{1,0:T(8,128)(2,1)}, u32[]{:S(2)}) copy-start(bf16[192,768]{1,0:T(8,128)(2,1)} %rest_2_.2) | copy-start | bytes 884740
  0.7 19.2 %copy-start.9 = (bf16[192,768]{1,0:T(8,128)(2,1)S(1)}, bf16[192,768]{1,0:T(8,128)(2,1)}, u32[]{:S(2)}) copy-start(bf16[192,768]{1,0:T(8,128)(2,1)} %rest_1_.4) | copy-start | bytes 884740
  1.7 12.9 %collective-permute-start = (bf16[96,768]{1,0:T(8,128)(2,1)S(1)}, bf16[96,768]{1,0:T(8,128)(2,1)S(1)}, u32[]{:S(2)}, u32[]{:S(2)}) collective-permute-start(bf16[96,768]{1,0:T(8,128)(2,1)S(1)} %constant_dynamic-slice_fusion.2), channel_id=1, source_target_pairs={{0,16},{8,24},{16,0},{24,8},{1,17},{9,25},{17,1},{25,9},{2,18},{10... | collective-permute-start | bytes 442376 | tf_op jit(solution)/shard_map/ppermute | solution.py:589
  5.6 6.8 %collective-permute-start.11 = (bf16[96,768]{1,0:T(8,128)(2,1)S(1)}, bf16[96,768]{1,0:T(8,128)(2,1)S(1)}, u32[]{:S(2)}, u32[]{:S(2)}) collective-permute-start(bf16[96,768]{1,0:T(8,128)(2,1)S(1)} %constant_dynamic-slice_fusion), channel_id=1, source_target_pairs={{0,16},{8,24},{16,0},{24,8},{1,17},{9,25},{17,1},{25,9},{2,18},{10... | collective-permute-start | bytes 442376 | tf_op jit(solution)/shard_map/ppermute | solution.py:589
  6.6 9.5 %collective-permute-start.7 = (bf16[96,768]{1,0:T(8,128)(2,1)S(1)}, bf16[96,768]{1,0:T(8,128)(2,1)S(1)}, u32[]{:S(2)}, u32[]{:S(2)}) collective-permute-start(bf16[96,768]{1,0:T(8,128)(2,1)S(1)} %constant_dynamic-slice_fusion.1), channel_id=1, source_target_pairs={{0,16},{8,24},{16,0},{24,8},{1,17},{9,25},{17,1},{25,9},{2,18},{10... | collective-permute-start | bytes 442376 | tf_op jit(solution)/shard_map/ppermute | solution.py:589
  12.5 16.3 %copy-start.17 = (bf16[96,768]{1,0:T(8,128)(2,1)}, bf16[96,768]{1,0:T(8,128)(2,1)S(1)}, u32[]{:S(2)}) copy-start(bf16[96,768]{1,0:T(8,128)(2,1)S(1)} %collective-permute-done.11.rest_14_) | copy-start | bytes 442372
  12.5 30.7 %collective-permute-start.15 = (bf16[5,96,768]{2,1,0:T(8,128)(2,1)}, bf16[5,96,768]{2,1,0:T(8,128)(2,1)}, u32[]{:S(2)}, u32[]{:S(2)}) collective-permute-start(bf16[5,96,768]{2,1,0:T(8,128)(2,1)} %get-tuple-element.77), channel_id=1, source_target_pairs={{0,16},{8,24},{16,0},{24,8},{1,17},{9,25},{17,1},{25,9},{2,18},{10... | collective-permute-start | bytes 2211848 | tf_op jit(solution)/shard_map/ppermute | solution.py:589
  14.6 14.1 %copy-start.16 = (bf16[96,768]{1,0:T(8,128)(2,1)}, bf16[96,768]{1,0:T(8,128)(2,1)S(1)}, u32[]{:S(2)}) copy-start(bf16[96,768]{1,0:T(8,128)(2,1)S(1)} %collective-permute-done.rest_6_) | copy-start | bytes 442372
  14.6 3.3 %collective-permute-start.4 = (bf16[96,768]{1,0:T(8,128)(2,1)S(1)}, bf16[96,768]{1,0:T(8,128)(2,1)S(1)}, u32[]{:S(2)}, u32[]{:S(2)}) collective-permute-start(bf16[96,768]{1,0:T(8,128)(2,1)S(1)} %collective-permute-done.rest_6_), channel_id=1, source_target_pairs={{0,8},{8,0},{16,24},{24,16},{1,9},{9,1},{17,25},{25,17},{2,10},{10... | collective-permute-start | bytes 442376 | tf_op jit(solution)/shard_map/ppermute | solution.py:589
  14.6 5.2 %collective-permute-start.5 = (bf16[96,768]{1,0:T(8,128)(2,1)S(1)}, bf16[96,768]{1,0:T(8,128)(2,1)S(1)}, u32[]{:S(2)}, u32[]{:S(2)}) collective-permute-start(bf16[96,768]{1,0:T(8,128)(2,1)S(1)} %collective-permute-done.rest_6_), channel_id=1, source_target_pairs={{0,1},{1,0},{2,3},{3,2},{4,5},{5,4},{6,7},{7,6},{8,10},{9,11},{10,... | collective-permute-start | bytes 442376 | tf_op jit(solution)/shard_map/ppermute | solution.py:598
  16.2 12.6 %copy-start.18 = (bf16[96,768]{1,0:T(8,128)(2,1)}, bf16[96,768]{1,0:T(8,128)(2,1)S(1)}, u32[]{:S(2)}) copy-start(bf16[96,768]{1,0:T(8,128)(2,1)S(1)} %collective-permute-done.7.rest_10_) | copy-start | bytes 442372
  16.2 3.7 %collective-permute-start.8 = (bf16[96,768]{1,0:T(8,128)(2,1)S(1)}, bf16[96,768]{1,0:T(8,128)(2,1)S(1)}, u32[]{:S(2)}, u32[]{:S(2)}) collective-permute-start(bf16[96,768]{1,0:T(8,128)(2,1)S(1)} %collective-permute-done.7.rest_10_), channel_id=1, source_target_pairs={{0,8},{8,0},{16,24},{24,16},{1,9},{9,1},{17,25},{25,17},{2,10},{10... | collective-permute-start | bytes 442376 | tf_op jit(solution)/shard_map/ppermute | solution.py:589
  16.4 5.1 %collective-permute-start.9 = (bf16[96,768]{1,0:T(8,128)(2,1)S(1)}, bf16[96,768]{1,0:T(8,128)(2,1)S(1)}, u32[]{:S(2)}, u32[]{:S(2)}) collective-permute-start(bf16[96,768]{1,0:T(8,128)(2,1)S(1)} %collective-permute-done.7.rest_10_), channel_id=1, source_target_pairs={{0,1},{1,0},{2,3},{3,2},{4,5},{5,4},{6,7},{7,6},{8,10},{9,11},{10,... | collective-permute-start | bytes 442376 | tf_op jit(solution)/shard_map/ppermute | solution.py:598
  17.9 10.8 %copy-start.19 = (bf16[96,768]{1,0:T(8,128)(2,1)}, bf16[96,768]{1,0:T(8,128)(2,1)S(1)}, u32[]{:S(2)}) copy-start(bf16[96,768]{1,0:T(8,128)(2,1)S(1)} %collective-permute-done.4.rest_7_) | copy-start | bytes 442372
  17.9 5.2 %collective-permute-start.13 = (bf16[96,768]{1,0:T(8,128)(2,1)S(1)}, bf16[96,768]{1,0:T(8,128)(2,1)S(1)}, u32[]{:S(2)}, u32[]{:S(2)}) collective-permute-start(bf16[96,768]{1,0:T(8,128)(2,1)S(1)} %collective-permute-done.11.rest_14_), channel_id=1, source_target_pairs={{0,1},{1,0},{2,3},{3,2},{4,5},{5,4},{6,7},{7,6},{8,10},{9,11},{10,... | collective-permute-start | bytes 442376 | tf_op jit(solution)/shard_map/ppermute | solution.py:598
  19.8 8.9 %copy-start.20 = (bf16[96,768]{1,0:T(8,128)(2,1)}, bf16[96,768]{1,0:T(8,128)(2,1)S(1)}, u32[]{:S(2)}) copy-start(bf16[96,768]{1,0:T(8,128)(2,1)S(1)} %collective-permute-done.5.rest_8_) | copy-start | bytes 442372
  19.8 4.8 %collective-permute-start.1 = (bf16[192,768]{1,0:T(8,128)(2,1)S(1)}, bf16[192,768]{1,0:T(8,128)(2,1)S(1)}, u32[]{:S(2)}, u32[]{:S(2)}) collective-permute-start(bf16[192,768]{1,0:T(8,128)(2,1)S(1)} %copy-done.8), channel_id=1, source_target_pairs={{0,8},{8,0},{16,24},{24,16},{1,9},{9,1},{17,25},{25,17},{2,10},{10... | collective-permute-start | bytes 884744 | tf_op jit(solution)/shard_map/ppermute | solution.py:589
  19.9 8.9 %copy-start.21 = (bf16[96,768]{1,0:T(8,128)(2,1)}, bf16[96,768]{1,0:T(8,128)(2,1)S(1)}, u32[]{:S(2)}) copy-start(bf16[96,768]{1,0:T(8,128)(2,1)S(1)} %collective-permute-done.8.rest_11_) | copy-start | bytes 442372
  19.9 5.2 %collective-permute-start.2 = (bf16[192,768]{1,0:T(8,128)(2,1)S(1)}, bf16[192,768]{1,0:T(8,128)(2,1)S(1)}, u32[]{:S(2)}, u32[]{:S(2)}) collective-permute-start(bf16[192,768]{1,0:T(8,128)(2,1)S(1)} %copy-done.9), channel_id=1, source_target_pairs={{0,8},{8,0},{16,24},{24,16},{1,9},{9,1},{17,25},{25,17},{2,10},{10... | collective-permute-start | bytes 884744 | tf_op jit(solution)/shard_map/ppermute | solution.py:589
  21.6 7.2 %copy-start.22 = (bf16[96,768]{1,0:T(8,128)(2,1)}, bf16[96,768]{1,0:T(8,128)(2,1)S(1)}, u32[]{:S(2)}) copy-start(bf16[96,768]{1,0:T(8,128)(2,1)S(1)} %collective-permute-done.9.rest_12_) | copy-start | bytes 442372
  21.6 3.6 %collective-permute-start.3 = (bf16[192,768]{1,0:T(8,128)(2,1)S(1)}, bf16[192,768]{1,0:T(8,128)(2,1)S(1)}, u32[]{:S(2)}, u32[]{:S(2)}) collective-permute-start(bf16[192,768]{1,0:T(8,128)(2,1)S(1)} %copy-done.10), channel_id=1, source_target_pairs={{0,8},{8,0},{16,24},{24,16},{1,9},{9,1},{17,25},{25,17},{2,10},{10... | collective-permute-start | bytes 884744 | tf_op jit(solution)/shard_map/ppermute | solution.py:589
  23.1 5.7 %copy-start.23 = (bf16[96,768]{1,0:T(8,128)(2,1)}, bf16[96,768]{1,0:T(8,128)(2,1)S(1)}, u32[]{:S(2)}) copy-start(bf16[96,768]{1,0:T(8,128)(2,1)S(1)} %collective-permute-done.13.rest_16_) | copy-start | bytes 442372
  23.1 1.4 collective-permute-start.12
  24.5 4.3 %copy-start.24 = (bf16[96,768]{1,0:T(8,128)(2,1)}, bf16[96,768]{1,0:T(8,128)(2,1)S(1)}, u32[]{:S(2)}) copy-start(bf16[96,768]{1,0:T(8,128)(2,1)S(1)} %collective-permute-done.12.rest_15_) | copy-start | bytes 442372
  24.5 1.4 collective-permute-start.6
  24.7 4.2 %copy-start.11 = (bf16[192,768]{1,0:T(8,128)(2,1)}, bf16[192,768]{1,0:T(8,128)(2,1)S(1)}, u32[]{:S(2)}) copy-start(bf16[192,768]{1,0:T(8,128)(2,1)S(1)} %collective-permute-done.1.rest_3_) | copy-start | bytes 884740
  24.7 2.7 %collective-permute-start.10 = (bf16[96,768]{1,0:T(8,128)(2,1)S(1)}, bf16[96,768]{1,0:T(8,128)(2,1)S(1)}, u32[]{:S(2)}, u32[]{:S(2)}) collective-permute-start(bf16[96,768]{1,0:T(8,128)(2,1)S(1)} %collective-permute-done.9.rest_12_), channel_id=1, source_target_pairs={{0,8},{8,0},{16,24},{24,16},{1,9},{9,1},{17,25},{25,17},{2,10},{10... | collective-permute-start | bytes 442376 | tf_op jit(solution)/shard_map/ppermute | solution.py:589
  25.0 3.8 %copy-start.12 = (bf16[192,768]{1,0:T(8,128)(2,1)}, bf16[192,768]{1,0:T(8,128)(2,1)S(1)}, u32[]{:S(2)}) copy-start(bf16[192,768]{1,0:T(8,128)(2,1)S(1)} %collective-permute-done.2.rest_4_) | copy-start | bytes 884740
  25.0 3.7 %collective-permute-start.14 = (bf16[96,768]{1,0:T(8,128)(2,1)S(1)}, bf16[96,768]{1,0:T(8,128)(2,1)S(1)}, u32[]{:S(2)}, u32[]{:S(2)}) collective-permute-start(bf16[96,768]{1,0:T(8,128)(2,1)S(1)} %collective-permute-done.13.rest_16_), channel_id=1, source_target_pairs={{0,8},{8,0},{16,24},{24,16},{1,9},{9,1},{17,25},{25,17},{2,10},{10... | collective-permute-start | bytes 442376 | tf_op jit(solution)/shard_map/ppermute | solution.py:589
  25.2 3.6 %copy-start.13 = (bf16[192,768]{1,0:T(8,128)(2,1)}, bf16[192,768]{1,0:T(8,128)(2,1)S(1)}, u32[]{:S(2)}) copy-start(bf16[192,768]{1,0:T(8,128)(2,1)S(1)} %collective-permute-done.3.rest_5_) | copy-start | bytes 884740
  25.2 35.8 %collective-permute-start.16 = (bf16[2,5,96,768]{3,2,1,0:T(8,128)(2,1)}, bf16[2,5,96,768]{3,2,1,0:T(8,128)(2,1)}, u32[]{:S(2)}, u32[]{:S(2)}) collective-permute-start(bf16[2,5,96,768]{3,2,1,0:T(8,128)(2,1)} %get-tuple-element.86), channel_id=1, source_target_pairs={{0,8},{8,0},{16,24},{24,16},{1,9},{9,1},{17,25},{25,17},{2,10},{10... | collective-permute-start | bytes 4423688 | tf_op jit(solution)/shard_map/ppermute | solution.py:589
  25.9 3.0 %copy-start.25 = (bf16[96,768]{1,0:T(8,128)(2,1)}, bf16[96,768]{1,0:T(8,128)(2,1)S(1)}, u32[]{:S(2)}) copy-start(bf16[96,768]{1,0:T(8,128)(2,1)S(1)} %collective-permute-done.6.rest_9_) | copy-start | bytes 442372
  25.9 30.7 %collective-permute-start.18 = (f32[1,2,24,128]{3,2,1,0:T(8,128)S(1)}, f32[1,2,24,128]{3,2,1,0:T(8,128)S(1)}, u32[]{:S(2)}, u32[]{:S(2)}) collective-permute-start(f32[1,2,24,128]{3,2,1,0:T(8,128)S(1)} %pad_maximum_fusion), channel_id=1, source_target_pairs={{0,1},{1,0},{2,3},{3,2},{4,5},{5,4},{6,7},{7,6},{8,9},{9,8},{10,11... | collective-permute-start | bytes 73736 | tf_op jit(solution)/shard_map/ppermute | solution.py:589
  27.4 1.5 %copy-start.26 = (bf16[96,768]{1,0:T(8,128)(2,1)}, bf16[96,768]{1,0:T(8,128)(2,1)S(1)}, u32[]{:S(2)}) copy-start(bf16[96,768]{1,0:T(8,128)(2,1)S(1)} %collective-permute-done.10.rest_13_) | copy-start | bytes 442372
  27.4 30.4 %collective-permute-start.20 = (bf16[768,768]{1,0:T(8,128)(2,1)}, bf16[768,768]{1,0:T(8,128)(2,1)}, u32[]{:S(2)}, u32[]{:S(2)}) collective-permute-start(bf16[768,768]{1,0:T(8,128)(2,1)} %rest_14_.1), channel_id=1, source_target_pairs={{0,16},{8,24},{16,0},{24,8},{1,17},{9,25},{17,1},{25,9},{2,18},{10... | collective-permute-start | bytes 3538952 | tf_op jit(solution)/shard_map/ppermute | solution.py:589
  28.7 0.7 copy-start.27
  43.2 15.2 %collective-permute-start.17 = (bf16[5,96,768]{2,1,0:T(8,128)(2,1)}, bf16[5,96,768]{2,1,0:T(8,128)(2,1)S(1)}, u32[]{:S(2)}, u32[]{:S(2)}) collective-permute-start(bf16[5,96,768]{2,1,0:T(8,128)(2,1)} %gate.2.rest_10_), channel_id=1, source_target_pairs={{0,8},{8,0},{16,24},{24,16},{1,9},{9,1},{17,25},{25,17},{2,10},{10... | collective-permute-start | bytes 2211848 | tf_op jit(solution)/shard_map/ppermute | solution.py:589
  43.3 14.6 %collective-permute-start.19 = (bf16[5,96,768]{2,1,0:T(8,128)(2,1)}, bf16[5,96,768]{2,1,0:T(8,128)(2,1)S(1)}, u32[]{:S(2)}, u32[]{:S(2)}) collective-permute-start(bf16[5,96,768]{2,1,0:T(8,128)(2,1)} %gate.2.rest_10_), channel_id=1, source_target_pairs={{0,1},{1,0},{2,3},{3,2},{4,5},{5,4},{6,7},{7,6},{8,10},{9,11},{10,... | collective-permute-start | bytes 2211848 | tf_op jit(solution)/shard_map/ppermute | solution.py:598
  43.9 12.7 %copy-start.30 = (bf16[768,768]{1,0:T(8,128)(2,1)S(1)}, bf16[768,768]{1,0:T(8,128)(2,1)}, u32[]{:S(2)}) copy-start(bf16[768,768]{1,0:T(8,128)(2,1)} %rest_14_.1) | copy-start | bytes 3538948
  56.6 4.4 %collective-permute-start.22 = (bf16[768,768]{1,0:T(8,128)(2,1)S(1)}, bf16[768,768]{1,0:T(8,128)(2,1)}, u32[]{:S(2)}, u32[]{:S(2)}) collective-permute-start(bf16[768,768]{1,0:T(8,128)(2,1)S(1)} %copy-done.30), channel_id=1, source_target_pairs={{0,8},{8,0},{16,24},{24,16},{1,9},{9,1},{17,25},{25,17},{2,10},{10... | collective-permute-start | bytes 3538952 | tf_op jit(solution)/shard_map/ppermute | solution.py:589
  57.8 1.5 %copy-start.31 = (bf16[5,96,768]{2,1,0:T(8,128)(2,1)}, bf16[5,96,768]{2,1,0:T(8,128)(2,1)S(1)}, u32[]{:S(2)}) copy-start(bf16[5,96,768]{2,1,0:T(8,128)(2,1)S(1)} %collective-permute-done.19.rest_12_) | copy-start | bytes 2211844
  57.8 5.5 %collective-permute-start.23 = (bf16[768,768]{1,0:T(8,128)(2,1)}, bf16[768,768]{1,0:T(8,128)(2,1)}, u32[]{:S(2)}, u32[]{:S(2)}) collective-permute-start(bf16[768,768]{1,0:T(8,128)(2,1)} %collective-permute-done.20.rest_16_), channel_id=1, source_target_pairs={{0,8},{8,0},{16,24},{24,16},{1,9},{9,1},{17,25},{25,17},{2,10},{10... | collective-permute-start | bytes 3538952 | tf_op jit(solution)/shard_map/ppermute | solution.py:589
  57.9 5.2 %collective-permute-start.21 = (bf16[5,96,768]{2,1,0:T(8,128)(2,1)S(1)}, bf16[5,96,768]{2,1,0:T(8,128)(2,1)}, u32[]{:S(2)}, u32[]{:S(2)}) collective-permute-start(bf16[5,96,768]{2,1,0:T(8,128)(2,1)S(1)} %collective-permute-done.19.rest_12_), channel_id=1, source_target_pairs={{0,8},{8,0},{16,24},{24,16},{1,9},{9,1},{17,25},{25,17},{2,10},{10... | collective-permute-start | bytes 2211848 | tf_op jit(solution)/shard_map/ppermute | solution.py:589
  58.4 0.9 copy-start.32
  58.4 40.6 %collective-permute-start.24 = (f32[2,2,24,128]{3,2,1,0:T(8,128)S(1)}, f32[2,2,24,128]{3,2,1,0:T(8,128)S(1)}, u32[]{:S(2)}, u32[]{:S(2)}) collective-permute-start(f32[2,2,24,128]{3,2,1,0:T(8,128)S(1)} %constant_dynamic-update-slice_fusion), channel_id=1, source_target_pairs={{0,2},{1,3},{2,0},{3,1},{4,6},{5,7},{6,4},{7,5},{8,10},{9,11},{10,... | collective-permute-start | bytes 147464 | tf_op jit(solution)/shard_map/ppermute | solution.py:589
  63.4 35.6 %copy-start.2 = (f32[24576]{0:T(1024)S(1)}, f32[24576]{0:T(1024)}, u32[]{:S(2)}) copy-start(f32[24576]{0:T(1024)} %param.39) | copy-start | bytes 294916
  63.4 35.7 %copy-start.3 = (bf16[1024,768]{1,0:T(8,128)(2,1)S(1)}, bf16[1024,768]{1,0:T(8,128)(2,1)}, u32[]{:S(2)}) copy-start(bf16[1024,768]{1,0:T(8,128)(2,1)} %x_ref.7) | copy-start | bytes 4718596
  63.4 35.7 %copy-start.4 = (s32[2,512]{1,0:T(2,128)S(1)}, s32[2,512]{1,0:T(2,128)}, u32[]{:S(2)}) copy-start(s32[2,512]{1,0:T(2,128)} %seg_ref.5) | copy-start | bytes 12292
  63.4 35.7 %copy-start.5 = (bf16[1024,768]{1,0:T(8,128)(2,1)S(1)}, bf16[1024,768]{1,0:T(8,128)(2,1)}, u32[]{:S(2)}) copy-start(bf16[1024,768]{1,0:T(8,128)(2,1)} %get-tuple-element.97.rest_0_) | copy-start | bytes 4718596
  63.4 35.7 %copy-start.6 = (bf16[1024,768]{1,0:T(8,128)(2,1)S(1)}, bf16[1024,768]{1,0:T(8,128)(2,1)}, u32[]{:S(2)}) copy-start(bf16[1024,768]{1,0:T(8,128)(2,1)} %get-tuple-element.98.rest_1_) | copy-start | bytes 4718596
  63.4 35.7 %copy-start.7 = (bf16[1024,16]{1,0:T(8,128)(2,1)S(1)}, bf16[1024,16]{1,0:T(8,128)(2,1)}, u32[]{:S(2)}) copy-start(bf16[1024,16]{1,0:T(8,128)(2,1)} %get-tuple-element.91.other_ref.down_ref) | copy-start | bytes 98308
  99.1 27.4 %copy-start = (bf16[3,768,768]{2,1,0:T(8,128)(2,1)S(1)}, bf16[3,768,768]{2,1,0:T(8,128)(2,1)}, u32[]{:S(2)}) copy-start(bf16[3,768,768]{2,1,0:T(8,128)(2,1)} %get-tuple-element.78.rest_0_.other_ref.weights) | copy-start | bytes 10616836
  99.1 27.3 %copy-start.1 = (bf16[1024,768]{1,0:T(8,128)(2,1)S(1)}, bf16[1024,768]{1,0:T(8,128)(2,1)}, u32[]{:S(2)}) copy-start(bf16[1024,768]{1,0:T(8,128)(2,1)} %get-tuple-element.121.dh_ref) | copy-start | bytes 4718596
  122.7 3.1 %collective-permute-start.25 = (bf16[32,768]{1,0:T(8,128)(2,1)S(1)}, bf16[32,768]{1,0:T(8,128)(2,1)S(1)}, u32[]{:S(2)}, u32[]{:S(2)}) collective-permute-start(bf16[32,768]{1,0:T(8,128)(2,1)S(1)} %get-tuple-element.105), channel_id=1, source_target_pairs={{0,8},{8,0},{16,24},{24,16},{1,9},{9,1},{17,25},{25,17},{2,10},{10... | collective-permute-start | bytes 147464 | tf_op jit(solution)/shard_map/ppermute | solution.py:589
  123.2 5.2 %copy-start.14 = (f32[4,2,24,128]{3,2,1,0:T(8,128)}, f32[4,2,24,128]{3,2,1,0:T(8,128)S(1)}, u32[]{:S(2)}) copy-start(f32[4,2,24,128]{3,2,1,0:T(8,128)S(1)} %constant_dynamic-update-slice_fusion.2.held_ref) | copy-start | bytes 294916
  123.2 18.0 %collective-permute-start.30 = (f32[4,2,24,128]{3,2,1,0:T(8,128)S(1)}, f32[4,2,24,128]{3,2,1,0:T(8,128)S(1)}, u32[]{:S(2)}, u32[]{:S(2)}) collective-permute-start(f32[4,2,24,128]{3,2,1,0:T(8,128)S(1)} %constant_dynamic-update-slice_fusion.2.held_ref), channel_id=1, source_target_pairs={{0,4},{1,5},{2,6},{3,7},{4,0},{5,1},{6,2},{7,3},{8,12},{9,13},{10,... | collective-permute-start | bytes 294920 | tf_op jit(solution)/shard_map/ppermute | solution.py:589
  125.9 4.2 %collective-permute-start.26 = (bf16[32,768]{1,0:T(8,128)(2,1)S(1)}, bf16[32,768]{1,0:T(8,128)(2,1)S(1)}, u32[]{:S(2)}, u32[]{:S(2)}) collective-permute-start(bf16[32,768]{1,0:T(8,128)(2,1)S(1)} %add.18), channel_id=1, source_target_pairs={{0,16},{8,24},{16,0},{24,8},{1,17},{9,25},{17,1},{25,9},{2,18},{10... | collective-permute-start | bytes 147464 | tf_op jit(solution)/shard_map/ppermute | solution.py:589
  130.0 4.2 %collective-permute-start.27 = (bf16[32,768]{1,0:T(8,128)(2,1)S(1)}, bf16[32,768]{1,0:T(8,128)(2,1)S(1)}, u32[]{:S(2)}, u32[]{:S(2)}) collective-permute-start(bf16[32,768]{1,0:T(8,128)(2,1)S(1)} %add.19), channel_id=1, source_target_pairs={{0,1},{1,0},{2,3},{3,2},{4,5},{5,4},{6,7},{7,6},{8,9},{9,8},{10,11... | collective-permute-start | bytes 147464 | tf_op jit(solution)/shard_map/ppermute | solution.py:589
  134.2 4.2 %collective-permute-start.28 = (bf16[32,768]{1,0:T(8,128)(2,1)S(1)}, bf16[32,768]{1,0:T(8,128)(2,1)S(1)}, u32[]{:S(2)}, u32[]{:S(2)}) collective-permute-start(bf16[32,768]{1,0:T(8,128)(2,1)S(1)} %add.20), channel_id=1, source_target_pairs={{0,2},{1,3},{2,0},{3,1},{4,6},{5,7},{6,4},{7,5},{8,10},{9,11},{10,... | collective-permute-start | bytes 147464 | tf_op jit(solution)/shard_map/ppermute | solution.py:589
  138.4 2.8 %copy-start.15 = (bf16[32,768]{1,0:T(8,128)(2,1)}, bf16[32,768]{1,0:T(8,128)(2,1)S(1)}, u32[]{:S(2)}) copy-start(bf16[32,768]{1,0:T(8,128)(2,1)S(1)} %add.21.near_ref) | copy-start | bytes 147460
  138.4 5.6 %collective-permute-start.29 = (bf16[32,768]{1,0:T(8,128)(2,1)S(1)}, bf16[32,768]{1,0:T(8,128)(2,1)S(1)}, u32[]{:S(2)}, u32[]{:S(2)}) collective-permute-start(bf16[32,768]{1,0:T(8,128)(2,1)S(1)} %add.21.near_ref), channel_id=1, source_target_pairs={{0,4},{1,5},{2,6},{3,7},{4,0},{5,1},{6,2},{7,3},{8,12},{9,13},{10,... | collective-permute-start | bytes 147464 | tf_op jit(solution)/shard_map/ppermute | solution.py:589
  141.2 2.8 %copy-start.28 = (f32[4,2,24,128]{3,2,1,0:T(8,128)}, f32[4,2,24,128]{3,2,1,0:T(8,128)S(1)}, u32[]{:S(2)}) copy-start(f32[4,2,24,128]{3,2,1,0:T(8,128)S(1)} %collective-permute-done.30.other_ref) | copy-start | bytes 294916
  144.0 0.6 copy-start.29

commit v4 on v3

--- a/solution.py
+++ b/solution.py
@@ -222,27 +222,36 @@
     ones = jnp.ones((rows, LANES), BF16)
     half = LANES // 2
     scale = BF16(half ** (-0.5))
-    for pair in range(width // LANES):
-        here = slice(LANES * pair, LANES * (pair + 1))
-        keys = beside(k_ref[:, here], aug_k)
-        values = beside(v_ref[:, here], ones)
-        query = q_ref[:, here] * scale
-        out = None
-        for side in range(2):
-            mask = (lane // half) == side
-            scores = dot(beside(jnp.where(mask, query, BF16(0)), aug_q), keys, NT)
-            top = jnp.max(scores, axis=1, keepdims=True)
-            expo = jnp.exp(scores - top).astype(BF16)
-            both = dot(expo, values, NN)
-            sums = both[:, LANES:]
-            ctx = both[:, :LANES] / sums
-            out = ctx if side == 0 else jnp.where(mask, ctx, out)
-            high, middle, little = three_parts(-(top + jnp.log(sums)))
+    second = lane >= half
+    spot = jnp.bitwise_and(lane, half - 1)
+
+    def scores(head):
+        here = slice(LANES * (head // 2), LANES * (head // 2 + 1))
+        query = jnp.where(second == (head % 2 == 1), q_ref[:, here] * scale, BF16(0))
+        return dot(beside(query, aug_q), beside(k_ref[:, here], aug_k), NT)
+
+    heads = 2 * width // LANES
+    ahead = scores(0)
+    found = []
+    for head in range(heads):
+        now = ahead
+        if head + 1 < heads:
+            ahead = scores(head + 1)
+        here = slice(LANES * (head // 2), LANES * (head // 2 + 1))
+        top = jnp.max(now, axis=1, keepdims=True)
+        expo = jnp.exp(now - top).astype(BF16)
+        both = dot(expo, beside(v_ref[:, here], ones), NN)
+        found.append((top, both[:, :LANES], both[:, LANES:]))
+        if head % 2 == 1:
+            (top0, ctx0, sums0), (top1, ctx1, sums1) = found[-2:]
+            sums = jnp.where(second, sums1, sums0)
+            ctx_ref[:, here] = (jnp.where(second, ctx1, ctx0) / sums).astype(BF16)
+            level = jnp.where(second, top1, top0) + jnp.log(sums)
+            high, middle, little = three_parts(-level)
             aug = jnp.where(
-                lane == 4, high, jnp.where(lane == 5, middle, jnp.where(lane == 6, little, own))
+                spot == 4, high, jnp.where(spot == 5, middle, jnp.where(spot == 6, little, own))
             )
-            aug_ref[:, (2 * pair + side) * LANES : (2 * pair + side + 1) * LANES] = aug.astype(BF16)
-        ctx_ref[:, here] = out.astype(BF16)
+            aug_ref[:, here] = aug.astype(BF16)
 
 
 def attend(rank, place, seg, x, factors, bq, bv, pairs, first, count, parts, weights=None, carry=()):
@@ -258,11 +267,10 @@
         block,
         block,
         block,
-        pl.BlockSpec((size, 2 * cut), lambda p, g: (first + p, g)),
+        block,
         pl.BlockSpec((size, 2 * ADAPTER_RANK), lambda p, g: (first + p, 0)),
     ]
-    out_shape = [like((rows, width), BF16)] * 4
-    out_shape += [like((rows, 2 * width), BF16), like((rows, 2 * ADAPTER_RANK), BF16)]
+    out_shape = [like((rows, width), BF16)] * 5 + [like((rows, 2 * ADAPTER_RANK), BF16)]
     scratch = [pltpu.VMEM((8, width), F32), pltpu.VMEM((4 * ADAPTER_RANK, width), F32)]
     if parts is None:
         operands, specs = [weights, *carry], [vmem] + [ANY] * len(carry)
@@ -317,37 +325,54 @@
         for copy in start:
             copy.wait()
 
-    row = lambda ref: ref[...].reshape(1, -1)
+    bo, bo2 = bo_ref[...].reshape(1, -1), bo2_ref[...].reshape(1, -1)
+    g1, s1 = g1_ref[...].reshape(1, -1), s1_ref[...].reshape(1, -1)
+    g2, s2 = g2_ref[...].reshape(1, -1), s2_ref[...].reshape(1, -1)
+    inner_bias = bi_ref[...].reshape(1, -1)
     wo = lambda: ahead[:, :width]
     w1 = lambda j: ahead[:, width + j : width + j + cut]
-    inner_bias = row(bi_ref)
-    h1 = x_ref[...].astype(F32) + dot(ctx_ref[...], wo(), NN) + row(bo_ref)
-    norm1, rstd1 = layer_norm(h1)
-    y1 = norm1 * row(g1_ref) + row(s1_ref)
-    y1_low = y1.astype(BF16)
+
+    def stages(rows):
+        h1 = x_ref[rows, :].astype(F32) + dot(ctx_ref[rows, :], wo(), NN) + bo
+        norm1, rstd1 = layer_norm(h1)
+        y1 = norm1 * g1 + s1
+        y1_low = y1.astype(BF16)
+        h2 = y1 + bo2
+        yield
+        for j in range(0, hidden, cut):
+            inner = dot(y1_low, w1(j), NN) + inner_bias[:, j : j + cut]
+            act, gradient = gelu_pair(inner)
+            slope[rows, j : j + cut] = gradient
+            h2 = h2 + dot(act.astype(BF16), outer[j : j + cut, :], NN)
+            yield
+        norm2, rstd2 = layer_norm(h2)
+        out_ref[rows, :] = (norm2 * g2 + s2).astype(BF16)
+        dh2 = norm_back(cot_ref[rows, :].astype(F32), norm2, rstd2, g2)
+        df = dh2.astype(BF16)
+        dy1 = dh2
+        yield
+        for j in range(0, hidden, cut):
+            du = (dot(df, outer[j : j + cut, :], NT) * slope[rows, j : j + cut]).astype(BF16)
+            dy1 = dy1 + dot(du, w1(j), NT)
+            yield
+        dh1 = norm_back(dy1, norm1, rstd1, g1).astype(BF16)
+        dh_ref[rows, :] = dh1
+        yield
+        dctx_ref[rows, :] = dot(dh1, wo(), NT).astype(BF16)
+
+    size = x_ref.shape[0] // 2
+    blocks = [stages(slice(start, start + size)) for start in (0, size)]
+    next(blocks[0])
 
     @pl.when(at == 0)
     def _():
         for copy in later:
             copy.wait()
 
-    h2 = y1 + row(bo2_ref)
-    for j in range(0, hidden, cut):
-        inner = dot(y1_low, w1(j), NN) + inner_bias[:, j : j + cut]
-        act, gradient = gelu_pair(inner)
-        slope[:, j : j + cut] = gradient
-        h2 = h2 + dot(act.astype(BF16), outer[j : j + cut, :], NN)
-    norm2, rstd2 = layer_norm(h2)
-    out_ref[...] = (norm2 * row(g2_ref) + row(s2_ref)).astype(BF16)
-    dh2 = norm_back(cot_ref[...].astype(F32), norm2, rstd2, row(g2_ref))
-    df = dh2.astype(BF16)
-    dy1 = dh2
-    for j in range(0, hidden, cut):
-        du = (dot(df, outer[j : j + cut, :], NT) * slope[:, j : j + cut]).astype(BF16)
-        dy1 = dy1 + dot(du, w1(j), NT)
-    dh1 = norm_back(dy1, norm1, rstd1, row(g1_ref)).astype(BF16)
-    dh_ref[...] = dh1
-    dctx_ref[...] = dot(dh1, wo(), NT).astype(BF16)
+    next(blocks[0])
+    live = True
+    while live:
+        live = any([next(block, True) is None for block in reversed(blocks)])
 
 
 def dense(rank, place, x, ctx, cot, vectors, first, second, size, cut):
@@ -393,9 +418,14 @@
 
     lane = lax.broadcasted_iota(jnp.int32, (rows, LANES), 1)
     seg = seg_ref[pl.ds(pl.program_id(0), 1), :].astype(F32).T.astype(jnp.int32)
-    aug_k = jnp.where(
-        (lane < 4) & (lane != seg), -MASKED, jnp.where((lane >= 4) & (lane < 7), 1.0, 0.0)
-    ).astype(BF16)
+    spot = jnp.bitwise_and(lane, LANES // 2 - 1)
+    level = (spot >= 4) & (spot < 7)
+    second = lane >= LANES // 2
+    differ = (lane < 4) & (lane != seg)
+    aug_ks = [
+        jnp.where(differ, -MASKED, jnp.where(level & (second == bool(side)), 1.0, 0.0)).astype(BF16)
+        for side in range(2)
+    ]
     aug_v = jnp.where(lane < 3, 1.0, 0.0).astype(BF16)
     zero = BF16(0)
     half = LANES // 2
@@ -405,7 +435,6 @@
         key = k_ref[:, here]
         query = q_ref[:, here] * scale
         grad = dctx_ref[:, here]
-        keys = beside(key, aug_k)
         values = beside(v_ref[:, here], aug_v)
         key = key * scale
         product = grad.astype(F32) * ctx_ref[:, here].astype(F32)
@@ -420,8 +449,8 @@
             aug_d = jnp.where(
                 lane == 0, high, jnp.where(lane == 1, middle, jnp.where(lane == 2, little, 0.0))
             ).astype(BF16)
-            aug_q = aug_ref[:, (2 * pair + side) * LANES : (2 * pair + side + 1) * LANES]
-            probs = jnp.exp(dot(keys, beside(one_query, aug_q), NT))
+            keys = beside(k_ref[:, here], aug_ks[side])
+            probs = jnp.exp(dot(keys, beside(one_query, aug_ref[:, here]), NT))
             dprobs = dot(values, beside(one_grad, aug_d), NT)
             dscores = (probs * dprobs).astype(BF16)
             dv = dv + dot(probs.astype(BF16), one_grad, NN)
@@ -477,7 +506,7 @@
             block,
             block,
             block,
-            pl.BlockSpec((size, 2 * cut), lambda p, g: (p, g)),
+            block,
         ],
         out_specs=[
             block,

time: 147 us -> 143 us (0.973)
  Pallas kernels: 98.2 us -> 93.8 us
    pallas_call x2, Pallas kernels: 26.5 us -> 24.3 us  [attend(): pl.pallas_call(functools.partial(attend_kernel, parts, first), grid=(coun...]
    pallas_call x1, Pallas kernels: 35.6 us -> 33.5 us  [dense(): pl.pallas_call(functools.partial(dense_kernel, first, second, cut), grid=...]
  transfers between devices with their start and end apart: 31 -> 31, of which waited for: 13 -> 13; matrix products, arithmetic and copies ran while one was open for 2% -> 2% of each run, Pallas kernels for 49% -> 48%
where the time goes in v4:
time: 143 us; the launch traced here: 142 us
  Pallas kernels  93.8 us (66%)
  starting transfers between devices  25.5 us (18%)
  waiting for transfers between devices  17 us (12%)
  local copies, waits for them, and re-layouts  4.1 us (3%)
    pallas_call x1, Pallas kernels, dense(): pl.pallas_call(functools.partial(dense_kernel, first, second, cut), grid=...  33.5 us
    pallas_call x2, Pallas kernels, attend(): pl.pallas_call(functools.partial(attend_kernel, parts, first), grid=(coun...  24.3 us
    pallas_call x1, Pallas kernels, attend_back(): pl.pallas_call(attend_back_kernel, grid=(packs, width // cut), in_specs=[...  23.5 us
    ppermute x27, starting transfers between devices, swap(): return lax.ppermute(value, axis, [(i, i ^ flip) for i in range(size)])  21.4 us
    ppermute x27, waiting for transfers between devices, swap(): return lax.ppermute(value, axis, [(i, i ^ flip) for i in range(size)])  12.9 us
    pallas_call x4, Pallas kernels, input_back(): pl.pallas_call(functools.partial(input_kernel, at * size), grid=(1,), in_...  7.61 us
    ppermute x4, starting transfers between devices, cross(): return lax.ppermute(value, ('rep', 'wide'), pairs)  4.18 us
    ppermute x4, waiting for transfers between devices, cross(): return lax.ppermute(value, ('rep', 'wide'), pairs)  4.1 us
  transfers between devices with their start and end apart: 31, of which 13 were waited for; matrix products, arithmetic and copies ran while one was open for 2% of the time, Pallas kernels for 48%

profile of v4, /device:TPU:0, one launch (start us, length us, event | category | flops | bytes accessed | tf_op | source)
XLA Modules:
  0.0 142.2 jit_solution(15212404699022894260)
XLA Ops:
  0.6 0.0 copy-start.8
  0.6 0.0 copy-start.10
  0.7 0.0 copy-start.9
  0.7 1.0 constant_dynamic-slice_fusion.2
  1.7 3.0 %collective-permute-start = (bf16[96,768]{1,0:T(8,128)(2,1)S(1)}, bf16[96,768]{1,0:T(8,128)(2,1)S(1)}, u32[]{:S(2)}, u32[]{:S(2)}) collective-permute-start(bf16[96,768]{1,0:T(8,128)(2,1)S(1)} %constant_dynamic-slice_fusion.2), channel_id=1, source_target_pairs={{0,16},{8,24},{16,0},{24,8},{1,17},{9,25},{17,1},{25,9},{2,18},{10... | collective-permute-start | bytes 442376 | tf_op jit(solution)/shard_map/ppermute | solution.py:618
  4.7 0.9 constant_dynamic-slice_fusion
  5.6 0.1 collective-permute-start.11
  5.7 0.9 constant_dynamic-slice_fusion.1
  6.6 2.1 %collective-permute-start.7 = (bf16[96,768]{1,0:T(8,128)(2,1)S(1)}, bf16[96,768]{1,0:T(8,128)(2,1)S(1)}, u32[]{:S(2)}, u32[]{:S(2)}) collective-permute-start(bf16[96,768]{1,0:T(8,128)(2,1)S(1)} %constant_dynamic-slice_fusion.1), channel_id=1, source_target_pairs={{0,16},{8,24},{16,0},{24,8},{1,17},{9,25},{17,1},{25,9},{2,18},{10... | collective-permute-start | bytes 442376 | tf_op jit(solution)/shard_map/ppermute | solution.py:618
  8.7 0.7 pad_maximum_fusion
  9.4 2.9 %pack_shards.1 = (bf16[2,5,96,768]{3,2,1,0:T(8,128)(2,1)}, bf16[5,96,768]{2,1,0:T(8,128)(2,1)}) custom-call(s32[1]{0:T(128)} %bitcast.1.place_ref, bf16[192,768]{1,0:T(8,128)(2,1)} %rest_7_.1, bf16[192,3072]{1,0:T(8,128)(2,1)} %rest_8_.1), custom_call_target="tpu_custom_call" | custom-call | tf_op jit(solution)/shard_map/pack_shards/pallas_call | solution.py:167
  12.3 0.1 collective-permute-done.11.rest_14_
  12.5 2.1 %collective-permute-start.15 = (bf16[5,96,768]{2,1,0:T(8,128)(2,1)}, bf16[5,96,768]{2,1,0:T(8,128)(2,1)}, u32[]{:S(2)}, u32[]{:S(2)}) collective-permute-start(bf16[5,96,768]{2,1,0:T(8,128)(2,1)} %get-tuple-element.77), channel_id=1, source_target_pairs={{0,16},{8,24},{16,0},{24,8},{1,17},{9,25},{17,1},{25,9},{2,18},{10... | collective-permute-start | bytes 2211848 | tf_op jit(solution)/shard_map/ppermute | solution.py:618
  14.6 0.0 collective-permute-done.rest_6_
  14.6 0.0 collective-permute-start.4
  14.6 1.6 %collective-permute-start.5 = (bf16[96,768]{1,0:T(8,128)(2,1)S(1)}, bf16[96,768]{1,0:T(8,128)(2,1)S(1)}, u32[]{:S(2)}, u32[]{:S(2)}) collective-permute-start(bf16[96,768]{1,0:T(8,128)(2,1)S(1)} %collective-permute-done.rest_6_), channel_id=1, source_target_pairs={{0,1},{1,0},{2,3},{3,2},{4,5},{5,4},{6,7},{7,6},{8,10},{9,11},{10,... | collective-permute-start | bytes 442376 | tf_op jit(solution)/shard_map/ppermute | solution.py:627
  16.2 0.0 collective-permute-done.7.rest_10_
  16.2 0.2 collective-permute-start.8
  16.4 1.5 %collective-permute-start.9 = (bf16[96,768]{1,0:T(8,128)(2,1)S(1)}, bf16[96,768]{1,0:T(8,128)(2,1)S(1)}, u32[]{:S(2)}, u32[]{:S(2)}) collective-permute-start(bf16[96,768]{1,0:T(8,128)(2,1)S(1)} %collective-permute-done.7.rest_10_), channel_id=1, source_target_pairs={{0,1},{1,0},{2,3},{3,2},{4,5},{5,4},{6,7},{7,6},{8,10},{9,11},{10,... | collective-permute-start | bytes 442376 | tf_op jit(solution)/shard_map/ppermute | solution.py:627
  17.9 0.5 collective-permute-start.13
  18.5 1.4 collective-permute-done.5.rest_8_
  19.8 0.0 collective-permute-start.1
  19.9 0.5 collective-permute-start.2
  20.4 1.2 collective-permute-done.9.rest_12_
  21.6 0.0 collective-permute-start.3
  21.6 1.6 %collective-permute-done.13.rest_16_ = bf16[96,768]{1,0:T(8,128)(2,1)S(1)} collective-permute-done((bf16[96,768]{1,0:T(8,128)(2,1)S(1)}, bf16[96,768]{1,0:T(8,128)(2,1)S(1)}, u32[]{:S(2)}, u32[]{:S(2)}) %collective-permute-start.13) | collective-permute-done | bytes 147488 | tf_op jit(solution)/shard_map/ppermute | solution.py:627
  23.1 0.0 collective-permute-start.12
  23.2 1.4 collective-permute-done.12.rest_15_
  24.5 0.1 collective-permute-start.6
  24.7 0.4 collective-permute-start.10
  25.0 0.1 collective-permute-start.14
  25.2 0.4 collective-permute-start.16
  25.6 0.3 collective-permute-done.6.rest_9_
  25.9 1.5 %collective-permute-start.18 = (f32[1,2,24,128]{3,2,1,0:T(8,128)S(1)}, f32[1,2,24,128]{3,2,1,0:T(8,128)S(1)}, u32[]{:S(2)}, u32[]{:S(2)}) collective-permute-start(f32[1,2,24,128]{3,2,1,0:T(8,128)S(1)} %pad_maximum_fusion), channel_id=1, source_target_pairs={{0,1},{1,0},{2,3},{3,2},{4,5},{5,4},{6,7},{7,6},{8,9},{9,8},{10,11... | collective-permute-start | bytes 73736 | tf_op jit(solution)/shard_map/ppermute | solution.py:618
  27.4 1.3 collective-permute-start.20
  28.9 0.5 copy-done.27
  29.4 12.6 %project_and_attend.2 = (bf16[1024,768]{1,0:T(8,128)(2,1)}, bf16[1024,768]{1,0:T(8,128)(2,1)}, bf16[1024,768]{1,0:T(8,128)(2,1)}, bf16[1024,768]{1,0:T(8,128)(2,...) custom-call(s32[1]{0:T(128)} %bitcast.rank_ref, s32[1]{0:T(128)} %bitcast.1.place_ref, ...), custom_call_target="tpu_custom_call" | custom-call | flops 1 | bytes 1 | tf_op jit(solution)/shard_map/project_and_attend/pallas_call | solution.py:282
  42.0 0.1 collective-permute-start.17
  42.1 0.6 collective-permute-start.19
  42.7 11.8 %project_and_attend.3 = (bf16[1024,768]{1,0:T(8,128)(2,1)}, bf16[1024,768]{1,0:T(8,128)(2,1)}, bf16[1024,768]{1,0:T(8,128)(2,1)}, bf16[1024,768]{1,0:T(8,128)(2,...) custom-call(s32[1]{0:T(128)} %bitcast.rank_ref, ...), custom_call_target="tpu_custom_call", output_to_operand_aliasing={{0}: (8, {}), {1}: (9, {}), {2}: (10, {}), {3}: (11, {}), {... | custom-call | flops 10000000000 | bytes 1 | tf_op jit(solution)/shard_map/project_and_attend/pallas_call | solution.py:282
  54.4 1.3 collective-permute-start.22
  55.7 0.4 collective-permute-done.20.rest_16_
  56.1 0.5 collective-permute-start.21
  56.6 1.9 %collective-permute-start.24 = (f32[2,2,24,128]{3,2,1,0:T(8,128)S(1)}, f32[2,2,24,128]{3,2,1,0:T(8,128)S(1)}, u32[]{:S(2)}, u32[]{:S(2)}) collective-permute-start(f32[2,2,24,128]{3,2,1,0:T(8,128)S(1)} %constant_dynamic-update-slice_fusion), channel_id=1, source_target_pairs={{0,2},{1,3},{2,0},{3,1},{4,6},{5,7},{6,4},{7,5},{8,10},{9,11},{10,... | collective-permute-start | bytes 147464 | tf_op jit(solution)/shard_map/ppermute | solution.py:618
  58.5 1.9 %collective-permute-done.21.rest_13_ = bf16[5,96,768]{2,1,0:T(8,128)(2,1)} collective-permute-done((bf16[5,96,768]{2,1,0:T(8,128)(2,1)S(1)}, bf16[5,96,768]{2,1,0:T(8,128)(2,1)}, u32[]{:S(2)}, u32[]{:S(2)}) %collective-permute-start.21) | collective-permute-done | bytes 737312 | tf_op jit(solution)/shard_map/ppermute | solution.py:618
  60.4 0.8 collective-permute-done.23.rest_17_
  61.3 33.5 %dense_both_ways.1 = (bf16[1024,768]{1,0:T(8,128)(2,1)}, bf16[1024,768]{1,0:T(8,128)(2,1)}, bf16[1024,768]{1,0:T(8,128)(2,1)}) custom-call(s32[1]{0:T(128)} %bitcast.rank_ref, s32[1]{0:T(128)} %bitcast.1.place_ref, bf16[1024,768]{1,0:T(8,128)(2,1)} %x_ref.7, bf16[1024,768]{1,0:T(8,128)(2,1)} %get-tuple-element.85.ctx_ref.rest_4_, bf16[1024,768]{1,0:T(8,128)(2,1)} %cot_ref.1, ...), custom_call_target="tpu_custom_call" | custom-call | flops 21743271936 | bytes 18874368 | tf_op jit(solution)/shard_map/dense_both_ways/pallas_call | solution.py:383
  94.8 23.5 %attend_back.1 = (bf16[1024,768]{1,0:T(8,128)(2,1)S(1)}, bf16[1024,768]{1,0:T(8,128)(2,1)S(1)}, bf16[1024,768]{1,0:T(8,128)(2,1)S(1)}, bf16[1024,16]{1,0:T(8,128)(2,1)S(1)}, bf16[32,768]{1,0:T(8,128)(2,1)S(1)}) custom-call(s32[2,512]{1,0:T(2,128)S(1)} %copy-done.4, bf16[1024,768]{1,0:T(8,128)(2,1)S(1)} %copy-done.3, f32[192,128]{1,0:T(8,128)S(1)} %bitcast.13, ...), custom_call_target="tpu_custom_call" | custom-call | flops 12079595520 | bytes 18874368 | tf_op jit(solution)/shard_map/attend_back/pallas_call | solution.py:496
  118.3 0.4 collective-permute-start.25
  118.8 2.6 %collective-permute-start.30 = (f32[4,2,24,128]{3,2,1,0:T(8,128)S(1)}, f32[4,2,24,128]{3,2,1,0:T(8,128)S(1)}, u32[]{:S(2)}, u32[]{:S(2)}) collective-permute-start(f32[4,2,24,128]{3,2,1,0:T(8,128)S(1)} %constant_dynamic-update-slice_fusion.2.held_ref), channel_id=1, source_target_pairs={{0,4},{1,5},{2,6},{3,7},{4,0},{5,1},{6,2},{7,3},{8,12},{9,13},{10,... | collective-permute-start | bytes 294920 | tf_op jit(solution)/shard_map/ppermute | solution.py:618
  121.5 0.6 collective-permute-start.26
  122.0 1.9 %input_gradient.4.rest_0_ = bf16[1024,768]{1,0:T(8,128)(2,1)} custom-call(bf16[1024,768]{1,0:T(8,128)(2,1)S(1)} %copy-done.1, bf16[1024,768]{1,0:T(8,128)(2,1)S(1)} %get-tuple-element.108.dq_ref, bf16[1024,768]{1,0:T(8,128)(2,1)S(1)} %get-tuple-element.109.dk_ref, bf16[1024,768]{1,0:T(8,128)(2,1)S(1)} %get-tuple-element.110.dv_ref, ...), custom_call_target="tpu_custom_call" | custom-call | flops 905969664 | bytes 1966080 | tf_op jit(solution)/shard_map/input_gradient/pallas_call | solution.py:546
  124.0 1.7 %collective-permute-done.26 = bf16[32,768]{1,0:T(8,128)(2,1)S(1)} collective-permute-done((bf16[32,768]{1,0:T(8,128)(2,1)S(1)}, bf16[32,768]{1,0:T(8,128)(2,1)S(1)}, u32[]{:S(2)}, u32[]{:S(2)}) %collective-permute-start.26) | collective-permute-done | bytes 49184 | tf_op jit(solution)/shard_map/ppermute | solution.py:618
  125.7 0.5 collective-permute-start.27
  126.2 1.9 %input_gradient.5.rest_0_ = bf16[1024,768]{1,0:T(8,128)(2,1)} custom-call(bf16[1024,768]{1,0:T(8,128)(2,1)S(1)} %copy-done.1, bf16[1024,768]{1,0:T(8,128)(2,1)S(1)} %get-tuple-element.108.dq_ref, bf16[1024,768]{1,0:T(8,128)(2,1)S(1)} %get-tuple-element.109.dk_ref, bf16[1024,768]{1,0:T(8,128)(2,1)S(1)} %get-tuple-element.110.dv_ref, ...), custom_call_target="tpu_custom_call", output_to_operand_aliasing={{}: (7, {})} | custom-call | flops 905969664 | bytes 1966080 | tf_op jit(solution)/shard_map/input_gradient/pallas_call | solution.py:546
  128.1 1.7 %collective-permute-done.27 = bf16[32,768]{1,0:T(8,128)(2,1)S(1)} collective-permute-done((bf16[32,768]{1,0:T(8,128)(2,1)S(1)}, bf16[32,768]{1,0:T(8,128)(2,1)S(1)}, u32[]{:S(2)}, u32[]{:S(2)}) %collective-permute-start.27) | collective-permute-done | bytes 49184 | tf_op jit(solution)/shard_map/ppermute | solution.py:618
  129.8 0.6 collective-permute-start.28
  130.5 1.9 %input_gradient.6.rest_0_ = bf16[1024,768]{1,0:T(8,128)(2,1)} custom-call(bf16[1024,768]{1,0:T(8,128)(2,1)S(1)} %copy-done.1, bf16[1024,768]{1,0:T(8,128)(2,1)S(1)} %get-tuple-element.108.dq_ref, bf16[1024,768]{1,0:T(8,128)(2,1)S(1)} %get-tuple-element.109.dk_ref, bf16[1024,768]{1,0:T(8,128)(2,1)S(1)} %get-tuple-element.110.dv_ref, ...), custom_call_target="tpu_custom_call", output_to_operand_aliasing={{}: (7, {})} | custom-call | flops 905969664 | bytes 1966080 | tf_op jit(solution)/shard_map/input_gradient/pallas_call | solution.py:546
  132.4 1.6 %collective-permute-done.28 = bf16[32,768]{1,0:T(8,128)(2,1)S(1)} collective-permute-done((bf16[32,768]{1,0:T(8,128)(2,1)S(1)}, bf16[32,768]{1,0:T(8,128)(2,1)S(1)}, u32[]{:S(2)}, u32[]{:S(2)}) %collective-permute-start.28) | collective-permute-done | bytes 49184 | tf_op jit(solution)/shard_map/ppermute | solution.py:618
  134.0 0.8 collective-permute-start.29
  134.9 1.9 %input_gradient.7 = bf16[1024,768]{1,0:T(8,128)(2,1)} custom-call(bf16[1024,768]{1,0:T(8,128)(2,1)S(1)} %copy-done.1, bf16[1024,768]{1,0:T(8,128)(2,1)S(1)} %get-tuple-element.108.dq_ref, bf16[1024,768]{1,0:T(8,128)(2,1)S(1)} %get-tuple-element.109.dk_ref, bf16[1024,768]{1,0:T(8,128)(2,1)S(1)} %get-tuple-element.110.dv_ref, ...), custom_call_target="tpu_custom_call", output_to_operand_aliasing={{}: (7, {})} | custom-call | flops 905969664 | bytes 1966080 | tf_op jit(solution)/shard_map/input_gradient/pallas_call | solution.py:546
  136.8 2.8 %collective-permute-done.29.far_ref = bf16[32,768]{1,0:T(8,128)(2,1)S(1)} collective-permute-done((bf16[32,768]{1,0:T(8,128)(2,1)S(1)}, bf16[32,768]{1,0:T(8,128)(2,1)S(1)}, u32[]{:S(2)}, u32[]{:S(2)}) %collective-permute-start.29) | collective-permute-done | bytes 49184 | tf_op jit(solution)/shard_map/ppermute | solution.py:618
  139.6 0.6 copy-done.29
  140.2 2.0 %adapter_update.1 = (f32[24,128]{1,0:T(8,128)}, f32[8,24,128]{2,1,0:T(8,128)}, f32[24,128]{1,0:T(8,128)}, f32[24,128]{1,0:T(8,128)}) custom-call(s32[1]{0:T(128)} %bitcast.1.place_ref, bf16[32,768]{1,0:T(8,128)(2,1)} %copy-done.15, bf16[32,768]{1,0:T(8,128)(2,1)} %copy-done.29, f32[8,24,128]{2,1,0:T(8,128)} %bitcast.12, f32[4,2,24,128]{3,2,1,0:T(8,128)} %copy-done.14, ...), custom_call_target="tpu_custom_call" | custom-call | tf_op jit(solution)/shard_map/adapter_update/pallas_call | solution.py:603
  (88 shorter events, 0.2 us)
Async XLA Ops:
  0.6 19.2 %copy-start.8 = (bf16[192,768]{1,0:T(8,128)(2,1)S(1)}, bf16[192,768]{1,0:T(8,128)(2,1)}, u32[]{:S(2)}) copy-start(bf16[192,768]{1,0:T(8,128)(2,1)} %rest_0_.4) | copy-start | bytes 884740
  0.6 20.9 %copy-start.10 = (bf16[192,768]{1,0:T(8,128)(2,1)S(1)}, bf16[192,768]{1,0:T(8,128)(2,1)}, u32[]{:S(2)}) copy-start(bf16[192,768]{1,0:T(8,128)(2,1)} %rest_2_.2) | copy-start | bytes 884740
  0.7 19.2 %copy-start.9 = (bf16[192,768]{1,0:T(8,128)(2,1)S(1)}, bf16[192,768]{1,0:T(8,128)(2,1)}, u32[]{:S(2)}) copy-start(bf16[192,768]{1,0:T(8,128)(2,1)} %rest_1_.4) | copy-start | bytes 884740
  1.7 12.9 %collective-permute-start = (bf16[96,768]{1,0:T(8,128)(2,1)S(1)}, bf16[96,768]{1,0:T(8,128)(2,1)S(1)}, u32[]{:S(2)}, u32[]{:S(2)}) collective-permute-start(bf16[96,768]{1,0:T(8,128)(2,1)S(1)} %constant_dynamic-slice_fusion.2), channel_id=1, source_target_pairs={{0,16},{8,24},{16,0},{24,8},{1,17},{9,25},{17,1},{25,9},{2,18},{10... | collective-permute-start | bytes 442376 | tf_op jit(solution)/shard_map/ppermute | solution.py:618
  5.6 6.8 %collective-permute-start.11 = (bf16[96,768]{1,0:T(8,128)(2,1)S(1)}, bf16[96,768]{1,0:T(8,128)(2,1)S(1)}, u32[]{:S(2)}, u32[]{:S(2)}) collective-permute-start(bf16[96,768]{1,0:T(8,128)(2,1)S(1)} %constant_dynamic-slice_fusion), channel_id=1, source_target_pairs={{0,16},{8,24},{16,0},{24,8},{1,17},{9,25},{17,1},{25,9},{2,18},{10... | collective-permute-start | bytes 442376 | tf_op jit(solution)/shard_map/ppermute | solution.py:618
  6.6 9.5 %collective-permute-start.7 = (bf16[96,768]{1,0:T(8,128)(2,1)S(1)}, bf16[96,768]{1,0:T(8,128)(2,1)S(1)}, u32[]{:S(2)}, u32[]{:S(2)}) collective-permute-start(bf16[96,768]{1,0:T(8,128)(2,1)S(1)} %constant_dynamic-slice_fusion.1), channel_id=1, source_target_pairs={{0,16},{8,24},{16,0},{24,8},{1,17},{9,25},{17,1},{25,9},{2,18},{10... | collective-permute-start | bytes 442376 | tf_op jit(solution)/shard_map/ppermute | solution.py:618
  12.5 16.3 %copy-start.17 = (bf16[96,768]{1,0:T(8,128)(2,1)}, bf16[96,768]{1,0:T(8,128)(2,1)S(1)}, u32[]{:S(2)}) copy-start(bf16[96,768]{1,0:T(8,128)(2,1)S(1)} %collective-permute-done.11.rest_14_) | copy-start | bytes 442372
  12.5 29.5 %collective-permute-start.15 = (bf16[5,96,768]{2,1,0:T(8,128)(2,1)}, bf16[5,96,768]{2,1,0:T(8,128)(2,1)}, u32[]{:S(2)}, u32[]{:S(2)}) collective-permute-start(bf16[5,96,768]{2,1,0:T(8,128)(2,1)} %get-tuple-element.77), channel_id=1, source_target_pairs={{0,16},{8,24},{16,0},{24,8},{1,17},{9,25},{17,1},{25,9},{2,18},{10... | collective-permute-start | bytes 2211848 | tf_op jit(solution)/shard_map/ppermute | solution.py:618
  14.6 14.1 %copy-start.16 = (bf16[96,768]{1,0:T(8,128)(2,1)}, bf16[96,768]{1,0:T(8,128)(2,1)S(1)}, u32[]{:S(2)}) copy-start(bf16[96,768]{1,0:T(8,128)(2,1)S(1)} %collective-permute-done.rest_6_) | copy-start | bytes 442372
  14.6 3.3 %collective-permute-start.4 = (bf16[96,768]{1,0:T(8,128)(2,1)S(1)}, bf16[96,768]{1,0:T(8,128)(2,1)S(1)}, u32[]{:S(2)}, u32[]{:S(2)}) collective-permute-start(bf16[96,768]{1,0:T(8,128)(2,1)S(1)} %collective-permute-done.rest_6_), channel_id=1, source_target_pairs={{0,8},{8,0},{16,24},{24,16},{1,9},{9,1},{17,25},{25,17},{2,10},{10... | collective-permute-start | bytes 442376 | tf_op jit(solution)/shard_map/ppermute | solution.py:618
  14.6 5.2 %collective-permute-start.5 = (bf16[96,768]{1,0:T(8,128)(2,1)S(1)}, bf16[96,768]{1,0:T(8,128)(2,1)S(1)}, u32[]{:S(2)}, u32[]{:S(2)}) collective-permute-start(bf16[96,768]{1,0:T(8,128)(2,1)S(1)} %collective-permute-done.rest_6_), channel_id=1, source_target_pairs={{0,1},{1,0},{2,3},{3,2},{4,5},{5,4},{6,7},{7,6},{8,10},{9,11},{10,... | collective-permute-start | bytes 442376 | tf_op jit(solution)/shard_map/ppermute | solution.py:627
  16.2 12.6 %copy-start.18 = (bf16[96,768]{1,0:T(8,128)(2,1)}, bf16[96,768]{1,0:T(8,128)(2,1)S(1)}, u32[]{:S(2)}) copy-start(bf16[96,768]{1,0:T(8,128)(2,1)S(1)} %collective-permute-done.7.rest_10_) | copy-start | bytes 442372
  16.2 3.7 %collective-permute-start.8 = (bf16[96,768]{1,0:T(8,128)(2,1)S(1)}, bf16[96,768]{1,0:T(8,128)(2,1)S(1)}, u32[]{:S(2)}, u32[]{:S(2)}) collective-permute-start(bf16[96,768]{1,0:T(8,128)(2,1)S(1)} %collective-permute-done.7.rest_10_), channel_id=1, source_target_pairs={{0,8},{8,0},{16,24},{24,16},{1,9},{9,1},{17,25},{25,17},{2,10},{10... | collective-permute-start | bytes 442376 | tf_op jit(solution)/shard_map/ppermute | solution.py:618
  16.4 5.1 %collective-permute-start.9 = (bf16[96,768]{1,0:T(8,128)(2,1)S(1)}, bf16[96,768]{1,0:T(8,128)(2,1)S(1)}, u32[]{:S(2)}, u32[]{:S(2)}) collective-permute-start(bf16[96,768]{1,0:T(8,128)(2,1)S(1)} %collective-permute-done.7.rest_10_), channel_id=1, source_target_pairs={{0,1},{1,0},{2,3},{3,2},{4,5},{5,4},{6,7},{7,6},{8,10},{9,11},{10,... | collective-permute-start | bytes 442376 | tf_op jit(solution)/shard_map/ppermute | solution.py:627
  17.9 10.8 %copy-start.19 = (bf16[96,768]{1,0:T(8,128)(2,1)}, bf16[96,768]{1,0:T(8,128)(2,1)S(1)}, u32[]{:S(2)}) copy-start(bf16[96,768]{1,0:T(8,128)(2,1)S(1)} %collective-permute-done.4.rest_7_) | copy-start | bytes 442372
  17.9 5.2 %collective-permute-start.13 = (bf16[96,768]{1,0:T(8,128)(2,1)S(1)}, bf16[96,768]{1,0:T(8,128)(2,1)S(1)}, u32[]{:S(2)}, u32[]{:S(2)}) collective-permute-start(bf16[96,768]{1,0:T(8,128)(2,1)S(1)} %collective-permute-done.11.rest_14_), channel_id=1, source_target_pairs={{0,1},{1,0},{2,3},{3,2},{4,5},{5,4},{6,7},{7,6},{8,10},{9,11},{10,... | collective-permute-start | bytes 442376 | tf_op jit(solution)/shard_map/ppermute | solution.py:627
  19.8 8.9 %copy-start.20 = (bf16[96,768]{1,0:T(8,128)(2,1)}, bf16[96,768]{1,0:T(8,128)(2,1)S(1)}, u32[]{:S(2)}) copy-start(bf16[96,768]{1,0:T(8,128)(2,1)S(1)} %collective-permute-done.5.rest_8_) | copy-start | bytes 442372
  19.8 4.8 %collective-permute-start.1 = (bf16[192,768]{1,0:T(8,128)(2,1)S(1)}, bf16[192,768]{1,0:T(8,128)(2,1)S(1)}, u32[]{:S(2)}, u32[]{:S(2)}) collective-permute-start(bf16[192,768]{1,0:T(8,128)(2,1)S(1)} %copy-done.8), channel_id=1, source_target_pairs={{0,8},{8,0},{16,24},{24,16},{1,9},{9,1},{17,25},{25,17},{2,10},{10... | collective-permute-start | bytes 884744 | tf_op jit(solution)/shard_map/ppermute | solution.py:618
  19.9 8.9 %copy-start.21 = (bf16[96,768]{1,0:T(8,128)(2,1)}, bf16[96,768]{1,0:T(8,128)(2,1)S(1)}, u32[]{:S(2)}) copy-start(bf16[96,768]{1,0:T(8,128)(2,1)S(1)} %collective-permute-done.8.rest_11_) | copy-start | bytes 442372
  19.9 5.2 %collective-permute-start.2 = (bf16[192,768]{1,0:T(8,128)(2,1)S(1)}, bf16[192,768]{1,0:T(8,128)(2,1)S(1)}, u32[]{:S(2)}, u32[]{:S(2)}) collective-permute-start(bf16[192,768]{1,0:T(8,128)(2,1)S(1)} %copy-done.9), channel_id=1, source_target_pairs={{0,8},{8,0},{16,24},{24,16},{1,9},{9,1},{17,25},{25,17},{2,10},{10... | collective-permute-start | bytes 884744 | tf_op jit(solution)/shard_map/ppermute | solution.py:618
  21.6 7.2 %copy-start.22 = (bf16[96,768]{1,0:T(8,128)(2,1)}, bf16[96,768]{1,0:T(8,128)(2,1)S(1)}, u32[]{:S(2)}) copy-start(bf16[96,768]{1,0:T(8,128)(2,1)S(1)} %collective-permute-done.9.rest_12_) | copy-start | bytes 442372
  21.6 3.6 %collective-permute-start.3 = (bf16[192,768]{1,0:T(8,128)(2,1)S(1)}, bf16[192,768]{1,0:T(8,128)(2,1)S(1)}, u32[]{:S(2)}, u32[]{:S(2)}) collective-permute-start(bf16[192,768]{1,0:T(8,128)(2,1)S(1)} %copy-done.10), channel_id=1, source_target_pairs={{0,8},{8,0},{16,24},{24,16},{1,9},{9,1},{17,25},{25,17},{2,10},{10... | collective-permute-start | bytes 884744 | tf_op jit(solution)/shard_map/ppermute | solution.py:618
  23.1 5.7 %copy-start.23 = (bf16[96,768]{1,0:T(8,128)(2,1)}, bf16[96,768]{1,0:T(8,128)(2,1)S(1)}, u32[]{:S(2)}) copy-start(bf16[96,768]{1,0:T(8,128)(2,1)S(1)} %collective-permute-done.13.rest_16_) | copy-start | bytes 442372
  23.1 1.4 collective-permute-start.12
  24.5 4.3 %copy-start.24 = (bf16[96,768]{1,0:T(8,128)(2,1)}, bf16[96,768]{1,0:T(8,128)(2,1)S(1)}, u32[]{:S(2)}) copy-start(bf16[96,768]{1,0:T(8,128)(2,1)S(1)} %collective-permute-done.12.rest_15_) | copy-start | bytes 442372
  24.5 1.4 collective-permute-start.6
  24.7 4.2 %copy-start.11 = (bf16[192,768]{1,0:T(8,128)(2,1)}, bf16[192,768]{1,0:T(8,128)(2,1)S(1)}, u32[]{:S(2)}) copy-start(bf16[192,768]{1,0:T(8,128)(2,1)S(1)} %collective-permute-done.1.rest_3_) | copy-start | bytes 884740
  24.7 2.7 %collective-permute-start.10 = (bf16[96,768]{1,0:T(8,128)(2,1)S(1)}, bf16[96,768]{1,0:T(8,128)(2,1)S(1)}, u32[]{:S(2)}, u32[]{:S(2)}) collective-permute-start(bf16[96,768]{1,0:T(8,128)(2,1)S(1)} %collective-permute-done.9.rest_12_), channel_id=1, source_target_pairs={{0,8},{8,0},{16,24},{24,16},{1,9},{9,1},{17,25},{25,17},{2,10},{10... | collective-permute-start | bytes 442376 | tf_op jit(solution)/shard_map/ppermute | solution.py:618
  25.0 3.8 %copy-start.12 = (bf16[192,768]{1,0:T(8,128)(2,1)}, bf16[192,768]{1,0:T(8,128)(2,1)S(1)}, u32[]{:S(2)}) copy-start(bf16[192,768]{1,0:T(8,128)(2,1)S(1)} %collective-permute-done.2.rest_4_) | copy-start | bytes 884740
  25.0 3.7 %collective-permute-start.14 = (bf16[96,768]{1,0:T(8,128)(2,1)S(1)}, bf16[96,768]{1,0:T(8,128)(2,1)S(1)}, u32[]{:S(2)}, u32[]{:S(2)}) collective-permute-start(bf16[96,768]{1,0:T(8,128)(2,1)S(1)} %collective-permute-done.13.rest_16_), channel_id=1, source_target_pairs={{0,8},{8,0},{16,24},{24,16},{1,9},{9,1},{17,25},{25,17},{2,10},{10... | collective-permute-start | bytes 442376 | tf_op jit(solution)/shard_map/ppermute | solution.py:618
  25.2 3.6 %copy-start.13 = (bf16[192,768]{1,0:T(8,128)(2,1)}, bf16[192,768]{1,0:T(8,128)(2,1)S(1)}, u32[]{:S(2)}) copy-start(bf16[192,768]{1,0:T(8,128)(2,1)S(1)} %collective-permute-done.3.rest_5_) | copy-start | bytes 884740
  25.2 33.3 %collective-permute-start.16 = (bf16[2,5,96,768]{3,2,1,0:T(8,128)(2,1)}, bf16[2,5,96,768]{3,2,1,0:T(8,128)(2,1)}, u32[]{:S(2)}, u32[]{:S(2)}) collective-permute-start(bf16[2,5,96,768]{3,2,1,0:T(8,128)(2,1)} %get-tuple-element.86), channel_id=1, source_target_pairs={{0,8},{8,0},{16,24},{24,16},{1,9},{9,1},{17,25},{25,17},{2,10},{10... | collective-permute-start | bytes 4423688 | tf_op jit(solution)/shard_map/ppermute | solution.py:618
  25.9 3.0 %copy-start.25 = (bf16[96,768]{1,0:T(8,128)(2,1)}, bf16[96,768]{1,0:T(8,128)(2,1)S(1)}, u32[]{:S(2)}) copy-start(bf16[96,768]{1,0:T(8,128)(2,1)S(1)} %collective-permute-done.6.rest_9_) | copy-start | bytes 442372
  25.9 28.5 %collective-permute-start.18 = (f32[1,2,24,128]{3,2,1,0:T(8,128)S(1)}, f32[1,2,24,128]{3,2,1,0:T(8,128)S(1)}, u32[]{:S(2)}, u32[]{:S(2)}) collective-permute-start(f32[1,2,24,128]{3,2,1,0:T(8,128)S(1)} %pad_maximum_fusion), channel_id=1, source_target_pairs={{0,1},{1,0},{2,3},{3,2},{4,5},{5,4},{6,7},{7,6},{8,9},{9,8},{10,11... | collective-permute-start | bytes 73736 | tf_op jit(solution)/shard_map/ppermute | solution.py:618
  27.4 1.5 %copy-start.26 = (bf16[96,768]{1,0:T(8,128)(2,1)}, bf16[96,768]{1,0:T(8,128)(2,1)S(1)}, u32[]{:S(2)}) copy-start(bf16[96,768]{1,0:T(8,128)(2,1)S(1)} %collective-permute-done.10.rest_13_) | copy-start | bytes 442372
  27.4 28.7 %collective-permute-start.20 = (bf16[768,768]{1,0:T(8,128)(2,1)}, bf16[768,768]{1,0:T(8,128)(2,1)}, u32[]{:S(2)}, u32[]{:S(2)}) collective-permute-start(bf16[768,768]{1,0:T(8,128)(2,1)} %rest_14_.1), channel_id=1, source_target_pairs={{0,16},{8,24},{16,0},{24,8},{1,17},{9,25},{17,1},{25,9},{2,18},{10... | collective-permute-start | bytes 3538952 | tf_op jit(solution)/shard_map/ppermute | solution.py:618
  28.7 0.6 copy-start.27
  42.0 14.6 %collective-permute-start.17 = (bf16[5,96,768]{2,1,0:T(8,128)(2,1)}, bf16[5,96,768]{2,1,0:T(8,128)(2,1)S(1)}, u32[]{:S(2)}, u32[]{:S(2)}) collective-permute-start(bf16[5,96,768]{2,1,0:T(8,128)(2,1)} %gate.2.rest_10_), channel_id=1, source_target_pairs={{0,8},{8,0},{16,24},{24,16},{1,9},{9,1},{17,25},{25,17},{2,10},{10... | collective-permute-start | bytes 2211848 | tf_op jit(solution)/shard_map/ppermute | solution.py:618
  42.1 14.0 %collective-permute-start.19 = (bf16[5,96,768]{2,1,0:T(8,128)(2,1)}, bf16[5,96,768]{2,1,0:T(8,128)(2,1)S(1)}, u32[]{:S(2)}, u32[]{:S(2)}) collective-permute-start(bf16[5,96,768]{2,1,0:T(8,128)(2,1)} %gate.2.rest_10_), channel_id=1, source_target_pairs={{0,1},{1,0},{2,3},{3,2},{4,5},{5,4},{6,7},{7,6},{8,10},{9,11},{10,... | collective-permute-start | bytes 2211848 | tf_op jit(solution)/shard_map/ppermute | solution.py:627
  42.7 11.8 %copy-start.30 = (bf16[768,768]{1,0:T(8,128)(2,1)S(1)}, bf16[768,768]{1,0:T(8,128)(2,1)}, u32[]{:S(2)}) copy-start(bf16[768,768]{1,0:T(8,128)(2,1)} %rest_14_.1) | copy-start | bytes 3538948
  54.4 4.0 %collective-permute-start.22 = (bf16[768,768]{1,0:T(8,128)(2,1)S(1)}, bf16[768,768]{1,0:T(8,128)(2,1)}, u32[]{:S(2)}, u32[]{:S(2)}) collective-permute-start(bf16[768,768]{1,0:T(8,128)(2,1)S(1)} %copy-done.30), channel_id=1, source_target_pairs={{0,8},{8,0},{16,24},{24,16},{1,9},{9,1},{17,25},{25,17},{2,10},{10... | collective-permute-start | bytes 3538952 | tf_op jit(solution)/shard_map/ppermute | solution.py:618
  56.1 2.4 %copy-start.31 = (bf16[5,96,768]{2,1,0:T(8,128)(2,1)}, bf16[5,96,768]{2,1,0:T(8,128)(2,1)S(1)}, u32[]{:S(2)}) copy-start(bf16[5,96,768]{2,1,0:T(8,128)(2,1)S(1)} %collective-permute-done.19.rest_12_) | copy-start | bytes 2211844
  56.1 5.2 %collective-permute-start.23 = (bf16[768,768]{1,0:T(8,128)(2,1)}, bf16[768,768]{1,0:T(8,128)(2,1)}, u32[]{:S(2)}, u32[]{:S(2)}) collective-permute-start(bf16[768,768]{1,0:T(8,128)(2,1)} %collective-permute-done.20.rest_16_), channel_id=1, source_target_pairs={{0,8},{8,0},{16,24},{24,16},{1,9},{9,1},{17,25},{25,17},{2,10},{10... | collective-permute-start | bytes 3538952 | tf_op jit(solution)/shard_map/ppermute | solution.py:618
  56.1 4.3 %collective-permute-start.21 = (bf16[5,96,768]{2,1,0:T(8,128)(2,1)S(1)}, bf16[5,96,768]{2,1,0:T(8,128)(2,1)}, u32[]{:S(2)}, u32[]{:S(2)}) collective-permute-start(bf16[5,96,768]{2,1,0:T(8,128)(2,1)S(1)} %collective-permute-done.19.rest_12_), channel_id=1, source_target_pairs={{0,8},{8,0},{16,24},{24,16},{1,9},{9,1},{17,25},{25,17},{2,10},{10... | collective-permute-start | bytes 2211848 | tf_op jit(solution)/shard_map/ppermute | solution.py:618
  56.6 1.9 %copy-start.32 = (bf16[5,96,768]{2,1,0:T(8,128)(2,1)}, bf16[5,96,768]{2,1,0:T(8,128)(2,1)S(1)}, u32[]{:S(2)}) copy-start(bf16[5,96,768]{2,1,0:T(8,128)(2,1)S(1)} %collective-permute-done.17.value_ref) | copy-start | bytes 2211844
  56.6 38.2 %collective-permute-start.24 = (f32[2,2,24,128]{3,2,1,0:T(8,128)S(1)}, f32[2,2,24,128]{3,2,1,0:T(8,128)S(1)}, u32[]{:S(2)}, u32[]{:S(2)}) collective-permute-start(f32[2,2,24,128]{3,2,1,0:T(8,128)S(1)} %constant_dynamic-update-slice_fusion), channel_id=1, source_target_pairs={{0,2},{1,3},{2,0},{3,1},{4,6},{5,7},{6,4},{7,5},{8,10},{9,11},{10,... | collective-permute-start | bytes 147464 | tf_op jit(solution)/shard_map/ppermute | solution.py:618
  61.3 33.5 %copy-start.2 = (f32[24576]{0:T(1024)S(1)}, f32[24576]{0:T(1024)}, u32[]{:S(2)}) copy-start(f32[24576]{0:T(1024)} %param.39) | copy-start | bytes 294916
  61.3 33.5 %copy-start.3 = (bf16[1024,768]{1,0:T(8,128)(2,1)S(1)}, bf16[1024,768]{1,0:T(8,128)(2,1)}, u32[]{:S(2)}) copy-start(bf16[1024,768]{1,0:T(8,128)(2,1)} %x_ref.7) | copy-start | bytes 4718596
  61.3 33.5 %copy-start.4 = (s32[2,512]{1,0:T(2,128)S(1)}, s32[2,512]{1,0:T(2,128)}, u32[]{:S(2)}) copy-start(s32[2,512]{1,0:T(2,128)} %seg_ref.5) | copy-start | bytes 12292
  61.3 33.5 %copy-start.5 = (bf16[1024,768]{1,0:T(8,128)(2,1)S(1)}, bf16[1024,768]{1,0:T(8,128)(2,1)}, u32[]{:S(2)}) copy-start(bf16[1024,768]{1,0:T(8,128)(2,1)} %get-tuple-element.97.rest_0_) | copy-start | bytes 4718596
  61.3 33.5 %copy-start.6 = (bf16[1024,768]{1,0:T(8,128)(2,1)S(1)}, bf16[1024,768]{1,0:T(8,128)(2,1)}, u32[]{:S(2)}) copy-start(bf16[1024,768]{1,0:T(8,128)(2,1)} %get-tuple-element.98.rest_1_) | copy-start | bytes 4718596
  61.3 33.5 %copy-start.7 = (bf16[1024,16]{1,0:T(8,128)(2,1)S(1)}, bf16[1024,16]{1,0:T(8,128)(2,1)}, u32[]{:S(2)}) copy-start(bf16[1024,16]{1,0:T(8,128)(2,1)} %get-tuple-element.91.other_ref.down_ref) | copy-start | bytes 98308
  94.8 27.2 %copy-start = (bf16[3,768,768]{2,1,0:T(8,128)(2,1)S(1)}, bf16[3,768,768]{2,1,0:T(8,128)(2,1)}, u32[]{:S(2)}) copy-start(bf16[3,768,768]{2,1,0:T(8,128)(2,1)} %get-tuple-element.78.rest_0_.other_ref.weights) | copy-start | bytes 10616836
  94.8 27.2 %copy-start.1 = (bf16[1024,768]{1,0:T(8,128)(2,1)S(1)}, bf16[1024,768]{1,0:T(8,128)(2,1)}, u32[]{:S(2)}) copy-start(bf16[1024,768]{1,0:T(8,128)(2,1)} %get-tuple-element.121.dh_ref) | copy-start | bytes 4718596
  118.3 3.1 %collective-permute-start.25 = (bf16[32,768]{1,0:T(8,128)(2,1)S(1)}, bf16[32,768]{1,0:T(8,128)(2,1)S(1)}, u32[]{:S(2)}, u32[]{:S(2)}) collective-permute-start(bf16[32,768]{1,0:T(8,128)(2,1)S(1)} %get-tuple-element.105), channel_id=1, source_target_pairs={{0,8},{8,0},{16,24},{24,16},{1,9},{9,1},{17,25},{25,17},{2,10},{10... | collective-permute-start | bytes 147464 | tf_op jit(solution)/shard_map/ppermute | solution.py:618
  118.8 5.2 %copy-start.14 = (f32[4,2,24,128]{3,2,1,0:T(8,128)}, f32[4,2,24,128]{3,2,1,0:T(8,128)S(1)}, u32[]{:S(2)}) copy-start(f32[4,2,24,128]{3,2,1,0:T(8,128)S(1)} %constant_dynamic-update-slice_fusion.2.held_ref) | copy-start | bytes 294916
  118.8 18.0 %collective-permute-start.30 = (f32[4,2,24,128]{3,2,1,0:T(8,128)S(1)}, f32[4,2,24,128]{3,2,1,0:T(8,128)S(1)}, u32[]{:S(2)}, u32[]{:S(2)}) collective-permute-start(f32[4,2,24,128]{3,2,1,0:T(8,128)S(1)} %constant_dynamic-update-slice_fusion.2.held_ref), channel_id=1, source_target_pairs={{0,4},{1,5},{2,6},{3,7},{4,0},{5,1},{6,2},{7,3},{8,12},{9,13},{10,... | collective-permute-start | bytes 294920 | tf_op jit(solution)/shard_map/ppermute | solution.py:618
  121.5 4.2 %collective-permute-start.26 = (bf16[32,768]{1,0:T(8,128)(2,1)S(1)}, bf16[32,768]{1,0:T(8,128)(2,1)S(1)}, u32[]{:S(2)}, u32[]{:S(2)}) collective-permute-start(bf16[32,768]{1,0:T(8,128)(2,1)S(1)} %add.18), channel_id=1, source_target_pairs={{0,16},{8,24},{16,0},{24,8},{1,17},{9,25},{17,1},{25,9},{2,18},{10... | collective-permute-start | bytes 147464 | tf_op jit(solution)/shard_map/ppermute | solution.py:618
  125.7 4.2 %collective-permute-start.27 = (bf16[32,768]{1,0:T(8,128)(2,1)S(1)}, bf16[32,768]{1,0:T(8,128)(2,1)S(1)}, u32[]{:S(2)}, u32[]{:S(2)}) collective-permute-start(bf16[32,768]{1,0:T(8,128)(2,1)S(1)} %add.19), channel_id=1, source_target_pairs={{0,1},{1,0},{2,3},{3,2},{4,5},{5,4},{6,7},{7,6},{8,9},{9,8},{10,11... | collective-permute-start | bytes 147464 | tf_op jit(solution)/shard_map/ppermute | solution.py:618
  129.8 4.2 %collective-permute-start.28 = (bf16[32,768]{1,0:T(8,128)(2,1)S(1)}, bf16[32,768]{1,0:T(8,128)(2,1)S(1)}, u32[]{:S(2)}, u32[]{:S(2)}) collective-permute-start(bf16[32,768]{1,0:T(8,128)(2,1)S(1)} %add.20), channel_id=1, source_target_pairs={{0,2},{1,3},{2,0},{3,1},{4,6},{5,7},{6,4},{7,5},{8,10},{9,11},{10,... | collective-permute-start | bytes 147464 | tf_op jit(solution)/shard_map/ppermute | solution.py:618
  134.0 2.8 %copy-start.15 = (bf16[32,768]{1,0:T(8,128)(2,1)}, bf16[32,768]{1,0:T(8,128)(2,1)S(1)}, u32[]{:S(2)}) copy-start(bf16[32,768]{1,0:T(8,128)(2,1)S(1)} %add.21.near_ref) | copy-start | bytes 147460
  134.0 5.6 %collective-permute-start.29 = (bf16[32,768]{1,0:T(8,128)(2,1)S(1)}, bf16[32,768]{1,0:T(8,128)(2,1)S(1)}, u32[]{:S(2)}, u32[]{:S(2)}) collective-permute-start(bf16[32,768]{1,0:T(8,128)(2,1)S(1)} %add.21.near_ref), channel_id=1, source_target_pairs={{0,4},{1,5},{2,6},{3,7},{4,0},{5,1},{6,2},{7,3},{8,12},{9,13},{10,... | collective-permute-start | bytes 147464 | tf_op jit(solution)/shard_map/ppermute | solution.py:618
  136.8 2.8 %copy-start.28 = (f32[4,2,24,128]{3,2,1,0:T(8,128)}, f32[4,2,24,128]{3,2,1,0:T(8,128)S(1)}, u32[]{:S(2)}) copy-start(f32[4,2,24,128]{3,2,1,0:T(8,128)S(1)} %collective-permute-done.30.other_ref) | copy-start | bytes 294916
  139.6 0.6 copy-start.29

commit v5 on v4

--- a/solution.py
+++ b/solution.py
@@ -25,6 +25,8 @@
 ANY = pl.BlockSpec(memory_space=pl.ANY)
 HBM = pl.BlockSpec(memory_space=pltpu.HBM)
 VMEM_LIMIT = 56 * 2**20
+LATE = 6 * 10**9
+SMALL_VMEM = 8 * 2**20
 INPUT_VMEM = 24 * 2**20
 BACK_VMEM = 44 * 2**20
 DENSE_VMEM = 56 * 2**20
@@ -298,7 +300,7 @@
         scratch_shapes=scratch,
         compiler_params=pltpu.CompilerParams(vmem_limit_bytes=ATTEND_VMEM),
         cost_estimate=pl.CostEstimate(
-            flops=1 if carry == () else 10**10, bytes_accessed=1, transcendentals=0
+            flops=1 if carry == () else LATE, bytes_accessed=1, transcendentals=0
         ),
         name="project_and_attend",
     )(rank, place, seg, x, factors, bq, bv, *operands)
@@ -606,6 +608,7 @@
         out_shape=[piece, like(factors.shape), piece, piece],
         scratch_shapes=[pltpu.VMEM((owners * length, lanes), F32)]
         + [pltpu.VMEM(factors.shape, F32)] * 3,
+        compiler_params=pltpu.CompilerParams(vmem_limit_bytes=SMALL_VMEM),
         name="adapter_update",
     )(place, near, far, factors, held, other)
 

time: 143 us -> 139 us (0.972)
  waiting for transfers between devices: 17 us -> 12.2 us
  starting transfers between devices: 25.5 us -> 28.8 us
    ppermute x27, waiting for transfers between devices: 12.9 us -> 8.14 us  [swap(): return lax.ppermute(value, axis, [(i, i ^ flip) for i in range(size)])]
    ppermute x27, starting transfers between devices: 21.4 us -> 23.6 us  [swap(): return lax.ppermute(value, axis, [(i, i ^ flip) for i in range(size)])]
  transfers between devices with their start and end apart: 31 -> 31, of which waited for: 13 -> 11; matrix products, arithmetic and copies ran while one was open for 2% -> 2% of each run, Pallas kernels for 48% -> 49%
where the time goes in v5:
time: 139 us
  Pallas kernels  92.7 us (67%)
  starting transfers between devices  28.8 us (21%)
  waiting for transfers between devices  12.2 us (9%)
  local copies, waits for them, and re-layouts  3.58 us (3%)
    pallas_call x1, Pallas kernels, dense(): pl.pallas_call(functools.partial(dense_kernel, first, second, cut), grid=...  33.5 us
    pallas_call x2, Pallas kernels, attend(): pl.pallas_call(functools.partial(attend_kernel, parts, first), grid=(coun...  24.2 us
    ppermute x27, starting transfers between devices, swap(): return lax.ppermute(value, axis, [(i, i ^ flip) for i in range(size)])  23.6 us
    pallas_call x1, Pallas kernels, attend_back(): pl.pallas_call(attend_back_kernel, grid=(packs, width // cut), in_specs=[...  23.5 us
    ppermute x27, waiting for transfers between devices, swap(): return lax.ppermute(value, axis, [(i, i ^ flip) for i in range(size)])  8.14 us
    pallas_call x4, Pallas kernels, input_back(): pl.pallas_call(functools.partial(input_kernel, at * size), grid=(1,), in_...  7.67 us
    ppermute x4, starting transfers between devices, cross(): return lax.ppermute(value, ('rep', 'wide'), pairs)  5.15 us
    ppermute x4, waiting for transfers between devices, cross(): return lax.ppermute(value, ('rep', 'wide'), pairs)  4.1 us
  transfers between devices with their start and end apart: 31, of which 11 were waited for; matrix products, arithmetic and copies ran while one was open for 2% of the time, Pallas kernels for 49%

profile of v5, /device:TPU:0, one launch (start us, length us, event | category | flops | bytes accessed | tf_op | source)
XLA Modules:
  0.0 139.2 jit_solution(16748169574052432426)
XLA Ops:
  0.6 0.0 copy-start.8
  0.6 0.0 copy-start.10
  0.7 0.0 copy-start.9
  0.7 1.0 constant_dynamic-slice_fusion.2
  1.7 3.0 %collective-permute-start = (bf16[96,768]{1,0:T(8,128)(2,1)S(1)}, bf16[96,768]{1,0:T(8,128)(2,1)S(1)}, u32[]{:S(2)}, u32[]{:S(2)}) collective-permute-start(bf16[96,768]{1,0:T(8,128)(2,1)S(1)} %constant_dynamic-slice_fusion.2), channel_id=1, source_target_pairs={{0,16},{8,24},{16,0},{24,8},{1,17},{9,25},{17,1},{25,9},{2,18},{10... | collective-permute-start | bytes 442376 | tf_op jit(solution)/shard_map/ppermute | solution.py:621
  4.7 0.9 constant_dynamic-slice_fusion
  5.6 0.1 collective-permute-start.11
  5.7 0.9 constant_dynamic-slice_fusion.1
  6.6 2.1 %collective-permute-start.7 = (bf16[96,768]{1,0:T(8,128)(2,1)S(1)}, bf16[96,768]{1,0:T(8,128)(2,1)S(1)}, u32[]{:S(2)}, u32[]{:S(2)}) collective-permute-start(bf16[96,768]{1,0:T(8,128)(2,1)S(1)} %constant_dynamic-slice_fusion.1), channel_id=1, source_target_pairs={{0,16},{8,24},{16,0},{24,8},{1,17},{9,25},{17,1},{25,9},{2,18},{10... | collective-permute-start | bytes 442376 | tf_op jit(solution)/shard_map/ppermute | solution.py:621
  8.7 0.7 pad_maximum_fusion
  9.4 2.9 %pack_shards.1 = (bf16[2,5,96,768]{3,2,1,0:T(8,128)(2,1)}, bf16[5,96,768]{2,1,0:T(8,128)(2,1)}) custom-call(s32[1]{0:T(128)} %bitcast.1.place_ref, bf16[192,768]{1,0:T(8,128)(2,1)} %rest_7_.1, bf16[192,3072]{1,0:T(8,128)(2,1)} %rest_8_.1), custom_call_target="tpu_custom_call" | custom-call | tf_op jit(solution)/shard_map/pack_shards/pallas_call | solution.py:169
  12.3 0.1 collective-permute-done.11.rest_14_
  12.5 2.1 %collective-permute-start.15 = (bf16[5,96,768]{2,1,0:T(8,128)(2,1)}, bf16[5,96,768]{2,1,0:T(8,128)(2,1)}, u32[]{:S(2)}, u32[]{:S(2)}) collective-permute-start(bf16[5,96,768]{2,1,0:T(8,128)(2,1)} %get-tuple-element.77), channel_id=1, source_target_pairs={{0,16},{8,24},{16,0},{24,8},{1,17},{9,25},{17,1},{25,9},{2,18},{10... | collective-permute-start | bytes 2211848 | tf_op jit(solution)/shard_map/ppermute | solution.py:621
  14.6 0.0 collective-permute-done.rest_6_
  14.6 0.0 collective-permute-start.4
  14.6 1.6 %collective-permute-start.5 = (bf16[96,768]{1,0:T(8,128)(2,1)S(1)}, bf16[96,768]{1,0:T(8,128)(2,1)S(1)}, u32[]{:S(2)}, u32[]{:S(2)}) collective-permute-start(bf16[96,768]{1,0:T(8,128)(2,1)S(1)} %collective-permute-done.rest_6_), channel_id=1, source_target_pairs={{0,1},{1,0},{2,3},{3,2},{4,5},{5,4},{6,7},{7,6},{8,10},{9,11},{10,... | collective-permute-start | bytes 442376 | tf_op jit(solution)/shard_map/ppermute | solution.py:630
  16.2 0.2 collective-permute-start.8
  16.4 1.5 %collective-permute-start.9 = (bf16[96,768]{1,0:T(8,128)(2,1)S(1)}, bf16[96,768]{1,0:T(8,128)(2,1)S(1)}, u32[]{:S(2)}, u32[]{:S(2)}) collective-permute-start(bf16[96,768]{1,0:T(8,128)(2,1)S(1)} %collective-permute-done.7.rest_10_), channel_id=1, source_target_pairs={{0,1},{1,0},{2,3},{3,2},{4,5},{5,4},{6,7},{7,6},{8,10},{9,11},{10,... | collective-permute-start | bytes 442376 | tf_op jit(solution)/shard_map/ppermute | solution.py:630
  17.9 0.5 collective-permute-start.13
  18.5 1.4 collective-permute-done.5.rest_8_
  19.8 0.0 collective-permute-done.8.rest_11_
  19.9 0.5 collective-permute-start.2
  20.4 1.2 collective-permute-done.9.rest_12_
  21.6 0.0 collective-permute-start.12
  21.6 1.6 %collective-permute-done.13.rest_16_ = bf16[96,768]{1,0:T(8,128)(2,1)S(1)} collective-permute-done((bf16[96,768]{1,0:T(8,128)(2,1)S(1)}, bf16[96,768]{1,0:T(8,128)(2,1)S(1)}, u32[]{:S(2)}, u32[]{:S(2)}) %collective-permute-start.13) | collective-permute-done | bytes 147488 | tf_op jit(solution)/shard_map/ppermute | solution.py:630
  23.2 0.5 collective-permute-start.6
  23.7 0.1 collective-permute-start.10
  23.8 0.4 collective-permute-start.14
  24.2 0.5 collective-permute-done.3.rest_5_
  24.7 1.3 collective-permute-start.20
  26.2 0.5 copy-done.23
  26.8 0.1 copy-done.24
  26.8 0.0 copy-done.25
  26.9 12.6 %project_and_attend.2 = (bf16[1024,768]{1,0:T(8,128)(2,1)}, bf16[1024,768]{1,0:T(8,128)(2,1)}, bf16[1024,768]{1,0:T(8,128)(2,1)}, bf16[1024,768]{1,0:T(8,128)(2,...) custom-call(s32[1]{0:T(128)} %bitcast.rank_ref, s32[1]{0:T(128)} %bitcast.1.place_ref, ...), custom_call_target="tpu_custom_call" | custom-call | flops 1 | bytes 1 | tf_op jit(solution)/shard_map/project_and_attend/pallas_call | solution.py:284
  39.4 0.0 copy-start.26
  39.5 1.6 %collective-permute-start.19 = (bf16[5,96,768]{2,1,0:T(8,128)(2,1)}, bf16[5,96,768]{2,1,0:T(8,128)(2,1)}, u32[]{:S(2)}, u32[]{:S(2)}) collective-permute-start(bf16[5,96,768]{2,1,0:T(8,128)(2,1)} %gate.2.rest_10_), channel_id=1, source_target_pairs={{0,1},{1,0},{2,3},{3,2},{4,5},{5,4},{6,7},{7,6},{8,10},{9,11},{10,... | collective-permute-start | bytes 2211848 | tf_op jit(solution)/shard_map/ppermute | solution.py:630
  41.0 1.3 collective-permute-start.18
  42.3 0.2 collective-permute-start.17
  42.5 11.6 %project_and_attend.3 = (bf16[1024,768]{1,0:T(8,128)(2,1)}, bf16[1024,768]{1,0:T(8,128)(2,1)}, bf16[1024,768]{1,0:T(8,128)(2,1)}, bf16[1024,768]{1,0:T(8,128)(2,...) custom-call(s32[1]{0:T(128)} %bitcast.rank_ref, ...), custom_call_target="tpu_custom_call", output_to_operand_aliasing={{0}: (8, {}), {1}: (9, {}), {2}: (10, {}), {3}: (11, {}), {... | custom-call | flops 6000000000 | bytes 1 | tf_op jit(solution)/shard_map/project_and_attend/pallas_call | solution.py:284
  54.1 0.3 collective-permute-start.22
  54.5 1.6 %collective-permute-done.20.rest_16_ = bf16[768,768]{1,0:T(8,128)(2,1)} collective-permute-done((bf16[768,768]{1,0:T(8,128)(2,1)}, bf16[768,768]{1,0:T(8,128)(2,1)}, u32[]{:S(2)}, u32[]{:S(2)}) %collective-permute-start.20) | collective-permute-done | bytes 1179680 | tf_op jit(solution)/shard_map/ppermute | solution.py:621
  56.1 0.5 collective-permute-start.21
  56.6 1.9 %collective-permute-start.24 = (f32[2,2,24,128]{3,2,1,0:T(8,128)S(1)}, f32[2,2,24,128]{3,2,1,0:T(8,128)S(1)}, u32[]{:S(2)}, u32[]{:S(2)}) collective-permute-start(f32[2,2,24,128]{3,2,1,0:T(8,128)S(1)} %constant_dynamic-update-slice_fusion), channel_id=1, source_target_pairs={{0,2},{1,3},{2,0},{3,1},{4,6},{5,7},{6,4},{7,5},{8,10},{9,11},{10,... | collective-permute-start | bytes 147464 | tf_op jit(solution)/shard_map/ppermute | solution.py:621
  58.5 1.8 %collective-permute-done.21.rest_13_ = bf16[5,96,768]{2,1,0:T(8,128)(2,1)} collective-permute-done((bf16[5,96,768]{2,1,0:T(8,128)(2,1)}, bf16[5,96,768]{2,1,0:T(8,128)(2,1)}, u32[]{:S(2)}, u32[]{:S(2)}) %collective-permute-start.21) | collective-permute-done | bytes 737312 | tf_op jit(solution)/shard_map/ppermute | solution.py:621
  60.3 0.0 copy-start.3
  60.3 0.0 copy-start.4
  60.3 0.0 copy-start.5
  60.4 33.5 %dense_both_ways.1 = (bf16[1024,768]{1,0:T(8,128)(2,1)}, bf16[1024,768]{1,0:T(8,128)(2,1)}, bf16[1024,768]{1,0:T(8,128)(2,1)}) custom-call(s32[1]{0:T(128)} %bitcast.rank_ref, s32[1]{0:T(128)} %bitcast.1.place_ref, bf16[1024,768]{1,0:T(8,128)(2,1)} %x_ref.7, bf16[1024,768]{1,0:T(8,128)(2,1)} %get-tuple-element.85.ctx_ref.rest_4_, bf16[1024,768]{1,0:T(8,128)(2,1)} %cot_ref.1, ...), custom_call_target="tpu_custom_call" | custom-call | flops 21743271936 | bytes 18874368 | tf_op jit(solution)/shard_map/dense_both_ways/pallas_call | solution.py:385
  94.0 23.5 %attend_back.1 = (bf16[1024,768]{1,0:T(8,128)(2,1)S(1)}, bf16[1024,768]{1,0:T(8,128)(2,1)S(1)}, bf16[1024,768]{1,0:T(8,128)(2,1)S(1)}, bf16[1024,16]{1,0:T(8,128)(2,1)S(1)}, bf16[32,768]{1,0:T(8,128)(2,1)S(1)}) custom-call(s32[2,512]{1,0:T(2,128)S(1)} %copy-done.4, bf16[1024,768]{1,0:T(8,128)(2,1)S(1)} %copy-done.3, f32[192,128]{1,0:T(8,128)S(1)} %bitcast.12, ...), custom_call_target="tpu_custom_call" | custom-call | flops 12079595520 | bytes 18874368 | tf_op jit(solution)/shard_map/attend_back/pallas_call | solution.py:498
  117.5 0.2 collective-permute-start.25
  117.7 2.9 %collective-permute-start.30 = (f32[4,2,24,128]{3,2,1,0:T(8,128)S(1)}, f32[4,2,24,128]{3,2,1,0:T(8,128)S(1)}, u32[]{:S(2)}, u32[]{:S(2)}) collective-permute-start(f32[4,2,24,128]{3,2,1,0:T(8,128)S(1)} %constant_dynamic-update-slice_fusion.2.held_ref), channel_id=1, source_target_pairs={{0,4},{1,5},{2,6},{3,7},{4,0},{5,1},{6,2},{7,3},{8,12},{9,13},{10,... | collective-permute-start | bytes 294920 | tf_op jit(solution)/shard_map/ppermute | solution.py:621
  120.6 1.6 %collective-permute-start.26 = (bf16[32,768]{1,0:T(8,128)(2,1)S(1)}, bf16[32,768]{1,0:T(8,128)(2,1)S(1)}, u32[]{:S(2)}, u32[]{:S(2)}) collective-permute-start(bf16[32,768]{1,0:T(8,128)(2,1)S(1)} %add.18), channel_id=1, source_target_pairs={{0,16},{8,24},{16,0},{24,8},{1,17},{9,25},{17,1},{25,9},{2,18},{10... | collective-permute-start | bytes 147464 | tf_op jit(solution)/shard_map/ppermute | solution.py:621
  122.2 1.9 %input_gradient.4.rest_0_ = bf16[1024,768]{1,0:T(8,128)(2,1)} custom-call(bf16[1024,768]{1,0:T(8,128)(2,1)S(1)} %copy-done.1, bf16[1024,768]{1,0:T(8,128)(2,1)S(1)} %get-tuple-element.108.dq_ref, bf16[1024,768]{1,0:T(8,128)(2,1)S(1)} %get-tuple-element.109.dk_ref, bf16[1024,768]{1,0:T(8,128)(2,1)S(1)} %get-tuple-element.110.dv_ref, ...), custom_call_target="tpu_custom_call" | custom-call | flops 905969664 | bytes 1966080 | tf_op jit(solution)/shard_map/input_gradient/pallas_call | solution.py:548
  124.1 0.6 collective-permute-done.26
  124.8 1.6 %collective-permute-start.27 = (bf16[32,768]{1,0:T(8,128)(2,1)S(1)}, bf16[32,768]{1,0:T(8,128)(2,1)S(1)}, u32[]{:S(2)}, u32[]{:S(2)}) collective-permute-start(bf16[32,768]{1,0:T(8,128)(2,1)S(1)} %add.19), channel_id=1, source_target_pairs={{0,1},{1,0},{2,3},{3,2},{4,5},{5,4},{6,7},{7,6},{8,9},{9,8},{10,11... | collective-permute-start | bytes 147464 | tf_op jit(solution)/shard_map/ppermute | solution.py:621
  126.3 1.9 %input_gradient.5.rest_0_ = bf16[1024,768]{1,0:T(8,128)(2,1)} custom-call(bf16[1024,768]{1,0:T(8,128)(2,1)S(1)} %copy-done.1, bf16[1024,768]{1,0:T(8,128)(2,1)S(1)} %get-tuple-element.108.dq_ref, bf16[1024,768]{1,0:T(8,128)(2,1)S(1)} %get-tuple-element.109.dk_ref, bf16[1024,768]{1,0:T(8,128)(2,1)S(1)} %get-tuple-element.110.dv_ref, ...), custom_call_target="tpu_custom_call", output_to_operand_aliasing={{}: (7, {})} | custom-call | flops 905969664 | bytes 1966080 | tf_op jit(solution)/shard_map/input_gradient/pallas_call | solution.py:548
  128.2 0.7 collective-permute-done.27
  128.9 1.6 %collective-permute-start.28 = (bf16[32,768]{1,0:T(8,128)(2,1)S(1)}, bf16[32,768]{1,0:T(8,128)(2,1)S(1)}, u32[]{:S(2)}, u32[]{:S(2)}) collective-permute-start(bf16[32,768]{1,0:T(8,128)(2,1)S(1)} %add.20), channel_id=1, source_target_pairs={{0,2},{1,3},{2,0},{3,1},{4,6},{5,7},{6,4},{7,5},{8,10},{9,11},{10,... | collective-permute-start | bytes 147464 | tf_op jit(solution)/shard_map/ppermute | solution.py:621
  130.6 1.9 %input_gradient.6.rest_0_ = bf16[1024,768]{1,0:T(8,128)(2,1)} custom-call(bf16[1024,768]{1,0:T(8,128)(2,1)S(1)} %copy-done.1, bf16[1024,768]{1,0:T(8,128)(2,1)S(1)} %get-tuple-element.108.dq_ref, bf16[1024,768]{1,0:T(8,128)(2,1)S(1)} %get-tuple-element.109.dk_ref, bf16[1024,768]{1,0:T(8,128)(2,1)S(1)} %get-tuple-element.110.dv_ref, ...), custom_call_target="tpu_custom_call", output_to_operand_aliasing={{}: (7, {})} | custom-call | flops 905969664 | bytes 1966080 | tf_op jit(solution)/shard_map/input_gradient/pallas_call | solution.py:548
  132.5 0.6 collective-permute-done.28
  133.1 1.1 collective-permute-start.29
  134.2 1.9 %input_gradient.7 = bf16[1024,768]{1,0:T(8,128)(2,1)} custom-call(bf16[1024,768]{1,0:T(8,128)(2,1)S(1)} %copy-done.1, bf16[1024,768]{1,0:T(8,128)(2,1)S(1)} %get-tuple-element.108.dq_ref, bf16[1024,768]{1,0:T(8,128)(2,1)S(1)} %get-tuple-element.109.dk_ref, bf16[1024,768]{1,0:T(8,128)(2,1)S(1)} %get-tuple-element.110.dv_ref, ...), custom_call_target="tpu_custom_call", output_to_operand_aliasing={{}: (7, {})} | custom-call | flops 905969664 | bytes 1966080 | tf_op jit(solution)/shard_map/input_gradient/pallas_call | solution.py:548
  136.1 2.1 %collective-permute-done.29.far_ref = bf16[32,768]{1,0:T(8,128)(2,1)S(1)} collective-permute-done((bf16[32,768]{1,0:T(8,128)(2,1)S(1)}, bf16[32,768]{1,0:T(8,128)(2,1)S(1)}, u32[]{:S(2)}, u32[]{:S(2)}) %collective-permute-start.29) | collective-permute-done | bytes 49184 | tf_op jit(solution)/shard_map/ppermute | solution.py:621
  138.2 1.0 adapter_update.1
  (78 shorter events, 0.2 us)
Async XLA Ops:
  0.6 19.2 %copy-start.8 = (bf16[192,768]{1,0:T(8,128)(2,1)S(1)}, bf16[192,768]{1,0:T(8,128)(2,1)}, u32[]{:S(2)}) copy-start(bf16[192,768]{1,0:T(8,128)(2,1)} %rest_0_.4) | copy-start | bytes 884740
  0.6 22.5 %copy-start.10 = (bf16[192,768]{1,0:T(8,128)(2,1)S(1)}, bf16[192,768]{1,0:T(8,128)(2,1)}, u32[]{:S(2)}) copy-start(bf16[192,768]{1,0:T(8,128)(2,1)} %rest_2_.2) | copy-start | bytes 884740
  0.7 19.2 %copy-start.9 = (bf16[192,768]{1,0:T(8,128)(2,1)S(1)}, bf16[192,768]{1,0:T(8,128)(2,1)}, u32[]{:S(2)}) copy-start(bf16[192,768]{1,0:T(8,128)(2,1)} %rest_1_.4) | copy-start | bytes 884740
  1.7 12.9 %collective-permute-start = (bf16[96,768]{1,0:T(8,128)(2,1)S(1)}, bf16[96,768]{1,0:T(8,128)(2,1)S(1)}, u32[]{:S(2)}, u32[]{:S(2)}) collective-permute-start(bf16[96,768]{1,0:T(8,128)(2,1)S(1)} %constant_dynamic-slice_fusion.2), channel_id=1, source_target_pairs={{0,16},{8,24},{16,0},{24,8},{1,17},{9,25},{17,1},{25,9},{2,18},{10... | collective-permute-start | bytes 442376 | tf_op jit(solution)/shard_map/ppermute | solution.py:621
  5.6 6.8 %collective-permute-start.11 = (bf16[96,768]{1,0:T(8,128)(2,1)S(1)}, bf16[96,768]{1,0:T(8,128)(2,1)S(1)}, u32[]{:S(2)}, u32[]{:S(2)}) collective-permute-start(bf16[96,768]{1,0:T(8,128)(2,1)S(1)} %constant_dynamic-slice_fusion), channel_id=1, source_target_pairs={{0,16},{8,24},{16,0},{24,8},{1,17},{9,25},{17,1},{25,9},{2,18},{10... | collective-permute-start | bytes 442376 | tf_op jit(solution)/shard_map/ppermute | solution.py:621
  6.6 9.5 %collective-permute-start.7 = (bf16[96,768]{1,0:T(8,128)(2,1)S(1)}, bf16[96,768]{1,0:T(8,128)(2,1)S(1)}, u32[]{:S(2)}, u32[]{:S(2)}) collective-permute-start(bf16[96,768]{1,0:T(8,128)(2,1)S(1)} %constant_dynamic-slice_fusion.1), channel_id=1, source_target_pairs={{0,16},{8,24},{16,0},{24,8},{1,17},{9,25},{17,1},{25,9},{2,18},{10... | collective-permute-start | bytes 442376 | tf_op jit(solution)/shard_map/ppermute | solution.py:621
  12.5 13.7 %copy-start.15 = (bf16[96,768]{1,0:T(8,128)(2,1)}, bf16[96,768]{1,0:T(8,128)(2,1)S(1)}, u32[]{:S(2)}) copy-start(bf16[96,768]{1,0:T(8,128)(2,1)S(1)} %collective-permute-done.11.rest_14_) | copy-start | bytes 442372
  12.5 27.0 %collective-permute-start.15 = (bf16[5,96,768]{2,1,0:T(8,128)(2,1)}, bf16[5,96,768]{2,1,0:T(8,128)(2,1)}, u32[]{:S(2)}, u32[]{:S(2)}) collective-permute-start(bf16[5,96,768]{2,1,0:T(8,128)(2,1)} %get-tuple-element.77), channel_id=1, source_target_pairs={{0,16},{8,24},{16,0},{24,8},{1,17},{9,25},{17,1},{25,9},{2,18},{10... | collective-permute-start | bytes 2211848 | tf_op jit(solution)/shard_map/ppermute | solution.py:621
  14.6 11.5 %copy-start.14 = (bf16[96,768]{1,0:T(8,128)(2,1)}, bf16[96,768]{1,0:T(8,128)(2,1)S(1)}, u32[]{:S(2)}) copy-start(bf16[96,768]{1,0:T(8,128)(2,1)S(1)} %collective-permute-done.rest_6_) | copy-start | bytes 442372
  14.6 3.3 %collective-permute-start.4 = (bf16[96,768]{1,0:T(8,128)(2,1)S(1)}, bf16[96,768]{1,0:T(8,128)(2,1)S(1)}, u32[]{:S(2)}, u32[]{:S(2)}) collective-permute-start(bf16[96,768]{1,0:T(8,128)(2,1)S(1)} %collective-permute-done.rest_6_), channel_id=1, source_target_pairs={{0,8},{8,0},{16,24},{24,16},{1,9},{9,1},{17,25},{25,17},{2,10},{10... | collective-permute-start | bytes 442376 | tf_op jit(solution)/shard_map/ppermute | solution.py:621
  14.6 5.2 %collective-permute-start.5 = (bf16[96,768]{1,0:T(8,128)(2,1)S(1)}, bf16[96,768]{1,0:T(8,128)(2,1)S(1)}, u32[]{:S(2)}, u32[]{:S(2)}) collective-permute-start(bf16[96,768]{1,0:T(8,128)(2,1)S(1)} %collective-permute-done.rest_6_), channel_id=1, source_target_pairs={{0,1},{1,0},{2,3},{3,2},{4,5},{5,4},{6,7},{7,6},{8,10},{9,11},{10,... | collective-permute-start | bytes 442376 | tf_op jit(solution)/shard_map/ppermute | solution.py:630
  16.2 10.0 %copy-start.16 = (bf16[96,768]{1,0:T(8,128)(2,1)}, bf16[96,768]{1,0:T(8,128)(2,1)S(1)}, u32[]{:S(2)}) copy-start(bf16[96,768]{1,0:T(8,128)(2,1)S(1)} %collective-permute-done.7.rest_10_) | copy-start | bytes 442372
  16.2 3.7 %collective-permute-start.8 = (bf16[96,768]{1,0:T(8,128)(2,1)S(1)}, bf16[96,768]{1,0:T(8,128)(2,1)S(1)}, u32[]{:S(2)}, u32[]{:S(2)}) collective-permute-start(bf16[96,768]{1,0:T(8,128)(2,1)S(1)} %collective-permute-done.7.rest_10_), channel_id=1, source_target_pairs={{0,8},{8,0},{16,24},{24,16},{1,9},{9,1},{17,25},{25,17},{2,10},{10... | collective-permute-start | bytes 442376 | tf_op jit(solution)/shard_map/ppermute | solution.py:621
  16.4 5.1 %collective-permute-start.9 = (bf16[96,768]{1,0:T(8,128)(2,1)S(1)}, bf16[96,768]{1,0:T(8,128)(2,1)S(1)}, u32[]{:S(2)}, u32[]{:S(2)}) collective-permute-start(bf16[96,768]{1,0:T(8,128)(2,1)S(1)} %collective-permute-done.7.rest_10_), channel_id=1, source_target_pairs={{0,1},{1,0},{2,3},{3,2},{4,5},{5,4},{6,7},{7,6},{8,10},{9,11},{10,... | collective-permute-start | bytes 442376 | tf_op jit(solution)/shard_map/ppermute | solution.py:630
  17.9 8.2 %copy-start.17 = (bf16[96,768]{1,0:T(8,128)(2,1)}, bf16[96,768]{1,0:T(8,128)(2,1)S(1)}, u32[]{:S(2)}) copy-start(bf16[96,768]{1,0:T(8,128)(2,1)S(1)} %collective-permute-done.4.rest_7_) | copy-start | bytes 442372
  17.9 5.2 %collective-permute-start.13 = (bf16[96,768]{1,0:T(8,128)(2,1)S(1)}, bf16[96,768]{1,0:T(8,128)(2,1)S(1)}, u32[]{:S(2)}, u32[]{:S(2)}) collective-permute-start(bf16[96,768]{1,0:T(8,128)(2,1)S(1)} %collective-permute-done.11.rest_14_), channel_id=1, source_target_pairs={{0,1},{1,0},{2,3},{3,2},{4,5},{5,4},{6,7},{7,6},{8,10},{9,11},{10,... | collective-permute-start | bytes 442376 | tf_op jit(solution)/shard_map/ppermute | solution.py:630
  19.8 6.3 %copy-start.18 = (bf16[96,768]{1,0:T(8,128)(2,1)}, bf16[96,768]{1,0:T(8,128)(2,1)S(1)}, u32[]{:S(2)}) copy-start(bf16[96,768]{1,0:T(8,128)(2,1)S(1)} %collective-permute-done.5.rest_8_) | copy-start | bytes 442372
  19.8 3.8 %collective-permute-start.1 = (bf16[192,768]{1,0:T(8,128)(2,1)S(1)}, bf16[192,768]{1,0:T(8,128)(2,1)S(1)}, u32[]{:S(2)}, u32[]{:S(2)}) collective-permute-start(bf16[192,768]{1,0:T(8,128)(2,1)S(1)} %copy-done.8), channel_id=1, source_target_pairs={{0,8},{8,0},{16,24},{24,16},{1,9},{9,1},{17,25},{25,17},{2,10},{10... | collective-permute-start | bytes 884744 | tf_op jit(solution)/shard_map/ppermute | solution.py:621
  19.9 6.3 %copy-start.19 = (bf16[96,768]{1,0:T(8,128)(2,1)}, bf16[96,768]{1,0:T(8,128)(2,1)S(1)}, u32[]{:S(2)}) copy-start(bf16[96,768]{1,0:T(8,128)(2,1)S(1)} %collective-permute-done.8.rest_11_) | copy-start | bytes 442372
  19.9 3.9 %collective-permute-start.2 = (bf16[192,768]{1,0:T(8,128)(2,1)S(1)}, bf16[192,768]{1,0:T(8,128)(2,1)S(1)}, u32[]{:S(2)}, u32[]{:S(2)}) collective-permute-start(bf16[192,768]{1,0:T(8,128)(2,1)S(1)} %copy-done.9), channel_id=1, source_target_pairs={{0,8},{8,0},{16,24},{24,16},{1,9},{9,1},{17,25},{25,17},{2,10},{10... | collective-permute-start | bytes 884744 | tf_op jit(solution)/shard_map/ppermute | solution.py:621
  21.6 4.6 %copy-start.20 = (bf16[96,768]{1,0:T(8,128)(2,1)}, bf16[96,768]{1,0:T(8,128)(2,1)S(1)}, u32[]{:S(2)}) copy-start(bf16[96,768]{1,0:T(8,128)(2,1)S(1)} %collective-permute-done.9.rest_12_) | copy-start | bytes 442372
  21.6 1.6 %collective-permute-start.12 = (bf16[96,768]{1,0:T(8,128)(2,1)S(1)}, bf16[96,768]{1,0:T(8,128)(2,1)S(1)}, u32[]{:S(2)}, u32[]{:S(2)}) collective-permute-start(bf16[96,768]{1,0:T(8,128)(2,1)S(1)} %collective-permute-done.11.rest_14_), channel_id=1, source_target_pairs={{0,8},{8,0},{16,24},{24,16},{1,9},{9,1},{17,25},{25,17},{2,10},{10... | collective-permute-start | bytes 442376 | tf_op jit(solution)/shard_map/ppermute | solution.py:621
  23.1 3.0 %copy-start.21 = (bf16[96,768]{1,0:T(8,128)(2,1)}, bf16[96,768]{1,0:T(8,128)(2,1)S(1)}, u32[]{:S(2)}) copy-start(bf16[96,768]{1,0:T(8,128)(2,1)S(1)} %collective-permute-done.13.rest_16_) | copy-start | bytes 442372
  23.2 1.6 %collective-permute-start.3 = (bf16[192,768]{1,0:T(8,128)(2,1)S(1)}, bf16[192,768]{1,0:T(8,128)(2,1)S(1)}, u32[]{:S(2)}, u32[]{:S(2)}) collective-permute-start(bf16[192,768]{1,0:T(8,128)(2,1)S(1)} %copy-done.10), channel_id=1, source_target_pairs={{0,8},{8,0},{16,24},{24,16},{1,9},{9,1},{17,25},{25,17},{2,10},{10... | collective-permute-start | bytes 884744 | tf_op jit(solution)/shard_map/ppermute | solution.py:621
  23.2 3.0 %copy-start.22 = (bf16[96,768]{1,0:T(8,128)(2,1)}, bf16[96,768]{1,0:T(8,128)(2,1)S(1)}, u32[]{:S(2)}) copy-start(bf16[96,768]{1,0:T(8,128)(2,1)S(1)} %collective-permute-done.12.rest_15_) | copy-start | bytes 442372
  23.2 2.9 %collective-permute-start.6 = (bf16[96,768]{1,0:T(8,128)(2,1)S(1)}, bf16[96,768]{1,0:T(8,128)(2,1)S(1)}, u32[]{:S(2)}, u32[]{:S(2)}) collective-permute-start(bf16[96,768]{1,0:T(8,128)(2,1)S(1)} %collective-permute-done.5.rest_8_), channel_id=1, source_target_pairs={{0,8},{8,0},{16,24},{24,16},{1,9},{9,1},{17,25},{25,17},{2,10},{10... | collective-permute-start | bytes 442376 | tf_op jit(solution)/shard_map/ppermute | solution.py:621
  23.7 2.5 %copy-start.11 = (bf16[192,768]{1,0:T(8,128)(2,1)}, bf16[192,768]{1,0:T(8,128)(2,1)S(1)}, u32[]{:S(2)}) copy-start(bf16[192,768]{1,0:T(8,128)(2,1)S(1)} %collective-permute-done.1.rest_3_) | copy-start | bytes 884740
  23.7 2.4 %collective-permute-start.10 = (bf16[96,768]{1,0:T(8,128)(2,1)S(1)}, bf16[96,768]{1,0:T(8,128)(2,1)S(1)}, u32[]{:S(2)}, u32[]{:S(2)}) collective-permute-start(bf16[96,768]{1,0:T(8,128)(2,1)S(1)} %collective-permute-done.9.rest_12_), channel_id=1, source_target_pairs={{0,8},{8,0},{16,24},{24,16},{1,9},{9,1},{17,25},{25,17},{2,10},{10... | collective-permute-start | bytes 442376 | tf_op jit(solution)/shard_map/ppermute | solution.py:621
  23.8 2.5 %copy-start.12 = (bf16[192,768]{1,0:T(8,128)(2,1)}, bf16[192,768]{1,0:T(8,128)(2,1)S(1)}, u32[]{:S(2)}) copy-start(bf16[192,768]{1,0:T(8,128)(2,1)S(1)} %collective-permute-done.2.rest_4_) | copy-start | bytes 884740
  23.8 2.3 %collective-permute-start.14 = (bf16[96,768]{1,0:T(8,128)(2,1)S(1)}, bf16[96,768]{1,0:T(8,128)(2,1)S(1)}, u32[]{:S(2)}, u32[]{:S(2)}) collective-permute-start(bf16[96,768]{1,0:T(8,128)(2,1)S(1)} %collective-permute-done.13.rest_16_), channel_id=1, source_target_pairs={{0,8},{8,0},{16,24},{24,16},{1,9},{9,1},{17,25},{25,17},{2,10},{10... | collective-permute-start | bytes 442376 | tf_op jit(solution)/shard_map/ppermute | solution.py:621
  24.7 1.5 %copy-start.13 = (bf16[192,768]{1,0:T(8,128)(2,1)}, bf16[192,768]{1,0:T(8,128)(2,1)S(1)}, u32[]{:S(2)}) copy-start(bf16[192,768]{1,0:T(8,128)(2,1)S(1)} %collective-permute-done.3.rest_5_) | copy-start | bytes 884740
  24.7 31.3 %collective-permute-start.20 = (bf16[768,768]{1,0:T(8,128)(2,1)}, bf16[768,768]{1,0:T(8,128)(2,1)}, u32[]{:S(2)}, u32[]{:S(2)}) collective-permute-start(bf16[768,768]{1,0:T(8,128)(2,1)} %rest_14_.1), channel_id=1, source_target_pairs={{0,16},{8,24},{16,0},{24,8},{1,17},{9,25},{17,1},{25,9},{2,18},{10... | collective-permute-start | bytes 3538952 | tf_op jit(solution)/shard_map/ppermute | solution.py:621
  26.1 0.7 copy-start.23
  26.1 0.7 copy-start.24
  26.1 0.7 copy-start.25
  39.4 1.6 %copy-start.26 = (bf16[2,5,96,768]{3,2,1,0:T(8,128)(2,1)S(1)}, bf16[2,5,96,768]{3,2,1,0:T(8,128)(2,1)}, u32[]{:S(2)}) copy-start(bf16[2,5,96,768]{3,2,1,0:T(8,128)(2,1)} %get-tuple-element.86) | copy-start | bytes 4423684
  39.5 16.6 %collective-permute-start.19 = (bf16[5,96,768]{2,1,0:T(8,128)(2,1)}, bf16[5,96,768]{2,1,0:T(8,128)(2,1)}, u32[]{:S(2)}, u32[]{:S(2)}) collective-permute-start(bf16[5,96,768]{2,1,0:T(8,128)(2,1)} %gate.2.rest_10_), channel_id=1, source_target_pairs={{0,1},{1,0},{2,3},{3,2},{4,5},{5,4},{6,7},{7,6},{8,10},{9,11},{10,... | collective-permute-start | bytes 2211848 | tf_op jit(solution)/shard_map/ppermute | solution.py:630
  41.0 17.4 %collective-permute-start.16 = (bf16[2,5,96,768]{3,2,1,0:T(8,128)(2,1)S(1)}, bf16[2,5,96,768]{3,2,1,0:T(8,128)(2,1)S(1)}, u32[]{:S(2)}, u32[]{:S(2)}) collective-permute-start(bf16[2,5,96,768]{3,2,1,0:T(8,128)(2,1)S(1)} %copy-done.26), channel_id=1, source_target_pairs={{0,8},{8,0},{16,24},{24,16},{1,9},{9,1},{17,25},{25,17},{2,10},{10... | collective-permute-start | bytes 4423688 | tf_op jit(solution)/shard_map/ppermute | solution.py:621
  41.0 13.1 %collective-permute-start.18 = (f32[1,2,24,128]{3,2,1,0:T(8,128)S(1)}, f32[1,2,24,128]{3,2,1,0:T(8,128)S(1)}, u32[]{:S(2)}, u32[]{:S(2)}) collective-permute-start(f32[1,2,24,128]{3,2,1,0:T(8,128)S(1)} %pad_maximum_fusion), channel_id=1, source_target_pairs={{0,1},{1,0},{2,3},{3,2},{4,5},{5,4},{6,7},{7,6},{8,9},{9,8},{10,11... | collective-permute-start | bytes 73736 | tf_op jit(solution)/shard_map/ppermute | solution.py:621
  42.3 14.3 %collective-permute-start.17 = (bf16[5,96,768]{2,1,0:T(8,128)(2,1)}, bf16[5,96,768]{2,1,0:T(8,128)(2,1)}, u32[]{:S(2)}, u32[]{:S(2)}) collective-permute-start(bf16[5,96,768]{2,1,0:T(8,128)(2,1)} %gate.2.rest_10_), channel_id=1, source_target_pairs={{0,8},{8,0},{16,24},{24,16},{1,9},{9,1},{17,25},{25,17},{2,10},{10... | collective-permute-start | bytes 2211848 | tf_op jit(solution)/shard_map/ppermute | solution.py:621
  54.1 4.3 %collective-permute-start.22 = (bf16[768,768]{1,0:T(8,128)(2,1)}, bf16[768,768]{1,0:T(8,128)(2,1)}, u32[]{:S(2)}, u32[]{:S(2)}) collective-permute-start(bf16[768,768]{1,0:T(8,128)(2,1)} %rest_14_.1), channel_id=1, source_target_pairs={{0,8},{8,0},{16,24},{24,16},{1,9},{9,1},{17,25},{25,17},{2,10},{10... | collective-permute-start | bytes 3538952 | tf_op jit(solution)/shard_map/ppermute | solution.py:621
  56.1 4.2 %collective-permute-start.23 = (bf16[768,768]{1,0:T(8,128)(2,1)}, bf16[768,768]{1,0:T(8,128)(2,1)}, u32[]{:S(2)}, u32[]{:S(2)}) collective-permute-start(bf16[768,768]{1,0:T(8,128)(2,1)} %collective-permute-done.20.rest_16_), channel_id=1, source_target_pairs={{0,8},{8,0},{16,24},{24,16},{1,9},{9,1},{17,25},{25,17},{2,10},{10... | collective-permute-start | bytes 3538952 | tf_op jit(solution)/shard_map/ppermute | solution.py:621
  56.1 4.2 %collective-permute-start.21 = (bf16[5,96,768]{2,1,0:T(8,128)(2,1)}, bf16[5,96,768]{2,1,0:T(8,128)(2,1)}, u32[]{:S(2)}, u32[]{:S(2)}) collective-permute-start(bf16[5,96,768]{2,1,0:T(8,128)(2,1)} %collective-permute-done.19.rest_12_), channel_id=1, source_target_pairs={{0,8},{8,0},{16,24},{24,16},{1,9},{9,1},{17,25},{25,17},{2,10},{10... | collective-permute-start | bytes 2211848 | tf_op jit(solution)/shard_map/ppermute | solution.py:621
  56.6 37.3 %collective-permute-start.24 = (f32[2,2,24,128]{3,2,1,0:T(8,128)S(1)}, f32[2,2,24,128]{3,2,1,0:T(8,128)S(1)}, u32[]{:S(2)}, u32[]{:S(2)}) collective-permute-start(f32[2,2,24,128]{3,2,1,0:T(8,128)S(1)} %constant_dynamic-update-slice_fusion), channel_id=1, source_target_pairs={{0,2},{1,3},{2,0},{3,1},{4,6},{5,7},{6,4},{7,5},{8,10},{9,11},{10,... | collective-permute-start | bytes 147464 | tf_op jit(solution)/shard_map/ppermute | solution.py:621
  58.5 1.9 %copy-start.27 = (bf16[2,5,96,768]{3,2,1,0:T(8,128)(2,1)}, bf16[2,5,96,768]{3,2,1,0:T(8,128)(2,1)S(1)}, u32[]{:S(2)}) copy-start(bf16[2,5,96,768]{3,2,1,0:T(8,128)(2,1)S(1)} %collective-permute-done.16.rest_9_) | copy-start | bytes 4423684
  60.3 33.6 %copy-start.2 = (f32[24576]{0:T(1024)S(1)}, f32[24576]{0:T(1024)}, u32[]{:S(2)}) copy-start(f32[24576]{0:T(1024)} %param.39) | copy-start | bytes 294916
  60.3 33.6 %copy-start.3 = (bf16[1024,768]{1,0:T(8,128)(2,1)S(1)}, bf16[1024,768]{1,0:T(8,128)(2,1)}, u32[]{:S(2)}) copy-start(bf16[1024,768]{1,0:T(8,128)(2,1)} %x_ref.7) | copy-start | bytes 4718596
  60.3 33.6 %copy-start.4 = (s32[2,512]{1,0:T(2,128)S(1)}, s32[2,512]{1,0:T(2,128)}, u32[]{:S(2)}) copy-start(s32[2,512]{1,0:T(2,128)} %seg_ref.5) | copy-start | bytes 12292
  60.3 33.6 %copy-start.5 = (bf16[1024,768]{1,0:T(8,128)(2,1)S(1)}, bf16[1024,768]{1,0:T(8,128)(2,1)}, u32[]{:S(2)}) copy-start(bf16[1024,768]{1,0:T(8,128)(2,1)} %get-tuple-element.97.rest_0_) | copy-start | bytes 4718596
  60.4 33.6 %copy-start.6 = (bf16[1024,768]{1,0:T(8,128)(2,1)S(1)}, bf16[1024,768]{1,0:T(8,128)(2,1)}, u32[]{:S(2)}) copy-start(bf16[1024,768]{1,0:T(8,128)(2,1)} %get-tuple-element.98.rest_1_) | copy-start | bytes 4718596
  60.4 33.6 %copy-start.7 = (bf16[1024,16]{1,0:T(8,128)(2,1)S(1)}, bf16[1024,16]{1,0:T(8,128)(2,1)}, u32[]{:S(2)}) copy-start(bf16[1024,16]{1,0:T(8,128)(2,1)} %get-tuple-element.91.other_ref.down_ref) | copy-start | bytes 98308
  94.0 28.2 %copy-start = (bf16[3,768,768]{2,1,0:T(8,128)(2,1)S(1)}, bf16[3,768,768]{2,1,0:T(8,128)(2,1)}, u32[]{:S(2)}) copy-start(bf16[3,768,768]{2,1,0:T(8,128)(2,1)} %get-tuple-element.78.rest_0_.other_ref.weights) | copy-start | bytes 10616836
  94.0 28.2 %copy-start.1 = (bf16[1024,768]{1,0:T(8,128)(2,1)S(1)}, bf16[1024,768]{1,0:T(8,128)(2,1)}, u32[]{:S(2)}) copy-start(bf16[1024,768]{1,0:T(8,128)(2,1)} %get-tuple-element.121.dh_ref) | copy-start | bytes 4718596
  117.5 3.1 %collective-permute-start.25 = (bf16[32,768]{1,0:T(8,128)(2,1)S(1)}, bf16[32,768]{1,0:T(8,128)(2,1)S(1)}, u32[]{:S(2)}, u32[]{:S(2)}) collective-permute-start(bf16[32,768]{1,0:T(8,128)(2,1)S(1)} %get-tuple-element.105), channel_id=1, source_target_pairs={{0,8},{8,0},{16,24},{24,16},{1,9},{9,1},{17,25},{25,17},{2,10},{10... | collective-permute-start | bytes 147464 | tf_op jit(solution)/shard_map/ppermute | solution.py:621
  117.7 18.4 %collective-permute-start.30 = (f32[4,2,24,128]{3,2,1,0:T(8,128)S(1)}, f32[4,2,24,128]{3,2,1,0:T(8,128)S(1)}, u32[]{:S(2)}, u32[]{:S(2)}) collective-permute-start(f32[4,2,24,128]{3,2,1,0:T(8,128)S(1)} %constant_dynamic-update-slice_fusion.2.held_ref), channel_id=1, source_target_pairs={{0,4},{1,5},{2,6},{3,7},{4,0},{5,1},{6,2},{7,3},{8,12},{9,13},{10,... | collective-permute-start | bytes 294920 | tf_op jit(solution)/shard_map/ppermute | solution.py:621
  120.6 4.2 %collective-permute-start.26 = (bf16[32,768]{1,0:T(8,128)(2,1)S(1)}, bf16[32,768]{1,0:T(8,128)(2,1)S(1)}, u32[]{:S(2)}, u32[]{:S(2)}) collective-permute-start(bf16[32,768]{1,0:T(8,128)(2,1)S(1)} %add.18), channel_id=1, source_target_pairs={{0,16},{8,24},{16,0},{24,8},{1,17},{9,25},{17,1},{25,9},{2,18},{10... | collective-permute-start | bytes 147464 | tf_op jit(solution)/shard_map/ppermute | solution.py:621
  124.8 4.2 %collective-permute-start.27 = (bf16[32,768]{1,0:T(8,128)(2,1)S(1)}, bf16[32,768]{1,0:T(8,128)(2,1)S(1)}, u32[]{:S(2)}, u32[]{:S(2)}) collective-permute-start(bf16[32,768]{1,0:T(8,128)(2,1)S(1)} %add.19), channel_id=1, source_target_pairs={{0,1},{1,0},{2,3},{3,2},{4,5},{5,4},{6,7},{7,6},{8,9},{9,8},{10,11... | collective-permute-start | bytes 147464 | tf_op jit(solution)/shard_map/ppermute | solution.py:621
  128.9 4.2 %collective-permute-start.28 = (bf16[32,768]{1,0:T(8,128)(2,1)S(1)}, bf16[32,768]{1,0:T(8,128)(2,1)S(1)}, u32[]{:S(2)}, u32[]{:S(2)}) collective-permute-start(bf16[32,768]{1,0:T(8,128)(2,1)S(1)} %add.20), channel_id=1, source_target_pairs={{0,2},{1,3},{2,0},{3,1},{4,6},{5,7},{6,4},{7,5},{8,10},{9,11},{10,... | collective-permute-start | bytes 147464 | tf_op jit(solution)/shard_map/ppermute | solution.py:621
  133.1 5.1 %collective-permute-start.29 = (bf16[32,768]{1,0:T(8,128)(2,1)S(1)}, bf16[32,768]{1,0:T(8,128)(2,1)S(1)}, u32[]{:S(2)}, u32[]{:S(2)}) collective-permute-start(bf16[32,768]{1,0:T(8,128)(2,1)S(1)} %add.21.near_ref), channel_id=1, source_target_pairs={{0,4},{1,5},{2,6},{3,7},{4,0},{5,1},{6,2},{7,3},{8,12},{9,13},{10,... | collective-permute-start | bytes 147464 | tf_op jit(solution)/shard_map/ppermute | solution.py:621

commit v6 on v5

--- a/solution.py
+++ b/solution.py
@@ -183,11 +183,12 @@
     at = pl.program_id(1)
     begin = (pl.program_id(0) == 0) & (at == 0)
     if parts is None:
-        weights, rest = rest[0], rest[7:]
-        q_ref, k_ref, v_ref, ctx_ref, aug_ref, down_ref, bias, table = rest
+        weights, rest = rest[0], rest[8:]
+        q_ref, k_ref, v_ref, ctx_ref, inverse_ref, expo_ref, down_ref, bias, table = rest
     else:
         shards, rest = rest[: len(parts.operands)], rest[len(parts.operands) :]
-        q_ref, k_ref, v_ref, ctx_ref, aug_ref, down_ref, weights, bias, table, semaphores = rest
+        q_ref, k_ref, v_ref, ctx_ref, inverse_ref, expo_ref, down_ref, *rest = rest
+        weights, bias, table, semaphores = rest
 
         @pl.when(begin)
         def _():
@@ -218,14 +219,12 @@
 
     lane = lax.broadcasted_iota(jnp.int32, (rows, LANES), 1)
     seg = seg_ref[pl.ds(first + pl.program_id(0), 1), :].astype(F32).T.astype(jnp.int32)
-    own = jnp.where(lane == seg, 1.0, 0.0)
     aug_k = jnp.where((lane < 4) & (lane != seg), -MASKED, 0.0).astype(BF16)
-    aug_q = own.astype(BF16)
+    aug_q = jnp.where(lane == seg, 1.0, 0.0).astype(BF16)
     ones = jnp.ones((rows, LANES), BF16)
     half = LANES // 2
     scale = BF16(half ** (-0.5))
     second = lane >= half
-    spot = jnp.bitwise_and(lane, half - 1)
 
     def scores(head):
         here = slice(LANES * (head // 2), LANES * (head // 2 + 1))
@@ -240,26 +239,22 @@
         if head + 1 < heads:
             ahead = scores(head + 1)
         here = slice(LANES * (head // 2), LANES * (head // 2 + 1))
-        top = jnp.max(now, axis=1, keepdims=True)
-        expo = jnp.exp(now - top).astype(BF16)
+        expo = jnp.exp(now - jnp.max(now, axis=1, keepdims=True)).astype(BF16)
+        expo_ref[head * rows : (head + 1) * rows, :] = expo
         both = dot(expo, beside(v_ref[:, here], ones), NN)
-        found.append((top, both[:, :LANES], both[:, LANES:]))
+        found.append((both[:, :LANES], both[:, LANES:]))
         if head % 2 == 1:
-            (top0, ctx0, sums0), (top1, ctx1, sums1) = found[-2:]
-            sums = jnp.where(second, sums1, sums0)
-            ctx_ref[:, here] = (jnp.where(second, ctx1, ctx0) / sums).astype(BF16)
-            level = jnp.where(second, top1, top0) + jnp.log(sums)
-            high, middle, little = three_parts(-level)
-            aug = jnp.where(
-                spot == 4, high, jnp.where(spot == 5, middle, jnp.where(spot == 6, little, own))
-            )
-            aug_ref[:, here] = aug.astype(BF16)
+            (ctx0, sums0), (ctx1, sums1) = found[-2:]
+            inverse = 1.0 / jnp.where(second, sums1, sums0)
+            inverse_ref[:, here] = inverse
+            ctx_ref[:, here] = (jnp.where(second, ctx1, ctx0) * inverse).astype(BF16)
 
 
 def attend(rank, place, seg, x, factors, bq, bv, pairs, first, count, parts, weights=None, carry=()):
     packs, size = seg.shape
     rows, width = x.shape
     cut = pairs * LANES
+    groups = width // cut
     block = pl.BlockSpec((size, cut), lambda p, g: (first + p, g))
     vmem = pl.BlockSpec(memory_space=pltpu.VMEM)
     smem = pl.BlockSpec(memory_space=pltpu.SMEM)
@@ -270,9 +265,11 @@
         block,
         block,
         block,
+        pl.BlockSpec((2 * pairs * size, size), lambda p, g: ((first + p) * groups + g, 0)),
         pl.BlockSpec((size, 2 * ADAPTER_RANK), lambda p, g: (first + p, 0)),
     ]
-    out_shape = [like((rows, width), BF16)] * 5 + [like((rows, 2 * ADAPTER_RANK), BF16)]
+    out_shape = [like((rows, width), BF16)] * 4 + [like((rows, width), F32)]
+    out_shape += [like((HEADS * rows, size), BF16), like((rows, 2 * ADAPTER_RANK), BF16)]
     scratch = [pltpu.VMEM((8, width), F32), pltpu.VMEM((4 * ADAPTER_RANK, width), F32)]
     if parts is None:
         operands, specs = [weights, *carry], [vmem] + [ANY] * len(carry)
@@ -406,8 +403,8 @@
     )(rank, place, x, ctx, cot, *vectors, *first.operands, *second.operands)
 
 
-def attend_back_kernel(seg_ref, x_ref, fac_ref, down_ref, *rest):
-    q_ref, k_ref, v_ref, dctx_ref, ctx_ref, aug_ref, *rest = rest
+def attend_back_kernel(x_ref, fac_ref, down_ref, *rest):
+    q_ref, k_ref, v_ref, dctx_ref, ctx_ref, inverse_ref, expo_ref, *rest = rest
     dq_ref, dk_ref, dv_ref, dlow_ref, grad_ref, low, total, table = rest
     pack, at = pl.program_id(0), pl.program_id(1)
     rows, width = q_ref.shape
@@ -419,26 +416,16 @@
         table[...] = adapter_rows(fac_ref, 0, *table.shape)
 
     lane = lax.broadcasted_iota(jnp.int32, (rows, LANES), 1)
-    seg = seg_ref[pl.ds(pl.program_id(0), 1), :].astype(F32).T.astype(jnp.int32)
-    spot = jnp.bitwise_and(lane, LANES // 2 - 1)
-    level = (spot >= 4) & (spot < 7)
-    second = lane >= LANES // 2
-    differ = (lane < 4) & (lane != seg)
-    aug_ks = [
-        jnp.where(differ, -MASKED, jnp.where(level & (second == bool(side)), 1.0, 0.0)).astype(BF16)
-        for side in range(2)
-    ]
     aug_v = jnp.where(lane < 3, 1.0, 0.0).astype(BF16)
     zero = BF16(0)
     half = LANES // 2
     scale = BF16(half ** (-0.5))
     for pair in range(width // LANES):
         here = slice(LANES * pair, LANES * (pair + 1))
-        key = k_ref[:, here]
+        key = k_ref[:, here] * scale
         query = q_ref[:, here] * scale
-        grad = dctx_ref[:, here]
+        grad = (dctx_ref[:, here].astype(F32) * inverse_ref[:, here]).astype(BF16)
         values = beside(v_ref[:, here], aug_v)
-        key = key * scale
         product = grad.astype(F32) * ctx_ref[:, here].astype(F32)
         dq = dk = dv = 0.0
         for side in range(2):
@@ -451,13 +438,13 @@
             aug_d = jnp.where(
                 lane == 0, high, jnp.where(lane == 1, middle, jnp.where(lane == 2, little, 0.0))
             ).astype(BF16)
-            keys = beside(k_ref[:, here], aug_ks[side])
-            probs = jnp.exp(dot(keys, beside(one_query, aug_ref[:, here]), NT))
-            dprobs = dot(values, beside(one_grad, aug_d), NT)
-            dscores = (probs * dprobs).astype(BF16)
-            dv = dv + dot(probs.astype(BF16), one_grad, NN)
-            dk = dk + dot(dscores, one_query, NN)
-            dq = dq + dot(dscores, one_key, TN)
+            head = 2 * pair + side
+            expo = expo_ref[head * rows : (head + 1) * rows, :]
+            dprobs = dot(beside(one_grad, aug_d), values, NT)
+            dscores = (expo.astype(F32) * dprobs).astype(BF16)
+            dv = dv + dot(expo, one_grad, TN)
+            dk = dk + dot(dscores, one_query, TN)
+            dq = dq + dot(dscores, one_key, NN)
         dq_ref[:, here] = dq.astype(BF16)
         dk_ref[:, here] = dk.astype(BF16)
         dv_ref[:, here] = dv.astype(BF16)
@@ -487,10 +474,11 @@
         grad_ref[...] = total[...].astype(BF16)
 
 
-def attend_back(seg, x, factors, down, q, k, v, dctx, ctx, aug, pairs):
-    packs, size = seg.shape
+def attend_back(x, factors, down, q, k, v, dctx, ctx, inverse, expo, pairs):
+    size = expo.shape[1]
     rows, width = x.shape
     cut = pairs * LANES
+    packs, groups = rows // size, width // cut
     rank2 = 2 * ADAPTER_RANK
     block = pl.BlockSpec((size, cut), lambda p, g: (p, g))
     whole = lambda shape: pl.BlockSpec(shape, lambda p, g: (0, 0), pipeline_mode=pl.Buffered(1))
@@ -499,7 +487,6 @@
         attend_back_kernel,
         grid=(packs, width // cut),
         in_specs=[
-            pl.BlockSpec(memory_space=pltpu.VMEM),
             pl.BlockSpec((size, width), lambda p, g: (p, 0)),
             pl.BlockSpec(memory_space=pltpu.VMEM),
             pl.BlockSpec((size, rank2), lambda p, g: (p, 0)),
@@ -509,6 +496,7 @@
             block,
             block,
             block,
+            pl.BlockSpec((2 * pairs * size, size), lambda p, g: (p * groups + g, 0)),
         ],
         out_specs=[
             block,
@@ -528,7 +516,7 @@
             transcendentals=rows * size * HEADS,
         ),
         name="attend_back",
-    )(seg, x, factors, down, q, k, v, dctx, ctx, aug)
+    )(x, factors, down, q, k, v, dctx, ctx, inverse, expo)
 
 
 def input_kernel(first, dh_ref, dq_ref, dk_ref, dv_ref, dlow_ref, fac_ref, weights, *rest):
@@ -738,7 +726,7 @@
     values = [gate(value, weights, GATE) for value in values]
     halves_ahead = [(flip, value) for (flip, _), value in zip(halves_ahead, values)]
     crossed_ahead = across(halves_ahead, reps, wide)
-    q, k, v, ctx, aug, down = attend(
+    q, k, v, ctx, inverse, expo, down = attend(
         *arguments, early, packs - early, None, weights, attended
     )
     flips_outer, whole_outer = zip(*whole_outer)
@@ -772,7 +760,7 @@
     held = jnp.concatenate([held, pending])
     other = swap(held, "wide", wide, flips[-1])
     dq, dk, dv, dlow, grad = attend_back(
-        segment_ids, tokens, table, down, q, k, v, dctx, ctx, aug, 3
+        tokens, table, down, q, k, v, dctx, ctx, inverse, expo, 3
     )
     rounds = [("rep", reps, flip) for flip in bits(reps)]
     rounds += [("wide", wide, flip) for flip in bits(wide)]

time: 139 us -> 139 us (level)
  starting transfers between devices: 28.8 us -> 26.8 us
  waiting for transfers between devices: 12.2 us -> 14.1 us
    pallas_call x1, Pallas kernels: 23.5 us -> 21 us  [attend_back(): pl.pallas_call(attend_back_kernel, grid=(packs, width // cut), in_specs=[...]
    pallas_call x2, Pallas kernels: 24.2 us -> 26.2 us  [attend(): pl.pallas_call(functools.partial(attend_kernel, parts, first), grid=(coun...]
    ppermute x27, starting transfers between devices: 23.6 us -> 21.6 us  [swap(): return lax.ppermute(value, axis, [(i, i ^ flip) for i in range(size)])]
    ppermute x27, waiting for transfers between devices: 8.14 us -> 9.97 us  [swap(): return lax.ppermute(value, axis, [(i, i ^ flip) for i in range(size)])]
  transfers between devices with their start and end apart: 31 -> 31, of which waited for: 11 -> 11; matrix products, arithmetic and copies ran while one was open for 2% -> 2% of each run, Pallas kernels for 49% -> 51%
where the time goes in v6:
time: 139 us; the launch traced here: 138 us
  Pallas kernels  92.2 us (66%)
  starting transfers between devices  26.8 us (19%)
  waiting for transfers between devices  14.1 us (10%)
  local copies, waits for them, and re-layouts  3.57 us (3%)
    pallas_call x1, Pallas kernels, dense(): pl.pallas_call(functools.partial(dense_kernel, first, second, cut), grid=...  33.5 us
    pallas_call x2, Pallas kernels, attend(): pl.pallas_call(functools.partial(attend_kernel, parts, first), grid=(coun...  26.2 us
    ppermute x27, starting transfers between devices, swap(): return lax.ppermute(value, axis, [(i, i ^ flip) for i in range(size)])  21.6 us
    pallas_call x1, Pallas kernels, attend_back(): pl.pallas_call(attend_back_kernel, grid=(packs, width // cut), in_specs=[...  21 us
    ppermute x27, waiting for transfers between devices, swap(): return lax.ppermute(value, axis, [(i, i ^ flip) for i in range(size)])  9.97 us
    pallas_call x4, Pallas kernels, input_back(): pl.pallas_call(functools.partial(input_kernel, at * size), grid=(1,), in_...  7.6 us
    ppermute x4, starting transfers between devices, cross(): return lax.ppermute(value, ('rep', 'wide'), pairs)  5.15 us
    ppermute x4, waiting for transfers between devices, cross(): return lax.ppermute(value, ('rep', 'wide'), pairs)  4.1 us
  transfers between devices with their start and end apart: 31, of which 11 were waited for; matrix products, arithmetic and copies ran while one was open for 2% of the time, Pallas kernels for 51%

profile of v6, /device:TPU:0, one launch (start us, length us, event | category | flops | bytes accessed | tf_op | source)
XLA Modules:
  0.0 138.5 jit_solution(15476826431637942068)
XLA Ops:
  0.6 0.0 copy-start.7
  0.6 0.0 copy-start.9
  0.7 0.0 copy-start.8
  0.7 1.0 constant_dynamic-slice_fusion.2
  1.7 3.0 %collective-permute-start = (bf16[96,768]{1,0:T(8,128)(2,1)S(1)}, bf16[96,768]{1,0:T(8,128)(2,1)S(1)}, u32[]{:S(2)}, u32[]{:S(2)}) collective-permute-start(bf16[96,768]{1,0:T(8,128)(2,1)S(1)} %constant_dynamic-slice_fusion.2), channel_id=1, source_target_pairs={{0,16},{8,24},{16,0},{24,8},{1,17},{9,25},{17,1},{25,9},{2,18},{10... | collective-permute-start | bytes 442376 | tf_op jit(solution)/shard_map/ppermute | solution.py:609
  4.7 0.9 constant_dynamic-slice_fusion
  5.6 0.1 collective-permute-start.11
  5.7 0.9 constant_dynamic-slice_fusion.1
  6.6 2.1 %collective-permute-start.7 = (bf16[96,768]{1,0:T(8,128)(2,1)S(1)}, bf16[96,768]{1,0:T(8,128)(2,1)S(1)}, u32[]{:S(2)}, u32[]{:S(2)}) collective-permute-start(bf16[96,768]{1,0:T(8,128)(2,1)S(1)} %constant_dynamic-slice_fusion.1), channel_id=1, source_target_pairs={{0,16},{8,24},{16,0},{24,8},{1,17},{9,25},{17,1},{25,9},{2,18},{10... | collective-permute-start | bytes 442376 | tf_op jit(solution)/shard_map/ppermute | solution.py:609
  8.7 0.7 pad_maximum_fusion
  9.4 2.9 %pack_shards.1 = (bf16[2,5,96,768]{3,2,1,0:T(8,128)(2,1)}, bf16[5,96,768]{2,1,0:T(8,128)(2,1)}) custom-call(s32[1]{0:T(128)} %bitcast.1.place_ref, bf16[192,768]{1,0:T(8,128)(2,1)} %rest_7_.1, bf16[192,3072]{1,0:T(8,128)(2,1)} %rest_8_.1), custom_call_target="tpu_custom_call" | custom-call | tf_op jit(solution)/shard_map/pack_shards/pallas_call | solution.py:169
  12.3 0.1 collective-permute-done.11.rest_14_
  12.5 2.1 %collective-permute-start.15 = (bf16[5,96,768]{2,1,0:T(8,128)(2,1)}, bf16[5,96,768]{2,1,0:T(8,128)(2,1)}, u32[]{:S(2)}, u32[]{:S(2)}) collective-permute-start(bf16[5,96,768]{2,1,0:T(8,128)(2,1)} %get-tuple-element.79), channel_id=1, source_target_pairs={{0,16},{8,24},{16,0},{24,8},{1,17},{9,25},{17,1},{25,9},{2,18},{10... | collective-permute-start | bytes 2211848 | tf_op jit(solution)/shard_map/ppermute | solution.py:609
  14.6 0.0 collective-permute-done.rest_6_
  14.6 0.0 collective-permute-start.4
  14.6 1.6 %collective-permute-start.5 = (bf16[96,768]{1,0:T(8,128)(2,1)S(1)}, bf16[96,768]{1,0:T(8,128)(2,1)S(1)}, u32[]{:S(2)}, u32[]{:S(2)}) collective-permute-start(bf16[96,768]{1,0:T(8,128)(2,1)S(1)} %collective-permute-done.rest_6_), channel_id=1, source_target_pairs={{0,1},{1,0},{2,3},{3,2},{4,5},{5,4},{6,7},{7,6},{8,10},{9,11},{10,... | collective-permute-start | bytes 442376 | tf_op jit(solution)/shard_map/ppermute | solution.py:618
  16.2 0.0 collective-permute-done.7.rest_10_
  16.2 0.2 collective-permute-start.8
  16.4 1.5 %collective-permute-start.9 = (bf16[96,768]{1,0:T(8,128)(2,1)S(1)}, bf16[96,768]{1,0:T(8,128)(2,1)S(1)}, u32[]{:S(2)}, u32[]{:S(2)}) collective-permute-start(bf16[96,768]{1,0:T(8,128)(2,1)S(1)} %collective-permute-done.7.rest_10_), channel_id=1, source_target_pairs={{0,1},{1,0},{2,3},{3,2},{4,5},{5,4},{6,7},{7,6},{8,10},{9,11},{10,... | collective-permute-start | bytes 442376 | tf_op jit(solution)/shard_map/ppermute | solution.py:618
  17.9 0.5 collective-permute-start.13
  18.5 1.4 collective-permute-done.5.rest_8_
  19.8 0.0 collective-permute-start.1
  19.9 0.5 collective-permute-start.2
  20.4 1.2 collective-permute-done.9.rest_12_
  21.6 1.6 %collective-permute-done.13.rest_16_ = bf16[96,768]{1,0:T(8,128)(2,1)S(1)} collective-permute-done((bf16[96,768]{1,0:T(8,128)(2,1)S(1)}, bf16[96,768]{1,0:T(8,128)(2,1)S(1)}, u32[]{:S(2)}, u32[]{:S(2)}) %collective-permute-start.13) | collective-permute-done | bytes 147488 | tf_op jit(solution)/shard_map/ppermute | solution.py:618
  23.2 0.5 collective-permute-start.6
  23.7 0.1 collective-permute-start.10
  23.8 0.4 collective-permute-start.14
  24.2 0.5 collective-permute-done.3.rest_5_
  24.7 1.3 collective-permute-start.20
  26.2 0.5 copy-done.22
  26.7 0.1 copy-done.23
  26.8 0.1 copy-done.24
  26.8 14.1 %project_and_attend.2 = (bf16[1024,768]{1,0:T(8,128)(2,1)}, bf16[1024,768]{1,0:T(8,128)(2,1)}, bf16[1024,768]{1,0:T(8,128)(2,1)}, bf16[1024,768]{1,0:T(8,128)(2,...) custom-call(s32[1]{0:T(128)} %bitcast.rank_ref, ...), custom_call_target="tpu_custom_call" | custom-call | flops 1 | bytes 1 | tf_op jit(solution)/shard_map/project_and_attend/pallas_call | solution.py:281
  40.9 0.0 copy-start.25
  41.0 1.6 %collective-permute-start.19 = (bf16[5,96,768]{2,1,0:T(8,128)(2,1)}, bf16[5,96,768]{2,1,0:T(8,128)(2,1)}, u32[]{:S(2)}, u32[]{:S(2)}) collective-permute-start(bf16[5,96,768]{2,1,0:T(8,128)(2,1)} %gate.2.rest_10_), channel_id=1, source_target_pairs={{0,1},{1,0},{2,3},{3,2},{4,5},{5,4},{6,7},{7,6},{8,10},{9,11},{10,... | collective-permute-start | bytes 2211848 | tf_op jit(solution)/shard_map/ppermute | solution.py:618
  42.5 1.3 collective-permute-start.18
  43.8 0.2 collective-permute-start.17
  44.0 12.2 %project_and_attend.3 = (bf16[1024,768]{1,0:T(8,128)(2,1)}, bf16[1024,768]{1,0:T(8,128)(2,1)}, bf16[1024,768]{1,0:T(8,128)(2,1)}, bf16[1024,768]{1,0:T(8,128)(2,...) custom-call(s32[1]{0:T(128)} %bitcast.rank_ref, ...), custom_call_target="tpu_custom_call", output_to_operand_aliasing={{0}: (8, {}), {1}: (9, {}), {2}: (10, {}), {3}: (11, {}), {... | custom-call | flops 6000000000 | bytes 1 | tf_op jit(solution)/shard_map/project_and_attend/pallas_call | solution.py:281
  56.2 0.3 collective-permute-start.22
  56.6 0.2 collective-permute-start.23
  56.8 0.3 collective-permute-start.21
  57.1 1.6 %collective-permute-start.24 = (f32[2,2,24,128]{3,2,1,0:T(8,128)S(1)}, f32[2,2,24,128]{3,2,1,0:T(8,128)S(1)}, u32[]{:S(2)}, u32[]{:S(2)}) collective-permute-start(f32[2,2,24,128]{3,2,1,0:T(8,128)S(1)} %constant_dynamic-update-slice_fusion), channel_id=1, source_target_pairs={{0,2},{1,3},{2,0},{3,1},{4,6},{5,7},{6,4},{7,5},{8,10},{9,11},{10,... | collective-permute-start | bytes 147464 | tf_op jit(solution)/shard_map/ppermute | solution.py:609
  58.7 0.7 collective-permute-done.22.rest_15_
  59.5 2.7 %collective-permute-done.21.rest_13_ = bf16[5,96,768]{2,1,0:T(8,128)(2,1)} collective-permute-done((bf16[5,96,768]{2,1,0:T(8,128)(2,1)}, bf16[5,96,768]{2,1,0:T(8,128)(2,1)}, u32[]{:S(2)}, u32[]{:S(2)}) %collective-permute-start.21) | collective-permute-done | bytes 737312 | tf_op jit(solution)/shard_map/ppermute | solution.py:609
  62.2 0.0 copy-start.3
  62.2 0.0 copy-start.4
  62.3 33.5 %dense_both_ways.1 = (bf16[1024,768]{1,0:T(8,128)(2,1)}, bf16[1024,768]{1,0:T(8,128)(2,1)}, bf16[1024,768]{1,0:T(8,128)(2,1)}) custom-call(s32[1]{0:T(128)} %bitcast.rank_ref, s32[1]{0:T(128)} %bitcast.1.place_ref, bf16[1024,768]{1,0:T(8,128)(2,1)} %x_ref.7, bf16[1024,768]{1,0:T(8,128)(2,1)} %get-tuple-element.88.ctx_ref.rest_4_, bf16[1024,768]{1,0:T(8,128)(2,1)} %cot_ref.1, ...), custom_call_target="tpu_custom_call" | custom-call | flops 21743271936 | bytes 18874368 | tf_op jit(solution)/shard_map/dense_both_ways/pallas_call | solution.py:382
  95.8 21.0 %attend_back.1 = (bf16[1024,768]{1,0:T(8,128)(2,1)S(1)}, bf16[1024,768]{1,0:T(8,128)(2,1)S(1)}, bf16[1024,768]{1,0:T(8,128)(2,1)S(1)}, bf16[1024,16]{1,0:T(8,128)(2,1)S(1)}, bf16[32,768]{1,0:T(8,128)(2,1)S(1)}) custom-call(bf16[1024,768]{1,0:T(8,128)(2,1)S(1)} %copy-done.2, f32[192,128]{1,0:T(8,128)S(1)} %bitcast.12, bf16[1024,16]{1,0:T(8,128)(2,1)S(1)} %copy-done.6, ...), custom_call_target="tpu_custom_call" | custom-call | flops 12079595520 | bytes 18874368 | tf_op jit(solution)/shard_map/attend_back/pallas_call | solution.py:486
  116.9 0.3 collective-permute-start.25
  117.2 2.6 %collective-permute-start.30 = (f32[4,2,24,128]{3,2,1,0:T(8,128)S(1)}, f32[4,2,24,128]{3,2,1,0:T(8,128)S(1)}, u32[]{:S(2)}, u32[]{:S(2)}) collective-permute-start(f32[4,2,24,128]{3,2,1,0:T(8,128)S(1)} %constant_dynamic-update-slice_fusion.2.held_ref), channel_id=1, source_target_pairs={{0,4},{1,5},{2,6},{3,7},{4,0},{5,1},{6,2},{7,3},{8,12},{9,13},{10,... | collective-permute-start | bytes 294920 | tf_op jit(solution)/shard_map/ppermute | solution.py:609
  119.9 0.8 collective-permute-start.26
  120.7 1.9 %input_gradient.4.rest_0_ = bf16[1024,768]{1,0:T(8,128)(2,1)} custom-call(bf16[1024,768]{1,0:T(8,128)(2,1)S(1)} %copy-done.1, bf16[1024,768]{1,0:T(8,128)(2,1)S(1)} %get-tuple-element.112.dq_ref, bf16[1024,768]{1,0:T(8,128)(2,1)S(1)} %get-tuple-element.113.dk_ref, bf16[1024,768]{1,0:T(8,128)(2,1)S(1)} %get-tuple-element.114.dv_ref, ...), custom_call_target="tpu_custom_call" | custom-call | flops 905969664 | bytes 1966080 | tf_op jit(solution)/shard_map/input_gradient/pallas_call | solution.py:536
  122.6 1.5 %collective-permute-done.26 = bf16[32,768]{1,0:T(8,128)(2,1)S(1)} collective-permute-done((bf16[32,768]{1,0:T(8,128)(2,1)S(1)}, bf16[32,768]{1,0:T(8,128)(2,1)S(1)}, u32[]{:S(2)}, u32[]{:S(2)}) %collective-permute-start.26) | collective-permute-done | bytes 49184 | tf_op jit(solution)/shard_map/ppermute | solution.py:609
  124.1 0.8 collective-permute-start.27
  124.9 1.9 %input_gradient.5.rest_0_ = bf16[1024,768]{1,0:T(8,128)(2,1)} custom-call(bf16[1024,768]{1,0:T(8,128)(2,1)S(1)} %copy-done.1, bf16[1024,768]{1,0:T(8,128)(2,1)S(1)} %get-tuple-element.112.dq_ref, bf16[1024,768]{1,0:T(8,128)(2,1)S(1)} %get-tuple-element.113.dk_ref, bf16[1024,768]{1,0:T(8,128)(2,1)S(1)} %get-tuple-element.114.dv_ref, ...), custom_call_target="tpu_custom_call", output_to_operand_aliasing={{}: (7, {})} | custom-call | flops 905969664 | bytes 1966080 | tf_op jit(solution)/shard_map/input_gradient/pallas_call | solution.py:536
  126.8 1.4 %collective-permute-done.27 = bf16[32,768]{1,0:T(8,128)(2,1)S(1)} collective-permute-done((bf16[32,768]{1,0:T(8,128)(2,1)S(1)}, bf16[32,768]{1,0:T(8,128)(2,1)S(1)}, u32[]{:S(2)}, u32[]{:S(2)}) %collective-permute-start.27) | collective-permute-done | bytes 49184 | tf_op jit(solution)/shard_map/ppermute | solution.py:609
  128.3 1.6 %collective-permute-start.28 = (bf16[32,768]{1,0:T(8,128)(2,1)S(1)}, bf16[32,768]{1,0:T(8,128)(2,1)S(1)}, u32[]{:S(2)}, u32[]{:S(2)}) collective-permute-start(bf16[32,768]{1,0:T(8,128)(2,1)S(1)} %add.20), channel_id=1, source_target_pairs={{0,2},{1,3},{2,0},{3,1},{4,6},{5,7},{6,4},{7,5},{8,10},{9,11},{10,... | collective-permute-start | bytes 147464 | tf_op jit(solution)/shard_map/ppermute | solution.py:609
  129.9 1.9 %input_gradient.6.rest_0_ = bf16[1024,768]{1,0:T(8,128)(2,1)} custom-call(bf16[1024,768]{1,0:T(8,128)(2,1)S(1)} %copy-done.1, bf16[1024,768]{1,0:T(8,128)(2,1)S(1)} %get-tuple-element.112.dq_ref, bf16[1024,768]{1,0:T(8,128)(2,1)S(1)} %get-tuple-element.113.dk_ref, bf16[1024,768]{1,0:T(8,128)(2,1)S(1)} %get-tuple-element.114.dv_ref, ...), custom_call_target="tpu_custom_call", output_to_operand_aliasing={{}: (7, {})} | custom-call | flops 905969664 | bytes 1966080 | tf_op jit(solution)/shard_map/input_gradient/pallas_call | solution.py:536
  131.8 0.6 collective-permute-done.28
  132.4 0.9 collective-permute-start.29
  133.4 1.9 %input_gradient.7 = bf16[1024,768]{1,0:T(8,128)(2,1)} custom-call(bf16[1024,768]{1,0:T(8,128)(2,1)S(1)} %copy-done.1, bf16[1024,768]{1,0:T(8,128)(2,1)S(1)} %get-tuple-element.112.dq_ref, bf16[1024,768]{1,0:T(8,128)(2,1)S(1)} %get-tuple-element.113.dk_ref, bf16[1024,768]{1,0:T(8,128)(2,1)S(1)} %get-tuple-element.114.dv_ref, ...), custom_call_target="tpu_custom_call", output_to_operand_aliasing={{}: (7, {})} | custom-call | flops 905969664 | bytes 1966080 | tf_op jit(solution)/shard_map/input_gradient/pallas_call | solution.py:536
  135.3 2.2 %collective-permute-done.29.far_ref = bf16[32,768]{1,0:T(8,128)(2,1)S(1)} collective-permute-done((bf16[32,768]{1,0:T(8,128)(2,1)S(1)}, bf16[32,768]{1,0:T(8,128)(2,1)S(1)}, u32[]{:S(2)}, u32[]{:S(2)}) %collective-permute-start.29) | collective-permute-done | bytes 49184 | tf_op jit(solution)/shard_map/ppermute | solution.py:609
  137.5 1.0 adapter_update.1
  (76 shorter events, 0.2 us)
Async XLA Ops:
  0.6 19.2 %copy-start.7 = (bf16[192,768]{1,0:T(8,128)(2,1)S(1)}, bf16[192,768]{1,0:T(8,128)(2,1)}, u32[]{:S(2)}) copy-start(bf16[192,768]{1,0:T(8,128)(2,1)} %rest_0_.4) | copy-start | bytes 884740
  0.6 22.5 %copy-start.9 = (bf16[192,768]{1,0:T(8,128)(2,1)S(1)}, bf16[192,768]{1,0:T(8,128)(2,1)}, u32[]{:S(2)}) copy-start(bf16[192,768]{1,0:T(8,128)(2,1)} %rest_2_.2) | copy-start | bytes 884740
  0.7 19.2 %copy-start.8 = (bf16[192,768]{1,0:T(8,128)(2,1)S(1)}, bf16[192,768]{1,0:T(8,128)(2,1)}, u32[]{:S(2)}) copy-start(bf16[192,768]{1,0:T(8,128)(2,1)} %rest_1_.4) | copy-start | bytes 884740
  1.7 12.9 %collective-permute-start = (bf16[96,768]{1,0:T(8,128)(2,1)S(1)}, bf16[96,768]{1,0:T(8,128)(2,1)S(1)}, u32[]{:S(2)}, u32[]{:S(2)}) collective-permute-start(bf16[96,768]{1,0:T(8,128)(2,1)S(1)} %constant_dynamic-slice_fusion.2), channel_id=1, source_target_pairs={{0,16},{8,24},{16,0},{24,8},{1,17},{9,25},{17,1},{25,9},{2,18},{10... | collective-permute-start | bytes 442376 | tf_op jit(solution)/shard_map/ppermute | solution.py:609
  5.6 6.8 %collective-permute-start.11 = (bf16[96,768]{1,0:T(8,128)(2,1)S(1)}, bf16[96,768]{1,0:T(8,128)(2,1)S(1)}, u32[]{:S(2)}, u32[]{:S(2)}) collective-permute-start(bf16[96,768]{1,0:T(8,128)(2,1)S(1)} %constant_dynamic-slice_fusion), channel_id=1, source_target_pairs={{0,16},{8,24},{16,0},{24,8},{1,17},{9,25},{17,1},{25,9},{2,18},{10... | collective-permute-start | bytes 442376 | tf_op jit(solution)/shard_map/ppermute | solution.py:609
  6.6 9.5 %collective-permute-start.7 = (bf16[96,768]{1,0:T(8,128)(2,1)S(1)}, bf16[96,768]{1,0:T(8,128)(2,1)S(1)}, u32[]{:S(2)}, u32[]{:S(2)}) collective-permute-start(bf16[96,768]{1,0:T(8,128)(2,1)S(1)} %constant_dynamic-slice_fusion.1), channel_id=1, source_target_pairs={{0,16},{8,24},{16,0},{24,8},{1,17},{9,25},{17,1},{25,9},{2,18},{10... | collective-permute-start | bytes 442376 | tf_op jit(solution)/shard_map/ppermute | solution.py:609
  12.5 13.7 %copy-start.14 = (bf16[96,768]{1,0:T(8,128)(2,1)}, bf16[96,768]{1,0:T(8,128)(2,1)S(1)}, u32[]{:S(2)}) copy-start(bf16[96,768]{1,0:T(8,128)(2,1)S(1)} %collective-permute-done.11.rest_14_) | copy-start | bytes 442372
  12.5 28.4 %collective-permute-start.15 = (bf16[5,96,768]{2,1,0:T(8,128)(2,1)}, bf16[5,96,768]{2,1,0:T(8,128)(2,1)}, u32[]{:S(2)}, u32[]{:S(2)}) collective-permute-start(bf16[5,96,768]{2,1,0:T(8,128)(2,1)} %get-tuple-element.79), channel_id=1, source_target_pairs={{0,16},{8,24},{16,0},{24,8},{1,17},{9,25},{17,1},{25,9},{2,18},{10... | collective-permute-start | bytes 2211848 | tf_op jit(solution)/shard_map/ppermute | solution.py:609
  14.6 11.5 %copy-start.13 = (bf16[96,768]{1,0:T(8,128)(2,1)}, bf16[96,768]{1,0:T(8,128)(2,1)S(1)}, u32[]{:S(2)}) copy-start(bf16[96,768]{1,0:T(8,128)(2,1)S(1)} %collective-permute-done.rest_6_) | copy-start | bytes 442372
  14.6 3.3 %collective-permute-start.4 = (bf16[96,768]{1,0:T(8,128)(2,1)S(1)}, bf16[96,768]{1,0:T(8,128)(2,1)S(1)}, u32[]{:S(2)}, u32[]{:S(2)}) collective-permute-start(bf16[96,768]{1,0:T(8,128)(2,1)S(1)} %collective-permute-done.rest_6_), channel_id=1, source_target_pairs={{0,8},{8,0},{16,24},{24,16},{1,9},{9,1},{17,25},{25,17},{2,10},{10... | collective-permute-start | bytes 442376 | tf_op jit(solution)/shard_map/ppermute | solution.py:609
  14.6 5.2 %collective-permute-start.5 = (bf16[96,768]{1,0:T(8,128)(2,1)S(1)}, bf16[96,768]{1,0:T(8,128)(2,1)S(1)}, u32[]{:S(2)}, u32[]{:S(2)}) collective-permute-start(bf16[96,768]{1,0:T(8,128)(2,1)S(1)} %collective-permute-done.rest_6_), channel_id=1, source_target_pairs={{0,1},{1,0},{2,3},{3,2},{4,5},{5,4},{6,7},{7,6},{8,10},{9,11},{10,... | collective-permute-start | bytes 442376 | tf_op jit(solution)/shard_map/ppermute | solution.py:618
  16.2 10.0 %copy-start.15 = (bf16[96,768]{1,0:T(8,128)(2,1)}, bf16[96,768]{1,0:T(8,128)(2,1)S(1)}, u32[]{:S(2)}) copy-start(bf16[96,768]{1,0:T(8,128)(2,1)S(1)} %collective-permute-done.7.rest_10_) | copy-start | bytes 442372
  16.2 3.7 %collective-permute-start.8 = (bf16[96,768]{1,0:T(8,128)(2,1)S(1)}, bf16[96,768]{1,0:T(8,128)(2,1)S(1)}, u32[]{:S(2)}, u32[]{:S(2)}) collective-permute-start(bf16[96,768]{1,0:T(8,128)(2,1)S(1)} %collective-permute-done.7.rest_10_), channel_id=1, source_target_pairs={{0,8},{8,0},{16,24},{24,16},{1,9},{9,1},{17,25},{25,17},{2,10},{10... | collective-permute-start | bytes 442376 | tf_op jit(solution)/shard_map/ppermute | solution.py:609
  16.4 5.1 %collective-permute-start.9 = (bf16[96,768]{1,0:T(8,128)(2,1)S(1)}, bf16[96,768]{1,0:T(8,128)(2,1)S(1)}, u32[]{:S(2)}, u32[]{:S(2)}) collective-permute-start(bf16[96,768]{1,0:T(8,128)(2,1)S(1)} %collective-permute-done.7.rest_10_), channel_id=1, source_target_pairs={{0,1},{1,0},{2,3},{3,2},{4,5},{5,4},{6,7},{7,6},{8,10},{9,11},{10,... | collective-permute-start | bytes 442376 | tf_op jit(solution)/shard_map/ppermute | solution.py:618
  17.9 8.2 %copy-start.16 = (bf16[96,768]{1,0:T(8,128)(2,1)}, bf16[96,768]{1,0:T(8,128)(2,1)S(1)}, u32[]{:S(2)}) copy-start(bf16[96,768]{1,0:T(8,128)(2,1)S(1)} %collective-permute-done.4.rest_7_) | copy-start | bytes 442372
  17.9 5.2 %collective-permute-start.13 = (bf16[96,768]{1,0:T(8,128)(2,1)S(1)}, bf16[96,768]{1,0:T(8,128)(2,1)S(1)}, u32[]{:S(2)}, u32[]{:S(2)}) collective-permute-start(bf16[96,768]{1,0:T(8,128)(2,1)S(1)} %collective-permute-done.11.rest_14_), channel_id=1, source_target_pairs={{0,1},{1,0},{2,3},{3,2},{4,5},{5,4},{6,7},{7,6},{8,10},{9,11},{10,... | collective-permute-start | bytes 442376 | tf_op jit(solution)/shard_map/ppermute | solution.py:618
  19.8 6.3 %copy-start.17 = (bf16[96,768]{1,0:T(8,128)(2,1)}, bf16[96,768]{1,0:T(8,128)(2,1)S(1)}, u32[]{:S(2)}) copy-start(bf16[96,768]{1,0:T(8,128)(2,1)S(1)} %collective-permute-done.5.rest_8_) | copy-start | bytes 442372
  19.8 3.8 %collective-permute-start.1 = (bf16[192,768]{1,0:T(8,128)(2,1)S(1)}, bf16[192,768]{1,0:T(8,128)(2,1)S(1)}, u32[]{:S(2)}, u32[]{:S(2)}) collective-permute-start(bf16[192,768]{1,0:T(8,128)(2,1)S(1)} %copy-done.7), channel_id=1, source_target_pairs={{0,8},{8,0},{16,24},{24,16},{1,9},{9,1},{17,25},{25,17},{2,10},{10... | collective-permute-start | bytes 884744 | tf_op jit(solution)/shard_map/ppermute | solution.py:609
  19.9 6.3 %copy-start.18 = (bf16[96,768]{1,0:T(8,128)(2,1)}, bf16[96,768]{1,0:T(8,128)(2,1)S(1)}, u32[]{:S(2)}) copy-start(bf16[96,768]{1,0:T(8,128)(2,1)S(1)} %collective-permute-done.8.rest_11_) | copy-start | bytes 442372
  19.9 3.9 %collective-permute-start.2 = (bf16[192,768]{1,0:T(8,128)(2,1)S(1)}, bf16[192,768]{1,0:T(8,128)(2,1)S(1)}, u32[]{:S(2)}, u32[]{:S(2)}) collective-permute-start(bf16[192,768]{1,0:T(8,128)(2,1)S(1)} %copy-done.8), channel_id=1, source_target_pairs={{0,8},{8,0},{16,24},{24,16},{1,9},{9,1},{17,25},{25,17},{2,10},{10... | collective-permute-start | bytes 884744 | tf_op jit(solution)/shard_map/ppermute | solution.py:609
  21.6 4.6 %copy-start.19 = (bf16[96,768]{1,0:T(8,128)(2,1)}, bf16[96,768]{1,0:T(8,128)(2,1)S(1)}, u32[]{:S(2)}) copy-start(bf16[96,768]{1,0:T(8,128)(2,1)S(1)} %collective-permute-done.9.rest_12_) | copy-start | bytes 442372
  21.6 1.6 %collective-permute-start.12 = (bf16[96,768]{1,0:T(8,128)(2,1)S(1)}, bf16[96,768]{1,0:T(8,128)(2,1)S(1)}, u32[]{:S(2)}, u32[]{:S(2)}) collective-permute-start(bf16[96,768]{1,0:T(8,128)(2,1)S(1)} %collective-permute-done.11.rest_14_), channel_id=1, source_target_pairs={{0,8},{8,0},{16,24},{24,16},{1,9},{9,1},{17,25},{25,17},{2,10},{10... | collective-permute-start | bytes 442376 | tf_op jit(solution)/shard_map/ppermute | solution.py:609
  23.1 3.0 %copy-start.20 = (bf16[96,768]{1,0:T(8,128)(2,1)}, bf16[96,768]{1,0:T(8,128)(2,1)S(1)}, u32[]{:S(2)}) copy-start(bf16[96,768]{1,0:T(8,128)(2,1)S(1)} %collective-permute-done.13.rest_16_) | copy-start | bytes 442372
  23.2 1.6 %collective-permute-start.3 = (bf16[192,768]{1,0:T(8,128)(2,1)S(1)}, bf16[192,768]{1,0:T(8,128)(2,1)S(1)}, u32[]{:S(2)}, u32[]{:S(2)}) collective-permute-start(bf16[192,768]{1,0:T(8,128)(2,1)S(1)} %copy-done.9), channel_id=1, source_target_pairs={{0,8},{8,0},{16,24},{24,16},{1,9},{9,1},{17,25},{25,17},{2,10},{10... | collective-permute-start | bytes 884744 | tf_op jit(solution)/shard_map/ppermute | solution.py:609
  23.2 3.0 %copy-start.21 = (bf16[96,768]{1,0:T(8,128)(2,1)}, bf16[96,768]{1,0:T(8,128)(2,1)S(1)}, u32[]{:S(2)}) copy-start(bf16[96,768]{1,0:T(8,128)(2,1)S(1)} %collective-permute-done.12.rest_15_) | copy-start | bytes 442372
  23.2 2.9 %collective-permute-start.6 = (bf16[96,768]{1,0:T(8,128)(2,1)S(1)}, bf16[96,768]{1,0:T(8,128)(2,1)S(1)}, u32[]{:S(2)}, u32[]{:S(2)}) collective-permute-start(bf16[96,768]{1,0:T(8,128)(2,1)S(1)} %collective-permute-done.5.rest_8_), channel_id=1, source_target_pairs={{0,8},{8,0},{16,24},{24,16},{1,9},{9,1},{17,25},{25,17},{2,10},{10... | collective-permute-start | bytes 442376 | tf_op jit(solution)/shard_map/ppermute | solution.py:609
  23.7 2.5 %copy-start.10 = (bf16[192,768]{1,0:T(8,128)(2,1)}, bf16[192,768]{1,0:T(8,128)(2,1)S(1)}, u32[]{:S(2)}) copy-start(bf16[192,768]{1,0:T(8,128)(2,1)S(1)} %collective-permute-done.1.rest_3_) | copy-start | bytes 884740
  23.7 2.4 %collective-permute-start.10 = (bf16[96,768]{1,0:T(8,128)(2,1)S(1)}, bf16[96,768]{1,0:T(8,128)(2,1)S(1)}, u32[]{:S(2)}, u32[]{:S(2)}) collective-permute-start(bf16[96,768]{1,0:T(8,128)(2,1)S(1)} %collective-permute-done.9.rest_12_), channel_id=1, source_target_pairs={{0,8},{8,0},{16,24},{24,16},{1,9},{9,1},{17,25},{25,17},{2,10},{10... | collective-permute-start | bytes 442376 | tf_op jit(solution)/shard_map/ppermute | solution.py:609
  23.8 2.5 %copy-start.11 = (bf16[192,768]{1,0:T(8,128)(2,1)}, bf16[192,768]{1,0:T(8,128)(2,1)S(1)}, u32[]{:S(2)}) copy-start(bf16[192,768]{1,0:T(8,128)(2,1)S(1)} %collective-permute-done.2.rest_4_) | copy-start | bytes 884740
  23.8 2.3 %collective-permute-start.14 = (bf16[96,768]{1,0:T(8,128)(2,1)S(1)}, bf16[96,768]{1,0:T(8,128)(2,1)S(1)}, u32[]{:S(2)}, u32[]{:S(2)}) collective-permute-start(bf16[96,768]{1,0:T(8,128)(2,1)S(1)} %collective-permute-done.13.rest_16_), channel_id=1, source_target_pairs={{0,8},{8,0},{16,24},{24,16},{1,9},{9,1},{17,25},{25,17},{2,10},{10... | collective-permute-start | bytes 442376 | tf_op jit(solution)/shard_map/ppermute | solution.py:609
  24.7 1.5 %copy-start.12 = (bf16[192,768]{1,0:T(8,128)(2,1)}, bf16[192,768]{1,0:T(8,128)(2,1)S(1)}, u32[]{:S(2)}) copy-start(bf16[192,768]{1,0:T(8,128)(2,1)S(1)} %collective-permute-done.3.rest_5_) | copy-start | bytes 884740
  24.7 31.8 %collective-permute-start.20 = (bf16[768,768]{1,0:T(8,128)(2,1)}, bf16[768,768]{1,0:T(8,128)(2,1)}, u32[]{:S(2)}, u32[]{:S(2)}) collective-permute-start(bf16[768,768]{1,0:T(8,128)(2,1)} %rest_14_.1), channel_id=1, source_target_pairs={{0,16},{8,24},{16,0},{24,8},{1,17},{9,25},{17,1},{25,9},{2,18},{10... | collective-permute-start | bytes 3538952 | tf_op jit(solution)/shard_map/ppermute | solution.py:609
  26.1 0.6 copy-start.22
  26.1 0.7 copy-start.23
  26.1 0.7 copy-start.24
  40.9 1.6 %copy-start.25 = (bf16[2,5,96,768]{3,2,1,0:T(8,128)(2,1)S(1)}, bf16[2,5,96,768]{3,2,1,0:T(8,128)(2,1)}, u32[]{:S(2)}) copy-start(bf16[2,5,96,768]{3,2,1,0:T(8,128)(2,1)} %get-tuple-element.89) | copy-start | bytes 4423684
  41.0 15.6 %collective-permute-start.19 = (bf16[5,96,768]{2,1,0:T(8,128)(2,1)}, bf16[5,96,768]{2,1,0:T(8,128)(2,1)}, u32[]{:S(2)}, u32[]{:S(2)}) collective-permute-start(bf16[5,96,768]{2,1,0:T(8,128)(2,1)} %gate.2.rest_10_), channel_id=1, source_target_pairs={{0,1},{1,0},{2,3},{3,2},{4,5},{5,4},{6,7},{7,6},{8,10},{9,11},{10,... | collective-permute-start | bytes 2211848 | tf_op jit(solution)/shard_map/ppermute | solution.py:618
  42.5 17.0 %collective-permute-start.16 = (bf16[2,5,96,768]{3,2,1,0:T(8,128)(2,1)S(1)}, bf16[2,5,96,768]{3,2,1,0:T(8,128)(2,1)S(1)}, u32[]{:S(2)}, u32[]{:S(2)}) collective-permute-start(bf16[2,5,96,768]{3,2,1,0:T(8,128)(2,1)S(1)} %copy-done.25), channel_id=1, source_target_pairs={{0,8},{8,0},{16,24},{24,16},{1,9},{9,1},{17,25},{25,17},{2,10},{10... | collective-permute-start | bytes 4423688 | tf_op jit(solution)/shard_map/ppermute | solution.py:609
  42.5 13.7 %collective-permute-start.18 = (f32[1,2,24,128]{3,2,1,0:T(8,128)S(1)}, f32[1,2,24,128]{3,2,1,0:T(8,128)S(1)}, u32[]{:S(2)}, u32[]{:S(2)}) collective-permute-start(f32[1,2,24,128]{3,2,1,0:T(8,128)S(1)} %pad_maximum_fusion), channel_id=1, source_target_pairs={{0,1},{1,0},{2,3},{3,2},{4,5},{5,4},{6,7},{7,6},{8,9},{9,8},{10,11... | collective-permute-start | bytes 73736 | tf_op jit(solution)/shard_map/ppermute | solution.py:609
  43.8 13.3 %collective-permute-start.17 = (bf16[5,96,768]{2,1,0:T(8,128)(2,1)}, bf16[5,96,768]{2,1,0:T(8,128)(2,1)}, u32[]{:S(2)}, u32[]{:S(2)}) collective-permute-start(bf16[5,96,768]{2,1,0:T(8,128)(2,1)} %gate.2.rest_10_), channel_id=1, source_target_pairs={{0,8},{8,0},{16,24},{24,16},{1,9},{9,1},{17,25},{25,17},{2,10},{10... | collective-permute-start | bytes 2211848 | tf_op jit(solution)/shard_map/ppermute | solution.py:609
  56.2 3.3 %collective-permute-start.22 = (bf16[768,768]{1,0:T(8,128)(2,1)}, bf16[768,768]{1,0:T(8,128)(2,1)}, u32[]{:S(2)}, u32[]{:S(2)}) collective-permute-start(bf16[768,768]{1,0:T(8,128)(2,1)} %rest_14_.1), channel_id=1, source_target_pairs={{0,8},{8,0},{16,24},{24,16},{1,9},{9,1},{17,25},{25,17},{2,10},{10... | collective-permute-start | bytes 3538952 | tf_op jit(solution)/shard_map/ppermute | solution.py:609
  56.6 5.6 %collective-permute-start.23 = (bf16[768,768]{1,0:T(8,128)(2,1)}, bf16[768,768]{1,0:T(8,128)(2,1)}, u32[]{:S(2)}, u32[]{:S(2)}) collective-permute-start(bf16[768,768]{1,0:T(8,128)(2,1)} %collective-permute-done.20.rest_16_), channel_id=1, source_target_pairs={{0,8},{8,0},{16,24},{24,16},{1,9},{9,1},{17,25},{25,17},{2,10},{10... | collective-permute-start | bytes 3538952 | tf_op jit(solution)/shard_map/ppermute | solution.py:609
  56.8 5.4 %collective-permute-start.21 = (bf16[5,96,768]{2,1,0:T(8,128)(2,1)}, bf16[5,96,768]{2,1,0:T(8,128)(2,1)}, u32[]{:S(2)}, u32[]{:S(2)}) collective-permute-start(bf16[5,96,768]{2,1,0:T(8,128)(2,1)} %collective-permute-done.19.rest_12_), channel_id=1, source_target_pairs={{0,8},{8,0},{16,24},{24,16},{1,9},{9,1},{17,25},{25,17},{2,10},{10... | collective-permute-start | bytes 2211848 | tf_op jit(solution)/shard_map/ppermute | solution.py:609
  57.1 38.7 %collective-permute-start.24 = (f32[2,2,24,128]{3,2,1,0:T(8,128)S(1)}, f32[2,2,24,128]{3,2,1,0:T(8,128)S(1)}, u32[]{:S(2)}, u32[]{:S(2)}) collective-permute-start(f32[2,2,24,128]{3,2,1,0:T(8,128)S(1)} %constant_dynamic-update-slice_fusion), channel_id=1, source_target_pairs={{0,2},{1,3},{2,0},{3,1},{4,6},{5,7},{6,4},{7,5},{8,10},{9,11},{10,... | collective-permute-start | bytes 147464 | tf_op jit(solution)/shard_map/ppermute | solution.py:609
  59.5 2.7 %copy-start.26 = (bf16[2,5,96,768]{3,2,1,0:T(8,128)(2,1)}, bf16[2,5,96,768]{3,2,1,0:T(8,128)(2,1)S(1)}, u32[]{:S(2)}) copy-start(bf16[2,5,96,768]{3,2,1,0:T(8,128)(2,1)S(1)} %collective-permute-done.16.rest_9_) | copy-start | bytes 4423684
  62.2 33.5 %copy-start.2 = (bf16[1024,768]{1,0:T(8,128)(2,1)S(1)}, bf16[1024,768]{1,0:T(8,128)(2,1)}, u32[]{:S(2)}) copy-start(bf16[1024,768]{1,0:T(8,128)(2,1)} %x_ref.7) | copy-start | bytes 4718596
  62.2 33.5 %copy-start.3 = (f32[24576]{0:T(1024)S(1)}, f32[24576]{0:T(1024)}, u32[]{:S(2)}) copy-start(f32[24576]{0:T(1024)} %param.39) | copy-start | bytes 294916
  62.2 33.5 %copy-start.4 = (bf16[1024,768]{1,0:T(8,128)(2,1)S(1)}, bf16[1024,768]{1,0:T(8,128)(2,1)}, u32[]{:S(2)}) copy-start(bf16[1024,768]{1,0:T(8,128)(2,1)} %get-tuple-element.100.rest_0_) | copy-start | bytes 4718596
  62.2 33.5 %copy-start.5 = (bf16[1024,768]{1,0:T(8,128)(2,1)S(1)}, bf16[1024,768]{1,0:T(8,128)(2,1)}, u32[]{:S(2)}) copy-start(bf16[1024,768]{1,0:T(8,128)(2,1)} %get-tuple-element.101.rest_1_) | copy-start | bytes 4718596
  62.3 33.5 %copy-start.6 = (bf16[1024,16]{1,0:T(8,128)(2,1)S(1)}, bf16[1024,16]{1,0:T(8,128)(2,1)}, u32[]{:S(2)}) copy-start(bf16[1024,16]{1,0:T(8,128)(2,1)} %get-tuple-element.94.other_ref.down_ref) | copy-start | bytes 98308
  95.8 24.9 %copy-start = (bf16[3,768,768]{2,1,0:T(8,128)(2,1)S(1)}, bf16[3,768,768]{2,1,0:T(8,128)(2,1)}, u32[]{:S(2)}) copy-start(bf16[3,768,768]{2,1,0:T(8,128)(2,1)} %get-tuple-element.80.rest_0_.other_ref.weights) | copy-start | bytes 10616836
  95.8 24.9 %copy-start.1 = (bf16[1024,768]{1,0:T(8,128)(2,1)S(1)}, bf16[1024,768]{1,0:T(8,128)(2,1)}, u32[]{:S(2)}) copy-start(bf16[1024,768]{1,0:T(8,128)(2,1)} %get-tuple-element.125.dh_ref) | copy-start | bytes 4718596
  116.9 3.0 %collective-permute-start.25 = (bf16[32,768]{1,0:T(8,128)(2,1)S(1)}, bf16[32,768]{1,0:T(8,128)(2,1)S(1)}, u32[]{:S(2)}, u32[]{:S(2)}) collective-permute-start(bf16[32,768]{1,0:T(8,128)(2,1)S(1)} %get-tuple-element.109), channel_id=1, source_target_pairs={{0,8},{8,0},{16,24},{24,16},{1,9},{9,1},{17,25},{25,17},{2,10},{10... | collective-permute-start | bytes 147464 | tf_op jit(solution)/shard_map/ppermute | solution.py:609
  117.2 18.0 %collective-permute-start.30 = (f32[4,2,24,128]{3,2,1,0:T(8,128)S(1)}, f32[4,2,24,128]{3,2,1,0:T(8,128)S(1)}, u32[]{:S(2)}, u32[]{:S(2)}) collective-permute-start(f32[4,2,24,128]{3,2,1,0:T(8,128)S(1)} %constant_dynamic-update-slice_fusion.2.held_ref), channel_id=1, source_target_pairs={{0,4},{1,5},{2,6},{3,7},{4,0},{5,1},{6,2},{7,3},{8,12},{9,13},{10,... | collective-permute-start | bytes 294920 | tf_op jit(solution)/shard_map/ppermute | solution.py:609
  119.9 4.2 %collective-permute-start.26 = (bf16[32,768]{1,0:T(8,128)(2,1)S(1)}, bf16[32,768]{1,0:T(8,128)(2,1)S(1)}, u32[]{:S(2)}, u32[]{:S(2)}) collective-permute-start(bf16[32,768]{1,0:T(8,128)(2,1)S(1)} %add.18), channel_id=1, source_target_pairs={{0,16},{8,24},{16,0},{24,8},{1,17},{9,25},{17,1},{25,9},{2,18},{10... | collective-permute-start | bytes 147464 | tf_op jit(solution)/shard_map/ppermute | solution.py:609
  124.1 4.2 %collective-permute-start.27 = (bf16[32,768]{1,0:T(8,128)(2,1)S(1)}, bf16[32,768]{1,0:T(8,128)(2,1)S(1)}, u32[]{:S(2)}, u32[]{:S(2)}) collective-permute-start(bf16[32,768]{1,0:T(8,128)(2,1)S(1)} %add.19), channel_id=1, source_target_pairs={{0,1},{1,0},{2,3},{3,2},{4,5},{5,4},{6,7},{7,6},{8,9},{9,8},{10,11... | collective-permute-start | bytes 147464 | tf_op jit(solution)/shard_map/ppermute | solution.py:609
  128.3 4.2 %collective-permute-start.28 = (bf16[32,768]{1,0:T(8,128)(2,1)S(1)}, bf16[32,768]{1,0:T(8,128)(2,1)S(1)}, u32[]{:S(2)}, u32[]{:S(2)}) collective-permute-start(bf16[32,768]{1,0:T(8,128)(2,1)S(1)} %add.20), channel_id=1, source_target_pairs={{0,2},{1,3},{2,0},{3,1},{4,6},{5,7},{6,4},{7,5},{8,10},{9,11},{10,... | collective-permute-start | bytes 147464 | tf_op jit(solution)/shard_map/ppermute | solution.py:609
  132.4 5.1 %collective-permute-start.29 = (bf16[32,768]{1,0:T(8,128)(2,1)S(1)}, bf16[32,768]{1,0:T(8,128)(2,1)S(1)}, u32[]{:S(2)}, u32[]{:S(2)}) collective-permute-start(bf16[32,768]{1,0:T(8,128)(2,1)S(1)} %add.21.near_ref), channel_id=1, source_target_pairs={{0,4},{1,5},{2,6},{3,7},{4,0},{5,1},{6,2},{7,3},{8,12},{9,13},{10,... | collective-permute-start | bytes 147464 | tf_op jit(solution)/shard_map/ppermute | solution.py:609

commit v7 on v6

--- a/solution.py
+++ b/solution.py
@@ -720,7 +720,7 @@
     halves_ahead = fetch(mine_ahead, reps)
 
     early = packs // 2
-    arguments = (rank, place, segment_ids, tokens, table, b_query, b_value, 3)
+    arguments = (rank, place, segment_ids, tokens, table, b_query, b_value, 2)
     *attended, weights = attend(*arguments, 0, early, heads)
     weights, *values = together(weights, *[value for _, value in halves_ahead])
     values = [gate(value, weights, GATE) for value in values]

time: 139 us -> 138 us (level)
  transfers between devices with their start and end apart: 31 -> 31, of which waited for: 11 -> 12; matrix products, arithmetic and copies ran while one was open for 2% -> 2% of each run, Pallas kernels for 51% -> 50%
where the time goes in v7:
time: 138 us
  Pallas kernels  91.6 us (66%)
  starting transfers between devices  27 us (20%)
  waiting for transfers between devices  13.9 us (10%)
  local copies, waits for them, and re-layouts  3.57 us (3%)
    pallas_call x1, Pallas kernels, dense(): pl.pallas_call(functools.partial(dense_kernel, first, second, cut), grid=...  33.5 us
    pallas_call x2, Pallas kernels, attend(): pl.pallas_call(functools.partial(attend_kernel, parts, first), grid=(coun...  25.6 us
    ppermute x27, starting transfers between devices, swap(): return lax.ppermute(value, axis, [(i, i ^ flip) for i in range(size)])  21.8 us
    pallas_call x1, Pallas kernels, attend_back(): pl.pallas_call(attend_back_kernel, grid=(packs, width // cut), in_specs=[...  21 us
    ppermute x27, waiting for transfers between devices, swap(): return lax.ppermute(value, axis, [(i, i ^ flip) for i in range(size)])  9.75 us
    pallas_call x4, Pallas kernels, input_back(): pl.pallas_call(functools.partial(input_kernel, at * size), grid=(1,), in_...  7.6 us
    ppermute x4, starting transfers between devices, cross(): return lax.ppermute(value, ('rep', 'wide'), pairs)  5.14 us
    ppermute x4, waiting for transfers between devices, cross(): return lax.ppermute(value, ('rep', 'wide'), pairs)  4.1 us
  transfers between devices with their start and end apart: 31, of which 12 were waited for; matrix products, arithmetic and copies ran while one was open for 2% of the time, Pallas kernels for 50%

profile of v7, /device:TPU:0, one launch (start us, length us, event | category | flops | bytes accessed | tf_op | source)
XLA Modules:
  0.0 137.9 jit_solution(13460028727051718136)
XLA Ops:
  0.6 0.0 copy-start.7
  0.6 0.0 copy-start.9
  0.7 0.0 copy-start.8
  0.7 1.0 constant_dynamic-slice_fusion.2
  1.7 3.0 %collective-permute-start = (bf16[96,768]{1,0:T(8,128)(2,1)S(1)}, bf16[96,768]{1,0:T(8,128)(2,1)S(1)}, u32[]{:S(2)}, u32[]{:S(2)}) collective-permute-start(bf16[96,768]{1,0:T(8,128)(2,1)S(1)} %constant_dynamic-slice_fusion.2), channel_id=1, source_target_pairs={{0,16},{8,24},{16,0},{24,8},{1,17},{9,25},{17,1},{25,9},{2,18},{10... | collective-permute-start | bytes 442376 | tf_op jit(solution)/shard_map/ppermute | solution.py:609
  4.7 0.9 constant_dynamic-slice_fusion
  5.6 0.1 collective-permute-start.11
  5.7 0.9 constant_dynamic-slice_fusion.1
  6.6 2.1 %collective-permute-start.7 = (bf16[96,768]{1,0:T(8,128)(2,1)S(1)}, bf16[96,768]{1,0:T(8,128)(2,1)S(1)}, u32[]{:S(2)}, u32[]{:S(2)}) collective-permute-start(bf16[96,768]{1,0:T(8,128)(2,1)S(1)} %constant_dynamic-slice_fusion.1), channel_id=1, source_target_pairs={{0,16},{8,24},{16,0},{24,8},{1,17},{9,25},{17,1},{25,9},{2,18},{10... | collective-permute-start | bytes 442376 | tf_op jit(solution)/shard_map/ppermute | solution.py:609
  8.7 0.7 pad_maximum_fusion
  9.4 2.9 %pack_shards.1 = (bf16[2,5,96,768]{3,2,1,0:T(8,128)(2,1)}, bf16[5,96,768]{2,1,0:T(8,128)(2,1)}) custom-call(s32[1]{0:T(128)} %bitcast.1.place_ref, bf16[192,768]{1,0:T(8,128)(2,1)} %rest_7_.1, bf16[192,3072]{1,0:T(8,128)(2,1)} %rest_8_.1), custom_call_target="tpu_custom_call" | custom-call | tf_op jit(solution)/shard_map/pack_shards/pallas_call | solution.py:169
  12.3 0.1 collective-permute-done.11.rest_14_
  12.5 2.1 %collective-permute-start.15 = (bf16[5,96,768]{2,1,0:T(8,128)(2,1)}, bf16[5,96,768]{2,1,0:T(8,128)(2,1)}, u32[]{:S(2)}, u32[]{:S(2)}) collective-permute-start(bf16[5,96,768]{2,1,0:T(8,128)(2,1)} %get-tuple-element.79), channel_id=1, source_target_pairs={{0,16},{8,24},{16,0},{24,8},{1,17},{9,25},{17,1},{25,9},{2,18},{10... | collective-permute-start | bytes 2211848 | tf_op jit(solution)/shard_map/ppermute | solution.py:609
  14.6 0.0 collective-permute-done.rest_6_
  14.6 0.0 collective-permute-start.4
  14.6 1.6 %collective-permute-start.5 = (bf16[96,768]{1,0:T(8,128)(2,1)S(1)}, bf16[96,768]{1,0:T(8,128)(2,1)S(1)}, u32[]{:S(2)}, u32[]{:S(2)}) collective-permute-start(bf16[96,768]{1,0:T(8,128)(2,1)S(1)} %collective-permute-done.rest_6_), channel_id=1, source_target_pairs={{0,1},{1,0},{2,3},{3,2},{4,5},{5,4},{6,7},{7,6},{8,10},{9,11},{10,... | collective-permute-start | bytes 442376 | tf_op jit(solution)/shard_map/ppermute | solution.py:618
  16.2 0.2 collective-permute-start.8
  16.4 1.5 %collective-permute-start.9 = (bf16[96,768]{1,0:T(8,128)(2,1)S(1)}, bf16[96,768]{1,0:T(8,128)(2,1)S(1)}, u32[]{:S(2)}, u32[]{:S(2)}) collective-permute-start(bf16[96,768]{1,0:T(8,128)(2,1)S(1)} %collective-permute-done.7.rest_10_), channel_id=1, source_target_pairs={{0,1},{1,0},{2,3},{3,2},{4,5},{5,4},{6,7},{7,6},{8,10},{9,11},{10,... | collective-permute-start | bytes 442376 | tf_op jit(solution)/shard_map/ppermute | solution.py:618
  17.9 0.5 collective-permute-start.13
  18.5 1.4 collective-permute-done.5.rest_8_
  19.8 0.0 collective-permute-start.1
  19.9 0.5 collective-permute-start.2
  20.4 1.2 collective-permute-done.9.rest_12_
  21.6 1.6 %collective-permute-done.13.rest_16_ = bf16[96,768]{1,0:T(8,128)(2,1)S(1)} collective-permute-done((bf16[96,768]{1,0:T(8,128)(2,1)S(1)}, bf16[96,768]{1,0:T(8,128)(2,1)S(1)}, u32[]{:S(2)}, u32[]{:S(2)}) %collective-permute-start.13) | collective-permute-done | bytes 147488 | tf_op jit(solution)/shard_map/ppermute | solution.py:618
  23.2 0.5 collective-permute-start.6
  23.7 0.1 collective-permute-start.10
  23.8 0.4 collective-permute-start.14
  24.2 0.5 collective-permute-done.3.rest_5_
  24.7 1.3 collective-permute-start.20
  26.2 0.5 copy-done.22
  26.7 0.1 copy-done.23
  26.8 0.1 copy-done.24
  26.8 13.7 %project_and_attend.2 = (bf16[1024,768]{1,0:T(8,128)(2,1)}, bf16[1024,768]{1,0:T(8,128)(2,1)}, bf16[1024,768]{1,0:T(8,128)(2,1)}, bf16[1024,768]{1,0:T(8,128)(2,...) custom-call(s32[1]{0:T(128)} %bitcast.rank_ref, ...), custom_call_target="tpu_custom_call" | custom-call | flops 1 | bytes 1 | tf_op jit(solution)/shard_map/project_and_attend/pallas_call | solution.py:281
  40.6 0.0 copy-start.25
  40.6 1.6 %collective-permute-start.19 = (bf16[5,96,768]{2,1,0:T(8,128)(2,1)}, bf16[5,96,768]{2,1,0:T(8,128)(2,1)}, u32[]{:S(2)}, u32[]{:S(2)}) collective-permute-start(bf16[5,96,768]{2,1,0:T(8,128)(2,1)} %gate.2.rest_10_), channel_id=1, source_target_pairs={{0,1},{1,0},{2,3},{3,2},{4,5},{5,4},{6,7},{7,6},{8,10},{9,11},{10,... | collective-permute-start | bytes 2211848 | tf_op jit(solution)/shard_map/ppermute | solution.py:618
  42.1 1.3 collective-permute-start.18
  43.4 0.2 collective-permute-start.17
  43.7 11.9 %project_and_attend.3 = (bf16[1024,768]{1,0:T(8,128)(2,1)}, bf16[1024,768]{1,0:T(8,128)(2,1)}, bf16[1024,768]{1,0:T(8,128)(2,1)}, bf16[1024,768]{1,0:T(8,128)(2,...) custom-call(s32[1]{0:T(128)} %bitcast.rank_ref, ...), custom_call_target="tpu_custom_call", output_to_operand_aliasing={{0}: (8, {}), {1}: (9, {}), {2}: (10, {}), {3}: (11, {}), {... | custom-call | flops 6000000000 | bytes 1 | tf_op jit(solution)/shard_map/project_and_attend/pallas_call | solution.py:281
  55.6 0.3 collective-permute-start.22
  55.9 0.1 collective-permute-done.20.rest_16_
  56.1 0.1 collective-permute-start.23
  56.2 0.4 collective-permute-start.21
  56.6 1.9 %collective-permute-start.24 = (f32[2,2,24,128]{3,2,1,0:T(8,128)S(1)}, f32[2,2,24,128]{3,2,1,0:T(8,128)S(1)}, u32[]{:S(2)}, u32[]{:S(2)}) collective-permute-start(f32[2,2,24,128]{3,2,1,0:T(8,128)S(1)} %constant_dynamic-update-slice_fusion), channel_id=1, source_target_pairs={{0,2},{1,3},{2,0},{3,1},{4,6},{5,7},{6,4},{7,5},{8,10},{9,11},{10,... | collective-permute-start | bytes 147464 | tf_op jit(solution)/shard_map/ppermute | solution.py:609
  58.5 0.4 collective-permute-done.22.rest_15_
  58.9 2.7 %collective-permute-done.21.rest_13_ = bf16[5,96,768]{2,1,0:T(8,128)(2,1)} collective-permute-done((bf16[5,96,768]{2,1,0:T(8,128)(2,1)}, bf16[5,96,768]{2,1,0:T(8,128)(2,1)}, u32[]{:S(2)}, u32[]{:S(2)}) %collective-permute-start.21) | collective-permute-done | bytes 737312 | tf_op jit(solution)/shard_map/ppermute | solution.py:609
  61.6 0.0 copy-start.3
  61.6 0.0 copy-start.4
  61.6 33.5 %dense_both_ways.1 = (bf16[1024,768]{1,0:T(8,128)(2,1)}, bf16[1024,768]{1,0:T(8,128)(2,1)}, bf16[1024,768]{1,0:T(8,128)(2,1)}) custom-call(s32[1]{0:T(128)} %bitcast.rank_ref, s32[1]{0:T(128)} %bitcast.1.place_ref, bf16[1024,768]{1,0:T(8,128)(2,1)} %x_ref.7, bf16[1024,768]{1,0:T(8,128)(2,1)} %get-tuple-element.88.ctx_ref.rest_4_, bf16[1024,768]{1,0:T(8,128)(2,1)} %cot_ref.1, ...), custom_call_target="tpu_custom_call" | custom-call | flops 21743271936 | bytes 18874368 | tf_op jit(solution)/shard_map/dense_both_ways/pallas_call | solution.py:382
  95.2 21.0 %attend_back.1 = (bf16[1024,768]{1,0:T(8,128)(2,1)S(1)}, bf16[1024,768]{1,0:T(8,128)(2,1)S(1)}, bf16[1024,768]{1,0:T(8,128)(2,1)S(1)}, bf16[1024,16]{1,0:T(8,128)(2,1)S(1)}, bf16[32,768]{1,0:T(8,128)(2,1)S(1)}) custom-call(bf16[1024,768]{1,0:T(8,128)(2,1)S(1)} %copy-done.2, f32[192,128]{1,0:T(8,128)S(1)} %bitcast.12, bf16[1024,16]{1,0:T(8,128)(2,1)S(1)} %copy-done.6, ...), custom_call_target="tpu_custom_call" | custom-call | flops 12079595520 | bytes 18874368 | tf_op jit(solution)/shard_map/attend_back/pallas_call | solution.py:486
  116.3 0.3 collective-permute-start.25
  116.6 2.7 %collective-permute-start.30 = (f32[4,2,24,128]{3,2,1,0:T(8,128)S(1)}, f32[4,2,24,128]{3,2,1,0:T(8,128)S(1)}, u32[]{:S(2)}, u32[]{:S(2)}) collective-permute-start(f32[4,2,24,128]{3,2,1,0:T(8,128)S(1)} %constant_dynamic-update-slice_fusion.2.held_ref), channel_id=1, source_target_pairs={{0,4},{1,5},{2,6},{3,7},{4,0},{5,1},{6,2},{7,3},{8,12},{9,13},{10,... | collective-permute-start | bytes 294920 | tf_op jit(solution)/shard_map/ppermute | solution.py:609
  119.3 0.8 collective-permute-start.26
  120.1 1.9 %input_gradient.4.rest_0_ = bf16[1024,768]{1,0:T(8,128)(2,1)} custom-call(bf16[1024,768]{1,0:T(8,128)(2,1)S(1)} %copy-done.1, bf16[1024,768]{1,0:T(8,128)(2,1)S(1)} %get-tuple-element.112.dq_ref, bf16[1024,768]{1,0:T(8,128)(2,1)S(1)} %get-tuple-element.113.dk_ref, bf16[1024,768]{1,0:T(8,128)(2,1)S(1)} %get-tuple-element.114.dv_ref, ...), custom_call_target="tpu_custom_call" | custom-call | flops 905969664 | bytes 1966080 | tf_op jit(solution)/shard_map/input_gradient/pallas_call | solution.py:536
  122.0 1.5 %collective-permute-done.26 = bf16[32,768]{1,0:T(8,128)(2,1)S(1)} collective-permute-done((bf16[32,768]{1,0:T(8,128)(2,1)S(1)}, bf16[32,768]{1,0:T(8,128)(2,1)S(1)}, u32[]{:S(2)}, u32[]{:S(2)}) %collective-permute-start.26) | collective-permute-done | bytes 49184 | tf_op jit(solution)/shard_map/ppermute | solution.py:609
  123.5 0.8 collective-permute-start.27
  124.3 1.9 %input_gradient.5.rest_0_ = bf16[1024,768]{1,0:T(8,128)(2,1)} custom-call(bf16[1024,768]{1,0:T(8,128)(2,1)S(1)} %copy-done.1, bf16[1024,768]{1,0:T(8,128)(2,1)S(1)} %get-tuple-element.112.dq_ref, bf16[1024,768]{1,0:T(8,128)(2,1)S(1)} %get-tuple-element.113.dk_ref, bf16[1024,768]{1,0:T(8,128)(2,1)S(1)} %get-tuple-element.114.dv_ref, ...), custom_call_target="tpu_custom_call", output_to_operand_aliasing={{}: (7, {})} | custom-call | flops 905969664 | bytes 1966080 | tf_op jit(solution)/shard_map/input_gradient/pallas_call | solution.py:536
  126.2 1.4 %collective-permute-done.27 = bf16[32,768]{1,0:T(8,128)(2,1)S(1)} collective-permute-done((bf16[32,768]{1,0:T(8,128)(2,1)S(1)}, bf16[32,768]{1,0:T(8,128)(2,1)S(1)}, u32[]{:S(2)}, u32[]{:S(2)}) %collective-permute-start.27) | collective-permute-done | bytes 49184 | tf_op jit(solution)/shard_map/ppermute | solution.py:609
  127.7 1.6 %collective-permute-start.28 = (bf16[32,768]{1,0:T(8,128)(2,1)S(1)}, bf16[32,768]{1,0:T(8,128)(2,1)S(1)}, u32[]{:S(2)}, u32[]{:S(2)}) collective-permute-start(bf16[32,768]{1,0:T(8,128)(2,1)S(1)} %add.20), channel_id=1, source_target_pairs={{0,2},{1,3},{2,0},{3,1},{4,6},{5,7},{6,4},{7,5},{8,10},{9,11},{10,... | collective-permute-start | bytes 147464 | tf_op jit(solution)/shard_map/ppermute | solution.py:609
  129.3 1.9 %input_gradient.6.rest_0_ = bf16[1024,768]{1,0:T(8,128)(2,1)} custom-call(bf16[1024,768]{1,0:T(8,128)(2,1)S(1)} %copy-done.1, bf16[1024,768]{1,0:T(8,128)(2,1)S(1)} %get-tuple-element.112.dq_ref, bf16[1024,768]{1,0:T(8,128)(2,1)S(1)} %get-tuple-element.113.dk_ref, bf16[1024,768]{1,0:T(8,128)(2,1)S(1)} %get-tuple-element.114.dv_ref, ...), custom_call_target="tpu_custom_call", output_to_operand_aliasing={{}: (7, {})} | custom-call | flops 905969664 | bytes 1966080 | tf_op jit(solution)/shard_map/input_gradient/pallas_call | solution.py:536
  131.2 0.6 collective-permute-done.28
  131.8 0.9 collective-permute-start.29
  132.8 1.9 %input_gradient.7 = bf16[1024,768]{1,0:T(8,128)(2,1)} custom-call(bf16[1024,768]{1,0:T(8,128)(2,1)S(1)} %copy-done.1, bf16[1024,768]{1,0:T(8,128)(2,1)S(1)} %get-tuple-element.112.dq_ref, bf16[1024,768]{1,0:T(8,128)(2,1)S(1)} %get-tuple-element.113.dk_ref, bf16[1024,768]{1,0:T(8,128)(2,1)S(1)} %get-tuple-element.114.dv_ref, ...), custom_call_target="tpu_custom_call", output_to_operand_aliasing={{}: (7, {})} | custom-call | flops 905969664 | bytes 1966080 | tf_op jit(solution)/shard_map/input_gradient/pallas_call | solution.py:536
  134.7 2.2 %collective-permute-done.29.far_ref = bf16[32,768]{1,0:T(8,128)(2,1)S(1)} collective-permute-done((bf16[32,768]{1,0:T(8,128)(2,1)S(1)}, bf16[32,768]{1,0:T(8,128)(2,1)S(1)}, u32[]{:S(2)}, u32[]{:S(2)}) %collective-permute-start.29) | collective-permute-done | bytes 49184 | tf_op jit(solution)/shard_map/ppermute | solution.py:609
  136.9 1.0 adapter_update.1
  (76 shorter events, 0.2 us)
Async XLA Ops:
  0.6 19.2 %copy-start.7 = (bf16[192,768]{1,0:T(8,128)(2,1)S(1)}, bf16[192,768]{1,0:T(8,128)(2,1)}, u32[]{:S(2)}) copy-start(bf16[192,768]{1,0:T(8,128)(2,1)} %rest_0_.4) | copy-start | bytes 884740
  0.6 22.5 %copy-start.9 = (bf16[192,768]{1,0:T(8,128)(2,1)S(1)}, bf16[192,768]{1,0:T(8,128)(2,1)}, u32[]{:S(2)}) copy-start(bf16[192,768]{1,0:T(8,128)(2,1)} %rest_2_.2) | copy-start | bytes 884740
  0.7 19.2 %copy-start.8 = (bf16[192,768]{1,0:T(8,128)(2,1)S(1)}, bf16[192,768]{1,0:T(8,128)(2,1)}, u32[]{:S(2)}) copy-start(bf16[192,768]{1,0:T(8,128)(2,1)} %rest_1_.4) | copy-start | bytes 884740
  1.7 12.9 %collective-permute-start = (bf16[96,768]{1,0:T(8,128)(2,1)S(1)}, bf16[96,768]{1,0:T(8,128)(2,1)S(1)}, u32[]{:S(2)}, u32[]{:S(2)}) collective-permute-start(bf16[96,768]{1,0:T(8,128)(2,1)S(1)} %constant_dynamic-slice_fusion.2), channel_id=1, source_target_pairs={{0,16},{8,24},{16,0},{24,8},{1,17},{9,25},{17,1},{25,9},{2,18},{10... | collective-permute-start | bytes 442376 | tf_op jit(solution)/shard_map/ppermute | solution.py:609
  5.6 6.8 %collective-permute-start.11 = (bf16[96,768]{1,0:T(8,128)(2,1)S(1)}, bf16[96,768]{1,0:T(8,128)(2,1)S(1)}, u32[]{:S(2)}, u32[]{:S(2)}) collective-permute-start(bf16[96,768]{1,0:T(8,128)(2,1)S(1)} %constant_dynamic-slice_fusion), channel_id=1, source_target_pairs={{0,16},{8,24},{16,0},{24,8},{1,17},{9,25},{17,1},{25,9},{2,18},{10... | collective-permute-start | bytes 442376 | tf_op jit(solution)/shard_map/ppermute | solution.py:609
  6.6 9.5 %collective-permute-start.7 = (bf16[96,768]{1,0:T(8,128)(2,1)S(1)}, bf16[96,768]{1,0:T(8,128)(2,1)S(1)}, u32[]{:S(2)}, u32[]{:S(2)}) collective-permute-start(bf16[96,768]{1,0:T(8,128)(2,1)S(1)} %constant_dynamic-slice_fusion.1), channel_id=1, source_target_pairs={{0,16},{8,24},{16,0},{24,8},{1,17},{9,25},{17,1},{25,9},{2,18},{10... | collective-permute-start | bytes 442376 | tf_op jit(solution)/shard_map/ppermute | solution.py:609
  12.5 13.7 %copy-start.14 = (bf16[96,768]{1,0:T(8,128)(2,1)}, bf16[96,768]{1,0:T(8,128)(2,1)S(1)}, u32[]{:S(2)}) copy-start(bf16[96,768]{1,0:T(8,128)(2,1)S(1)} %collective-permute-done.11.rest_14_) | copy-start | bytes 442372
  12.5 28.1 %collective-permute-start.15 = (bf16[5,96,768]{2,1,0:T(8,128)(2,1)}, bf16[5,96,768]{2,1,0:T(8,128)(2,1)}, u32[]{:S(2)}, u32[]{:S(2)}) collective-permute-start(bf16[5,96,768]{2,1,0:T(8,128)(2,1)} %get-tuple-element.79), channel_id=1, source_target_pairs={{0,16},{8,24},{16,0},{24,8},{1,17},{9,25},{17,1},{25,9},{2,18},{10... | collective-permute-start | bytes 2211848 | tf_op jit(solution)/shard_map/ppermute | solution.py:609
  14.6 11.5 %copy-start.13 = (bf16[96,768]{1,0:T(8,128)(2,1)}, bf16[96,768]{1,0:T(8,128)(2,1)S(1)}, u32[]{:S(2)}) copy-start(bf16[96,768]{1,0:T(8,128)(2,1)S(1)} %collective-permute-done.rest_6_) | copy-start | bytes 442372
  14.6 3.3 %collective-permute-start.4 = (bf16[96,768]{1,0:T(8,128)(2,1)S(1)}, bf16[96,768]{1,0:T(8,128)(2,1)S(1)}, u32[]{:S(2)}, u32[]{:S(2)}) collective-permute-start(bf16[96,768]{1,0:T(8,128)(2,1)S(1)} %collective-permute-done.rest_6_), channel_id=1, source_target_pairs={{0,8},{8,0},{16,24},{24,16},{1,9},{9,1},{17,25},{25,17},{2,10},{10... | collective-permute-start | bytes 442376 | tf_op jit(solution)/shard_map/ppermute | solution.py:609
  14.6 5.2 %collective-permute-start.5 = (bf16[96,768]{1,0:T(8,128)(2,1)S(1)}, bf16[96,768]{1,0:T(8,128)(2,1)S(1)}, u32[]{:S(2)}, u32[]{:S(2)}) collective-permute-start(bf16[96,768]{1,0:T(8,128)(2,1)S(1)} %collective-permute-done.rest_6_), channel_id=1, source_target_pairs={{0,1},{1,0},{2,3},{3,2},{4,5},{5,4},{6,7},{7,6},{8,10},{9,11},{10,... | collective-permute-start | bytes 442376 | tf_op jit(solution)/shard_map/ppermute | solution.py:618
  16.2 10.0 %copy-start.15 = (bf16[96,768]{1,0:T(8,128)(2,1)}, bf16[96,768]{1,0:T(8,128)(2,1)S(1)}, u32[]{:S(2)}) copy-start(bf16[96,768]{1,0:T(8,128)(2,1)S(1)} %collective-permute-done.7.rest_10_) | copy-start | bytes 442372
  16.2 3.7 %collective-permute-start.8 = (bf16[96,768]{1,0:T(8,128)(2,1)S(1)}, bf16[96,768]{1,0:T(8,128)(2,1)S(1)}, u32[]{:S(2)}, u32[]{:S(2)}) collective-permute-start(bf16[96,768]{1,0:T(8,128)(2,1)S(1)} %collective-permute-done.7.rest_10_), channel_id=1, source_target_pairs={{0,8},{8,0},{16,24},{24,16},{1,9},{9,1},{17,25},{25,17},{2,10},{10... | collective-permute-start | bytes 442376 | tf_op jit(solution)/shard_map/ppermute | solution.py:609
  16.4 5.1 %collective-permute-start.9 = (bf16[96,768]{1,0:T(8,128)(2,1)S(1)}, bf16[96,768]{1,0:T(8,128)(2,1)S(1)}, u32[]{:S(2)}, u32[]{:S(2)}) collective-permute-start(bf16[96,768]{1,0:T(8,128)(2,1)S(1)} %collective-permute-done.7.rest_10_), channel_id=1, source_target_pairs={{0,1},{1,0},{2,3},{3,2},{4,5},{5,4},{6,7},{7,6},{8,10},{9,11},{10,... | collective-permute-start | bytes 442376 | tf_op jit(solution)/shard_map/ppermute | solution.py:618
  17.9 8.2 %copy-start.16 = (bf16[96,768]{1,0:T(8,128)(2,1)}, bf16[96,768]{1,0:T(8,128)(2,1)S(1)}, u32[]{:S(2)}) copy-start(bf16[96,768]{1,0:T(8,128)(2,1)S(1)} %collective-permute-done.4.rest_7_) | copy-start | bytes 442372
  17.9 5.2 %collective-permute-start.13 = (bf16[96,768]{1,0:T(8,128)(2,1)S(1)}, bf16[96,768]{1,0:T(8,128)(2,1)S(1)}, u32[]{:S(2)}, u32[]{:S(2)}) collective-permute-start(bf16[96,768]{1,0:T(8,128)(2,1)S(1)} %collective-permute-done.11.rest_14_), channel_id=1, source_target_pairs={{0,1},{1,0},{2,3},{3,2},{4,5},{5,4},{6,7},{7,6},{8,10},{9,11},{10,... | collective-permute-start | bytes 442376 | tf_op jit(solution)/shard_map/ppermute | solution.py:618
  19.8 6.3 %copy-start.17 = (bf16[96,768]{1,0:T(8,128)(2,1)}, bf16[96,768]{1,0:T(8,128)(2,1)S(1)}, u32[]{:S(2)}) copy-start(bf16[96,768]{1,0:T(8,128)(2,1)S(1)} %collective-permute-done.5.rest_8_) | copy-start | bytes 442372
  19.8 3.8 %collective-permute-start.1 = (bf16[192,768]{1,0:T(8,128)(2,1)S(1)}, bf16[192,768]{1,0:T(8,128)(2,1)S(1)}, u32[]{:S(2)}, u32[]{:S(2)}) collective-permute-start(bf16[192,768]{1,0:T(8,128)(2,1)S(1)} %copy-done.7), channel_id=1, source_target_pairs={{0,8},{8,0},{16,24},{24,16},{1,9},{9,1},{17,25},{25,17},{2,10},{10... | collective-permute-start | bytes 884744 | tf_op jit(solution)/shard_map/ppermute | solution.py:609
  19.9 6.3 %copy-start.18 = (bf16[96,768]{1,0:T(8,128)(2,1)}, bf16[96,768]{1,0:T(8,128)(2,1)S(1)}, u32[]{:S(2)}) copy-start(bf16[96,768]{1,0:T(8,128)(2,1)S(1)} %collective-permute-done.8.rest_11_) | copy-start | bytes 442372
  19.9 3.9 %collective-permute-start.2 = (bf16[192,768]{1,0:T(8,128)(2,1)S(1)}, bf16[192,768]{1,0:T(8,128)(2,1)S(1)}, u32[]{:S(2)}, u32[]{:S(2)}) collective-permute-start(bf16[192,768]{1,0:T(8,128)(2,1)S(1)} %copy-done.8), channel_id=1, source_target_pairs={{0,8},{8,0},{16,24},{24,16},{1,9},{9,1},{17,25},{25,17},{2,10},{10... | collective-permute-start | bytes 884744 | tf_op jit(solution)/shard_map/ppermute | solution.py:609
  21.6 4.6 %copy-start.19 = (bf16[96,768]{1,0:T(8,128)(2,1)}, bf16[96,768]{1,0:T(8,128)(2,1)S(1)}, u32[]{:S(2)}) copy-start(bf16[96,768]{1,0:T(8,128)(2,1)S(1)} %collective-permute-done.9.rest_12_) | copy-start | bytes 442372
  21.6 1.6 %collective-permute-start.12 = (bf16[96,768]{1,0:T(8,128)(2,1)S(1)}, bf16[96,768]{1,0:T(8,128)(2,1)S(1)}, u32[]{:S(2)}, u32[]{:S(2)}) collective-permute-start(bf16[96,768]{1,0:T(8,128)(2,1)S(1)} %collective-permute-done.11.rest_14_), channel_id=1, source_target_pairs={{0,8},{8,0},{16,24},{24,16},{1,9},{9,1},{17,25},{25,17},{2,10},{10... | collective-permute-start | bytes 442376 | tf_op jit(solution)/shard_map/ppermute | solution.py:609
  23.1 3.0 %copy-start.20 = (bf16[96,768]{1,0:T(8,128)(2,1)}, bf16[96,768]{1,0:T(8,128)(2,1)S(1)}, u32[]{:S(2)}) copy-start(bf16[96,768]{1,0:T(8,128)(2,1)S(1)} %collective-permute-done.13.rest_16_) | copy-start | bytes 442372
  23.2 1.6 %collective-permute-start.3 = (bf16[192,768]{1,0:T(8,128)(2,1)S(1)}, bf16[192,768]{1,0:T(8,128)(2,1)S(1)}, u32[]{:S(2)}, u32[]{:S(2)}) collective-permute-start(bf16[192,768]{1,0:T(8,128)(2,1)S(1)} %copy-done.9), channel_id=1, source_target_pairs={{0,8},{8,0},{16,24},{24,16},{1,9},{9,1},{17,25},{25,17},{2,10},{10... | collective-permute-start | bytes 884744 | tf_op jit(solution)/shard_map/ppermute | solution.py:609
  23.2 3.0 %copy-start.21 = (bf16[96,768]{1,0:T(8,128)(2,1)}, bf16[96,768]{1,0:T(8,128)(2,1)S(1)}, u32[]{:S(2)}) copy-start(bf16[96,768]{1,0:T(8,128)(2,1)S(1)} %collective-permute-done.12.rest_15_) | copy-start | bytes 442372
  23.2 2.9 %collective-permute-start.6 = (bf16[96,768]{1,0:T(8,128)(2,1)S(1)}, bf16[96,768]{1,0:T(8,128)(2,1)S(1)}, u32[]{:S(2)}, u32[]{:S(2)}) collective-permute-start(bf16[96,768]{1,0:T(8,128)(2,1)S(1)} %collective-permute-done.5.rest_8_), channel_id=1, source_target_pairs={{0,8},{8,0},{16,24},{24,16},{1,9},{9,1},{17,25},{25,17},{2,10},{10... | collective-permute-start | bytes 442376 | tf_op jit(solution)/shard_map/ppermute | solution.py:609
  23.7 2.5 %copy-start.10 = (bf16[192,768]{1,0:T(8,128)(2,1)}, bf16[192,768]{1,0:T(8,128)(2,1)S(1)}, u32[]{:S(2)}) copy-start(bf16[192,768]{1,0:T(8,128)(2,1)S(1)} %collective-permute-done.1.rest_3_) | copy-start | bytes 884740
  23.7 2.4 %collective-permute-start.10 = (bf16[96,768]{1,0:T(8,128)(2,1)S(1)}, bf16[96,768]{1,0:T(8,128)(2,1)S(1)}, u32[]{:S(2)}, u32[]{:S(2)}) collective-permute-start(bf16[96,768]{1,0:T(8,128)(2,1)S(1)} %collective-permute-done.9.rest_12_), channel_id=1, source_target_pairs={{0,8},{8,0},{16,24},{24,16},{1,9},{9,1},{17,25},{25,17},{2,10},{10... | collective-permute-start | bytes 442376 | tf_op jit(solution)/shard_map/ppermute | solution.py:609
  23.8 2.5 %copy-start.11 = (bf16[192,768]{1,0:T(8,128)(2,1)}, bf16[192,768]{1,0:T(8,128)(2,1)S(1)}, u32[]{:S(2)}) copy-start(bf16[192,768]{1,0:T(8,128)(2,1)S(1)} %collective-permute-done.2.rest_4_) | copy-start | bytes 884740
  23.8 2.3 %collective-permute-start.14 = (bf16[96,768]{1,0:T(8,128)(2,1)S(1)}, bf16[96,768]{1,0:T(8,128)(2,1)S(1)}, u32[]{:S(2)}, u32[]{:S(2)}) collective-permute-start(bf16[96,768]{1,0:T(8,128)(2,1)S(1)} %collective-permute-done.13.rest_16_), channel_id=1, source_target_pairs={{0,8},{8,0},{16,24},{24,16},{1,9},{9,1},{17,25},{25,17},{2,10},{10... | collective-permute-start | bytes 442376 | tf_op jit(solution)/shard_map/ppermute | solution.py:609
  24.7 1.5 %copy-start.12 = (bf16[192,768]{1,0:T(8,128)(2,1)}, bf16[192,768]{1,0:T(8,128)(2,1)S(1)}, u32[]{:S(2)}) copy-start(bf16[192,768]{1,0:T(8,128)(2,1)S(1)} %collective-permute-done.3.rest_5_) | copy-start | bytes 884740
  24.7 31.3 %collective-permute-start.20 = (bf16[768,768]{1,0:T(8,128)(2,1)}, bf16[768,768]{1,0:T(8,128)(2,1)}, u32[]{:S(2)}, u32[]{:S(2)}) collective-permute-start(bf16[768,768]{1,0:T(8,128)(2,1)} %rest_14_.1), channel_id=1, source_target_pairs={{0,16},{8,24},{16,0},{24,8},{1,17},{9,25},{17,1},{25,9},{2,18},{10... | collective-permute-start | bytes 3538952 | tf_op jit(solution)/shard_map/ppermute | solution.py:609
  26.1 0.6 copy-start.22
  26.1 0.7 copy-start.23
  26.1 0.7 copy-start.24
  40.6 1.6 %copy-start.25 = (bf16[2,5,96,768]{3,2,1,0:T(8,128)(2,1)S(1)}, bf16[2,5,96,768]{3,2,1,0:T(8,128)(2,1)}, u32[]{:S(2)}) copy-start(bf16[2,5,96,768]{3,2,1,0:T(8,128)(2,1)} %get-tuple-element.89) | copy-start | bytes 4423684
  40.6 15.5 %collective-permute-start.19 = (bf16[5,96,768]{2,1,0:T(8,128)(2,1)}, bf16[5,96,768]{2,1,0:T(8,128)(2,1)}, u32[]{:S(2)}, u32[]{:S(2)}) collective-permute-start(bf16[5,96,768]{2,1,0:T(8,128)(2,1)} %gate.2.rest_10_), channel_id=1, source_target_pairs={{0,1},{1,0},{2,3},{3,2},{4,5},{5,4},{6,7},{7,6},{8,10},{9,11},{10,... | collective-permute-start | bytes 2211848 | tf_op jit(solution)/shard_map/ppermute | solution.py:618
  42.1 16.7 %collective-permute-start.16 = (bf16[2,5,96,768]{3,2,1,0:T(8,128)(2,1)S(1)}, bf16[2,5,96,768]{3,2,1,0:T(8,128)(2,1)S(1)}, u32[]{:S(2)}, u32[]{:S(2)}) collective-permute-start(bf16[2,5,96,768]{3,2,1,0:T(8,128)(2,1)S(1)} %copy-done.25), channel_id=1, source_target_pairs={{0,8},{8,0},{16,24},{24,16},{1,9},{9,1},{17,25},{25,17},{2,10},{10... | collective-permute-start | bytes 4423688 | tf_op jit(solution)/shard_map/ppermute | solution.py:609
  42.1 13.4 %collective-permute-start.18 = (f32[1,2,24,128]{3,2,1,0:T(8,128)S(1)}, f32[1,2,24,128]{3,2,1,0:T(8,128)S(1)}, u32[]{:S(2)}, u32[]{:S(2)}) collective-permute-start(f32[1,2,24,128]{3,2,1,0:T(8,128)S(1)} %pad_maximum_fusion), channel_id=1, source_target_pairs={{0,1},{1,0},{2,3},{3,2},{4,5},{5,4},{6,7},{7,6},{8,9},{9,8},{10,11... | collective-permute-start | bytes 73736 | tf_op jit(solution)/shard_map/ppermute | solution.py:609
  43.4 13.1 %collective-permute-start.17 = (bf16[5,96,768]{2,1,0:T(8,128)(2,1)}, bf16[5,96,768]{2,1,0:T(8,128)(2,1)}, u32[]{:S(2)}, u32[]{:S(2)}) collective-permute-start(bf16[5,96,768]{2,1,0:T(8,128)(2,1)} %gate.2.rest_10_), channel_id=1, source_target_pairs={{0,8},{8,0},{16,24},{24,16},{1,9},{9,1},{17,25},{25,17},{2,10},{10... | collective-permute-start | bytes 2211848 | tf_op jit(solution)/shard_map/ppermute | solution.py:609
  55.6 3.3 %collective-permute-start.22 = (bf16[768,768]{1,0:T(8,128)(2,1)}, bf16[768,768]{1,0:T(8,128)(2,1)}, u32[]{:S(2)}, u32[]{:S(2)}) collective-permute-start(bf16[768,768]{1,0:T(8,128)(2,1)} %rest_14_.1), channel_id=1, source_target_pairs={{0,8},{8,0},{16,24},{24,16},{1,9},{9,1},{17,25},{25,17},{2,10},{10... | collective-permute-start | bytes 3538952 | tf_op jit(solution)/shard_map/ppermute | solution.py:609
  56.1 5.5 %collective-permute-start.23 = (bf16[768,768]{1,0:T(8,128)(2,1)}, bf16[768,768]{1,0:T(8,128)(2,1)}, u32[]{:S(2)}, u32[]{:S(2)}) collective-permute-start(bf16[768,768]{1,0:T(8,128)(2,1)} %collective-permute-done.20.rest_16_), channel_id=1, source_target_pairs={{0,8},{8,0},{16,24},{24,16},{1,9},{9,1},{17,25},{25,17},{2,10},{10... | collective-permute-start | bytes 3538952 | tf_op jit(solution)/shard_map/ppermute | solution.py:609
  56.2 5.4 %collective-permute-start.21 = (bf16[5,96,768]{2,1,0:T(8,128)(2,1)}, bf16[5,96,768]{2,1,0:T(8,128)(2,1)}, u32[]{:S(2)}, u32[]{:S(2)}) collective-permute-start(bf16[5,96,768]{2,1,0:T(8,128)(2,1)} %collective-permute-done.19.rest_12_), channel_id=1, source_target_pairs={{0,8},{8,0},{16,24},{24,16},{1,9},{9,1},{17,25},{25,17},{2,10},{10... | collective-permute-start | bytes 2211848 | tf_op jit(solution)/shard_map/ppermute | solution.py:609
  56.6 38.6 %collective-permute-start.24 = (f32[2,2,24,128]{3,2,1,0:T(8,128)S(1)}, f32[2,2,24,128]{3,2,1,0:T(8,128)S(1)}, u32[]{:S(2)}, u32[]{:S(2)}) collective-permute-start(f32[2,2,24,128]{3,2,1,0:T(8,128)S(1)} %constant_dynamic-update-slice_fusion), channel_id=1, source_target_pairs={{0,2},{1,3},{2,0},{3,1},{4,6},{5,7},{6,4},{7,5},{8,10},{9,11},{10,... | collective-permute-start | bytes 147464 | tf_op jit(solution)/shard_map/ppermute | solution.py:609
  58.9 2.7 %copy-start.26 = (bf16[2,5,96,768]{3,2,1,0:T(8,128)(2,1)}, bf16[2,5,96,768]{3,2,1,0:T(8,128)(2,1)S(1)}, u32[]{:S(2)}) copy-start(bf16[2,5,96,768]{3,2,1,0:T(8,128)(2,1)S(1)} %collective-permute-done.16.rest_9_) | copy-start | bytes 4423684
  61.6 33.6 %copy-start.2 = (bf16[1024,768]{1,0:T(8,128)(2,1)S(1)}, bf16[1024,768]{1,0:T(8,128)(2,1)}, u32[]{:S(2)}) copy-start(bf16[1024,768]{1,0:T(8,128)(2,1)} %x_ref.7) | copy-start | bytes 4718596
  61.6 33.6 %copy-start.3 = (f32[24576]{0:T(1024)S(1)}, f32[24576]{0:T(1024)}, u32[]{:S(2)}) copy-start(f32[24576]{0:T(1024)} %param.39) | copy-start | bytes 294916
  61.6 33.6 %copy-start.4 = (bf16[1024,768]{1,0:T(8,128)(2,1)S(1)}, bf16[1024,768]{1,0:T(8,128)(2,1)}, u32[]{:S(2)}) copy-start(bf16[1024,768]{1,0:T(8,128)(2,1)} %get-tuple-element.100.rest_0_) | copy-start | bytes 4718596
  61.6 33.6 %copy-start.5 = (bf16[1024,768]{1,0:T(8,128)(2,1)S(1)}, bf16[1024,768]{1,0:T(8,128)(2,1)}, u32[]{:S(2)}) copy-start(bf16[1024,768]{1,0:T(8,128)(2,1)} %get-tuple-element.101.rest_1_) | copy-start | bytes 4718596
  61.6 33.6 %copy-start.6 = (bf16[1024,16]{1,0:T(8,128)(2,1)S(1)}, bf16[1024,16]{1,0:T(8,128)(2,1)}, u32[]{:S(2)}) copy-start(bf16[1024,16]{1,0:T(8,128)(2,1)} %get-tuple-element.94.other_ref.down_ref) | copy-start | bytes 98308
  95.2 24.9 %copy-start = (bf16[3,768,768]{2,1,0:T(8,128)(2,1)S(1)}, bf16[3,768,768]{2,1,0:T(8,128)(2,1)}, u32[]{:S(2)}) copy-start(bf16[3,768,768]{2,1,0:T(8,128)(2,1)} %get-tuple-element.80.rest_0_.other_ref.weights) | copy-start | bytes 10616836
  95.2 24.9 %copy-start.1 = (bf16[1024,768]{1,0:T(8,128)(2,1)S(1)}, bf16[1024,768]{1,0:T(8,128)(2,1)}, u32[]{:S(2)}) copy-start(bf16[1024,768]{1,0:T(8,128)(2,1)} %get-tuple-element.125.dh_ref) | copy-start | bytes 4718596
  116.3 3.0 %collective-permute-start.25 = (bf16[32,768]{1,0:T(8,128)(2,1)S(1)}, bf16[32,768]{1,0:T(8,128)(2,1)S(1)}, u32[]{:S(2)}, u32[]{:S(2)}) collective-permute-start(bf16[32,768]{1,0:T(8,128)(2,1)S(1)} %get-tuple-element.109), channel_id=1, source_target_pairs={{0,8},{8,0},{16,24},{24,16},{1,9},{9,1},{17,25},{25,17},{2,10},{10... | collective-permute-start | bytes 147464 | tf_op jit(solution)/shard_map/ppermute | solution.py:609
  116.6 18.0 %collective-permute-start.30 = (f32[4,2,24,128]{3,2,1,0:T(8,128)S(1)}, f32[4,2,24,128]{3,2,1,0:T(8,128)S(1)}, u32[]{:S(2)}, u32[]{:S(2)}) collective-permute-start(f32[4,2,24,128]{3,2,1,0:T(8,128)S(1)} %constant_dynamic-update-slice_fusion.2.held_ref), channel_id=1, source_target_pairs={{0,4},{1,5},{2,6},{3,7},{4,0},{5,1},{6,2},{7,3},{8,12},{9,13},{10,... | collective-permute-start | bytes 294920 | tf_op jit(solution)/shard_map/ppermute | solution.py:609
  119.3 4.2 %collective-permute-start.26 = (bf16[32,768]{1,0:T(8,128)(2,1)S(1)}, bf16[32,768]{1,0:T(8,128)(2,1)S(1)}, u32[]{:S(2)}, u32[]{:S(2)}) collective-permute-start(bf16[32,768]{1,0:T(8,128)(2,1)S(1)} %add.18), channel_id=1, source_target_pairs={{0,16},{8,24},{16,0},{24,8},{1,17},{9,25},{17,1},{25,9},{2,18},{10... | collective-permute-start | bytes 147464 | tf_op jit(solution)/shard_map/ppermute | solution.py:609
  123.5 4.2 %collective-permute-start.27 = (bf16[32,768]{1,0:T(8,128)(2,1)S(1)}, bf16[32,768]{1,0:T(8,128)(2,1)S(1)}, u32[]{:S(2)}, u32[]{:S(2)}) collective-permute-start(bf16[32,768]{1,0:T(8,128)(2,1)S(1)} %add.19), channel_id=1, source_target_pairs={{0,1},{1,0},{2,3},{3,2},{4,5},{5,4},{6,7},{7,6},{8,9},{9,8},{10,11... | collective-permute-start | bytes 147464 | tf_op jit(solution)/shard_map/ppermute | solution.py:609
  127.7 4.2 %collective-permute-start.28 = (bf16[32,768]{1,0:T(8,128)(2,1)S(1)}, bf16[32,768]{1,0:T(8,128)(2,1)S(1)}, u32[]{:S(2)}, u32[]{:S(2)}) collective-permute-start(bf16[32,768]{1,0:T(8,128)(2,1)S(1)} %add.20), channel_id=1, source_target_pairs={{0,2},{1,3},{2,0},{3,1},{4,6},{5,7},{6,4},{7,5},{8,10},{9,11},{10,... | collective-permute-start | bytes 147464 | tf_op jit(solution)/shard_map/ppermute | solution.py:609
  131.8 5.1 %collective-permute-start.29 = (bf16[32,768]{1,0:T(8,128)(2,1)S(1)}, bf16[32,768]{1,0:T(8,128)(2,1)S(1)}, u32[]{:S(2)}, u32[]{:S(2)}) collective-permute-start(bf16[32,768]{1,0:T(8,128)(2,1)S(1)} %add.21.near_ref), channel_id=1, source_target_pairs={{0,4},{1,5},{2,6},{3,7},{4,0},{5,1},{6,2},{7,3},{8,12},{9,13},{10,... | collective-permute-start | bytes 147464 | tf_op jit(solution)/shard_map/ppermute | solution.py:609
